TPU v7x, 32 devices: a whole 2x2x4 slice. The times are simulated.
32 devices in a mesh: fsdp: 8 (over z, x), rep: 4 (over y, core).
Axes of the slice: x: 2, y: 2, z: 4, core: 2. Of those that a mesh axis runs over, the one named last changes fastest.
Arguments:
- tokens: bfloat16 [2, 2048, 2048], P(None, ('fsdp', 'rep')), may hold values from -6 to 6
- lengths: int32 [2, 32], P(None, ('fsdp', 'rep')), may hold values from 16 to 64, as said below
- offsets: int32 [2, 32], P(None, ('fsdp', 'rep')), may hold values from 0 to 48, as said below
- norm_gain: bfloat16 [2048], P(('fsdp', 'rep')), may hold values from 0.5 to 1.5
- mamba_in: bfloat16 [2048, 6704], P(('fsdp', 'rep')), may hold values from -0.125 to 0.125
- conv_taps: float32 [4, 3584], replicated, may hold values from -3 to 3
- conv_bias: float32 [3584], replicated, may hold values from -3 to 3
- step_bias: float32 [48], replicated, may hold values from -4 to -1
- decay_log: float32 [48], replicated, may hold values from -3 to 1
- skip_weight: float32 [48], replicated, may hold values from 0.5 to 1.5
- mamba_gain: float32 [3072], replicated, may hold values from 0.5 to 1.5
- mamba_out: bfloat16 [3072, 2048], P(None, ('fsdp', 'rep')), may hold values from -0.109375 to 0.109375
- query_weight: bfloat16 [2048, 1024], P(('fsdp', 'rep')), may hold values from -0.125 to 0.125
- key_weight: bfloat16 [2048, 256], P(('fsdp', 'rep')), may hold values from -0.125 to 0.125
- value_weight: bfloat16 [2048, 256], P(('fsdp', 'rep')), may hold values from -0.125 to 0.125
- output_weight: bfloat16 [1024, 2048], P(None, ('fsdp', 'rep')), may hold values from -0.75 to 0.75
- second_gain: bfloat16 [2048], P(('fsdp', 'rep')), may hold values from 0.5 to 1.5
- gate_weight: bfloat16 [2048, 4096], P(('fsdp', 'rep')), may hold values from -0.125 to 0.125
- up_weight: bfloat16 [2048, 4096], P(('fsdp', 'rep')), may hold values from -0.125 to 0.125
- down_weight: bfloat16 [4096, 2048], P(None, ('fsdp', 'rep')), may hold values from -0.09375 to 0.09375
- cotangent: bfloat16 [2, 2048, 2048], P(None, ('fsdp', 'rep')), may hold values from -6 to 6
Outputs:
- output: bfloat16 [2, 2048, 2048], P(None, ('fsdp', 'rep'))
- grad_tokens: float32 [2, 2048, 2048], P(None, ('fsdp', 'rep'))
- grad_norm_gain: float32 [2048], P(('fsdp', 'rep'))
- grad_mamba_in: float32 [2048, 6704], P(('fsdp', 'rep'))
- grad_conv_taps: float32 [4, 3584], replicated
- grad_conv_bias: float32 [3584], replicated
- grad_step_bias: float32 [48], replicated
- grad_decay_log: float32 [48], replicated
- grad_skip_weight: float32 [48], replicated
- grad_mamba_gain: float32 [3072], replicated
- grad_mamba_out: float32 [3072, 2048], P(None, ('fsdp', 'rep'))
- grad_query_weight: float32 [2048, 1024], P(('fsdp', 'rep'))
- grad_key_weight: float32 [2048, 256], P(('fsdp', 'rep'))
- grad_value_weight: float32 [2048, 256], P(('fsdp', 'rep'))
- grad_output_weight: float32 [1024, 2048], P(None, ('fsdp', 'rep'))
- grad_second_gain: float32 [2048], P(('fsdp', 'rep'))
- grad_gate_weight: float32 [2048, 4096], P(('fsdp', 'rep'))
- grad_up_weight: float32 [2048, 4096], P(('fsdp', 'rep'))
- grad_down_weight: float32 [4096, 2048], P(None, ('fsdp', 'rep'))
Inputs may be any that keep to these rules, and one draw needn't show every extreme that they name: `lengths`: each block holds a sequence of 16 to 64 tokens; in every draw some block holds exactly 64 and some exactly 16. offsets + lengths <= 64 in every block.
All inputs are finite; a program needn't handle non-finite values.
Results may differ from a plain program's by a relative error of at most 0.0095.
Values may be sent and summed in bfloat16 or wider, within the bound.
No kernel may reach another device: no remote copies, remote signals or barrier semaphores. Data moves between devices by JAX's collectives and lax.ppermute only.
A program may use at most 448 MiB of HBM per device.

v0:
```python
from functools import partial
import math

import jax
import jax.numpy as jnp
from jax import lax
from jax.sharding import PartitionSpec as P

QH = 8
KVH = 2
HD = 128


epsilon = 1e-05
rope_base = 100000000000.0
highest = lax.Precision.HIGHEST


def root_norm(values, gain):
    return values * lax.rsqrt(jnp.mean(values * values, axis=-1, keepdims=True) + epsilon) * gain


def swish_product(gate_act, up_act):
    return jax.nn.silu(gate_act) * up_act


def dense(left, weight):
    return jnp.dot(left, weight, preferred_element_type=jnp.float32)


def weight_grad(left, grad):
    return jnp.einsum("lf,lg->fg", left, grad, preferred_element_type=jnp.float32)


def input_grad(grad, weight):
    return jnp.einsum("lg,fg->lf", grad, weight, preferred_element_type=jnp.float32)


def layout(lengths, offsets, width):
    rows = jnp.arange(width, dtype=jnp.int32)
    starts = offsets[:, None]
    inside = (rows[None, :] >= starts) & (rows[None, :] < starts + lengths[:, None])
    causal = rows[:, None] >= rows[None, :]
    segment = inside[:, :, None] & inside[:, None, :] & causal[None]
    positions = (rows[None, :] - starts).astype(jnp.float32)
    return (inside.astype(jnp.float32), segment, positions)


def mamba_core(
    projected, conv_taps, conv_bias, step_bias, decay_log, skip_weight, mamba_gain, inside, segment
):
    inner = mamba_gain.shape[0]
    heads = step_bias.shape[0]
    state = (projected.shape[-1] - 2 * inner - heads) // 2
    taps = conv_taps.shape[0]
    batch = projected.shape[0]
    length = projected.shape[1]
    gate = projected[..., :inner]
    conv_in = projected[..., inner : 2 * inner + 2 * state] * inside[..., None]
    step_raw = projected[..., 2 * inner + 2 * state :]
    padded = jnp.pad(conv_in, ((0, 0), (taps - 1, 0), (0, 0)))
    convolved = conv_bias + jnp.zeros_like(conv_in)
    for tap in range(taps):
        convolved = convolved + conv_taps[tap] * padded[:, tap : tap + length]
    active = jax.nn.silu(convolved)
    head_values = active[..., :inner].reshape(batch, length, heads, inner // heads)
    b_state = active[..., inner : inner + state]
    c_state = active[..., inner + state :]
    step_size = jax.nn.softplus(step_raw + step_bias)
    cumulative = jnp.cumsum(step_size * -jnp.exp(decay_log), axis=1)
    spread = cumulative[:, :, None, :] - cumulative[:, None, :, :]
    allowed = segment[..., None]
    decay = jnp.where(allowed, jnp.exp(jnp.where(allowed, spread, 0.0)), 0.0)
    intersection = jnp.einsum("sin,sjn->sij", c_state, b_state, precision=highest)
    mixing = decay * intersection[..., None]
    scaled = head_values * step_size[..., None]
    result = jnp.einsum("sijh,sjhp->sihp", mixing, scaled, precision=highest)
    result = result + skip_weight[:, None] * head_values
    result = result.reshape(batch, length, inner) * jax.nn.silu(gate)
    return root_norm(result, mamba_gain)


def attention_core(queries, keys, values, positions, segment):
    batch = queries.shape[0]
    length = queries.shape[1]
    half = HD // 2
    freqs = rope_base ** (-jnp.arange(half, dtype=jnp.float32) * 2.0 / HD)
    angles = positions[..., None] * freqs
    cosine = jnp.cos(angles)[:, :, None, :]
    sine = jnp.sin(angles)[:, :, None, :]

    def rotate(tensor, heads):
        split = tensor.reshape(batch, length, heads, HD)
        first = split[..., :half]
        second = split[..., half:]
        return jnp.concatenate(
            [first * cosine - second * sine, first * sine + second * cosine], axis=-1
        )

    rot_query = rotate(queries, QH).reshape(batch, length, KVH, QH // KVH, HD)
    rot_key = rotate(keys, KVH)
    head_values = values.reshape(batch, length, KVH, HD)
    scores = jnp.einsum("sikgd,sjkd->skgij", rot_query, rot_key, precision=highest) / math.sqrt(HD)
    allowed = segment | jnp.eye(length, dtype=jnp.bool_)[None]
    scores = jnp.where(allowed[:, None, None], scores, -1e30)
    peak = jnp.max(scores, axis=-1, keepdims=True)
    probs = jnp.exp(scores - peak)
    probs = probs / jnp.sum(probs, axis=-1, keepdims=True)
    mixed = jnp.einsum("skgij,sjkd->sikgd", probs, head_values, precision=highest)
    return mixed.reshape(batch, length, QH * HD)


def local(
    tokens,
    lengths,
    offsets,
    norm_gain,
    mamba_in,
    conv_taps,
    conv_bias,
    step_bias,
    decay_log,
    skip_weight,
    mamba_gain,
    mamba_out,
    query_weight,
    key_weight,
    value_weight,
    output_weight,
    second_gain,
    gate_weight,
    up_weight,
    down_weight,
    cotangent,
):
    mixer_shards = (
        norm_gain,
        mamba_in,
        query_weight,
        key_weight,
        value_weight,
        mamba_out,
        output_weight,
    )
    mlp_shards = (second_gain, gate_weight, up_weight, down_weight)
    batches = tokens.shape[0]
    width = tokens.shape[1]
    model_width = tokens.shape[2]
    total_rows = batches * width
    inside, segment, positions = layout(lengths[:, 0], offsets[:, 0], width)
    mask_col = inside.reshape(total_rows, 1)
    mixer_full = (
        lax.all_gather(mixer_shards[0], ("fsdp", "rep"), axis=0, tiled=True),
        lax.all_gather(mixer_shards[1], ("fsdp", "rep"), axis=0, tiled=True),
        lax.all_gather(mixer_shards[2], ("fsdp", "rep"), axis=0, tiled=True),
        lax.all_gather(mixer_shards[3], ("fsdp", "rep"), axis=0, tiled=True),
        lax.all_gather(mixer_shards[4], ("fsdp", "rep"), axis=0, tiled=True),
        lax.all_gather(mixer_shards[5], ("fsdp", "rep"), axis=1, tiled=True),
        lax.all_gather(mixer_shards[6], ("fsdp", "rep"), axis=1, tiled=True),
    )
    source = tokens.astype(jnp.float32).reshape(total_rows, model_width)
    normed_f, norm_pull = jax.vjp(root_norm, source, mixer_full[0].astype(jnp.float32))
    normed = normed_f.astype(jnp.bfloat16)
    projected = dense(normed, mixer_full[1])
    queries = dense(normed, mixer_full[2])
    keys = dense(normed, mixer_full[3])
    values = dense(normed, mixer_full[4])
    mamba_f, mamba_pull = jax.vjp(
        partial(mamba_core, inside=inside, segment=segment),
        projected.reshape(batches, width, -1),
        conv_taps,
        conv_bias,
        step_bias,
        decay_log,
        skip_weight,
        mamba_gain,
    )
    mamba_norm = mamba_f.reshape(total_rows, -1).astype(jnp.bfloat16)
    attn_f, attn_pull = jax.vjp(
        partial(attention_core, positions=positions, segment=segment),
        queries.reshape(batches, width, -1),
        keys.reshape(batches, width, -1),
        values.reshape(batches, width, -1),
    )
    attn_mix = attn_f.reshape(total_rows, -1).astype(jnp.bfloat16)
    hidden = source + mask_col * (dense(mamba_norm, mixer_full[5]) + dense(attn_mix, mixer_full[6]))
    mlp_full = (
        lax.all_gather(mlp_shards[0], ("fsdp", "rep"), axis=0, tiled=True),
        lax.all_gather(mlp_shards[1], ("fsdp", "rep"), axis=0, tiled=True),
        lax.all_gather(mlp_shards[2], ("fsdp", "rep"), axis=0, tiled=True),
        lax.all_gather(mlp_shards[3], ("fsdp", "rep"), axis=1, tiled=True),
    )
    second_f, second_pull = jax.vjp(root_norm, hidden, mlp_full[0].astype(jnp.float32))
    second = second_f.astype(jnp.bfloat16)
    gate_act = dense(second, mlp_full[1])
    up_act = dense(second, mlp_full[2])
    product_f, product_pull = jax.vjp(swish_product, gate_act, up_act)
    product = product_f.astype(jnp.bfloat16)
    result = hidden + mask_col * dense(product, mlp_full[3])
    output = result.astype(jnp.bfloat16).reshape(tokens.shape)
    mlp_back = (
        lax.all_gather(mlp_shards[0], ("fsdp", "rep"), axis=0, tiled=True),
        lax.all_gather(mlp_shards[1], ("fsdp", "rep"), axis=0, tiled=True),
        lax.all_gather(mlp_shards[2], ("fsdp", "rep"), axis=0, tiled=True),
        lax.all_gather(mlp_shards[3], ("fsdp", "rep"), axis=1, tiled=True),
    )
    upstream = cotangent.astype(jnp.float32).reshape(total_rows, model_width)
    down_grad = (mask_col * upstream).astype(jnp.bfloat16)
    grad_down = weight_grad(product, down_grad)
    d_product = input_grad(down_grad, mlp_back[3])
    gate_grad_f, up_grad_f = product_pull(d_product)
    gate_grad = gate_grad_f.astype(jnp.bfloat16)
    up_grad = up_grad_f.astype(jnp.bfloat16)
    grad_gate = weight_grad(second, gate_grad)
    grad_up = weight_grad(second, up_grad)
    d_second = input_grad(gate_grad, mlp_back[1]) + input_grad(up_grad, mlp_back[2])
    d_hidden_norm, grad_second = second_pull(d_second)
    d_hidden = upstream + d_hidden_norm
    mlp_sums = (
        lax.psum_scatter(grad_second, ("fsdp", "rep"), scatter_dimension=0, tiled=True),
        lax.psum_scatter(grad_gate, ("fsdp", "rep"), scatter_dimension=0, tiled=True),
        lax.psum_scatter(grad_up, ("fsdp", "rep"), scatter_dimension=0, tiled=True),
        lax.psum_scatter(grad_down, ("fsdp", "rep"), scatter_dimension=1, tiled=True),
    )
    mixer_back = (
        lax.all_gather(mixer_shards[0], ("fsdp", "rep"), axis=0, tiled=True),
        lax.all_gather(mixer_shards[1], ("fsdp", "rep"), axis=0, tiled=True),
        lax.all_gather(mixer_shards[2], ("fsdp", "rep"), axis=0, tiled=True),
        lax.all_gather(mixer_shards[3], ("fsdp", "rep"), axis=0, tiled=True),
        lax.all_gather(mixer_shards[4], ("fsdp", "rep"), axis=0, tiled=True),
        lax.all_gather(mixer_shards[5], ("fsdp", "rep"), axis=1, tiled=True),
        lax.all_gather(mixer_shards[6], ("fsdp", "rep"), axis=1, tiled=True),
    )
    branch_grad = (mask_col * d_hidden).astype(jnp.bfloat16)
    grad_mamba_out = weight_grad(mamba_norm, branch_grad)
    grad_output = weight_grad(attn_mix, branch_grad)
    d_mamba = input_grad(branch_grad, mixer_back[5])
    d_attn = input_grad(branch_grad, mixer_back[6])
    mamba_grads = mamba_pull(d_mamba.reshape(batches, width, -1))
    proj_grad = mamba_grads[0].reshape(total_rows, -1).astype(jnp.bfloat16)
    attn_grads = attn_pull(d_attn.reshape(batches, width, -1))
    query_grad = attn_grads[0].reshape(total_rows, -1).astype(jnp.bfloat16)
    key_grad = attn_grads[1].reshape(total_rows, -1).astype(jnp.bfloat16)
    value_grad = attn_grads[2].reshape(total_rows, -1).astype(jnp.bfloat16)
    grad_mamba_in = weight_grad(normed, proj_grad)
    grad_query = weight_grad(normed, query_grad)
    grad_key = weight_grad(normed, key_grad)
    grad_value = weight_grad(normed, value_grad)
    d_normed = (
        input_grad(proj_grad, mixer_back[1])
        + input_grad(query_grad, mixer_back[2])
        + input_grad(key_grad, mixer_back[3])
        + input_grad(value_grad, mixer_back[4])
    )
    d_source, grad_norm = norm_pull(d_normed)
    token_grads = (d_hidden + d_source).reshape(tokens.shape)
    mixer_sums = (
        lax.psum_scatter(grad_norm, ("fsdp", "rep"), scatter_dimension=0, tiled=True),
        lax.psum_scatter(grad_mamba_in, ("fsdp", "rep"), scatter_dimension=0, tiled=True),
        lax.psum_scatter(grad_query, ("fsdp", "rep"), scatter_dimension=0, tiled=True),
        lax.psum_scatter(grad_key, ("fsdp", "rep"), scatter_dimension=0, tiled=True),
        lax.psum_scatter(grad_value, ("fsdp", "rep"), scatter_dimension=0, tiled=True),
        lax.psum_scatter(grad_mamba_out, ("fsdp", "rep"), scatter_dimension=1, tiled=True),
        lax.psum_scatter(grad_output, ("fsdp", "rep"), scatter_dimension=1, tiled=True),
    )
    small_sums = lax.psum(
        (
            mamba_grads[1],
            mamba_grads[2],
            mamba_grads[3],
            mamba_grads[4],
            mamba_grads[5],
            mamba_grads[6],
        ),
        ("fsdp", "rep"),
    )
    return (
        output,
        token_grads,
        mixer_sums[0],
        mixer_sums[1],
        small_sums[0],
        small_sums[1],
        small_sums[2],
        small_sums[3],
        small_sums[4],
        small_sums[5],
        mixer_sums[5],
        mixer_sums[2],
        mixer_sums[3],
        mixer_sums[4],
        mixer_sums[6],
        mlp_sums[0],
        mlp_sums[1],
        mlp_sums[2],
        mlp_sums[3],
    )


def solution(mesh):
    placed = (
        P(None, ("fsdp", "rep"), None),
        P(None, ("fsdp", "rep")),
        P(None, ("fsdp", "rep")),
        P(("fsdp", "rep")),
        P(("fsdp", "rep"), None),
        P(),
        P(),
        P(),
        P(),
        P(),
        P(),
        P(None, ("fsdp", "rep")),
        P(("fsdp", "rep"), None),
        P(("fsdp", "rep"), None),
        P(("fsdp", "rep"), None),
        P(None, ("fsdp", "rep")),
        P(("fsdp", "rep")),
        P(("fsdp", "rep"), None),
        P(("fsdp", "rep"), None),
        P(None, ("fsdp", "rep")),
        P(None, ("fsdp", "rep"), None),
    )
    return jax.shard_map(
        local,
        mesh=mesh,
        in_specs=placed,
        out_specs=(
            P(None, ("fsdp", "rep"), None),
            P(None, ("fsdp", "rep"), None),
            P(("fsdp", "rep")),
            P(("fsdp", "rep"), None),
            P(),
            P(),
            P(),
            P(),
            P(),
            P(),
            P(None, ("fsdp", "rep")),
            P(("fsdp", "rep"), None),
            P(("fsdp", "rep"), None),
            P(("fsdp", "rep"), None),
            P(None, ("fsdp", "rep")),
            P(("fsdp", "rep")),
            P(("fsdp", "rep"), None),
            P(("fsdp", "rep"), None),
            P(None, ("fsdp", "rep")),
        ),
        check_vma=False,
    )
```

profile of v0, /device:TPU:8, one launch (start us, length us, event | category | flops | bytes accessed | tf_op | source)
XLA Modules:
  0.0 3756.3 jit_solution(14289895534293403112)
XLA Ops:
  14.0 40.6 %all-reduce.24 = (bf16[2048]{0:T(1024)(128)(2,1)S(1)}, bf16[2048]{0:T(1024)(128)(2,1)S(1)}) all-reduce(bf16[2048]{0:T(1024)(128)(2,1)S(1)} %dynamic-update-slice, bf16[2048]{0:T(1024)(128)(2,1)S(1)} %dynamic-update-slice.1), channel_id=1, replica_groups=mesh['fsdp'=8,'rep'=4] {'fsdp','rep'}, use_global_device_ids=true, to_apply=%add.19 | all-reduce | flops 4096 | bytes 16384
  58.9 6.2 all-gather.16.cloned.1.call-done
  66.7 54.0 %all-gather.14.cloned.1.call-done = bf16[2048,256]{1,0:T(8,128)(2,1)} async-done(((bf16[64,256]{1,0:T(8,128)(2,1)}), bf16[2048,256]{1,0:T(8,128)(2,1)}) %all-gather.14.cloned.1.call-update) | async-done | bytes 1048592 | tf_op jit(solution)/shard_map/all_gather | solution.py:157
  123.3 62.0 %all-gather.18.cloned.1.call-done = bf16[2048,1024]{1,0:T(8,128)(2,1)} async-done(((bf16[64,1024]{1,0:T(8,128)(2,1)}), bf16[2048,1024]{1,0:T(8,128)(2,1)}) %all-gather.18.cloned.1.call-update) | async-done | bytes 4194320 | tf_op jit(solution)/shard_map/all_gather | solution.py:155
  185.3 6.5 copy.119
  191.8 3.7 fusion.74
  200.6 151.4 %all-gather.10.cloned.1.call-done = bf16[2048,6704]{1,0:T(8,128)(2,1)} async-done(((bf16[64,6704]{1,0:T(8,128)(2,1)}), bf16[2048,6704]{1,0:T(8,128)(2,1)}) %all-gather.10.cloned.1.call-update) | async-done | bytes 27459600 | tf_op jit(solution)/shard_map/all_gather | solution.py:154
  352.0 11.0 fusion
  372.4 10.4 bitcast_add_fusion
  388.8 61.4 %all-gather.12.cloned.1.call-done = bf16[3072,2048]{0,1:T(8,128)(2,1)} async-done(((bf16[3072,64]{0,1:T(8,128)(2,1)}), bf16[3072,2048]{0,1:T(8,128)(2,1)}) %all-gather.12.cloned.1.call-update) | async-done | bytes 12582928 | tf_op jit(solution)/shard_map/all_gather | solution.py:158
  450.2 9.8 fusion.132
  460.0 53.8 %all-gather.20.cloned.1.call-done = bf16[1024,2048]{0,1:T(8,128)(2,1)} async-done(((bf16[1024,64]{0,1:T(8,128)(2,1)}), bf16[1024,2048]{0,1:T(8,128)(2,1)}) %all-gather.20.cloned.1.call-update) | async-done | bytes 4194320 | tf_op jit(solution)/shard_map/all_gather | solution.py:159
  513.8 4.3 multiply_reduce_fusion.10
  519.6 109.5 %all-gather.22.cloned.1.call-done = bf16[2048,4096]{1,0:T(8,128)(2,1)} async-done(((bf16[64,4096]{1,0:T(8,128)(2,1)}), bf16[2048,4096]{1,0:T(8,128)(2,1)}) %all-gather.22.cloned.1.call-update) | async-done | bytes 16777232 | tf_op jit(solution)/shard_map/all_gather | solution.py:189
  629.1 9.6 fusion.133
  638.7 106.3 %all-gather.24.cloned.1.call-done = bf16[2048,4096]{1,0:T(8,128)(2,1)} async-done(((bf16[64,4096]{1,0:T(8,128)(2,1)}), bf16[2048,4096]{1,0:T(8,128)(2,1)}) %all-gather.24.cloned.1.call-update) | async-done | bytes 16777232 | tf_op jit(solution)/shard_map/all_gather | solution.py:190
  745.0 9.7 fusion.134
  754.7 106.3 %all-gather.26.cloned.1.call-done = bf16[4096,2048]{0,1:T(8,128)(2,1)} async-done(((bf16[4096,64]{0,1:T(8,128)(2,1)}), bf16[4096,2048]{0,1:T(8,128)(2,1)}) %all-gather.26.cloned.1.call-update) | async-done | bytes 16777232 | tf_op jit(solution)/shard_map/all_gather | solution.py:191
  861.0 12.7 multiply_convert_fusion
  873.6 12.7 fusion.135
  886.4 13.6 multiply_reduce_fusion.8
  901.8 6.6 fusion.136
  910.4 5.0 multiply_reduce_fusion.5
  918.7 9.5 fusion.35
  928.2 4.2 copy.129
  946.8 10.0 fusion.6
  960.9 4.0 multiply_reduce_fusion.3
  972.2 3.5 fusion.38
  976.6 15.5 fusion.137
  995.7 4.6 fusion.65
  1004.1 5.5 fusion.83
  1009.7 5.6 fusion.140
  1015.4 11.7 fusion.139
  1028.1 14.5 fusion.141
  1042.6 14.4 fusion.142
  1058.0 14.5 fusion.143
  1072.6 21.7 convolution_bitcast_fusion
  1098.8 12.7 fusion.25
  1111.4 145.7 %all-reduce.27.cloned.1.call-done = (f32[2048]{0:T(1024)}, f32[4,3584]{1,0:T(4,128)}, f32[3584]{0:T(1024)}, f32[48]{0:T(128)}, f32[48]{0:T(128)}, /*index=5*/f32[48]{0:T(128)}, f32[3072]{0:T(1024)}, f32[2048]{0:T(1024)}) async-done(((f32[2048]{0:T(1024)}, f32[4,3584]{1,0:T(4,128)}, f32[3584]{0:T(1024)}, f32[48]{0:T(128)}, f32[48]{0:T(128)}, /*index=5*/f32[48]{0:T(128)}, f32[3072]{0:T(1024)}, ...) | async-done | bytes 100944
  1259.6 121.1 %reduce-scatter.16.cloned.1.call-done = f32[64,256]{1,0:T(8,128)} async-done(((f32[2048,256]{1,0:T(8,128)}), f32[64,256]{1,0:T(8,128)}) %reduce-scatter.16.cloned.1.call-update) | async-done | bytes 65552 | tf_op jit(solution)/shard_map/reduce_scatter | solution.py:261
  1380.6 135.3 %reduce-scatter.18.cloned.1.call-done = f32[64,256]{1,0:T(8,128)} async-done(((f32[2048,256]{1,0:T(8,128)}), f32[64,256]{1,0:T(8,128)}) %reduce-scatter.18.cloned.1.call-update) | async-done | bytes 65552 | tf_op jit(solution)/shard_map/reduce_scatter | solution.py:262
  1515.9 149.2 %reduce-scatter.14.cloned.1.call-done = f32[64,1024]{1,0:T(8,128)} async-done(((f32[2048,1024]{1,0:T(8,128)}), f32[64,1024]{1,0:T(8,128)}) %reduce-scatter.14.cloned.1.call-update) | async-done | bytes 262160 | tf_op jit(solution)/shard_map/reduce_scatter | solution.py:260
  1665.1 148.1 %reduce-scatter.20.cloned.1.call-done = f32[1024,64]{0,1:T(8,128)} async-done(((f32[1024,2048]{0,1:T(8,128)}), f32[1024,64]{0,1:T(8,128)}) %reduce-scatter.20.cloned.1.call-update) | async-done | bytes 262160 | tf_op jit(solution)/shard_map/reduce_scatter | solution.py:264
  1813.2 266.2 %reduce-scatter.12.cloned.1.call-done = f32[3072,64]{0,1:T(8,128)} async-done(((f32[3072,2048]{0,1:T(8,128)}), f32[3072,64]{0,1:T(8,128)}) %reduce-scatter.12.cloned.1.call-update) | async-done | bytes 786448 | tf_op jit(solution)/shard_map/reduce_scatter | solution.py:263
  2079.4 355.7 %reduce-scatter.22.cloned.1.call-done = f32[64,4096]{1,0:T(8,128)} async-done(((f32[2048,4096]{1,0:T(8,128)}), f32[64,4096]{1,0:T(8,128)}) %reduce-scatter.22.cloned.1.call-update) | async-done | bytes 1048592 | tf_op jit(solution)/shard_map/reduce_scatter | solution.py:221
  2435.1 360.3 %reduce-scatter.24.cloned.1.call-done = f32[64,4096]{1,0:T(8,128)} async-done(((f32[2048,4096]{1,0:T(8,128)}), f32[64,4096]{1,0:T(8,128)}) %reduce-scatter.24.cloned.1.call-update) | async-done | bytes 1048592 | tf_op jit(solution)/shard_map/reduce_scatter | solution.py:222
  2795.5 360.3 %reduce-scatter.26.cloned.1.call-done = f32[4096,64]{0,1:T(8,128)} async-done(((f32[4096,2048]{0,1:T(8,128)}), f32[4096,64]{0,1:T(8,128)}) %reduce-scatter.26.cloned.1.call-update) | async-done | bytes 1048592 | tf_op jit(solution)/shard_map/reduce_scatter | solution.py:223
  3155.8 586.1 %reduce-scatter.10.cloned.1.call-done = f32[64,6704]{1,0:T(8,128)} async-done(((f32[2048,6704]{1,0:T(8,128)}), f32[64,6704]{1,0:T(8,128)}) %reduce-scatter.10.cloned.1.call-update) | async-done | bytes 1716240 | tf_op jit(solution)/shard_map/reduce_scatter | solution.py:259
  (359 shorter events, 93.7 us)
Async XLA Ops:
  7.2 47.5 %copy-start.98 = (s32[2,1]{0,1:T(1,128)S(1)}, s32[2,1]{0,1:T(1,128)}, u32[]{:S(2)}) copy-start(s32[2,1]{0,1:T(1,128)} %param.23) | copy-start | bytes 28
  7.2 47.5 %copy-start.103 = (s32[2,1]{0,1:T(1,128)S(1)}, s32[2,1]{0,1:T(1,128)}, u32[]{:S(2)}) copy-start(s32[2,1]{0,1:T(1,128)} %param.22) | copy-start | bytes 28
  7.2 49.1 %copy-start.12 = (bf16[2,64,2048]{2,1,0:T(8,128)(2,1)S(1)}, bf16[2,64,2048]{2,1,0:T(8,128)(2,1)}, u32[]{:S(2)}) copy-start(bf16[2,64,2048]{2,1,0:T(8,128)(2,1)} %param.21) | copy-start | bytes 1572868
  7.2 49.9 %copy-start.70 = (f32[4,3584]{1,0:T(4,128)S(1)}, f32[4,3584]{1,0:T(4,128)}, u32[]{:S(2)}) copy-start(f32[4,3584]{1,0:T(4,128)} %param.26) | copy-start | bytes 172036
  7.3 50.0 %copy-start.104 = (f32[48]{0:T(128)S(1)}, f32[48]{0:T(128)}, u32[]{:S(2)}) copy-start(f32[48]{0:T(128)} %param.29) | copy-start | bytes 580
  7.3 50.5 %copy-start.19 = (bf16[2,64,2048]{2,1,0:T(8,128)(2,1)S(1)}, bf16[2,64,2048]{2,1,0:T(8,128)(2,1)}, u32[]{:S(2)}) copy-start(bf16[2,64,2048]{2,1,0:T(8,128)(2,1)} %param.41) | copy-start | bytes 1572868
  7.3 57.9 %all-gather.16.cloned.1.call-start = ((), (), s32[]{:S(2)}) async-start(), calls=%async_computation.12 | async-start | bytes 1081344 | tf_op jit(solution)/shard_map/all_gather | solution.py:156
  8.0 112.7 %all-gather.14.cloned.1.call-start = ((), (), s32[]{:S(2)}) async-start(), calls=%async_computation.11 | async-start | bytes 1081344 | tf_op jit(solution)/shard_map/all_gather | solution.py:157
  8.8 176.5 %all-gather.18.cloned.1.call-start = ((), (), s32[]{:S(2)}) async-start(), calls=%async_computation.13 | async-start | bytes 4325376 | tf_op jit(solution)/shard_map/all_gather | solution.py:155
  9.5 342.5 %all-gather.10.cloned.1.call-start = ((), (), s32[]{:S(2)}) async-start(), calls=%async_computation.9 | async-start | bytes 28655616 | tf_op jit(solution)/shard_map/all_gather | solution.py:154
  10.1 440.1 %all-gather.12.cloned.1.call-start = ((), (), s32[]{:S(2)}) async-start(), calls=%async_computation.10 | async-start | bytes 12976128 | tf_op jit(solution)/shard_map/all_gather | solution.py:158
  10.7 503.1 %all-gather.20.cloned.1.call-start = ((), (), s32[]{:S(2)}) async-start(), calls=%async_computation.14 | async-start | bytes 4325376 | tf_op jit(solution)/shard_map/all_gather | solution.py:159
  11.2 617.8 %all-gather.22.cloned.1.call-start = ((), (), s32[]{:S(2)}) async-start(), calls=%async_computation.15 | async-start | bytes 17301504 | tf_op jit(solution)/shard_map/all_gather | solution.py:189
  12.0 733.0 %all-gather.24.cloned.1.call-start = ((), (), s32[]{:S(2)}) async-start(), calls=%async_computation.16 | async-start | bytes 17301504 | tf_op jit(solution)/shard_map/all_gather | solution.py:190
  12.7 848.2 %all-gather.26.cloned.1.call-start = ((), (), s32[]{:S(2)}) async-start(), calls=%async_computation.17 | async-start | bytes 17301504 | tf_op jit(solution)/shard_map/all_gather | solution.py:191
  13.5 1243.6 %all-reduce.27.cloned.1.call-start = ((), (), s32[]{:S(2)}) async-start(), calls=%async_computation.27 | async-start | bytes 207872
  54.6 12.0 copy-start.59
  55.5 316.9 %copy-start.66 = (pred[2,64,64]{2,1,0:T(8,128)(4,1)}, pred[2,64,64]{2,1,0:T(8,128)(4,1)S(1)}, u32[]{:S(2)}) copy-start(pred[2,64,64]{2,1,0:T(8,128)(4,1)S(1)} %get-tuple-element.82) | copy-start | bytes 24580
  57.3 306.0 %copy-start.48 = (f32[3584]{0:T(1024)}, f32[3584]{0:T(1024)S(1)}, u32[]{:S(2)}) copy-start(f32[3584]{0:T(1024)S(1)} %get-tuple-element.35) | copy-start | bytes 43012
  57.3 306.0 %copy-start.50 = (f32[3584]{0:T(1024)}, f32[3584]{0:T(1024)S(1)}, u32[]{:S(2)}) copy-start(f32[3584]{0:T(1024)S(1)} %get-tuple-element.36) | copy-start | bytes 43012
  57.3 306.0 %copy-start.52 = (f32[3584]{0:T(1024)}, f32[3584]{0:T(1024)S(1)}, u32[]{:S(2)}) copy-start(f32[3584]{0:T(1024)S(1)} %get-tuple-element.37) | copy-start | bytes 43012
  57.3 306.0 %copy-start.54 = (f32[3584]{0:T(1024)}, f32[3584]{0:T(1024)S(1)}, u32[]{:S(2)}) copy-start(f32[3584]{0:T(1024)S(1)} %get-tuple-element.38) | copy-start | bytes 43012
  57.3 313.6 %copy-start.96 = (f32[48]{0:T(128)}, f32[48]{0:T(128)S(1)}, u32[]{:S(2)}) copy-start(f32[48]{0:T(128)S(1)} %exponential_negate_fusion) | copy-start | bytes 580
  122.7 75.2 %copy-start.32 = (f32[2,64,2,128,1]{3,1,4,2,0:T(8,128)}, f32[2,64,2,128,1]{3,1,4,2,0:T(8,128)S(1)}, u32[]{:S(2)}) copy-start(f32[2,64,2,128,1]{3,1,4,2,0:T(8,128)S(1)} %convolution_bitcast_fusion.3) | copy-start | bytes 393220
  123.3 72.7 %copy-start.28 = (f32[2,64,2,64]{3,1,2,0:T(8,128)}, f32[2,64,2,64]{3,1,2,0:T(8,128)S(1)}, u32[]{:S(2)}) copy-start(f32[2,64,2,64]{3,1,2,0:T(8,128)S(1)} %get-tuple-element.78) | copy-start | bytes 196612
  123.3 72.7 %copy-start.30 = (f32[2,64,2,64]{3,1,2,0:T(8,128)}, f32[2,64,2,64]{3,1,2,0:T(8,128)S(1)}, u32[]{:S(2)}) copy-start(f32[2,64,2,64]{3,1,2,0:T(8,128)S(1)} %get-tuple-element.79) | copy-start | bytes 196612
  197.7 165.3 %copy-start.56 = (f32[2,2,4,64]{3,2,1,0:T(4,128)}, f32[2,2,4,64]{3,2,1,0:T(4,128)S(1)}, u32[]{:S(2)}) copy-start(f32[2,2,4,64]{3,2,1,0:T(4,128)S(1)} %get-tuple-element.90) | copy-start | bytes 12292
  198.5 164.5 %copy-start.63 = (f32[2,2,4,64]{3,2,1,0:T(4,128)}, f32[2,2,4,64]{3,2,1,0:T(4,128)S(1)}, u32[]{:S(2)}) copy-start(f32[2,2,4,64]{3,2,1,0:T(4,128)S(1)} %fusion.96) | copy-start | bytes 12292
  199.9 313.9 %copy-start.21 = (bf16[128,1024]{1,0:T(8,128)(2,1)}, bf16[128,1024]{1,0:T(8,128)(2,1)S(1)}, u32[]{:S(2)}) copy-start(bf16[128,1024]{1,0:T(8,128)(2,1)S(1)} %convert_element_type.130) | copy-start | bytes 786436
  200.6 162.4 %copy-start.82 = (f32[2,64]{1,0:T(2,128)S(1)}, f32[2,64]{1,0:T(2,128)}, u32[]{:S(2)}) copy-start(f32[2,64]{1,0:T(2,128)} %copy-done.81) | copy-start | bytes 1540
  388.5 71.5 %copy-start.79 = (f32[2,64]{1,0:T(2,128)}, f32[2,64]{1,0:T(2,128)S(1)}, u32[]{:S(2)}) copy-start(f32[2,64]{1,0:T(2,128)S(1)} %get-tuple-element.54) | copy-start | bytes 1540
  388.5 71.5 %copy-start.77 = (f32[2,64]{1,0:T(2,128)}, f32[2,64]{1,0:T(2,128)S(1)}, u32[]{:S(2)}) copy-start(f32[2,64]{1,0:T(2,128)S(1)} %fusion.115) | copy-start | bytes 1540
  388.8 71.2 %copy-start.15 = (bf16[2,64,3072]{2,1,0:T(8,128)(2,1)}, bf16[2,64,3072]{2,1,0:T(8,128)(2,1)S(1)}, u32[]{:S(2)}) copy-start(bf16[2,64,3072]{2,1,0:T(8,128)(2,1)S(1)} %multiply_convert_fusion.2) | copy-start | bytes 2359300
  518.1 381.9 %copy-start = (f32[128,2048]{1,0:T(8,128)}, f32[128,2048]{1,0:T(8,128)S(1)}, u32[]{:S(2)}) copy-start(f32[128,2048]{1,0:T(8,128)S(1)} %get-tuple-element.93) | copy-start | bytes 3145732
  518.6 381.4 %copy-start.84 = (f32[128]{0:T(128)}, f32[128]{0:T(128)S(1)}, u32[]{:S(2)}) copy-start(f32[128]{0:T(128)S(1)} %fusion.116) | copy-start | bytes 1540
  873.6 12.7 copy-start.43
  886.4 13.6 copy-start.100
  886.4 13.7 copy-start.87
  976.6 19.0 copy-start.13
  1000.3 380.3 %reduce-scatter.16.cloned.1.call-start = ((), (), s32[]{:S(2)}) async-start(), calls=%async_computation.21 | async-start | bytes 2162688 | tf_op jit(solution)/shard_map/reduce_scatter | solution.py:261
  1002.2 513.8 %reduce-scatter.18.cloned.1.call-start = ((), (), s32[]{:S(2)}) async-start(), calls=%async_computation.22 | async-start | bytes 2162688 | tf_op jit(solution)/shard_map/reduce_scatter | solution.py:262
  1004.0 661.1 %reduce-scatter.14.cloned.1.call-start = ((), (), s32[]{:S(2)}) async-start(), calls=%async_computation.20 | async-start | bytes 8650752 | tf_op jit(solution)/shard_map/reduce_scatter | solution.py:260
  1009.6 803.6 %reduce-scatter.20.cloned.1.call-start = ((), (), s32[]{:S(2)}) async-start(), calls=%async_computation.23 | async-start | bytes 8650752 | tf_op jit(solution)/shard_map/reduce_scatter | solution.py:264
  1015.3 1064.1 %reduce-scatter.12.cloned.1.call-start = ((), (), s32[]{:S(2)}) async-start(), calls=%async_computation.19 | async-start | bytes 25952256 | tf_op jit(solution)/shard_map/reduce_scatter | solution.py:263
  1027.1 1408.1 %reduce-scatter.22.cloned.1.call-start = ((), (), s32[]{:S(2)}) async-start(), calls=%async_computation.24 | async-start | bytes 34603008 | tf_op jit(solution)/shard_map/reduce_scatter | solution.py:221
  1042.6 1752.9 %reduce-scatter.24.cloned.1.call-start = ((), (), s32[]{:S(2)}) async-start(), calls=%async_computation.25 | async-start | bytes 34603008 | tf_op jit(solution)/shard_map/reduce_scatter | solution.py:222
  1057.0 2098.8 %reduce-scatter.26.cloned.1.call-start = ((), (), s32[]{:S(2)}) async-start(), calls=%async_computation.26 | async-start | bytes 34603008 | tf_op jit(solution)/shard_map/reduce_scatter | solution.py:223
  1072.5 2669.3 %reduce-scatter.10.cloned.1.call-start = ((), (), s32[]{:S(2)}) async-start(), calls=%async_computation.18 | async-start | bytes 57311232 | tf_op jit(solution)/shard_map/reduce_scatter | solution.py:259
  (79 other events, 281.2 us)
Sparse Core Ops, SparseCore 0:
  11.0 54.1 all-gather.15
  68.0 52.6 all-gather.13
  123.6 61.6 all-gather.17
  188.0 163.9 all-gather.9
  354.7 95.4 all-gather.11
  452.9 60.8 all-gather.19
  516.6 112.3 all-gather.21
  631.9 113.0 all-gather.23
  747.9 113.0 all-gather.25
  1000.4 256.5 all-reduce.26
  1261.9 118.6 reduce-scatter.15
  1383.3 132.5 reduce-scatter.17
  1518.9 146.2 reduce-scatter.13
  1668.0 145.2 reduce-scatter.19
  1821.2 258.1 reduce-scatter.11
  2082.1 352.9 reduce-scatter.21
  2437.9 357.5 reduce-scatter.23
  2798.2 357.5 reduce-scatter.25
  3158.7 583.1 reduce-scatter.9
where the time goes:
time: 3780 us; the launch traced here: 3760 us
  waiting for transfers between devices  3340 us (88%)
  matrix products  267 us (7%)
  local copies, waits for them, and re-layouts  48.6 us (1%)
  blocking collectives  40.6 us (1%)
  other arithmetic  38.3 us (1%)
    reduce_scatter x1, waiting for transfers between devices, local(): lax.psum_scatter(grad_mamba_in, ('fsdp', 'rep'), scatter_dimension=0, til...  586 us
    reduce_scatter x1, waiting for transfers between devices, local(): lax.psum_scatter(grad_down, ('fsdp', 'rep'), scatter_dimension=1, tiled=T...  360 us
    reduce_scatter x1, waiting for transfers between devices, local(): lax.psum_scatter(grad_up, ('fsdp', 'rep'), scatter_dimension=0, tiled=True)  360 us
    reduce_scatter x1, waiting for transfers between devices, local(): lax.psum_scatter(grad_gate, ('fsdp', 'rep'), scatter_dimension=0, tiled=T...  356 us
    reduce_scatter x1, waiting for transfers between devices, local(): lax.psum_scatter(grad_mamba_out, ('fsdp', 'rep'), scatter_dimension=1, ti...  266 us
    unnamed x20, waiting for transfers between devices  152 us
    all_gather x1, waiting for transfers between devices, local(): lax.all_gather(mixer_shards[1], ('fsdp', 'rep'), axis=0, tiled=True)  151 us
    reduce_scatter x1, waiting for transfers between devices, local(): lax.psum_scatter(grad_query, ('fsdp', 'rep'), scatter_dimension=0, tiled=...  149 us
  transfers between devices with their start and end apart: 19, of which 19 were waited for; matrix products, arithmetic and copies ran while one was open for 5% of the time, Pallas kernels for 0%

commit v1 on v0

v1 whole, which is shorter than its diff:
```python
import math

import jax
import jax.numpy as jnp
from jax import lax
from jax.sharding import Mesh
from jax.sharding import PartitionSpec as P

HD = 128
TP = 4

epsilon = 1e-05
rope_base = 100000000000.0
highest = lax.Precision.HIGHEST
f32 = jnp.float32
bf16 = jnp.bfloat16


def inverse_root(values):
    return lax.rsqrt(jnp.mean(values * values, axis=-1, keepdims=True) + epsilon)


def norm_back(values, root, grad):
    return root * grad - values * root**3 * jnp.mean(values * grad, axis=-1, keepdims=True)


def dot_nn(left, right):
    return jnp.dot(left, right, preferred_element_type=f32)


def dot_nt(left, right):
    return lax.dot_general(left, right, (((1,), (1,)), ((), ())), preferred_element_type=f32)


def dot_tn(left, right):
    return lax.dot_general(left, right, (((0,), (0,)), ((), ())), preferred_element_type=f32)


def layout(lengths, offsets, width):
    rows = jnp.arange(width, dtype=jnp.int32)
    starts = offsets[:, None]
    inside = (rows[None, :] >= starts) & (rows[None, :] < starts + lengths[:, None])
    causal = rows[:, None] >= rows[None, :]
    segment = inside[:, :, None] & inside[:, None, :] & causal[None]
    positions = (rows[None, :] - starts).astype(f32)
    return inside.astype(f32), segment, positions


def mamba_core(gate, conv_in, step_raw, taps, bias, step_bias, decay_log, skip_weight, inside, segment):
    batch, length, inner = gate.shape
    heads = step_bias.shape[0]
    state = (conv_in.shape[-1] - inner) // 2
    conv_in = conv_in * inside[..., None]
    padded = jnp.pad(conv_in, ((0, 0), (taps.shape[0] - 1, 0), (0, 0)))
    convolved = bias + jnp.zeros_like(conv_in)
    for tap in range(taps.shape[0]):
        convolved = convolved + taps[tap] * padded[:, tap : tap + length]
    active = jax.nn.silu(convolved)
    head_values = active[..., :inner].reshape(batch, length, heads, inner // heads)
    b_state = active[..., inner : inner + state]
    c_state = active[..., inner + state :]
    step_size = jax.nn.softplus(step_raw + step_bias)
    cumulative = jnp.cumsum(step_size * -jnp.exp(decay_log), axis=1)
    spread = cumulative[:, :, None, :] - cumulative[:, None, :, :]
    allowed = segment[..., None]
    decay = jnp.where(allowed, jnp.exp(jnp.where(allowed, spread, 0.0)), 0.0)
    intersection = jnp.einsum("sin,sjn->sij", c_state, b_state, precision=highest)
    mixing = decay * intersection[..., None]
    scaled = head_values * step_size[..., None]
    result = jnp.einsum("sijh,sjhp->sihp", mixing, scaled, precision=highest)
    result = result + skip_weight[:, None] * head_values
    return result.reshape(batch, length, inner) * jax.nn.silu(gate)


def attention_core(queries, keys, values, positions, segment):
    batch, length = queries.shape[:2]
    half = HD // 2
    freqs = rope_base ** (-jnp.arange(half, dtype=f32) * 2.0 / HD)
    angles = positions[..., None] * freqs
    cosine = jnp.cos(angles)[:, :, None, :]
    sine = jnp.sin(angles)[:, :, None, :]

    def rotate(tensor):
        split = tensor.reshape(batch, length, -1, HD)
        first = split[..., :half]
        second = split[..., half:]
        return jnp.concatenate(
            [first * cosine - second * sine, first * sine + second * cosine], axis=-1
        )

    rot_query = rotate(queries)
    rot_key = rotate(keys)[:, :, 0]
    scores = jnp.einsum("sigd,sjd->sgij", rot_query, rot_key, precision=highest) / math.sqrt(HD)
    allowed = segment | jnp.eye(length, dtype=jnp.bool_)[None]
    scores = jnp.where(allowed[:, None], scores, -1e30)
    peak = jnp.max(scores, axis=-1, keepdims=True)
    probs = jnp.exp(scores - peak)
    probs = probs / jnp.sum(probs, axis=-1, keepdims=True)
    mixed = jnp.einsum("sgij,sjd->sigd", probs, values, precision=highest)
    return mixed.reshape(batch, length, -1)


def local(
    tokens,
    lengths,
    offsets,
    norm_gain,
    mamba_in,
    conv_taps,
    conv_bias,
    step_bias,
    decay_log,
    skip_weight,
    mamba_gain,
    mamba_out,
    query_weight,
    key_weight,
    value_weight,
    output_weight,
    second_gain,
    gate_weight,
    up_weight,
    down_weight,
    cotangent,
):
    me = lax.axis_index("tp")
    peers = lax.axis_size("fs")
    batches, width, model = tokens.shape
    rows = batches * width
    shard = mamba_in.shape[0]
    inner = mamba_gain.shape[0]
    heads = step_bias.shape[0]
    state = (mamba_in.shape[1] - 2 * inner - heads) // 2
    q_cols = query_weight.shape[1]
    kv_heads = key_weight.shape[1] // HD
    hidden_units = gate_weight.shape[1]
    inner_t, heads_t, q_t, ff_t = inner // TP, heads // TP, q_cols // TP, hidden_units // TP
    kv_of = [t * kv_heads // TP for t in range(TP)]
    pad = 128

    def cut(weight, size):
        return weight.reshape(shard, TP, size).transpose(1, 0, 2)

    def same(weight):
        return jnp.broadcast_to(weight[None], (TP,) + weight.shape)

    def per_kv(weight):
        split = weight.reshape(shard, kv_heads, HD).transpose(1, 0, 2)
        return jnp.stack([split[k] for k in kv_of])

    steps = cut(mamba_in[:, 2 * inner + 2 * state :], heads_t)
    steps = jnp.concatenate(
        [
            steps,
            same(norm_gain[:, None]),
            same(second_gain[:, None]),
            jnp.zeros((TP, shard, pad - heads_t - 2), bf16),
        ],
        axis=2,
    )
    mixer_shard = jnp.concatenate(
        [
            cut(mamba_in[:, :inner], inner_t),
            cut(mamba_in[:, inner : 2 * inner], inner_t),
            same(mamba_in[:, 2 * inner : 2 * inner + 2 * state]),
            steps,
            cut(query_weight, q_t),
            per_kv(key_weight),
            per_kv(value_weight),
            cut(mamba_out.T, inner_t),
            cut(output_weight.T, q_t),
        ],
        axis=2,
    )
    mlp_shard = jnp.concatenate(
        [cut(gate_weight, ff_t), cut(up_weight, ff_t), cut(down_weight.T, ff_t)], axis=2
    )
    in_cols = mixer_shard.shape[2] - inner_t - q_t

    def collect(shards):
        mine = lax.all_to_all(shards, "tp", split_axis=0, concat_axis=0)
        return lax.all_gather(mine.reshape(TP * shard, -1), "fs", axis=0, tiled=True)

    def deliver(grads):
        part = lax.psum_scatter(grads.astype(bf16), "fs", scatter_dimension=0, tiled=True)
        part = part.reshape(TP, shard, -1)
        return lax.all_to_all(part, "tp", split_axis=0, concat_axis=0).astype(f32)

    def order(values):
        split = values.reshape(values.shape[:-1] + (TP, peers, shard))
        return jnp.swapaxes(split, -3, -2).reshape(values.shape)

    def unorder(values):
        split = values.reshape(values.shape[:-1] + (peers, TP, shard))
        return jnp.swapaxes(split, -3, -2).reshape(values.shape)

    def spread(values):
        return lax.all_gather(values, "tp", axis=0, tiled=True)

    def reduce(values):
        return lax.psum_scatter(
            values.astype(bf16), "tp", scatter_dimension=0, tiled=True
        ).astype(f32)

    mixer = collect(mixer_shard)
    mlp = collect(mlp_shard)
    w_in, w_out = mixer[:, :in_cols], mixer[:, in_cols:]
    w_gate, w_up, w_down = mlp[:, :ff_t], mlp[:, ff_t : 2 * ff_t], mlp[:, 2 * ff_t :]

    inside_own, _, _ = layout(lengths[:, 0], offsets[:, 0], width)
    mask_own = inside_own.reshape(rows, 1)
    inside, segment, positions = layout(spread(lengths[:, 0]), spread(offsets[:, 0]), width)
    mask = inside.reshape(-1, 1)
    seqs = inside.shape[0]

    source = order(tokens.reshape(rows, model))
    upstream = order(cotangent.reshape(rows, model))
    source_all = spread(source).astype(f32)
    upstream_all = spread(upstream)
    source = source.astype(f32)
    upstream = upstream.astype(f32)

    gain_col = 2 * inner_t + 2 * state + heads_t
    gain_first = w_in[:, gain_col].astype(f32)
    gain_second = w_in[:, gain_col + 1].astype(f32)

    def own(values, size):
        return lax.dynamic_slice_in_dim(values, me * size, size, axis=-1)

    taps_t = jnp.concatenate([own(conv_taps[:, :inner], inner_t), conv_taps[:, inner:]], axis=1)
    bias_t = jnp.concatenate([own(conv_bias[:inner], inner_t), conv_bias[inner:]])
    step_bias_t = own(step_bias, heads_t)
    decay_t = own(decay_log, heads_t)
    skip_t = own(skip_weight, heads_t)
    mamba_gain_t = own(mamba_gain, inner_t)

    normed = (source_all * inverse_root(source_all) * gain_first).astype(bf16)
    projected = dot_nn(normed, w_in).reshape(seqs, width, in_cols)
    conv_cols = inner_t + 2 * state
    gate = projected[..., :inner_t]
    conv_in = projected[..., inner_t : inner_t + conv_cols]
    step_raw = projected[..., inner_t + conv_cols : inner_t + conv_cols + heads_t]
    at = inner_t + conv_cols + pad
    queries, keys, values = (
        projected[..., at : at + q_t],
        projected[..., at + q_t : at + q_t + HD],
        projected[..., at + q_t + HD :],
    )
    gated, mamba_pull = jax.vjp(
        lambda *a: mamba_core(*a, inside, segment),
        gate,
        conv_in,
        step_raw,
        taps_t,
        bias_t,
        step_bias_t,
        decay_t,
        skip_t,
    )
    gated = gated.reshape(-1, inner_t)
    squares = lax.psum(jnp.sum(gated * gated, axis=-1, keepdims=True), "tp")
    mamba_root = lax.rsqrt(squares / inner + epsilon)
    mamba_norm = (gated * mamba_root * mamba_gain_t).astype(bf16)
    mixed, attn_pull = jax.vjp(
        lambda q, k, v: attention_core(q, k, v, positions, segment), queries, keys, values
    )
    branches = jnp.concatenate([mamba_norm, mixed.reshape(-1, q_t).astype(bf16)], axis=1)
    hidden = source + mask_own * reduce(dot_nt(branches, w_out))

    second_root = inverse_root(hidden)
    second = spread((hidden * second_root * gain_second).astype(bf16))
    gate_act = dot_nn(second, w_gate)
    up_act = dot_nn(second, w_up)
    product = (jax.nn.silu(gate_act) * up_act).astype(bf16)
    output = (hidden + mask_own * reduce(dot_nt(product, w_down))).astype(bf16)

    down_grad = (mask * upstream_all.astype(f32)).astype(bf16)
    d_product = dot_nn(down_grad, w_down)
    sig = jax.nn.sigmoid(gate_act)
    gate_grad = (d_product * up_act * sig * (1.0 + gate_act * (1.0 - sig))).astype(bf16)
    up_grad = (d_product * gate_act * sig).astype(bf16)
    d_second = reduce(dot_nt(gate_grad, w_gate) + dot_nt(up_grad, w_up))
    d_hidden = upstream + norm_back(hidden, second_root, d_second * gain_second)
    mlp_grads = deliver(
        jnp.concatenate(
            [dot_tn(second, gate_grad), dot_tn(second, up_grad), dot_tn(down_grad, product)], axis=1
        )
    )

    branch_grad = spread((mask_own * d_hidden).astype(bf16))
    d_branches = dot_nn(branch_grad, w_out)
    grad_out = dot_tn(branch_grad, branches)
    d_mamba = d_branches[:, :inner_t] * mamba_gain_t
    dots = lax.psum(jnp.sum(gated * d_mamba, axis=-1, keepdims=True), "tp")
    d_gated = mamba_root * d_mamba - gated * mamba_root**3 * (dots / inner)
    grad_mamba_gain = jnp.sum(gated * mamba_root * d_branches[:, :inner_t], axis=0)
    mamba_grads = mamba_pull(d_gated.reshape(seqs, width, -1))
    attn_grads = attn_pull(d_branches[:, inner_t:].reshape(seqs, width, -1))
    proj_grad = jnp.concatenate(
        [
            mamba_grads[0],
            mamba_grads[1],
            jnp.pad(mamba_grads[2], ((0, 0), (0, 0), (0, pad - heads_t))),
            attn_grads[0],
            attn_grads[1],
            attn_grads[2],
        ],
        axis=-1,
    )
    proj_grad = proj_grad.reshape(-1, in_cols).astype(bf16)
    d_normed = reduce(dot_nt(proj_grad, w_in))
    source_root = inverse_root(source)
    token_grads = unorder(d_hidden + norm_back(source, source_root, d_normed * gain_first))
    mixer_grads = deliver(jnp.concatenate([dot_tn(normed, proj_grad), grad_out], axis=1))

    def whole(grads, start, size):
        return grads[:, :, start : start + size].transpose(1, 0, 2).reshape(shard, TP * size)

    def joined(grads, start):
        split = grads[:, :, start : start + HD]
        return jnp.concatenate(
            [sum(split[t] for t in range(TP) if kv_of[t] == k) for k in range(kv_heads)], axis=1
        )

    at = inner_t + conv_cols
    grad_mamba_in = jnp.concatenate(
        [
            whole(mixer_grads, 0, inner_t),
            whole(mixer_grads, inner_t, inner_t),
            mixer_grads[:, :, 2 * inner_t : at].sum(0),
            whole(mixer_grads, at, heads_t),
        ],
        axis=1,
    )
    at += pad
    grad_query = whole(mixer_grads, at, q_t)
    grad_key = joined(mixer_grads, at + q_t)
    grad_value = joined(mixer_grads, at + q_t + HD)
    grad_mamba_out = whole(mixer_grads, in_cols, inner_t).T
    grad_output = whole(mixer_grads, in_cols + inner_t, q_t).T
    grad_gate = whole(mlp_grads, 0, ff_t)
    grad_up = whole(mlp_grads, ff_t, ff_t)
    grad_down = whole(mlp_grads, 2 * ff_t, ff_t).T

    def gain_grad(pairs, gain):
        return sum(jnp.sum(w.astype(f32) * g, axis=1) for w, g in pairs) / gain.astype(f32)

    grad_norm_gain = gain_grad(
        (
            (mamba_in, grad_mamba_in),
            (query_weight, grad_query),
            (key_weight, grad_key),
            (value_weight, grad_value),
        ),
        norm_gain,
    )
    grad_second_gain = gain_grad(((gate_weight, grad_gate), (up_weight, grad_up)), second_gain)

    small = jnp.concatenate(
        [
            mamba_grads[3].reshape(-1),
            mamba_grads[4],
            grad_mamba_gain,
            mamba_grads[5],
            mamba_grads[6],
            mamba_grads[7],
        ]
    )
    small = lax.all_gather(lax.psum(small, "fs"), "tp", axis=0)
    kernel = conv_taps.shape[0]
    conv = small[:, : (kernel + 1) * conv_cols].reshape(TP, kernel + 1, conv_cols)
    conv = jnp.concatenate(
        [conv[:, :, :inner_t].transpose(1, 0, 2).reshape(kernel + 1, inner), conv[:, :, inner_t:].sum(0)],
        axis=1,
    )
    at = (kernel + 1) * conv_cols
    return (
        unorder(output).reshape(tokens.shape),
        token_grads.reshape(tokens.shape),
        grad_norm_gain,
        grad_mamba_in,
        conv[:kernel],
        conv[kernel],
        small[:, at + inner_t : at + inner_t + heads_t].reshape(-1),
        small[:, at + inner_t + heads_t : at + inner_t + 2 * heads_t].reshape(-1),
        small[:, at + inner_t + 2 * heads_t :].reshape(-1),
        small[:, at : at + inner_t].reshape(-1),
        grad_mamba_out,
        grad_query,
        grad_key,
        grad_value,
        grad_output,
        grad_second_gain,
        grad_gate,
        grad_up,
        grad_down,
    )


def solution(mesh):
    count = mesh.devices.size
    grid = Mesh(mesh.devices.reshape(TP, count // TP), ("tp", "fs"))
    every = ("tp", "fs")
    down, across, slots = P(every, None), P(None, every), P(None, every, None)
    line, copied = P(every), P()
    return jax.shard_map(
        local,
        mesh=grid,
        in_specs=(
            slots, across, across, line, down, copied, copied, copied, copied, copied, copied,
            across, down, down, down, across, line, down, down, across, slots,
        ),
        out_specs=(
            slots, slots, line, down, copied, copied, copied, copied, copied, copied,
            across, down, down, down, across, line, down, down, across,
        ),
        check_vma=False,
    )
```

time: 3780 us -> 980 us (0.26)
  waiting for transfers between devices: 3340 us -> 380 us
  blocking collectives: 40.6 us -> 247 us
  matrix products: 267 us -> 123 us
  other arithmetic: 38.3 us -> 99.5 us
  local copies, waits for them, and re-layouts: 48.6 us -> 90.9 us
    reduce_scatter x9 -> x6, waiting for transfers between devices: 2480 us -> 119 us  [the longest x4 71.8 us: reduce(): lax.psum_scatter(values.astype(bf16), 'tp', scatter_dimension=0, tiled=True)]
    all_gather x9 -> x6, waiting for transfers between devices: 711 us -> 229 us  [the longest x2 141 us: collect(): lax.all_gather(mine.reshape(TP * shard, -1), 'fs', axis=0, tiled=True)]
    unnamed x20 -> x12, waiting for transfers between devices: 152 us -> 0.2 us
    dot_general x33 -> x21, matrix products: 234 us -> 89 us  [the longest x5 31.8 us: dot_nn(): return jnp.dot(left, right, preferred_element_type=f32)]
    all_to_all x0 -> x2, blocking collectives: none -> 138 us  [collect(): mine = lax.all_to_all(shards, 'tp', split_axis=0, concat_axis=0)]
    all_gather x0 -> x2, blocking collectives: none -> 66.8 us  [the longest x1 59.8 us: local(): small = lax.all_gather(lax.psum(small, 'fs'), 'tp', axis=0)]
    psum x0 -> x3, blocking collectives: none -> 42.7 us  [the longest x1 22.7 us: local(): small = lax.all_gather(lax.psum(small, 'fs'), 'tp', axis=0)]
    unnamed x1 -> x0, blocking collectives: 40.6 us -> none
  transfers between devices with their start and end apart: 19 -> 14, of which waited for: 19 -> 9; matrix products, arithmetic and copies ran while one was open for 5% -> 22% of each run, Pallas kernels for 0% -> 0%
where the time goes in v1:
time: 980 us; the launch traced here: 969 us
  waiting for transfers between devices  380 us (39%)
  blocking collectives  247 us (25%)
  matrix products  123 us (13%)
  other arithmetic  99.5 us (10%)
  local copies, waits for them, and re-layouts  90.9 us (9%)
  between operations  17.2 us (2%)
  starting transfers between devices  11.9 us (1%)
    all_gather x2, waiting for transfers between devices, collect(): lax.all_gather(mine.reshape(TP * shard, -1), 'fs', axis=0, tiled=True)  141 us
    all_to_all x2, blocking collectives, collect(): mine = lax.all_to_all(shards, 'tp', split_axis=0, concat_axis=0)  138 us
    all_gather x4, waiting for transfers between devices, spread(): return lax.all_gather(values, 'tp', axis=0, tiled=True)  88.3 us
    reduce_scatter x4, waiting for transfers between devices, reduce(): lax.psum_scatter(values.astype(bf16), 'tp', scatter_dimension=0, tiled=True)  71.8 us
    all_gather x1, blocking collectives, local(): small = lax.all_gather(lax.psum(small, 'fs'), 'tp', axis=0)  59.8 us
    reduce_scatter x2, waiting for transfers between devices, deliver(): lax.psum_scatter(grads.astype(bf16), 'fs', scatter_dimension=0, tiled=True)  46.9 us
    all_to_all x2, waiting for transfers between devices, deliver(): return lax.all_to_all(part, 'tp', split_axis=0, concat_axis=0).astype(f32)  32 us
    dot_general x5, matrix products, dot_nn(): return jnp.dot(left, right, preferred_element_type=f32)  31.8 us
  transfers between devices with their start and end apart: 14, of which 9 were waited for; matrix products, arithmetic and copies ran while one was open for 22% of the time, Pallas kernels for 0%

profile of v1, /device:TPU:8, one launch (start us, length us, event | category | flops | bytes accessed | tf_op | source)
XLA Modules:
  0.0 969.1 jit_solution(8920182975292770800)
XLA Ops:
  18.3 4.4 concatenate.63
  23.0 74.7 %all_to_all.20 = bf16[4,64,3712]{2,1,0:T(8,128)(2,1)} all-to-all(bf16[4,64,3712]{2,1,0:T(8,128)(2,1)S(1)} %copy.390), channel_id=1, replica_groups=mesh['fsdp'=8,'rep'=4] {'fsdp':(1)4}, dimensions={0} | all-to-all | bytes 3801088 | tf_op jit(solution)/shard_map/all_to_all | solution.py:181
  99.3 7.0 all-reduce.19
  114.0 66.9 %all-gather.12.cloned.1.call-done = bf16[2048,3712]{1,0:T(8,128)(2,1)} async-done(((bf16[256,3712]{1,0:T(8,128)(2,1)}), bf16[2048,3712]{1,0:T(8,128)(2,1)}) %all-gather.12.cloned.1.call-update) | async-done | bytes 15204368 | tf_op jit(solution)/shard_map/all_gather | solution.py:182
  182.9 9.4 fusion.2
  192.6 3.4 fusion.53
  210.9 8.5 bitcast_add_fusion
  219.4 3.4 copy.447
  222.9 3.0 multiply_reduce_fusion.8
  233.1 8.9 psum.21
  243.7 5.9 fusion.38
  252.6 3.0 copy.407
  261.8 63.2 %all_to_all.21 = bf16[4,64,3072]{2,1,0:T(8,128)(2,1)} all-to-all(bf16[4,64,3072]{2,1,0:T(8,128)(2,1)S(1)} %copy.404), channel_id=1, replica_groups=mesh['fsdp'=8,'rep'=4] {'fsdp':(1)4}, dimensions={0} | all-to-all | bytes 3145728 | tf_op jit(solution)/shard_map/all_to_all | solution.py:181
  331.6 34.7 %all-gather.18.cloned.1.call-done = bf16[512,2048]{0,1:T(8,128)(2,1)} async-done(((bf16[128,2048]{0,1:T(8,128)(2,1)}), bf16[512,2048]{0,1:T(8,128)(2,1)}) %all-gather.18.cloned.1.call-update) | async-done | bytes 2097168 | tf_op jit(solution)/shard_map/all_gather | solution.py:198
  366.2 73.6 %all-gather.16.cloned.1.call-done = bf16[2048,3072]{1,0:T(8,128)(2,1)} async-done(((bf16[256,3072]{1,0:T(8,128)(2,1)}), bf16[2048,3072]{1,0:T(8,128)(2,1)}) %all-gather.16.cloned.1.call-update) | async-done | bytes 12582928 | tf_op jit(solution)/shard_map/all_gather | solution.py:182
  439.8 6.5 fusion.7
  446.3 40.0 %all-gather.14.cloned.1.call-done = bf16[512,2048]{1,0:T(8,128)(2,1)} async-done(((bf16[128,2048]{1,0:T(8,128)(2,1)}), bf16[512,2048]{1,0:T(8,128)(2,1)}) %all-gather.14.cloned.1.call-update) | async-done | bytes 2097168 | tf_op jit(solution)/shard_map/all_gather | solution.py:198
  486.3 5.3 fusion.13
  493.3 5.5 multiply_convert_fusion.2
  501.2 3.7 add_convert_fusion
  507.1 39.9 %reduce-scatter.11.cloned.1.call-done = bf16[128,2048]{1,0:T(8,128)(2,1)} async-done(((bf16[512,2048]{1,0:T(8,128)(2,1)}), bf16[128,2048]{1,0:T(8,128)(2,1)}) %reduce-scatter.11.cloned.1.call-update) | async-done | bytes 524304 | tf_op jit(solution)/shard_map/reduce_scatter | solution.py:201
  551.8 4.4 convolution_convert_fusion.2
  561.1 21.3 %pad_maximum_fusion.1 = bf16[2048,3072]{0,1:T(8,128)(2,1)} fusion(bf16[2048,1024]{0,1:T(8,128)(2,1)S(1)} %convolution_convert_fusion.1, bf16[2048,1024]{0,1:T(8,128)(2,1)S(1)} %convolution_convert_fusion.2, bf16[2048,1024]{0,1:T(8,128)(2,1)S(1)} %convolution_convert_fusion.3), kind=kLoop, calls=%fused_computation.1 | loop fusion | flops 37748736 | bytes 25165824 | tf_op jit(solution)/shard_map/concatenate | solution.py:285
  584.0 13.7 %all-gather.20.cloned.1.call-done = bf16[512,2048]{1,0:T(8,128)(2,1)} async-done(((bf16[128,2048]{1,0:T(8,128)(2,1)}), bf16[512,2048]{1,0:T(8,128)(2,1)}) %all-gather.20.cloned.1.call-update) | async-done | bytes 2097168 | tf_op jit(solution)/shard_map/all_gather | solution.py:198
  597.7 5.1 fusion.19
  605.3 11.1 %psum.22 = f32[512,1]{0,1:T(1,128)} all-reduce(f32[512,1]{0,1:T(1,128)} %bitcast.336), channel_id=1, replica_groups=mesh['fsdp'=8,'rep'=4] {'fsdp':(1)4}, use_global_device_ids=true, to_apply=%region_13.14 | all-reduce | flops 512 | bytes 4096 | tf_op jit(solution)/shard_map/psum | solution.py:294
  617.1 6.2 multiply_reduce_fusion.6
  623.3 4.0 reshape.593
  627.3 5.2 copy.412
  632.6 5.2 copy.413
  637.8 9.1 fusion.24
  646.9 3.5 copy.448
  650.4 10.8 %fusion.59 = (f32[8,64,12]{1,2,0:T(8,128)S(1)}, f32[8,64,12]{1,2,0:T(8,128)S(1)}, f32[8,64,64]{2,1,0:T(8,128)}) fusion(f32[8,64,64]{2,1,0:T(8,128)S(1)} %copy-done.36, f32[8,64,12]{1,2,0:T(8,128)S(1)} %copy.395, pred[8,64,64]{2,1,0:T(8,128)(4,1)S(1)} %copy-done.49, f32[8,12,64,64]{3,2,1,0:T(8,128)} %copy.413, f32[8,64,12,64]{1,3,2,0:T(8,128)} %bitcast.262, ...), kind=kOutput, calls=%fused_computation.82 | convolution fusion | flops 306663424 | bytes 3538944 | tf_op jit(solution)/shard_map/transpose(jvp(sijh,sjhp->sihp))/dot_general | solution.py:70
  661.4 6.8 fusion.164
  680.9 3.0 multiply_reduce_fusion.3
  693.6 6.5 convolution_convert_fusion
  700.0 6.4 pad_maximum_fusion
  706.5 10.9 %fusion.35 = bf16[512,2048]{1,0:T(8,128)(2,1)} fusion(bf16[512,2688]{1,0:T(8,128)(2,1)} %copy-done.54, bf16[2048,3712]{1,0:T(8,128)(2,1)} %all-gather.12.cloned.1.call-done), kind=kOutput, calls=%fused_computation.51 | convolution fusion | flops 5638193152 | bytes 15859712 | tf_op jit(solution)/shard_map/dot_general | solution.py:32
  717.5 6.9 fusion.41
  724.5 2.9 copy.434
  727.4 5.3 all-to-all-start.3
  734.1 32.0 %all-to-all-done.3 = bf16[4,64,3072]{2,1,0:T(8,128)(2,1)} async-done(((bf16[4,64,3072]{2,1,0:T(8,128)(2,1)}), bf16[4,64,3072]{2,1,0:T(8,128)(2,1)}, u32[]{:S(2)}, u32[]{:S(2)}) %all-to-all-start.3) | async-done | bytes 1572896 | tf_op jit(solution)/shard_map/all_to_all | solution.py:187
  766.1 46.9 %reduce-scatter.15.cloned.1.call-done = bf16[256,3712]{1,0:T(8,128)(2,1)} async-done(((bf16[2048,3712]{1,0:T(8,128)(2,1)}), bf16[256,3712]{1,0:T(8,128)(2,1)}) %reduce-scatter.15.cloned.1.call-update) | async-done | bytes 1900560 | tf_op jit(solution)/shard_map/reduce_scatter | solution.py:185
  813.0 5.3 all-to-all-start.2
  818.5 22.7 %psum.23 = f32[1,7204]{1,0:T(1,128)S(1)} all-reduce(f32[1,7204]{1,0:T(1,128)S(1)} %all_gather.38), channel_id=1, replica_groups=mesh['fsdp'=8,'rep'=4] {'fsdp':(4)2,'rep'}, use_global_device_ids=true, to_apply=%region_40.41 | all-reduce | flops 7204 | bytes 57632 | tf_op jit(solution)/shard_map/psum | solution.py:369
  841.2 59.8 %all-gather.2 = f32[4,1,7204]{2,1,0:T(1,128)S(1)} all-gather(f32[1,1,7204]{2,1,0:T(1,128)S(1)} %bitcast.328), channel_id=1, replica_groups=mesh['fsdp'=8,'rep'=4] {'fsdp':(1)4}, dimensions={0}, use_global_device_ids=true | all-gather | bytes 144080 | tf_op jit(solution)/shard_map/all_gather | solution.py:369
  906.2 31.9 %reduce-scatter.9.cloned.1.call-done = bf16[128,2048]{1,0:T(8,128)(2,1)} async-done(((bf16[512,2048]{1,0:T(8,128)(2,1)}), bf16[128,2048]{1,0:T(8,128)(2,1)}) %reduce-scatter.9.cloned.1.call-update) | async-done | bytes 524304 | tf_op jit(solution)/shard_map/reduce_scatter | solution.py:201
  938.1 3.2 fusion.83
  (481 shorter events, 130.9 us)
Async XLA Ops:
  7.2 104.5 %all-gather.10.cloned.1.call-start = ((), (), s32[]{:S(2)}) async-start(), calls=%async_computation.10 | async-start | bytes 2621440 | tf_op jit(solution)/shard_map/all_gather | solution.py:198
  11.4 169.5 %all-gather.12.cloned.1.call-start = ((), (), s32[]{:S(2)}) async-start(), calls=%async_computation.11 | async-start | bytes 17104896 | tf_op jit(solution)/shard_map/all_gather | solution.py:182
  22.9 74.9 %copy-start.121 = (u32[32]{0:T(128)S(1)}, u32[32]{0:T(128)}, u32[]{:S(2)}) copy-start(u32[32]{0:T(128)} %constant.117) | copy-start | bytes 388
  22.9 76.2 %copy-start.110 = (s32[2,1]{0,1:T(1,128)S(1)}, s32[2,1]{0,1:T(1,128)}, u32[]{:S(2)}) copy-start(s32[2,1]{0,1:T(1,128)} %param.23) | copy-start | bytes 28
  22.9 76.3 %copy-start.120 = (s32[2,1]{0,1:T(1,128)S(1)}, s32[2,1]{0,1:T(1,128)}, u32[]{:S(2)}) copy-start(s32[2,1]{0,1:T(1,128)} %param.22) | copy-start | bytes 28
  22.9 83.3 %copy-start.118 = (f32[48]{0:T(128)S(1)}, f32[48]{0:T(128)}, u32[]{:S(2)}) copy-start(f32[48]{0:T(128)} %param.30) | copy-start | bytes 580
  22.9 83.9 %copy-start.119 = (f32[48]{0:T(128)S(1)}, f32[48]{0:T(128)}, u32[]{:S(2)}) copy-start(f32[48]{0:T(128)} %param.28) | copy-start | bytes 580
  22.9 85.1 %slice-start.6 = ((f32[3584]{0:T(1024)}), f32[3072]{0:T(1024)S(1)}, s32[]{:S(2)}) async-start(f32[3584]{0:T(1024)} %param.27), calls=%async_computation.28 | async-start | bytes 24576 | tf_op jit(solution)/shard_map/slice | solution.py:231
  23.0 86.5 %slice-start.4 = ((f32[4,3584]{1,0:T(4,128)}), f32[4,3072]{1,0:T(4,128)S(1)}, s32[]{:S(2)}) async-start(f32[4,3584]{1,0:T(4,128)} %param.26), calls=%async_computation.26 | async-start | bytes 98304 | tf_op jit(solution)/shard_map/slice | solution.py:230
  23.0 86.5 %slice-start.3 = ((f32[4,3584]{1,0:T(4,128)}), f32[4,512]{1,0:T(4,128)S(1)}, s32[]{:S(2)}) async-start(f32[4,3584]{1,0:T(4,128)} %param.26), calls=%async_computation.25 | async-start | bytes 16384 | tf_op jit(solution)/shard_map/slice | solution.py:230
  23.0 86.6 %copy-start.111 = (f32[48]{0:T(128)S(1)}, f32[48]{0:T(128)}, u32[]{:S(2)}) copy-start(f32[48]{0:T(128)} %param.29) | copy-start | bytes 580
  23.0 86.7 %slice-start.5 = ((f32[3584]{0:T(1024)}), f32[512]{0:T(512)S(1)}, s32[]{:S(2)}) async-start(f32[3584]{0:T(1024)} %param.27), calls=%async_computation.27 | async-start | bytes 4096 | tf_op jit(solution)/shard_map/slice | solution.py:231
  97.7 229.5 %reduce-scatter.7.cloned.1.call-start = ((), (), s32[]{:S(2)}) async-start(), calls=%async_computation.12 | async-start | bytes 2621440 | tf_op jit(solution)/shard_map/reduce_scatter | solution.py:201
  106.9 98.0 %copy-start.97 = (f32[12]{0:T(128)}, f32[12]{0:T(128)S(1)}, u32[]{:S(2)}) copy-start(f32[12]{0:T(128)S(1)} %dynamic_slice.20) | copy-start | bytes 148
  107.0 85.3 %copy-start.77 = (f32[8,64]{1,0:T(8,128)}, f32[8,64]{1,0:T(8,128)S(1)}, u32[]{:S(2)}) copy-start(f32[8,64]{1,0:T(8,128)S(1)} %get-tuple-element.109) | copy-start | bytes 6148
  109.6 83.1 %copy-start.64 = (f32[1280]{0:T(1024)}, f32[1280]{0:T(1024)S(1)}, u32[]{:S(2)}) copy-start(f32[1280]{0:T(1024)S(1)} %get-tuple-element.33) | copy-start | bytes 15364
  109.6 83.1 %copy-start.66 = (f32[1280]{0:T(1024)}, f32[1280]{0:T(1024)S(1)}, u32[]{:S(2)}) copy-start(f32[1280]{0:T(1024)S(1)} %get-tuple-element.34) | copy-start | bytes 15364
  109.6 83.1 %copy-start.68 = (f32[1280]{0:T(1024)}, f32[1280]{0:T(1024)S(1)}, u32[]{:S(2)}) copy-start(f32[1280]{0:T(1024)S(1)} %get-tuple-element.35) | copy-start | bytes 15364
  109.6 83.1 %copy-start.70 = (f32[1280]{0:T(1024)}, f32[1280]{0:T(1024)S(1)}, u32[]{:S(2)}) copy-start(f32[1280]{0:T(1024)S(1)} %get-tuple-element.36) | copy-start | bytes 15364
  109.6 117.2 %copy-start.92 = (f32[64]{0:T(128)}, f32[64]{0:T(128)S(1)}, u32[]{:S(2)}) copy-start(f32[64]{0:T(128)S(1)} %multiply_power_fusion) | copy-start | bytes 772
  109.7 95.1 %copy-start.98 = (f32[12]{0:T(128)}, f32[12]{0:T(128)S(1)}, u32[]{:S(2)}) copy-start(f32[12]{0:T(128)S(1)} %fusion.149) | copy-start | bytes 148
  109.8 117.0 %copy-start.72 = (f32[8,64]{1,0:T(8,128)}, f32[8,64]{1,0:T(8,128)S(1)}, u32[]{:S(2)}) copy-start(f32[8,64]{1,0:T(8,128)S(1)} %subtract_convert_fusion) | copy-start | bytes 6148
  114.0 78.3 %copy-start.107 = (f32[512]{0:T(512)}, f32[512]{0:T(512)S(1)}, u32[]{:S(2)}) copy-start(f32[512]{0:T(512)S(1)} %add_rsqrt_fusion.1) | copy-start | bytes 6148
  249.7 116.5 %all-gather.18.cloned.1.call-start = ((), (), s32[]{:S(2)}) async-start(), calls=%async_computation.16 | async-start | bytes 2621440 | tf_op jit(solution)/shard_map/all_gather | solution.py:198
  255.6 184.2 %all-gather.16.cloned.1.call-start = ((), (), s32[]{:S(2)}) async-start(), calls=%async_computation.14 | async-start | bytes 14155776 | tf_op jit(solution)/shard_map/all_gather | solution.py:182
  325.0 161.2 %all-gather.14.cloned.1.call-start = ((), (), s32[]{:S(2)}) async-start(), calls=%async_computation.13 | async-start | bytes 2621440 | tf_op jit(solution)/shard_map/all_gather | solution.py:198
  327.2 119.1 %copy-start.88 = (f32[128]{0:T(128)}, f32[128]{0:T(128)S(1)}, u32[]{:S(2)}) copy-start(f32[128]{0:T(128)S(1)} %reshape.614) | copy-start | bytes 1540
  329.2 117.1 %copy-start.90 = (f32[128]{0:T(128)}, f32[128]{0:T(128)S(1)}, u32[]{:S(2)}) copy-start(f32[128]{0:T(128)S(1)} %get-tuple-element.114) | copy-start | bytes 1540
  331.4 215.6 %reduce-scatter.11.cloned.1.call-start = ((), (), s32[]{:S(2)}) async-start(), calls=%async_computation.17 | async-start | bytes 2621440 | tf_op jit(solution)/shard_map/reduce_scatter | solution.py:201
  331.6 114.7 %copy-start.105 = (f32[512]{0:T(512)}, f32[512]{0:T(512)S(1)}, u32[]{:S(2)}) copy-start(f32[512]{0:T(512)S(1)} %reshape.617) | copy-start | bytes 6148
  504.9 92.8 %all-gather.20.cloned.1.call-start = ((), (), s32[]{:S(2)}) async-start(), calls=%async_computation.18 | async-start | bytes 2621440 | tf_op jit(solution)/shard_map/all_gather | solution.py:198
  551.6 172.9 %reduce-scatter.17.cloned.1.call-start = ((), (), s32[]{:S(2)}) async-start(), calls=%async_computation.21 | async-start | bytes 14155776 | tf_op jit(solution)/shard_map/reduce_scatter | solution.py:185
  582.5 230.5 %reduce-scatter.15.cloned.1.call-start = ((), (), s32[]{:S(2)}) async-start(), calls=%async_computation.20 | async-start | bytes 17104896 | tf_op jit(solution)/shard_map/reduce_scatter | solution.py:185
  706.5 198.4 %reduce-scatter.13.cloned.1.call-start = ((), (), s32[]{:S(2)}) async-start(), calls=%async_computation.19 | async-start | bytes 2621440 | tf_op jit(solution)/shard_map/reduce_scatter | solution.py:201
  717.5 220.7 %reduce-scatter.9.cloned.1.call-start = ((), (), s32[]{:S(2)}) async-start(), calls=%async_computation.15 | async-start | bytes 2621440 | tf_op jit(solution)/shard_map/reduce_scatter | solution.py:201
  727.4 38.7 %all-to-all-start.3 = ((bf16[4,64,3072]{2,1,0:T(8,128)(2,1)}), bf16[4,64,3072]{2,1,0:T(8,128)(2,1)}, u32[]{:S(2)}, u32[]{:S(2)}) async-start(bf16[4,64,3072]{2,1,0:T(8,128)(2,1)} %bitcast.275), calls=%async_computation.9 | async-start | bytes 3145728 | tf_op jit(solution)/shard_map/all_to_all | solution.py:187
  732.7 85.6 %copy-start.104 = (f32[12]{0:T(128)S(1)}, f32[12]{0:T(128)}, u32[]{:S(2)}) copy-start(f32[12]{0:T(128)} %get-tuple-element.95) | copy-start | bytes 148
  732.7 85.6 %copy-start.112 = (f32[48]{0:T(128)S(1)}, f32[48]{0:T(128)}, u32[]{:S(2)}) copy-start(f32[48]{0:T(128)} %param.29) | copy-start | bytes 580
  732.7 85.6 %copy-start.84 = (f32[1280]{0:T(1024)S(1)}, f32[1280]{0:T(1024)}, u32[]{:S(2)}) copy-start(f32[1280]{0:T(1024)} %get-tuple-element.30) | copy-start | bytes 15364
  732.8 85.6 %copy-start.85 = (f32[768]{0:T(1024)S(1)}, f32[768]{0:T(1024)}, u32[]{:S(2)}) copy-start(f32[768]{0:T(1024)} %get-tuple-element.25) | copy-start | bytes 9220
  732.8 85.6 %copy-start.99 = (f32[12]{0:T(128)S(1)}, f32[12]{0:T(128)}, u32[]{:S(2)}) copy-start(f32[12]{0:T(128)} %get-tuple-element.41) | copy-start | bytes 148
  813.0 125.1 %copy-start.12 = (bf16[128,2048]{1,0:T(8,128)(2,1)S(1)}, bf16[128,2048]{1,0:T(8,128)(2,1)}, u32[]{:S(2)}) copy-start(bf16[128,2048]{1,0:T(8,128)(2,1)} %copy.408) | copy-start | bytes 1572868
  813.0 125.1 %copy-start.13 = (bf16[128,2048]{1,0:T(8,128)(2,1)S(1)}, bf16[128,2048]{1,0:T(8,128)(2,1)}, u32[]{:S(2)}) copy-start(bf16[128,2048]{1,0:T(8,128)(2,1)} %reduce-scatter.11.cloned.1.call-done) | copy-start | bytes 1572868
  813.0 125.1 %copy-start.89 = (f32[128]{0:T(128)S(1)}, f32[128]{0:T(128)}, u32[]{:S(2)}) copy-start(f32[128]{0:T(128)} %copy-done.88) | copy-start | bytes 1540
  813.0 125.1 %copy-start.91 = (f32[128]{0:T(128)S(1)}, f32[128]{0:T(128)}, u32[]{:S(2)}) copy-start(f32[128]{0:T(128)} %copy-done.90) | copy-start | bytes 1540
  813.0 125.1 %copy-start.94 = (f32[128]{0:T(128)S(1)}, f32[128]{0:T(128)}, u32[]{:S(2)}) copy-start(f32[128]{0:T(128)} %get-tuple-element.113) | copy-start | bytes 1540
  813.0 125.1 %copy-start.96 = (f32[128]{0:T(128)S(1)}, f32[128]{0:T(128)}, u32[]{:S(2)}) copy-start(f32[128]{0:T(128)} %copy-done.95) | copy-start | bytes 1540
  813.0 140.6 %all-to-all-start.2 = ((bf16[4,64,3712]{2,1,0:T(8,128)(2,1)}), bf16[4,64,3712]{2,1,0:T(8,128)(2,1)}, u32[]{:S(2)}, u32[]{:S(2)}) async-start(bf16[4,64,3712]{2,1,0:T(8,128)(2,1)} %bitcast.295), calls=%async_computation.7 | async-start | bytes 3801088 | tf_op jit(solution)/shard_map/all_to_all | solution.py:187
  (100 other events, 607.1 us)
Sparse Core Ops, SparseCore 0:
  11.5 78.4 all-gather.9
  97.9 82.9 all-gather.11
  249.8 70.6 reduce-scatter.6
  322.0 44.1 all-gather.17
  368.1 71.6 all-gather.15
  441.9 44.3 all-gather.13
  505.0 41.9 reduce-scatter.10
  551.7 45.9 all-gather.19
  601.2 92.7 reduce-scatter.16
  706.6 106.3 reduce-scatter.14
  815.3 78.5 reduce-scatter.12
  896.1 41.9 reduce-scatter.8

commit v2 on v1

v2 whole, which is shorter than its diff:
```python
import functools
import math

import jax
import jax.numpy as jnp
from jax import lax
from jax.experimental import pallas as pl
from jax.experimental.pallas import tpu as pltpu
from jax.sharding import Mesh
from jax.sharding import PartitionSpec as P

HD = 128
TP = 4

epsilon = 1e-05
rope_base = 100000000000.0
highest = lax.Precision.HIGHEST
f32 = jnp.float32
bf16 = jnp.bfloat16


def inverse_root(values):
    return lax.rsqrt(jnp.mean(values * values, axis=-1, keepdims=True) + epsilon)


def norm_back(values, root, grad):
    return root * grad - values * root**3 * jnp.mean(values * grad, axis=-1, keepdims=True)


def dot_nn(left, right):
    return jnp.dot(left, right, preferred_element_type=f32)


def dot_nt(left, right):
    return lax.dot_general(left, right, (((1,), (1,)), ((), ())), preferred_element_type=f32)


def inside_rows(length, offset, width):
    rows = jnp.arange(width, dtype=jnp.int32)[:, None]
    return ((rows >= offset) & (rows < offset + length)).astype(f32)


def turn_table(offsets, width):
    half = HD // 2
    freqs = rope_base ** (-jnp.arange(half, dtype=f32) * 2.0 / HD)
    rows = jnp.arange(width, dtype=jnp.int32)
    positions = (rows[None, :] - offsets[:, None]).astype(f32)
    angles = positions.reshape(-1, 1) * freqs
    cosine, sine = jnp.cos(angles), jnp.sin(angles)
    return jnp.concatenate([cosine, cosine, -sine, sine], axis=1)


def mm(left, right, dims, precision=lax.Precision.HIGH):
    return lax.dot_general(left, right, (dims, ((), ())), precision=precision, preferred_element_type=f32)


NN = ((1,), (0,))
NT = ((1,), (1,))
TN = ((0,), (0,))


def iota(shape, axis):
    return lax.broadcasted_iota(jnp.int32, shape, axis)


def down_rows(values, count):
    if count == 0:
        return values
    return jnp.where(iota(values.shape, 0) >= count, pltpu.roll(values, count, axis=0), 0.0)


def up_rows(values, count):
    if count == 0:
        return values
    length = values.shape[0]
    return jnp.where(
        iota(values.shape, 0) < length - count, pltpu.roll(values, length - count, axis=0), 0.0
    )


def head_sums(values, spread):
    return mm(values, spread, NT)


def mamba_shared(proj, start, count, taps_ref, bias_ref, steps_ref, inner, state, heads):
    length = proj.shape[0]
    conv_cols = inner + 2 * state
    row = iota((length, 1), 0)
    inside = ((row >= start) & (row < start + count)).astype(f32)
    conv_in = proj[:, inner : inner + conv_cols] * inside
    kernel = taps_ref.shape[0]
    conv = bias_ref[...] + jnp.zeros_like(conv_in)
    for tap in range(kernel):
        conv = conv + taps_ref[tap : tap + 1, :] * down_rows(conv_in, kernel - 1 - tap)
    sig = jax.nn.sigmoid(conv)
    active = conv * sig
    pad = steps_ref.shape[1]
    lane = iota((length, pad), 1)
    raw = jnp.where(lane < heads, proj[:, inner + conv_cols : inner + conv_cols + pad] + steps_ref[0:1, :], 0.0)
    step = jnp.where(lane < heads, jnp.maximum(raw, 0.0) + jnp.log1p(jnp.exp(-jnp.abs(raw))), 0.0)
    rate = -jnp.exp(steps_ref[1:2, :])
    lower = (iota((length, length), 0) >= iota((length, length), 1)).astype(f32)
    cum = mm(lower, step * rate, NN, highest)
    size = inner // heads
    spread = (iota((pad, inner), 0) == iota((pad, inner), 1) // size).astype(f32)
    step_x = mm(step, spread, NN)
    cum_x = mm(cum, spread, NN, highest)
    at = iota((length, inner), 1) % length
    diagonal = iota((length, inner), 0) == at
    cum_row = jnp.sum(jnp.where(diagonal, cum_x, 0.0), axis=0, keepdims=True)
    allowed = (
        (at <= iota((length, inner), 0)) & (inside > 0.0) & (at >= start) & (at < start + count)
    )
    decay = jnp.where(allowed, jnp.exp(jnp.where(allowed, cum_x - cum_row, 0.0)), 0.0)
    xs = active[:, :inner]
    b_state = active[:, inner : inner + state]
    c_state = active[:, inner + state :]
    inter = mm(c_state, b_state, NT)
    pair = jnp.concatenate([inter, inter], axis=1)
    mixing = decay * jnp.concatenate([pair] * (inner // pair.shape[1]), axis=1)
    return dict(
        inside=inside, conv_in=conv_in, conv=conv, sig=sig, raw=raw, step=step, rate=rate,
        spread=spread, step_x=step_x, diagonal=diagonal, decay=decay, mixing=mixing, xs=xs,
        b_state=b_state, c_state=c_state, lower=lower, lane=lane,
    )


def two_blocks(values):
    left = iota(values.shape, 1) < values.shape[1] // 2
    return jnp.concatenate([jnp.where(left, values, 0.0), jnp.where(left, 0.0, values)], axis=0)


def turn(values, cosine, sine):
    return values * cosine + pltpu.roll(values, HD // 2, axis=1) * sine


def attention_shared(proj, at, start, count, cosine, sine):
    length = proj.shape[0]
    kv = proj.shape[1] - 2 * HD
    queries = jnp.concatenate(
        [turn(proj[:, c : c + HD], cosine, sine) for c in range(at, kv, HD)], axis=0
    )
    keys = turn(proj[:, kv : kv + HD], cosine, sine)
    values = proj[:, kv + HD :]
    scores = mm(queries, keys, NT) * (1.0 / math.sqrt(HD))
    row = iota(scores.shape, 0) % length
    col = iota(scores.shape, 1)
    end = start + count
    allowed = ((row >= start) & (row < end) & (col >= start) & (col <= row)) | (row == col)
    scores = jnp.where(allowed, scores, -1e30)
    probs = jnp.exp(scores - jnp.max(scores, axis=1, keepdims=True))
    probs = probs / jnp.sum(probs, axis=1, keepdims=True)
    return queries, keys, values, probs


def specs(*shapes):
    return [pl.BlockSpec(s, lambda i: (0, 0)) for s in shapes]


def rows_spec(length, cols):
    return pl.BlockSpec((length, cols), lambda i: (i, 0))


def their_spec(length, each, k):
    return pl.BlockSpec((1, 1, length), lambda i: (i ^ (THEIRS[k][0] * each), 0, 0))


big = pltpu.CompilerParams(vmem_limit_bytes=50 * 1024 * 1024)


def costs(microseconds):
    return pl.CostEstimate(
        flops=microseconds * 10**9, bytes_accessed=microseconds * 10**5, transcendentals=0
    )


def inside_of(slots_ref, seq, length):
    row = iota((length, 1), 0)
    start = slots_ref[seq, 1]
    return ((row >= start) & (row < start + slots_ref[seq, 0])).astype(f32)


def as_row(column):
    length = column.shape[0]
    same = iota((length, length), 0) == iota((length, length), 1)
    return jnp.sum(jnp.where(same, column, 0.0), axis=0, keepdims=True)


def as_column(row):
    length = row.shape[1]
    same = iota((length, length), 0) == iota((length, length), 1)
    return jnp.sum(jnp.where(same, row, 0.0), axis=1, keepdims=True)


THEIRS = ((0, 1, 2, 3), (2, 3, 0, 1), (3, 2, 1, 0), (1, 0, 3, 2))


def group_total(refs, seq):
    each = refs[0].shape[0] // TP
    return sum(ref[THEIRS[k][seq // each] * each + seq % each] for k, ref in enumerate(refs))


def joined_rows(refs):
    own, far, pair, near, last = refs
    half = far.shape[1]
    count = own.shape[0]
    left = jnp.concatenate([own[:, :half], far[...], pair[...]], axis=0)
    right = jnp.concatenate([own[:, half:], last[:count, :], near[...], last[count:, :]], axis=0)
    return jnp.concatenate([left, right], axis=1)


def put_left(values, refs):
    half = values.shape[0] // 2
    refs[0][...] = values[:half]
    refs[1][...] = values[half:].astype(bf16)


def put_right(values, refs):
    one = values.shape[0] // TP
    refs[2][:one, :] = values[:one]
    refs[2][one:, :] = values[2 * one : 3 * one]
    refs[3][:one, :] = values[one : 2 * one].astype(bf16)
    refs[3][one:, :] = values[3 * one :].astype(bf16)


def put_tiles(values, refs):
    step = pl.program_id(0)
    middle = pl.num_programs(0) // 2

    @pl.when(step < middle)
    def _():
        put_left(values, refs)

    @pl.when(step >= middle)
    def _():
        put_right(values, refs)


def halves_out(rows, model, tile):
    middle = model // tile // 2
    left = pl.BlockSpec((rows // 2, tile), lambda j: (0, jnp.minimum(j, middle - 1)))
    right = pl.BlockSpec((rows // 2, tile), lambda j: (0, jnp.maximum(j - middle, 0)))
    shapes = [jax.ShapeDtypeStruct((rows // 2, model // 2), t) for t in (f32, bf16, f32, bf16)]
    return [left, left, right, right], shapes


def both_halves(refs):
    kept, got, kept_right, got_right = refs
    return jnp.concatenate(
        [kept[...] + got[...].astype(f32), kept_right[...] + got_right[...].astype(f32)], axis=1
    )


def inner_kernel(
    inner, state, heads, tiles, slots_ref, p0, p1, p2, p3, p4, weight_ref, gains_in_ref, taps_ref, bias_ref,
    steps_ref, skip_ref, turn_ref, normed_ref, proj_ref, y_ref, square_ref, mixed_ref, gains_ref,
):
    step = pl.program_id(0)
    tile = weight_ref.shape[1]

    @pl.when(step == 0)
    def _():
        rows = joined_rows((p0, p1, p2, p3, p4)).astype(f32)
        turned = jnp.transpose(gains_in_ref[...].astype(f32))
        gains_ref[0:1, :] = turned[heads : heads + 1]
        gains_ref[1:2, :] = turned[heads + 1 : heads + 2]
        normed_ref[...] = (rows * inverse_root(rows) * turned[heads : heads + 1]).astype(bf16)

    @pl.when(step < tiles)
    def _():
        at = pl.multiple_of(step * tile, tile)
        proj_ref[:, pl.ds(at, tile)] = jnp.dot(
            normed_ref[...], weight_ref[...], preferred_element_type=f32
        )

    @pl.when(step >= tiles)
    def _():
        seq = step - tiles
        length = y_ref.shape[0]
        proj = proj_ref[pl.ds(pl.multiple_of(seq * length, length), length), :]
        start = slots_ref[seq, 1]
        count = slots_ref[seq, 0]
        m = mamba_shared(proj, start, count, taps_ref, bias_ref, steps_ref, inner, state, heads)
        scaled = m["xs"] * m["step_x"]
        wide = 2 * length
        parts = [
            mm(m["mixing"][:, c : c + wide], two_blocks(scaled[:, c : c + wide]), NN)
            for c in range(0, inner, wide)
        ]
        y = jnp.concatenate(parts, axis=1) + skip_ref[...] * m["xs"]
        y_ref[...] = y
        gate = proj[:, :inner]
        gated = y * gate * jax.nn.sigmoid(gate)
        square_ref[0] = as_row(jnp.sum(gated * gated, axis=1, keepdims=True))
        at = 2 * inner + 2 * state + steps_ref.shape[1]
        _, _, values, probs = attention_shared(
            proj, at, start, count, turn_ref[:, :HD], turn_ref[:, HD:]
        )
        mixed = mm(probs, values, NN)
        mixed_ref[...] = jnp.concatenate(
            [mixed[r : r + length] for r in range(0, mixed.shape[0], length)], axis=1
        ).astype(mixed_ref.dtype)


def mixer_inner(slots, rows, weight, taps, bias, steps, skip, turns, inner, state, heads, tile=384):
    model, cols = weight.shape
    seqs = slots.shape[0]
    pieces = rows
    rows = TP * pieces[0].shape[0]
    length = rows // seqs
    tiles = cols // tile
    pad = steps.shape[1]
    at_steps = (2 * inner + 2 * state) // pad
    q_cols = cols - 2 * inner - 2 * state - pad - 2 * HD

    def seq_spec(*shape):
        zeros = (0,) * (len(shape) - 1)
        return pl.BlockSpec(shape, lambda j: (jnp.maximum(j - tiles, 0),) + zeros)

    return pl.pallas_call(
        functools.partial(inner_kernel, inner, state, heads, tiles),
        grid=(tiles + seqs,),
        in_specs=[pl.BlockSpec(memory_space=pltpu.SMEM)]
        + specs(*[p.shape for p in pieces])
        + [
            pl.BlockSpec((model, tile), lambda j: (0, jnp.minimum(j, tiles - 1))),
            pl.BlockSpec((model, pad), lambda j: (0, at_steps)),
        ]
        + specs(taps.shape, bias.shape, steps.shape, skip.shape)
        + [seq_spec(length, turns.shape[1])],
        out_specs=specs((rows, model), (rows, cols))
        + [seq_spec(length, inner), seq_spec(1, 1, length), seq_spec(length, q_cols)]
        + specs((8, model)),
        out_shape=[
            jax.ShapeDtypeStruct((rows, model), bf16),
            jax.ShapeDtypeStruct((rows, cols), f32),
            jax.ShapeDtypeStruct((rows, inner), f32),
            jax.ShapeDtypeStruct((seqs, 1, length), f32),
            jax.ShapeDtypeStruct((rows, q_cols), bf16),
            jax.ShapeDtypeStruct((8, model), f32),
        ],
        compiler_params=big,
        cost_estimate=costs(18),
    )(slots, *pieces, weight, weight, taps, bias, steps, skip, turns)


def outer_kernel(inner, gate_ref, y_ref, mixed_ref, gain_ref, s0, s1, s2, s3, weight_ref, branches_ref, root_ref, *halves):
    @pl.when(pl.program_id(0) == 0)
    def _():
        length = root_ref.shape[2]
        for seq in range(root_ref.shape[0]):
            rows = slice(seq * length, (seq + 1) * length)
            root = lax.rsqrt(group_total((s0, s1, s2, s3), seq) / (TP * inner) + epsilon)
            root_ref[seq] = root
            gate = gate_ref[rows, :]
            gated = y_ref[rows, :] * gate * jax.nn.sigmoid(gate)
            branches_ref[rows, :inner] = (gated * as_column(root) * gain_ref[...]).astype(bf16)
        branches_ref[:, inner:] = mixed_ref[...]

    put_tiles(dot_nt(branches_ref[...], weight_ref[...]), halves)


def mixer_outer(proj, y, mixed, gain, squares, weight, tile=512):
    rows, inner = y.shape
    model, cols = weight.shape
    half_specs, half_shapes = halves_out(rows, model, tile)
    return pl.pallas_call(
        functools.partial(outer_kernel, inner),
        grid=(model // tile,),
        in_specs=specs((rows, inner), y.shape, mixed.shape, gain.shape)
        + [pl.BlockSpec(squares[0].shape, lambda j: (0, 0, 0))] * TP
        + [pl.BlockSpec((tile, cols), lambda j: (j, 0))],
        out_specs=specs((rows, cols))
        + [pl.BlockSpec(squares[0].shape, lambda j: (0, 0, 0))]
        + half_specs,
        out_shape=[
            jax.ShapeDtypeStruct((rows, cols), bf16),
            jax.ShapeDtypeStruct(squares[0].shape, f32),
        ]
        + half_shapes,
        compiler_params=big,
        cost_estimate=costs(4),
    )(proj, y, mixed, gain, *squares, weight)


def back_out_kernel(left_ref, weight_ref, *halves):
    put_tiles(dot_nt(left_ref[...], weight_ref[...]), halves)


def back_out(left, weight, column, tile=512):
    rows, cols = left.shape
    model = weight.shape[0]
    half_specs, half_shapes = halves_out(rows, model, tile)
    return pl.pallas_call(
        back_out_kernel,
        grid=(model // tile,),
        in_specs=specs(left.shape) + [pl.BlockSpec((tile, cols), lambda j: (j, column))],
        out_specs=half_specs,
        out_shape=half_shapes,
        compiler_params=big,
        cost_estimate=costs(4),
    )(left, weight)


def inside_all(slots_ref, seqs, length):
    return jnp.concatenate([inside_of(slots_ref, seq, length) for seq in range(seqs)], axis=0)


def hidden_kernel(slots_ref, k0, k1, k2, k3, source_ref, gains_ref, hidden_ref, second_ref):
    length = source_ref.shape[0] * TP // slots_ref.shape[0]
    inside = inside_all(slots_ref, slots_ref.shape[0] // TP, length)
    hidden = source_ref[...].astype(f32) + inside * both_halves((k0, k1, k2, k3))
    hidden_ref[...] = hidden
    second_ref[...] = (hidden * inverse_root(hidden) * gains_ref[1:2, :]).astype(bf16)


def row_call(kernel, slots, halves, *others):
    shape = others[0].shape
    return pl.pallas_call(
        kernel,
        grid=(1,),
        in_specs=[pl.BlockSpec(memory_space=pltpu.SMEM)]
        + specs(*[h.shape for h in halves], *[o.shape for o in others]),
        out_specs=specs(shape, shape),
        out_shape=[jax.ShapeDtypeStruct(shape, f32), jax.ShapeDtypeStruct(shape, bf16)],
        compiler_params=big,
        cost_estimate=costs(2),
    )(slots, *halves, *others)


def feed_kernel(
    slots_ref, s0, s1, s2, s3, s4, c0, c1, c2, c3, c4, gate_ref, up_ref, down_ref,
    second_ref, down_grad_ref, product_ref, gate_grad_ref, up_grad_ref, h0, h1, h2, h3, total,
):
    step = pl.program_id(0)

    @pl.when(step == 0)
    def _():
        second_ref[...] = joined_rows((s0, s1, s2, s3, s4))
        seqs = slots_ref.shape[0]
        inside = inside_all(slots_ref, seqs, TP * s0.shape[0] // seqs)
        down_grad_ref[...] = (inside * joined_rows((c0, c1, c2, c3, c4)).astype(f32)).astype(bf16)
        total[...] = jnp.zeros_like(total)

    second = second_ref[...]
    gate = jnp.dot(second, gate_ref[...], preferred_element_type=f32)
    up = jnp.dot(second, up_ref[...], preferred_element_type=f32)
    d_product = jnp.dot(down_grad_ref[...], down_ref[...], preferred_element_type=f32)
    sig = jax.nn.sigmoid(gate)
    swish = gate * sig
    product_ref[...] = (swish * up).astype(bf16)
    gate_grad = (d_product * up * sig * (1.0 + gate * (1.0 - sig))).astype(bf16)
    up_grad = (d_product * swish).astype(bf16)
    gate_grad_ref[...] = gate_grad
    up_grad_ref[...] = up_grad
    total[...] += dot_nt(gate_grad, gate_ref[...]) + dot_nt(up_grad, up_ref[...])

    @pl.when(step == pl.num_programs(0) - 1)
    def _():
        middle = total.shape[1] // 2
        put_left(total[:, :middle], (h0, h1))
        put_right(total[:, middle:], (h0, h1, h2, h3))


def feed_forward(slots, second, cotangent, weight, units, tile=512):
    count, model = second[0].shape
    rows = TP * count
    steps = units // tile
    half_shapes = halves_out(rows, model, tile)[1]
    shapes = [p.shape for p in second]
    unit = pl.BlockSpec((rows, tile), lambda j: (0, j))
    return pl.pallas_call(
        feed_kernel,
        grid=(steps,),
        in_specs=[pl.BlockSpec(memory_space=pltpu.SMEM)]
        + specs(*shapes, *shapes)
        + [
            pl.BlockSpec((model, tile), lambda j, at=at: (0, at * steps + j))
            for at in range(3)
        ],
        out_specs=specs((rows, model), (rows, model))
        + [unit] * 3
        + specs(*[h.shape for h in half_shapes]),
        out_shape=[jax.ShapeDtypeStruct((rows, model), bf16)] * 2
        + [jax.ShapeDtypeStruct((rows, units), bf16)] * 3
        + half_shapes,
        scratch_shapes=[pltpu.VMEM((rows, model), f32)],
        compiler_params=big,
        cost_estimate=costs(9),
    )(slots, *second, *cotangent, weight, weight, weight)


def back_hidden_kernel(slots_ref, k0, k1, k2, k3, hidden_ref, cotangent_ref, gains_ref, d_hidden_ref, branch_ref):
    grad = both_halves((k0, k1, k2, k3)) * gains_ref[1:2, :]
    hidden = hidden_ref[...]
    d_hidden = cotangent_ref[...].astype(f32) + norm_back(hidden, inverse_root(hidden), grad)
    d_hidden_ref[...] = d_hidden
    seqs = slots_ref.shape[0]
    inside = inside_all(slots_ref, seqs // TP, hidden.shape[0] * TP // seqs)
    branch_ref[...] = (inside * d_hidden).astype(bf16)


def back_outer_kernel(tiles, b0, b1, b2, b3, b4, weight_ref, gate_ref, y_ref, gain_ref, branch_ref, grad_ref, dots_ref, total):
    step = pl.program_id(0)

    @pl.when(step == 0)
    def _():
        branch_ref[...] = joined_rows((b0, b1, b2, b3, b4))
        total[...] = jnp.zeros_like(total)

    grad = jnp.dot(branch_ref[...], weight_ref[...], preferred_element_type=f32)
    grad_ref[...] = grad

    @pl.when(step < tiles)
    def _():
        gate = gate_ref[...]
        gated = y_ref[...] * gate * jax.nn.sigmoid(gate)
        total[...] += jnp.sum(gated * gain_ref[...] * grad, axis=1, keepdims=True)

    @pl.when(step == pl.num_programs(0) - 1)
    def _():
        length = dots_ref.shape[2]
        for seq in range(dots_ref.shape[0]):
            dots_ref[seq] = as_row(total[seq * length : (seq + 1) * length, :])


def back_outer(branch, weight, proj, y, gain, seqs, tile=256):
    model = weight.shape[0]
    rows, inner = y.shape
    cols = weight.shape[1]
    tiles = inner // tile
    length = rows // seqs
    inner_spec = pl.BlockSpec((rows, tile), lambda j: (0, jnp.minimum(j, tiles - 1)))
    return pl.pallas_call(
        functools.partial(back_outer_kernel, tiles),
        grid=(cols // tile,),
        in_specs=specs(*[p.shape for p in branch])
        + [
            pl.BlockSpec((model, tile), lambda j: (0, j)),
            inner_spec,
            inner_spec,
            pl.BlockSpec((1, tile), lambda j: (0, jnp.minimum(j, tiles - 1))),
        ],
        out_specs=specs((rows, model))
        + [
            pl.BlockSpec((rows, tile), lambda j: (0, j)),
            pl.BlockSpec((seqs, 1, length), lambda j: (0, 0, 0)),
        ],
        out_shape=[
            jax.ShapeDtypeStruct((rows, model), bf16),
            jax.ShapeDtypeStruct((rows, cols), f32),
            jax.ShapeDtypeStruct((seqs, 1, length), f32),
        ],
        scratch_shapes=[pltpu.VMEM((rows, 1), f32)],
        compiler_params=big,
        cost_estimate=costs(5),
    )(*branch, weight, proj, y, gain)


def backward_kernel(
    inner, state, heads, slots_ref, proj_ref, taps_ref, bias_ref, steps_ref, skip_ref, turn_ref,
    gain_ref, y_ref, grad_ref, root_ref, d0, d1, d2, d3, proj_grad_ref, conv_grad_ref, inner_grad_ref, step_grad_ref,
):
    step_id = pl.program_id(0)
    start = slots_ref[step_id, 1]
    count = slots_ref[step_id, 0]
    proj = proj_ref[...]
    length = proj.shape[0]
    conv_cols = inner + 2 * state
    pad = steps_ref.shape[1]
    m = mamba_shared(proj, start, count, taps_ref, bias_ref, steps_ref, inner, state, heads)
    xs, decay, mixing = m["xs"], m["decay"], m["mixing"]
    scaled = xs * m["step_x"]
    gate = proj[:, :inner]
    gate_sig = jax.nn.sigmoid(gate)
    y = y_ref[...]
    root = as_column(root_ref[0])
    mean = as_column(sum(ref[0] for ref in (d0, d1, d2, d3))) / (TP * inner)
    gated = y * gate * gate_sig
    d_norm = grad_ref[:, :inner]
    d_gated = root * (d_norm * gain_ref[...]) - gated * (root * root * root * mean)
    dy = d_gated * gate * gate_sig
    d_gate = d_gated * y * gate_sig * (1.0 + gate * (1.0 - gate_sig))
    wide = 2 * length
    back, d_mix = [], []
    for c in range(0, inner, wide):
        dy_pair = dy[:, c : c + wide]
        full = mm(mixing[:, c : c + wide], dy_pair, TN)
        left = iota((length, wide), 1) < length
        back.append(jnp.where(left, full[:length], full[length:]))
        d_mix.append(mm(dy_pair, two_blocks(scaled[:, c : c + wide]), NT))
    back = jnp.concatenate(back, axis=1)
    d_mix = jnp.concatenate(d_mix, axis=1)
    d_xs = skip_ref[...] * dy + m["step_x"] * back
    flow = d_mix * mixing
    flow = flow - jnp.where(m["diagonal"], jnp.sum(flow, axis=0, keepdims=True), 0.0)
    d_cum = head_sums(flow, m["spread"])
    d_rate = mm(m["lower"], d_cum, TN, highest)
    d_step = head_sums(xs * back, m["spread"]) + d_rate * m["rate"]
    d_raw = jnp.where(m["lane"] < heads, d_step * jax.nn.sigmoid(m["raw"]), 0.0)
    d_inter = d_mix * decay
    pair = d_inter[:, :wide]
    for c in range(wide, inner, wide):
        pair = pair + d_inter[:, c : c + wide]
    d_inter = pair[:, :length] + pair[:, length:]
    d_b = mm(d_inter, m["c_state"], TN)
    d_c = mm(d_inter, m["b_state"], NN)
    d_active = jnp.concatenate([d_xs, d_b, d_c], axis=1)
    sig, conv = m["sig"], m["conv"]
    d_conv = d_active * sig * (1.0 + conv * (1.0 - sig))
    kernel = taps_ref.shape[0]
    d_in = jnp.zeros_like(d_conv)
    conv_rows = []
    for tap in range(kernel):
        back_by = kernel - 1 - tap
        d_in = d_in + taps_ref[tap : tap + 1, :] * up_rows(d_conv, back_by)
        conv_rows.append(jnp.sum(d_conv * down_rows(m["conv_in"], back_by), axis=0, keepdims=True))
    conv_rows.append(jnp.sum(d_conv, axis=0, keepdims=True))
    conv_rows.append(jnp.zeros((8 - kernel - 1, conv_cols), f32))
    conv_rows = jnp.concatenate(conv_rows, axis=0)
    inner_rows = jnp.concatenate(
        [
            jnp.sum(gated * root * d_norm, axis=0, keepdims=True),
            jnp.sum(dy * xs, axis=0, keepdims=True),
            jnp.zeros((6, inner), f32),
        ],
        axis=0,
    )
    step_rows = jnp.concatenate(
        [
            jnp.sum(d_raw, axis=0, keepdims=True),
            jnp.sum(d_rate * m["step"] * m["rate"], axis=0, keepdims=True),
            jnp.zeros((6, pad), f32),
        ],
        axis=0,
    )

    @pl.when(step_id == 0)
    def _():
        conv_grad_ref[...] = jnp.zeros_like(conv_grad_ref)
        inner_grad_ref[...] = jnp.zeros_like(inner_grad_ref)
        step_grad_ref[...] = jnp.zeros_like(step_grad_ref)

    conv_grad_ref[...] += conv_rows
    inner_grad_ref[...] += inner_rows
    step_grad_ref[...] += step_rows

    at = inner + conv_cols + pad
    cosine, sine = turn_ref[:, :HD], turn_ref[:, HD:]
    queries, keys, values, probs = attention_shared(proj, at, start, count, cosine, sine)
    d_out = jnp.concatenate(
        [grad_ref[:, c : c + HD] for c in range(inner, grad_ref.shape[1], HD)], axis=0
    )
    d_values = mm(probs, d_out, TN)
    d_probs = mm(d_out, values, NT)
    d_scores = probs * (d_probs - jnp.sum(probs * d_probs, axis=1, keepdims=True)) * (1.0 / math.sqrt(HD))
    d_queries = mm(d_scores, keys, NN)
    d_keys = mm(d_scores, queries, TN)
    outs = [d_gate, d_in * m["inside"], d_raw]
    outs += [turn(d_queries[r : r + length], cosine, -sine) for r in range(0, d_queries.shape[0], length)]
    outs += [turn(d_keys, cosine, -sine), d_values]
    proj_grad_ref[...] = jnp.concatenate(outs, axis=1).astype(proj_grad_ref.dtype)


def mixer_backward(
    slots, proj, taps, bias, steps, skip, turns, gain, y, grads, root, dots, inner, state, heads
):
    seqs = slots.shape[0]
    rows, cols = proj.shape
    length = rows // seqs
    conv_cols = inner + 2 * state
    pad = steps.shape[1]
    return pl.pallas_call(
        functools.partial(backward_kernel, inner, state, heads),
        grid=(seqs,),
        in_specs=[pl.BlockSpec(memory_space=pltpu.SMEM), rows_spec(length, cols)]
        + specs(taps.shape, bias.shape, steps.shape, skip.shape)
        + [rows_spec(length, turns.shape[1])]
        + specs(gain.shape)
        + [rows_spec(length, inner), rows_spec(length, grads.shape[1])]
        + [pl.BlockSpec((1, 1, length), lambda i: (i, 0, 0))]
        + [their_spec(length, seqs // TP, k) for k in range(TP)],
        out_specs=[rows_spec(length, cols)] + specs((8, conv_cols), (8, inner), (8, pad)),
        out_shape=[
            jax.ShapeDtypeStruct((rows, cols), bf16),
            jax.ShapeDtypeStruct((8, conv_cols), f32),
            jax.ShapeDtypeStruct((8, inner), f32),
            jax.ShapeDtypeStruct((8, pad), f32),
        ],
        compiler_params=big,
        cost_estimate=costs(17),
    )(slots, proj, taps, bias, steps, skip, turns, gain, y, grads, root, *dots)


def chip_kernel(keep_ref, got_ref, mine_ref, along_y_ref, along_x_ref, across_x_ref, across_y_ref):
    total = (keep_ref[...].astype(f32) + got_ref[...].astype(f32)).astype(bf16)
    block = mine_ref.shape[0]
    half = across_x_ref.shape[0]
    mine_ref[...] = total[:block]
    along_y_ref[...] = total[block : 2 * block]
    along_x_ref[...] = total[2 * block : 3 * block]
    across_x_ref[...] = total[3 * block : 3 * block + half]
    across_y_ref[...] = total[3 * block + half :]


def along_kernel(along_y_ref, along_x_ref, by_x_ref, by_y_ref, to_y_ref, to_x_ref):
    half = by_x_ref.shape[0]
    to_y_ref[...] = along_y_ref[...]
    to_y_ref[:half, :] = (along_y_ref[:half, :].astype(f32) + by_x_ref[...].astype(f32)).astype(bf16)
    to_x_ref[...] = along_x_ref[...]
    to_x_ref[half:, :] = (along_x_ref[half:, :].astype(f32) + by_y_ref[...].astype(f32)).astype(bf16)


def plane_kernel(mine_ref, by_x_ref, by_y_ref, *outs):
    total = mine_ref[...].astype(f32) + by_x_ref[...].astype(f32) + by_y_ref[...].astype(f32)
    size = outs[0].shape[0]
    for k, out in enumerate(outs):
        out[...] = total[k * size : (k + 1) * size].astype(bf16)


def by_columns(kernel, row_counts, *arrays, tile=896):
    cols = arrays[0].shape[1]

    def of(rows):
        return pl.BlockSpec((rows, tile), lambda j: (0, j))

    return pl.pallas_call(
        kernel,
        grid=(cols // tile,),
        in_specs=[of(a.shape[0]) for a in arrays],
        out_specs=[of(r) for r in row_counts],
        out_shape=[jax.ShapeDtypeStruct((r, cols), bf16) for r in row_counts],
        compiler_params=big,
        cost_estimate=costs(3),
    )(*arrays)


def own_columns(me, refs, start, size, out_ref, at=0):
    for k, ref in enumerate(refs):
        place = pl.multiple_of((me ^ k) * size, 128)
        out_ref[:, pl.ds(at + place, size)] = ref[:, start : start + size].astype(f32)


def gain_sum(pairs, gain_ref):
    total = sum(
        jnp.sum(weight[...].astype(f32) * grad[...], axis=1, keepdims=True) for weight, grad in pairs
    )
    return total / gain_ref[...].astype(f32)


def unpack_mlp_kernel(units, me_ref, g0, g1, g2, g3, gate_ref, up_ref, gain_ref, grad_gate, grad_up, grad_down, grad_gain):
    for i, out in enumerate((grad_gate, grad_up, grad_down)):
        own_columns(me_ref[0], (g0, g1, g2, g3), i * units, units, out)
    grad_gain[...] = gain_sum(((gate_ref, grad_gate), (up_ref, grad_up)), gain_ref)


def unpack_out_kernel(inner, q_cols, me_ref, g0, g1, g2, g3, grad_mamba, grad_output):
    own_columns(me_ref[0], (g0, g1, g2, g3), 0, inner, grad_mamba)
    own_columns(me_ref[0], (g0, g1, g2, g3), inner, q_cols, grad_output)


def unpack_in_kernel(
    inner, state, heads, pad, me_ref, g0, g1, g2, g3, mamba_ref, query_ref, key_ref, value_ref, gain_ref,
    grad_mamba, grad_query, grad_key, grad_value, grad_gain,
):
    me = me_ref[0]
    refs = (g0, g1, g2, g3)
    own_columns(me, refs, 0, inner, grad_mamba)
    own_columns(me, refs, inner, inner, grad_mamba, TP * inner)
    at, out_at = 2 * inner, 2 * TP * inner
    shared = sum(ref[:, at : at + 2 * state].astype(f32) for ref in refs)
    grad_mamba[:, out_at : out_at + 2 * state] = shared
    at, out_at = at + 2 * state, out_at + 2 * state
    lane = iota((grad_mamba.shape[0], pad), 1)
    steps = jnp.zeros((grad_mamba.shape[0], pad), f32)
    for k, ref in enumerate(refs):
        piece = jnp.where(lane < heads, ref[:, at : at + pad].astype(f32), 0.0)
        steps = steps + pltpu.roll(piece, (me ^ k) * heads, axis=1)
    grad_mamba[:, out_at : out_at + TP * heads] = steps[:, : TP * heads]
    at += pad
    q_cols = query_ref.shape[1] // TP
    own_columns(me, refs, at, q_cols, grad_query)
    at += q_cols
    for out, start in ((grad_key, at), (grad_value, at + HD)):
        for first in (0, 2):
            both = refs[first][:, start : start + HD].astype(f32)
            both = both + refs[first + 1][:, start : start + HD].astype(f32)
            place = pl.multiple_of(((me ^ first) // 2) * HD, HD)
            out[:, pl.ds(place, HD)] = both
    pairs = ((mamba_ref, grad_mamba), (query_ref, grad_query), (key_ref, grad_key), (value_ref, grad_value))
    grad_gain[...] = gain_sum(pairs, gain_ref)


def unpack(kernel, me, parts, others, widths):
    rows = parts[0].shape[0]
    shapes = [(rows, w) for w in widths]
    return pl.pallas_call(
        kernel,
        grid=(1,),
        in_specs=[pl.BlockSpec(memory_space=pltpu.SMEM)]
        + specs(*[p.shape for p in parts], *[o.shape for o in others]),
        out_specs=specs(*shapes),
        out_shape=[jax.ShapeDtypeStruct(shape, f32) for shape in shapes],
        compiler_params=big,
        cost_estimate=costs(5),
    )(me, *parts, *others)


def weight_grad_kernel(bounds, mine, blocks, table_ref, *refs):
    parts = len(bounds)
    lefts = [refs[2 * mine * p : 2 * mine * p + mine] for p in range(parts)]
    rights = [refs[2 * mine * p + mine : 2 * mine * (p + 1)] for p in range(parts)]
    rest = refs[2 * mine * parts :]
    outs, plain, turned = rest[: -1 - parts], rest[-1 - parts], rest[-parts:]
    step = pl.program_id(0)
    size = plain.shape[0] // blocks

    @pl.when(step == 0)
    def _():
        for part in range(parts):
            plain[...] = jnp.concatenate([jnp.transpose(ref[...]) for ref in lefts[part]], axis=1)
            for block in range(blocks):
                at = pl.multiple_of(table_ref[block] * size, size)
                turned[part][block * size : (block + 1) * size, :] = plain[pl.ds(at, size), :]

    for part, (low, high) in enumerate(bounds):

        @pl.when((step >= low) & (step < high))
        def _(part=part):
            right = jnp.concatenate([ref[...] for ref in rights[part]], axis=0)
            full = jnp.dot(turned[part][...], right, preferred_element_type=f32)
            half = full.shape[0] // len(outs)
            for i, out in enumerate(outs):
                out[...] = full[i * half : (i + 1) * half].astype(out.dtype)


def weight_grads(table, pieces, pairs, tile=512):
    mine = len(pairs[0][0])
    rows, model = pairs[0][0][0].shape
    bounds, specs_in, args, low, cols = [], [], [], 0, 0
    for left, right, start, count in pairs:
        tiles = pl.cdiv(count, tile)
        first, last = low - start // tile, low + tiles - 1
        specs_in += [pl.BlockSpec((rows, model), lambda j: (0, 0))] * mine
        specs_in += [
            pl.BlockSpec(
                (rows, tile),
                lambda j, low=low, last=last, first=first: (0, jnp.clip(j, low, last) - first),
            )
        ] * mine
        args += list(left) + list(right)
        bounds.append((low, low + tiles))
        low += tiles
        cols += count
    return pl.pallas_call(
        functools.partial(weight_grad_kernel, tuple(bounds), mine, table.shape[0]),
        grid=(low,),
        in_specs=[pl.BlockSpec(memory_space=pltpu.SMEM)] + specs_in,
        out_specs=[pl.BlockSpec((model // pieces, tile), lambda j: (0, j))] * pieces,
        out_shape=[jax.ShapeDtypeStruct((model // pieces, cols), bf16)] * pieces,
        scratch_shapes=[pltpu.VMEM((model, mine * rows), bf16)] * (1 + len(pairs)),
        compiler_params=big,
        cost_estimate=costs(1 + cols // 256),
    )(table, *args)


def local(
    plane,
    tokens,
    lengths,
    offsets,
    norm_gain,
    mamba_in,
    conv_taps,
    conv_bias,
    step_bias,
    decay_log,
    skip_weight,
    mamba_gain,
    mamba_out,
    query_weight,
    key_weight,
    value_weight,
    output_weight,
    second_gain,
    gate_weight,
    up_weight,
    down_weight,
    cotangent,
):
    me = lax.axis_index("tp")
    peers = lax.axis_size(plane)
    batches, width, model = tokens.shape
    rows = batches * width
    shard = mamba_in.shape[0]
    inner = mamba_gain.shape[0]
    heads = step_bias.shape[0]
    state = (mamba_in.shape[1] - 2 * inner - heads) // 2
    q_cols = query_weight.shape[1]
    kv_heads = key_weight.shape[1] // HD
    hidden_units = gate_weight.shape[1]
    inner_t, heads_t, q_t, ff_t = inner // TP, heads // TP, q_cols // TP, hidden_units // TP
    pad = 128

    def swap(values, k, axis="tp"):
        size = lax.axis_size(axis)
        return lax.ppermute(values, axis, [(i, i ^ k) for i in range(size)])

    def spread_first(values):
        half = values.shape[1] // 2
        return swap(values[:, :half], 3), swap(values[:, half:], 1)

    def spread_second(values, far, near):
        half = values.shape[1] // 2
        pair = swap(jnp.concatenate([values[:, :half], far], axis=0), 1)
        last = swap(jnp.concatenate([values[:, half:], near], axis=0), 3)
        return values, far, pair, near, last

    def spread(values):
        return spread_second(values, *spread_first(values))

    def reduce_send(halves):
        return swap(halves[1], 1), swap(halves[3], 3)

    def reduce_add(halves, got, got_right):
        return halves[0] + got.astype(f32), halves[2] + got_right.astype(f32)

    def reduce_first(*halves):
        return reduce_add(halves, *reduce_send(halves))

    def reduce_second(pair, last):
        half = pair.shape[0] // 2
        got = swap(pair[half:].astype(bf16), 3)
        got_right = swap(last[half:].astype(bf16), 1)
        return pair[:half], got, last[:half], got_right

    def reduce(*halves):
        return reduce_second(*reduce_first(*halves))

    def everywhere(values):
        return [values] + [swap(values, k) for k in range(1, TP)]

    def absolute(parts):
        stacked = jnp.stack(parts)
        return jnp.concatenate(
            [lax.dynamic_index_in_dim(stacked, me ^ t, 0) for t in range(TP)], axis=0
        )

    cube = len(plane) == 3

    def order(values):
        lead = values.shape[:-1]
        if cube:
            split = values.reshape(lead + (TP, 2, 2, 2, shard))
            split = jnp.moveaxis(split, (-2, -4, -3, -5), (-5, -4, -3, -2))
        else:
            split = jnp.swapaxes(values.reshape(lead + (TP, peers, shard)), -3, -2)
        return split.reshape(values.shape)

    def unorder(values):
        lead = values.shape[:-1]
        if cube:
            split = values.reshape(lead + (2, 2, 2, TP, shard))
            split = jnp.moveaxis(split, (-5, -4, -3, -2), (-2, -4, -3, -5))
        else:
            split = jnp.swapaxes(values.reshape(lead + (peers, TP, shard)), -3, -2)
        return split.reshape(values.shape)

    blocks = jnp.arange(peers * TP, dtype=jnp.int32)
    in_group = blocks ^ me
    in_plane = blocks ^ (lax.axis_index(plane) * TP + me)

    def cut(weight, start, size, t):
        return lax.dynamic_slice_in_dim(weight, start + t * size, size, axis=1)

    def kv(weight, t):
        return cut(weight, 0, HD, t * kv_heads // TP)

    def in_slice(t):
        return jnp.concatenate(
            [
                cut(mamba_in, 0, inner_t, t),
                cut(mamba_in, inner, inner_t, t),
                mamba_in[:, 2 * inner : 2 * inner + 2 * state],
                cut(mamba_in, 2 * inner + 2 * state, heads_t, t),
                norm_gain[:, None],
                second_gain[:, None],
                jnp.zeros((shard, pad - heads_t - 2), bf16),
                cut(query_weight, 0, q_t, t),
                kv(key_weight, t),
                kv(value_weight, t),
            ],
            axis=1,
        )

    def out_slice(t):
        return jnp.concatenate([cut(mamba_out.T, 0, inner_t, t), cut(output_weight.T, 0, q_t, t)], axis=1)

    def mlp_slice(t):
        return jnp.concatenate(
            [
                cut(gate_weight, 0, ff_t, t),
                cut(up_weight, 0, ff_t, t),
                cut(down_weight.T, 0, ff_t, t),
            ],
            axis=1,
        )

    def after(values, *earlier):
        return lax.optimization_barrier((values, earlier))[0]

    def slices(make):
        return [make(me ^ k) for k in range(TP)]

    def exchange(pieces):
        return [pieces[0]] + [swap(pieces[k], k) for k in range(1, TP)]

    def gather(parts):
        return lax.all_gather(absolute(parts).reshape(TP * shard, -1), plane, axis=0, tiled=True)

    def scatter(grads):
        return lax.psum_scatter(grads, plane, scatter_dimension=0, tiled=True)

    def pass_on(part):
        part = part.reshape(TP, shard, -1)
        return exchange([part[k] for k in range(TP)])

    conv_cols = inner_t + 2 * state
    at_q = inner_t + conv_cols + pad
    in_cols = at_q + q_t + 2 * HD

    def own(values, size):
        return lax.dynamic_slice_in_dim(values, me * size, size, axis=-1)

    taps_t = jnp.concatenate([own(conv_taps[:, :inner], inner_t), conv_taps[:, inner:]], axis=1)
    bias_t = jnp.concatenate([own(conv_bias[:inner], inner_t), conv_bias[inner:]])[None]
    steps_t = jnp.pad(
        jnp.stack([own(step_bias, heads_t), own(decay_log, heads_t)]), ((0, 0), (0, pad - heads_t))
    )
    skip_t = jnp.repeat(own(skip_weight, heads_t), inner_t // heads_t)[None]
    gain_t = own(mamba_gain, inner_t)[None]
    sizes = (inner_t, state, heads_t)

    in_parts = exchange(slices(in_slice))
    w_in = gather(in_parts)
    slots = jnp.stack([lengths[:, 0], offsets[:, 0]], axis=1)
    slots = jnp.concatenate([slots] + [swap(slots, k) for k in (3, 1, 2)], axis=0)
    turns = turn_table(slots[:, 1], width)
    source = order(tokens.reshape(rows, model))
    upstream = order(cotangent.reshape(rows, model))
    prepared = (slots, turns, taps_t, bias_t, steps_t, skip_t, gain_t, in_plane, in_group, upstream)
    source, prepared = lax.optimization_barrier((source, (prepared, in_parts[1:])))
    slots, turns, taps_t, bias_t, steps_t, skip_t, gain_t, in_plane, in_group, upstream = prepared[0]
    source_all = spread(source)
    out_parts = exchange(after(slices(out_slice), source_all))
    w_out = gather(out_parts)
    mlp_parts = exchange(after(slices(mlp_slice), out_parts[1:]))

    normed, projected, y, squares, mixed, gains = mixer_inner(
        slots, source_all, w_in, taps_t, bias_t, steps_t, skip_t, turns, *sizes
    )
    w_mlp = gather(after(mlp_parts, squares))
    squares = everywhere(squares)
    upstream_all = spread(after(upstream, squares))
    branches, root, *halves = mixer_outer(projected, y, mixed, gain_t, squares, w_out)
    hidden, second = row_call(hidden_kernel, slots, reduce(*halves), source, gains)

    second_all, down_grad, product, gate_grad, up_grad, *halves = feed_forward(
        slots, spread(second), upstream_all, w_mlp, ff_t
    )
    mlp_sums = weight_grads(
        in_group,
        1,
        [
            ([second_all], [gate_grad], 0, ff_t),
            ([second_all], [up_grad], 0, ff_t),
            ([down_grad], [product], 0, ff_t),
        ],
    )
    sums = reduce_second(*reduce_add(halves, *after(reduce_send(halves), mlp_sums)))
    mlp_sums = scatter(mlp_sums[0])
    d_hidden, branch_grad = row_call(
        back_hidden_kernel, slots, sums, hidden, upstream, gains
    )
    branch_all = spread(branch_grad)
    last_halves = back_out(product, w_mlp, 2)
    branch_grad = after(branch_all, last_halves)
    branch_all, d_branches, dots = back_outer(
        branch_grad, w_out, projected, y, gain_t, slots.shape[0]
    )
    last_halves = after(last_halves, branch_grad)
    last_pair = reduce_add(last_halves, *reduce_send(last_halves))
    out_sums = weight_grads(in_group, 1, [([branch_all], [branches], 0, inner_t + q_t)])
    dots = after(everywhere(dots), (out_sums, last_pair))
    out_sums = scatter(out_sums[0])
    mlp_grads = pass_on(after(mlp_sums, dots))
    proj_grad, conv_rows, inner_rows, step_rows = mixer_backward(
        slots, projected, taps_t, bias_t, steps_t, skip_t, turns, gain_t, y, d_branches, root,
        dots, *sizes,
    )

    normed, last_pair = after((normed, last_pair), mlp_grads)
    in_sums = weight_grads(
        in_plane if cube else in_group, 2 if cube else 1, [([normed], [proj_grad], 0, in_cols)]
    )
    kernel = conv_taps.shape[0]
    small = jnp.concatenate(
        [
            conv_rows[: kernel + 1].reshape(-1),
            inner_rows[0],
            step_rows[0, :heads_t],
            step_rows[1, :heads_t],
            inner_rows[1].reshape(heads_t, -1).sum(1),
        ]
    )
    small, proj_grad = after((small, proj_grad), in_sums)
    norm_halves = back_out(proj_grad, w_in, 0)
    if cube:
        block, half = TP * shard, TP * shard // 2
        counts = (block, block, block, half, half)
        keep, send = in_sums
        mine, along_y, along_x, across_x, across_y = by_columns(
            chip_kernel, counts, keep, after(swap(send, 1, "core"), (norm_halves, out_sums))
        )
        in_parts = swap(across_x, 1, "x"), swap(across_y, 1, "y")
        norm_halves, last_pair, small = after((norm_halves, last_pair, small), across_x)
    norm_pair = reduce_send(norm_halves)
    small = everywhere(small)
    if cube:
        to_y, to_x = by_columns(
            along_kernel, (block, block), along_y, along_x, *after(in_parts, small)
        )
        in_parts = swap(to_x, 1, "x"), swap(to_y, 1, "y")
        norm_pair, last_pair, out_sums = after((norm_pair, last_pair, out_sums), to_x)
    norm_parts = reduce_second(*reduce_add(norm_halves, *norm_pair))
    last_parts = reduce_second(*last_pair)
    out_grads = pass_on(out_sums)
    if cube:
        in_parts = after(in_parts, (norm_parts, last_parts, out_grads))
        in_sums = by_columns(plane_kernel, (shard,) * TP, mine, *in_parts)
        in_grads = exchange(in_sums)
    else:
        in_sums = scatter(in_sums[0])
        in_grads = pass_on(in_sums)
    last_parts, norm_parts, small, mlp_grads, out_grads = after(
        (last_parts, norm_parts, small, mlp_grads, out_grads), in_sums
    )
    small = absolute(small)
    if cube:
        for axis in plane:
            small = small + swap(small, 1, axis)
    else:
        small = lax.psum(small, plane)

    inside_own = jnp.concatenate(
        [inside_rows(slots[m, 0], slots[m, 1], width) for m in range(batches)], axis=0
    )

    def summed(parts):
        keep, got, keep_right, got_right = parts
        return jnp.concatenate([keep + got.astype(f32), keep_right + got_right.astype(f32)], axis=1)

    output = hidden + inside_own * summed(last_parts)
    output = unorder(output.astype(bf16)).reshape(tokens.shape)
    d_normed = summed(norm_parts) * gains[0:1]
    wide = source.astype(f32)
    token_grads = d_hidden + norm_back(wide, inverse_root(wide), d_normed)
    token_grads = unorder(token_grads).reshape(tokens.shape)

    at_group = me[None].astype(jnp.int32)
    grad_gate, grad_up, grad_down, grad_second_gain = unpack(
        functools.partial(unpack_mlp_kernel, ff_t),
        at_group,
        mlp_grads,
        (gate_weight, up_weight, second_gain[:, None]),
        (hidden_units, hidden_units, hidden_units, 1),
    )
    grad_mamba_out, grad_output = unpack(
        functools.partial(unpack_out_kernel, inner_t, q_t), at_group, out_grads, (), (inner, q_cols)
    )
    grad_mamba_in, grad_query, grad_key, grad_value, grad_norm_gain = unpack(
        functools.partial(unpack_in_kernel, *sizes, pad),
        at_group,
        in_grads,
        (mamba_in, query_weight, key_weight, value_weight, norm_gain[:, None]),
        (mamba_in.shape[1], q_cols, kv_heads * HD, kv_heads * HD, 1),
    )
    grad_mamba_out, grad_output, grad_down = grad_mamba_out.T, grad_output.T, grad_down.T
    grad_norm_gain, grad_second_gain = grad_norm_gain[:, 0], grad_second_gain[:, 0]

    conv = small[:, : (kernel + 1) * conv_cols].reshape(TP, kernel + 1, conv_cols)
    conv = jnp.concatenate(
        [conv[:, :, :inner_t].transpose(1, 0, 2).reshape(kernel + 1, inner), conv[:, :, inner_t:].sum(0)],
        axis=1,
    )
    at = (kernel + 1) * conv_cols
    return (
        output,
        token_grads,
        grad_norm_gain,
        grad_mamba_in,
        conv[:kernel],
        conv[kernel],
        small[:, at + inner_t : at + inner_t + heads_t].reshape(-1),
        small[:, at + inner_t + heads_t : at + inner_t + 2 * heads_t].reshape(-1),
        small[:, at + inner_t + 2 * heads_t :].reshape(-1),
        small[:, at : at + inner_t].reshape(-1),
        grad_mamba_out,
        grad_query,
        grad_key,
        grad_value,
        grad_output,
        grad_second_gain,
        grad_gate,
        grad_up,
        grad_down,
    )


def solution(mesh):
    count = mesh.devices.size
    if tuple(mesh.devices.shape) == (8, 4):
        grid = Mesh(mesh.devices.reshape(TP, 2, 2, 2), ("tp", "x", "y", "core"))
        plane = ("core", "x", "y")
    else:
        grid = Mesh(mesh.devices.reshape(TP, count // TP), ("tp", "fs"))
        plane = ("fs",)
    every = grid.axis_names
    down, across, slots = P(every, None), P(None, every), P(None, every, None)
    line, copied = P(every), P()
    return jax.shard_map(
        functools.partial(local, plane),
        mesh=grid,
        in_specs=(
            slots, across, across, line, down, copied, copied, copied, copied, copied, copied,
            across, down, down, down, across, line, down, down, across, slots,
        ),
        out_specs=(
            slots, slots, line, down, copied, copied, copied, copied, copied, copied,
            across, down, down, down, across, line, down, down, across,
        ),
        check_vma=False,
    )
```

time: 980 us -> 640 us (0.65)
  blocking collectives: 247 us -> 0 us
  Pallas kernels: 0 us -> 157 us
  matrix products: 123 us -> 0 us
  waiting for transfers between devices: 380 us -> 283 us
  starting transfers between devices: 11.9 us -> 83 us
  other arithmetic: 99.5 us -> 30.1 us
  local copies, waits for them, and re-layouts: 90.9 us -> 62.5 us
    ppermute x0 -> x70, waiting for transfers between devices: none -> 282 us  [swap(): return lax.ppermute(values, axis, [(i, i ^ k) for i in range(size)])]
    all_gather x6 -> x3, waiting for transfers between devices: 229 us -> 0.02 us  [gather(): lax.all_gather(absolute(parts).reshape(TP * shard, -1), plane, axis=0, ti...]
    pallas_call x0 -> x18, Pallas kernels: none -> 157 us  [the longest x3 31 us: weight_grads(): pl.pallas_call(functools.partial(weight_grad_kernel, tuple(bounds), mine,...]
    all_to_all x2 -> x0, blocking collectives: 138 us -> none  [collect(): mine = lax.all_to_all(shards, 'tp', split_axis=0, concat_axis=0)]
    dot_general x27 -> x0, matrix products: 123 us -> none  [the longest x5 31.8 us: dot_nn(): return jnp.dot(left, right, preferred_element_type=f32)]
    reduce_scatter x6 -> x2, waiting for transfers between devices: 119 us -> 0.02 us  [scatter(): return lax.psum_scatter(grads, plane, scatter_dimension=0, tiled=True)]
    ppermute x0 -> x70, starting transfers between devices: none -> 71.3 us  [swap(): return lax.ppermute(values, axis, [(i, i ^ k) for i in range(size)])]
    all_gather x2 -> x0, blocking collectives: 66.8 us -> none  [the longest x1 59.8 us: local(): small = lax.all_gather(lax.psum(small, 'fs'), 'tp', axis=0)]
  transfers between devices with their start and end apart: 14 -> 75, of which waited for: 9 -> 41; matrix products, arithmetic and copies ran while one was open for 22% -> 10% of each run, Pallas kernels for 0% -> 18%
where the time goes in v2:
time: 640 us; the launch traced here: 634 us
  waiting for transfers between devices  283 us (44%)
  Pallas kernels  157 us (25%)
  starting transfers between devices  83 us (13%)
  local copies, waits for them, and re-layouts  62.5 us (10%)
  other arithmetic  30.1 us (5%)
  between operations  18.4 us (3%)
    ppermute x70, waiting for transfers between devices, swap(): return lax.ppermute(values, axis, [(i, i ^ k) for i in range(size)])  282 us
    ppermute x70, starting transfers between devices, swap(): return lax.ppermute(values, axis, [(i, i ^ k) for i in range(size)])  71.3 us
    pallas_call x3, Pallas kernels, weight_grads(): pl.pallas_call(functools.partial(weight_grad_kernel, tuple(bounds), mine,...  31 us
    pallas_call x1, Pallas kernels, mixer_inner(): pl.pallas_call(functools.partial(inner_kernel, inner, state, heads, tiles...  26.4 us
    pallas_call x1, Pallas kernels, mixer_backward(): pl.pallas_call(functools.partial(backward_kernel, inner, state, heads), g...  25.6 us
    pallas_call x1, Pallas kernels, feed_forward(): pl.pallas_call(feed_kernel, grid=(steps,), in_specs=[pl.BlockSpec(memory_...  19.9 us
    pallas_call x2, Pallas kernels, back_out(): pl.pallas_call(back_out_kernel, grid=(model // tile,), in_specs=specs(lef...  17.4 us
    unnamed x192, local copies, waits for them, and re-layouts  16.8 us
  transfers between devices with their start and end apart: 75, of which 41 were waited for; matrix products, arithmetic and copies ran while one was open for 10% of the time, Pallas kernels for 18%

profile of v2, /device:TPU:8, one launch (start us, length us, event | category | flops | bytes accessed | tf_op | source)
XLA Modules:
  0.0 633.5 jit_solution(13390706604469018450)
XLA Ops:
  17.3 10.2 %collective-permute-done.3 = bf16[64,2688]{1,0:T(8,128)(2,1)S(1)} collective-permute-done((bf16[64,2688]{1,0:T(8,128)(2,1)S(1)}, bf16[64,2688]{1,0:T(8,128)(2,1)S(1)}, u32[]{:S(2)}, u32[]{:S(2)}) %collective-permute-start.3) | collective-permute-done | bytes 344096 | tf_op jit(solution)/shard_map/ppermute | solution.py:907
  27.4 12.3 %collective-permute-done.4 = bf16[64,2688]{1,0:T(8,128)(2,1)S(1)} collective-permute-done((bf16[64,2688]{1,0:T(8,128)(2,1)S(1)}, bf16[64,2688]{1,0:T(8,128)(2,1)S(1)}, u32[]{:S(2)}, u32[]{:S(2)}) %collective-permute-start.4) | collective-permute-done | bytes 344096 | tf_op jit(solution)/shard_map/ppermute | solution.py:907
  39.8 6.9 %collective-permute-done.5 = bf16[64,2688]{1,0:T(8,128)(2,1)S(1)} collective-permute-done((bf16[64,2688]{1,0:T(8,128)(2,1)S(1)}, bf16[64,2688]{1,0:T(8,128)(2,1)S(1)}, u32[]{:S(2)}, u32[]{:S(2)}) %collective-permute-start.5) | collective-permute-done | bytes 344096 | tf_op jit(solution)/shard_map/ppermute | solution.py:907
  62.9 7.6 %collective-permute-done.8.p3 = bf16[128,1024]{1,0:T(8,128)(2,1)S(1)} collective-permute-done((bf16[128,1024]{1,0:T(8,128)(2,1)S(1)}, bf16[128,1024]{1,0:T(8,128)(2,1)S(1)}, u32[]{:S(2)}, u32[]{:S(2)}) %collective-permute-start.8) | collective-permute-done | bytes 262176 | tf_op jit(solution)/shard_map/ppermute | solution.py:907
  72.2 11.4 %collective-permute-done.6.p1 = bf16[128,1024]{1,0:T(8,128)(2,1)S(1)} collective-permute-done((bf16[128,1024]{1,0:T(8,128)(2,1)S(1)}, bf16[128,1024]{1,0:T(8,128)(2,1)S(1)}, u32[]{:S(2)}, u32[]{:S(2)}) %collective-permute-start.6) | collective-permute-done | bytes 262176 | tf_op jit(solution)/shard_map/ppermute | solution.py:907
  85.6 10.2 %collective-permute-done.9.p4 = bf16[256,1024]{1,0:T(8,128)(2,1)S(1)} collective-permute-done((bf16[256,1024]{1,0:T(8,128)(2,1)S(1)}, bf16[256,1024]{1,0:T(8,128)(2,1)S(1)}, u32[]{:S(2)}, u32[]{:S(2)}) %collective-permute-start.9) | collective-permute-done | bytes 524320 | tf_op jit(solution)/shard_map/ppermute | solution.py:907
  99.4 3.5 collective-permute-done.13
  102.9 3.7 collective-permute-done.14
  118.8 26.4 %shard_map.348 = (bf16[512,2048]{1,0:T(8,128)(2,1)}, f32[512,2688]{1,0:T(8,128)}, f32[512,768]{1,0:T(8,128)}, f32[8,1,64]{2,1,0:T(1,128)S(1)}, bf16[512,256]{1,0:T(8,128)(2,1)S(1)}, /*index=5*/f32[8,2048]{1,0:T(8,128)S(1)}) custom-call(s32[8,2]{1,0:T(8,128)S(1)} %copy.129.slots_ref, bf16[128,2048]{1,0:T(8,128)(2,1)S(1)} %copy.128.p0.source_ref, ...), custom_call_target="tpu_custom_call" | custom-call | flops 17999998976 | bytes 1800000 | tf_op jit(solution)/shard_map/pallas_call | solution.py:320
  145.3 7.0 %collective-permute-done.30 = bf16[64,3072]{1,0:T(8,128)(2,1)} collective-permute-done((bf16[64,3072]{1,0:T(8,128)(2,1)}, bf16[64,3072]{1,0:T(8,128)(2,1)}, u32[]{:S(2)}, u32[]{:S(2)}) %collective-permute-start.30) | collective-permute-done | bytes 393248 | tf_op jit(solution)/shard_map/ppermute | solution.py:907
  155.3 11.5 %reduce-scatter.3.cloned.1.call-start = ((), (), s32[]{:S(2)}) async-start(), calls=%async_computation.5 | async-start | bytes 14155776 | tf_op jit(solution)/shard_map/reduce_scatter | solution.py:1022
  172.7 7.3 %shard_map.349 = (bf16[512,1024]{1,0:T(8,128)(2,1)S(1)}, f32[8,1,64]{2,1,0:T(1,128)S(1)}, f32[256,1024]{1,0:T(8,128)S(1)}, bf16[256,1024]{1,0:T(8,128)(2,1)S(1)}...) custom-call(f32[512,2688]{1,0:T(8,128)} %get-tuple-element.172.gate_ref.proj_ref, ...), custom_call_target="tpu_custom_call" | custom-call | flops 4000000000 | bytes 400000 | tf_op jit(solution)/shard_map/pallas_call | solution.py:367
  184.0 17.6 %collective-permute-done.18 = bf16[256,1024]{1,0:T(8,128)(2,1)S(1)} collective-permute-done((bf16[256,1024]{1,0:T(8,128)(2,1)S(1)}, bf16[256,1024]{1,0:T(8,128)(2,1)S(1)}, u32[]{:S(2)}, u32[]{:S(2)}) %collective-permute-start.18) | collective-permute-done | bytes 524320 | tf_op jit(solution)/shard_map/ppermute | solution.py:907
  206.7 3.2 collective-permute-start.26
  210.6 9.3 %collective-permute-done.17.k1 = bf16[128,1024]{1,0:T(8,128)(2,1)S(1)} collective-permute-done((bf16[128,1024]{1,0:T(8,128)(2,1)}, bf16[128,1024]{1,0:T(8,128)(2,1)S(1)}, u32[]{:S(2)}, u32[]{:S(2)}) %collective-permute-start.17) | collective-permute-done | bytes 262176 | tf_op jit(solution)/shard_map/ppermute | solution.py:907
  223.3 7.8 %collective-permute-done.24.c1 = bf16[128,1024]{1,0:T(8,128)(2,1)S(1)} collective-permute-done((bf16[128,1024]{1,0:T(8,128)(2,1)S(1)}, bf16[128,1024]{1,0:T(8,128)(2,1)S(1)}, u32[]{:S(2)}, u32[]{:S(2)}) %collective-permute-start.24) | collective-permute-done | bytes 262176 | tf_op jit(solution)/shard_map/ppermute | solution.py:907
  233.9 19.7 %collective-permute-done.20.s1 = bf16[128,1024]{1,0:T(8,128)(2,1)S(1)} collective-permute-done((bf16[128,1024]{1,0:T(8,128)(2,1)S(1)}, bf16[128,1024]{1,0:T(8,128)(2,1)S(1)}, u32[]{:S(2)}, u32[]{:S(2)}) %collective-permute-start.20) | collective-permute-done | bytes 262176 | tf_op jit(solution)/shard_map/ppermute | solution.py:907
  253.7 22.4 %collective-permute-done.27.c4 = bf16[256,1024]{1,0:T(8,128)(2,1)S(1)} collective-permute-done((bf16[256,1024]{1,0:T(8,128)(2,1)S(1)}, bf16[256,1024]{1,0:T(8,128)(2,1)S(1)}, u32[]{:S(2)}, u32[]{:S(2)}) %collective-permute-start.27) | collective-permute-done | bytes 524320 | tf_op jit(solution)/shard_map/ppermute | solution.py:907
  276.1 9.4 %collective-permute-done.23.s4 = bf16[256,1024]{1,0:T(8,128)(2,1)S(1)} collective-permute-done((bf16[256,1024]{1,0:T(8,128)(2,1)S(1)}, bf16[256,1024]{1,0:T(8,128)(2,1)S(1)}, u32[]{:S(2)}, u32[]{:S(2)}) %collective-permute-start.23) | collective-permute-done | bytes 524320 | tf_op jit(solution)/shard_map/ppermute | solution.py:907
  285.5 19.9 %shard_map.351 = (bf16[512,2048]{1,0:T(8,128)(2,1)}, bf16[512,2048]{1,0:T(8,128)(2,1)}, bf16[512,1024]{1,0:T(8,128)(2,1)}, bf16[512,1024]{1,0:T(8,128)(2,1)}, bf...) custom-call(s32[8,2]{1,0:T(8,128)S(1)} %copy.129.slots_ref, ...), custom_call_target="tpu_custom_call" | custom-call | flops 8999999488 | bytes 900000 | tf_op jit(solution)/shard_map/pallas_call | solution.py:472
  310.7 14.8 %shard_map.352 = bf16[2048,3072]{1,0:T(8,128)(2,1)} custom-call(s32[32]{0:T(128)S(1)} %get-tuple-element.201.table_ref, bf16[512,2048]{1,0:T(8,128)(2,1)} %get-tuple-element.202.refs_0_.refs_2_, bf16[512,1024]{1,0:T(8,128)(2,1)S(1)} %copy-done.19, bf16[512,2048]{1,0:T(8,128)(2,1)} %get-tuple-element.202.refs_0_.refs_2_, bf16[512,1024]{1,0:T(8,128)(2,1)S(1)} %copy-done.20, ...), custom_call_target="tpu_custom_call" | custom-call | flops 12999999488 | bytes 1300000 | tf_op jit(solution)/shard_map/pallas_call | solution.py:855
  326.9 14.4 %collective-permute-done.31 = bf16[256,1024]{1,0:T(8,128)(2,1)S(1)} collective-permute-done((bf16[256,1024]{1,0:T(8,128)(2,1)S(1)}, bf16[256,1024]{1,0:T(8,128)(2,1)S(1)}, u32[]{:S(2)}, u32[]{:S(2)}) %collective-permute-start.31) | collective-permute-done | bytes 524320 | tf_op jit(solution)/shard_map/ppermute | solution.py:907
  341.3 8.6 %collective-permute-done.32 = bf16[256,1024]{1,0:T(8,128)(2,1)S(1)} collective-permute-done((bf16[256,1024]{1,0:T(8,128)(2,1)S(1)}, bf16[256,1024]{1,0:T(8,128)(2,1)S(1)}, u32[]{:S(2)}, u32[]{:S(2)}) %collective-permute-start.32) | collective-permute-done | bytes 524320 | tf_op jit(solution)/shard_map/ppermute | solution.py:907
  355.6 3.5 collective-permute-done.34.k3
  359.1 4.9 collective-permute-done.33.k1
  367.4 6.5 %collective-permute-done.37.b3 = bf16[128,1024]{1,0:T(8,128)(2,1)S(1)} collective-permute-done((bf16[128,1024]{1,0:T(8,128)(2,1)S(1)}, bf16[128,1024]{1,0:T(8,128)(2,1)S(1)}, u32[]{:S(2)}, u32[]{:S(2)}) %collective-permute-start.37) | collective-permute-done | bytes 262176 | tf_op jit(solution)/shard_map/ppermute | solution.py:907
  375.4 9.5 %collective-permute-done.35.b1 = bf16[128,1024]{1,0:T(8,128)(2,1)S(1)} collective-permute-done((bf16[128,1024]{1,0:T(8,128)(2,1)S(1)}, bf16[128,1024]{1,0:T(8,128)(2,1)S(1)}, u32[]{:S(2)}, u32[]{:S(2)}) %collective-permute-start.35) | collective-permute-done | bytes 262176 | tf_op jit(solution)/shard_map/ppermute | solution.py:907
  385.0 6.7 %shard_map.354 = (f32[256,1024]{1,0:T(8,128)S(1)}, bf16[256,1024]{1,0:T(8,128)(2,1)}, f32[256,1024]{1,0:T(8,128)S(1)}, bf16[256,1024]{1,0:T(8,128)(2,1)}) custom-call(bf16[512,1024]{1,0:T(8,128)(2,1)} %get-tuple-element.206.refs_5_.left_ref, bf16[2048,3072]{1,0:T(8,128)(2,1)} %all-gather.8.cloned.1.call-done.gate_ref.up_ref.down_ref.weight_ref), custom_call_target="tpu_custom_call" | custom-call | flops 4000000000 | bytes 400000 | tf_op jit(solution)/shard_map/pallas_call | solution.py:394
  392.7 18.7 %collective-permute-done.38.b4 = bf16[256,1024]{1,0:T(8,128)(2,1)S(1)} collective-permute-done((bf16[256,1024]{1,0:T(8,128)(2,1)S(1)}, bf16[256,1024]{1,0:T(8,128)(2,1)S(1)}, u32[]{:S(2)}, u32[]{:S(2)}) %collective-permute-start.38) | collective-permute-done | bytes 524320 | tf_op jit(solution)/shard_map/ppermute | solution.py:907
  413.0 7.4 %shard_map.355 = (bf16[512,2048]{1,0:T(8,128)(2,1)}, f32[512,1024]{1,0:T(8,128)}, f32[8,1,64]{2,1,0:T(1,128)S(1)}) custom-call(bf16[128,2048]{1,0:T(8,128)(2,1)S(1)} %get-tuple-element.215.b0, bf16[128,1024]{1,0:T(8,128)(2,1)S(1)} %collective-permute-done.35.b1, bf16[256,1024]{1,0:T(8,128)(2,1)S(1)} %collective-permute-done.36.b2, ...), custom_call_target="tpu_custom_call" | custom-call | flops 5000000000 | bytes 500000 | tf_op jit(solution)/shard_map/pallas_call | solution.py:534
  426.4 5.3 shard_map.356
  434.2 5.0 collective-permute-done.42
  447.3 25.6 %shard_map.357 = (bf16[512,2688]{1,0:T(8,128)(2,1)}, f32[8,1280]{1,0:T(8,128)S(1)}, f32[8,768]{1,0:T(8,128)S(1)}, f32[8,128]{1,0:T(8,128)S(1)}) custom-call(s32[8,2]{1,0:T(8,128)S(1)} %copy.129.slots_ref, f32[512,2688]{1,0:T(8,128)} %get-tuple-element.172.gate_ref.proj_ref, f32[4,1280]{1,0:T(4,128)S(1)} %pad_maximum_fusion.25.taps_ref, ...), custom_call_target="tpu_custom_call" | custom-call | flops 16999999488 | bytes 1700000 | tf_op jit(solution)/shard_map/pallas_call | solution.py:673
  473.8 10.9 %shard_map.358 = (bf16[1024,2688]{1,0:T(8,128)(2,1)}, bf16[1024,2688]{1,0:T(8,128)(2,1)}) custom-call(s32[32]{0:T(128)S(1)} %get-tuple-element.237.table_ref, bf16[512,2048]{1,0:T(8,128)(2,1)S(1)} %copy-done.49, bf16[512,2688]{1,0:T(8,128)(2,1)} %get-tuple-element.243.refs_1_.left_ref), custom_call_target="tpu_custom_call" | custom-call | flops 11000000512 | bytes 1100000 | tf_op jit(solution)/shard_map/pallas_call | solution.py:855
  485.1 10.7 %shard_map.359 = (f32[256,1024]{1,0:T(8,128)S(1)}, bf16[256,1024]{1,0:T(8,128)(2,1)}, f32[256,1024]{1,0:T(8,128)S(1)}, bf16[256,1024]{1,0:T(8,128)(2,1)}) custom-call(bf16[512,2688]{1,0:T(8,128)(2,1)} %get-tuple-element.243.refs_1_.left_ref, bf16[2048,2688]{1,0:T(8,128)(2,1)} %all-gather.4.cloned.1.call-done.weight_ref.gains_in_ref), custom_call_target="tpu_custom_call" | custom-call | flops 4000000000 | bytes 400000 | tf_op jit(solution)/shard_map/pallas_call | solution.py:394
  496.8 6.3 %shard_map.360 = (bf16[256,2688]{1,0:T(8,128)(2,1)S(1)}, bf16[256,2688]{1,0:T(8,128)(2,1)S(1)}, bf16[256,2688]{1,0:T(8,128)(2,1)}, bf16[128,2688]{1,0:T(8,128)(2,1)S(1)}, bf16[128,2688]{1,0:T(8,128)(2,1)S(1)}) custom-call(bf16[1024,2688]{1,0:T(8,128)(2,1)} %get-tuple-element.241.keep_ref, bf16[1024,2688]{1,0:T(8,128)(2,1)} %collective-permute-done.47.got_ref), custom_call_target="tpu_custom_call" | custom-call | flops 3000000000 | bytes 300000 | tf_op jit(solution)/shard_map/pallas_call | solution.py:727
  516.7 6.4 %collective-permute-done.50.by_x_ref = bf16[128,2688]{1,0:T(8,128)(2,1)S(1)} collective-permute-done((bf16[128,2688]{1,0:T(8,128)(2,1)S(1)}, bf16[128,2688]{1,0:T(8,128)(2,1)S(1)}, u32[]{:S(2)}, u32[]{:S(2)}) %collective-permute-start.50) | collective-permute-done | bytes 688160 | tf_op jit(solution)/shard_map/ppermute | solution.py:907
  524.3 4.4 shard_map.361
  532.4 7.7 %collective-permute-done.49 = bf16[256,1024]{1,0:T(8,128)(2,1)} collective-permute-done((bf16[256,1024]{1,0:T(8,128)(2,1)}, bf16[256,1024]{1,0:T(8,128)(2,1)}, u32[]{:S(2)}, u32[]{:S(2)}) %collective-permute-start.49) | collective-permute-done | bytes 524320 | tf_op jit(solution)/shard_map/ppermute | solution.py:907
  550.7 5.1 collective-permute-done.60.g2
  558.3 7.0 %collective-permute-done.61.g3 = bf16[64,1024]{1,0:T(8,128)(2,1)S(1)} collective-permute-done((bf16[64,1024]{1,0:T(8,128)(2,1)S(1)}, bf16[64,1024]{1,0:T(8,128)(2,1)S(1)}, u32[]{:S(2)}, u32[]{:S(2)}) %collective-permute-start.61) | collective-permute-done | bytes 131104 | tf_op jit(solution)/shard_map/ppermute | solution.py:907
  568.7 5.5 collective-permute-done.57
  574.2 5.5 collective-permute-done.55
  579.8 3.8 shard_map.362
  599.1 4.0 copy.142
  603.1 4.1 reshape_reshape.15
  608.3 3.7 copy.139
  612.0 3.9 reshape_reshape.14
  (477 shorter events, 167.9 us)
Async XLA Ops:
  7.2 111.6 %all-gather.4.cloned.1.call-start = ((), (), s32[]{:S(2)}) async-start(), calls=%async_computation.2 | async-start | bytes 12386304 | tf_op jit(solution)/shard_map/all_gather | solution.py:1019
  13.4 26.3 %collective-permute-start.4 = (bf16[64,2688]{1,0:T(8,128)(2,1)S(1)}, bf16[64,2688]{1,0:T(8,128)(2,1)S(1)}, u32[]{:S(2)}, u32[]{:S(2)}) collective-permute-start(bf16[64,2688]{1,0:T(8,128)(2,1)S(1)} %concatenate.105), channel_id=1, source_target_pairs={{0,16},{8,24},{16,0},{24,8},{1,17},{9,25},{17,1},{25,9},{2,18},{10... | collective-permute-start | bytes 1032200 | tf_op jit(solution)/shard_map/ppermute | solution.py:907
  16.6 30.0 %collective-permute-start.5 = (bf16[64,2688]{1,0:T(8,128)(2,1)S(1)}, bf16[64,2688]{1,0:T(8,128)(2,1)S(1)}, u32[]{:S(2)}, u32[]{:S(2)}) collective-permute-start(bf16[64,2688]{1,0:T(8,128)(2,1)S(1)} %concatenate.106), channel_id=1, source_target_pairs={{0,24},{8,16},{16,8},{24,0},{1,25},{9,17},{17,9},{25,1},{2,26},{10... | collective-permute-start | bytes 1032200 | tf_op jit(solution)/shard_map/ppermute | solution.py:907
  48.4 121.9 %all-gather.6.cloned.1.call-start = ((), (), s32[]{:S(2)}) async-start(), calls=%async_computation.3 | async-start | bytes 4718592 | tf_op jit(solution)/shard_map/all_gather | solution.py:1019
  61.4 22.2 %collective-permute-start.6 = (bf16[128,1024]{1,0:T(8,128)(2,1)S(1)}, bf16[128,1024]{1,0:T(8,128)(2,1)S(1)}, u32[]{:S(2)}, u32[]{:S(2)}) collective-permute-start(bf16[128,1024]{1,0:T(8,128)(2,1)S(1)} %get-tuple-element.366), channel_id=1, source_target_pairs={{0,24},{8,16},{16,8},{24,0},{1,25},{9,17},{17,9},{25,1},{2,26},{10... | collective-permute-start | bytes 786440 | tf_op jit(solution)/shard_map/ppermute | solution.py:907
  70.5 25.3 %collective-permute-start.9 = (bf16[256,1024]{1,0:T(8,128)(2,1)S(1)}, bf16[256,1024]{1,0:T(8,128)(2,1)S(1)}, u32[]{:S(2)}, u32[]{:S(2)}) collective-permute-start(bf16[256,1024]{1,0:T(8,128)(2,1)S(1)} %pad_maximum_fusion.6), channel_id=1, source_target_pairs={{0,24},{8,16},{16,8},{24,0},{1,25},{9,17},{17,9},{25,1},{2,26},{10... | collective-permute-start | bytes 1572872 | tf_op jit(solution)/shard_map/ppermute | solution.py:907
  110.8 174.7 %all-gather.8.cloned.1.call-start = ((), (), s32[]{:S(2)}) async-start(), calls=%async_computation.4 | async-start | bytes 14155776 | tf_op jit(solution)/shard_map/all_gather | solution.py:1019
  115.3 29.9 %collective-permute-start.28 = (bf16[64,3072]{1,0:T(8,128)(2,1)}, bf16[64,3072]{1,0:T(8,128)(2,1)}, u32[]{:S(2)}, u32[]{:S(2)}) collective-permute-start(bf16[64,3072]{1,0:T(8,128)(2,1)} %pad_maximum_fusion.16), channel_id=1, source_target_pairs={{0,8},{8,0},{16,24},{24,16},{1,9},{9,1},{17,25},{25,17},{2,10},{10... | collective-permute-start | bytes 1179656 | tf_op jit(solution)/shard_map/ppermute | solution.py:907
  115.3 29.9 %collective-permute-start.29 = (bf16[64,3072]{1,0:T(8,128)(2,1)}, bf16[64,3072]{1,0:T(8,128)(2,1)}, u32[]{:S(2)}, u32[]{:S(2)}) collective-permute-start(bf16[64,3072]{1,0:T(8,128)(2,1)} %pad_maximum_fusion.17), channel_id=1, source_target_pairs={{0,16},{8,24},{16,0},{24,8},{1,17},{9,25},{17,1},{25,9},{2,18},{10... | collective-permute-start | bytes 1179656 | tf_op jit(solution)/shard_map/ppermute | solution.py:907
  117.7 34.5 %collective-permute-start.30 = (bf16[64,3072]{1,0:T(8,128)(2,1)}, bf16[64,3072]{1,0:T(8,128)(2,1)}, u32[]{:S(2)}, u32[]{:S(2)}) collective-permute-start(bf16[64,3072]{1,0:T(8,128)(2,1)} %pad_maximum_fusion.18), channel_id=1, source_target_pairs={{0,24},{8,16},{16,8},{24,0},{1,25},{9,17},{17,9},{25,1},{2,26},{10... | collective-permute-start | bytes 1179656 | tf_op jit(solution)/shard_map/ppermute | solution.py:907
  155.3 286.2 %reduce-scatter.3.cloned.1.call-start = ((), (), s32[]{:S(2)}) async-start(), calls=%async_computation.5 | async-start | bytes 14155776 | tf_op jit(solution)/shard_map/reduce_scatter | solution.py:1022
  180.0 21.5 %collective-permute-start.18 = (bf16[256,1024]{1,0:T(8,128)(2,1)S(1)}, bf16[256,1024]{1,0:T(8,128)(2,1)S(1)}, u32[]{:S(2)}, u32[]{:S(2)}) collective-permute-start(bf16[256,1024]{1,0:T(8,128)(2,1)S(1)} %get-tuple-element.184), channel_id=1, source_target_pairs={{0,24},{8,16},{16,8},{24,0},{1,25},{9,17},{17,9},{25,1},{2,26},{10... | collective-permute-start | bytes 1572872 | tf_op jit(solution)/shard_map/ppermute | solution.py:907
  181.2 22.3 %collective-permute-start.16 = (bf16[256,1024]{1,0:T(8,128)(2,1)S(1)}, bf16[256,1024]{1,0:T(8,128)(2,1)S(1)}, u32[]{:S(2)}, u32[]{:S(2)}) collective-permute-start(bf16[256,1024]{1,0:T(8,128)(2,1)S(1)} %get-tuple-element.182), channel_id=1, source_target_pairs={{0,8},{8,0},{16,24},{24,16},{1,9},{9,1},{17,25},{25,17},{2,10},{10... | collective-permute-start | bytes 1572872 | tf_op jit(solution)/shard_map/ppermute | solution.py:907
  204.8 15.1 %collective-permute-start.17 = (bf16[128,1024]{1,0:T(8,128)(2,1)}, bf16[128,1024]{1,0:T(8,128)(2,1)S(1)}, u32[]{:S(2)}, u32[]{:S(2)}) collective-permute-start(bf16[128,1024]{1,0:T(8,128)(2,1)} %slice.309), channel_id=1, source_target_pairs={{0,24},{8,16},{16,8},{24,0},{1,25},{9,17},{17,9},{25,1},{2,26},{10... | collective-permute-start | bytes 786440 | tf_op jit(solution)/shard_map/ppermute | solution.py:907
  206.7 15.2 %collective-permute-start.26 = (bf16[128,1024]{1,0:T(8,128)(2,1)S(1)}, bf16[128,1024]{1,0:T(8,128)(2,1)S(1)}, u32[]{:S(2)}, u32[]{:S(2)}) collective-permute-start(bf16[128,1024]{1,0:T(8,128)(2,1)S(1)} %get-tuple-element.357), channel_id=1, source_target_pairs={{0,8},{8,0},{16,24},{24,16},{1,9},{9,1},{17,25},{25,17},{2,10},{10... | collective-permute-start | bytes 786440 | tf_op jit(solution)/shard_map/ppermute | solution.py:907
  209.8 21.3 %collective-permute-start.24 = (bf16[128,1024]{1,0:T(8,128)(2,1)S(1)}, bf16[128,1024]{1,0:T(8,128)(2,1)S(1)}, u32[]{:S(2)}, u32[]{:S(2)}) collective-permute-start(bf16[128,1024]{1,0:T(8,128)(2,1)S(1)} %get-tuple-element.358), channel_id=1, source_target_pairs={{0,24},{8,16},{16,8},{24,0},{1,25},{9,17},{17,9},{25,1},{2,26},{10... | collective-permute-start | bytes 786440 | tf_op jit(solution)/shard_map/ppermute | solution.py:907
  221.1 32.5 %collective-permute-start.20 = (bf16[128,1024]{1,0:T(8,128)(2,1)S(1)}, bf16[128,1024]{1,0:T(8,128)(2,1)S(1)}, u32[]{:S(2)}, u32[]{:S(2)}) collective-permute-start(bf16[128,1024]{1,0:T(8,128)(2,1)S(1)} %get-tuple-element.360), channel_id=1, source_target_pairs={{0,24},{8,16},{16,8},{24,0},{1,25},{9,17},{17,9},{25,1},{2,26},{10... | collective-permute-start | bytes 786440 | tf_op jit(solution)/shard_map/ppermute | solution.py:907
  221.9 54.1 %collective-permute-start.27 = (bf16[256,1024]{1,0:T(8,128)(2,1)S(1)}, bf16[256,1024]{1,0:T(8,128)(2,1)S(1)}, u32[]{:S(2)}, u32[]{:S(2)}) collective-permute-start(bf16[256,1024]{1,0:T(8,128)(2,1)S(1)} %pad_maximum_fusion.12), channel_id=1, source_target_pairs={{0,24},{8,16},{16,8},{24,0},{1,25},{9,17},{17,9},{25,1},{2,26},{10... | collective-permute-start | bytes 1572872 | tf_op jit(solution)/shard_map/ppermute | solution.py:907
  231.2 44.9 %collective-permute-start.25 = (bf16[256,1024]{1,0:T(8,128)(2,1)S(1)}, bf16[256,1024]{1,0:T(8,128)(2,1)S(1)}, u32[]{:S(2)}, u32[]{:S(2)}) collective-permute-start(bf16[256,1024]{1,0:T(8,128)(2,1)S(1)} %pad_maximum_fusion.11), channel_id=1, source_target_pairs={{0,8},{8,0},{16,24},{24,16},{1,9},{9,1},{17,25},{25,17},{2,10},{10... | collective-permute-start | bytes 1572872 | tf_op jit(solution)/shard_map/ppermute | solution.py:907
  233.2 52.2 %collective-permute-start.23 = (bf16[256,1024]{1,0:T(8,128)(2,1)S(1)}, bf16[256,1024]{1,0:T(8,128)(2,1)S(1)}, u32[]{:S(2)}, u32[]{:S(2)}) collective-permute-start(bf16[256,1024]{1,0:T(8,128)(2,1)S(1)} %pad_maximum_fusion.10), channel_id=1, source_target_pairs={{0,24},{8,16},{16,8},{24,0},{1,25},{9,17},{17,9},{25,1},{2,26},{10... | collective-permute-start | bytes 1572872 | tf_op jit(solution)/shard_map/ppermute | solution.py:907
  253.6 31.8 %collective-permute-start.21 = (bf16[256,1024]{1,0:T(8,128)(2,1)S(1)}, bf16[256,1024]{1,0:T(8,128)(2,1)S(1)}, u32[]{:S(2)}, u32[]{:S(2)}) collective-permute-start(bf16[256,1024]{1,0:T(8,128)(2,1)S(1)} %pad_maximum_fusion.9), channel_id=1, source_target_pairs={{0,8},{8,0},{16,24},{24,16},{1,9},{9,1},{17,25},{25,17},{2,10},{10... | collective-permute-start | bytes 1572872 | tf_op jit(solution)/shard_map/ppermute | solution.py:907
  325.5 171.3 %reduce-scatter.5.cloned.1.call-start = ((), (), s32[]{:S(2)}) async-start(), calls=%async_computation.6 | async-start | bytes 4718592 | tf_op jit(solution)/shard_map/reduce_scatter | solution.py:1022
  326.5 14.9 %collective-permute-start.31 = (bf16[256,1024]{1,0:T(8,128)(2,1)S(1)}, bf16[256,1024]{1,0:T(8,128)(2,1)S(1)}, u32[]{:S(2)}, u32[]{:S(2)}) collective-permute-start(bf16[256,1024]{1,0:T(8,128)(2,1)S(1)} %copy-done.26), channel_id=1, source_target_pairs={{0,8},{8,0},{16,24},{24,16},{1,9},{9,1},{17,25},{25,17},{2,10},{10... | collective-permute-start | bytes 1572872 | tf_op jit(solution)/shard_map/ppermute | solution.py:907
  326.6 23.3 %collective-permute-start.32 = (bf16[256,1024]{1,0:T(8,128)(2,1)S(1)}, bf16[256,1024]{1,0:T(8,128)(2,1)S(1)}, u32[]{:S(2)}, u32[]{:S(2)}) collective-permute-start(bf16[256,1024]{1,0:T(8,128)(2,1)S(1)} %copy-done.24), channel_id=1, source_target_pairs={{0,24},{8,16},{16,8},{24,0},{1,25},{9,17},{17,9},{25,1},{2,26},{10... | collective-permute-start | bytes 1572872 | tf_op jit(solution)/shard_map/ppermute | solution.py:907
  366.0 18.9 %collective-permute-start.35 = (bf16[128,1024]{1,0:T(8,128)(2,1)S(1)}, bf16[128,1024]{1,0:T(8,128)(2,1)S(1)}, u32[]{:S(2)}, u32[]{:S(2)}) collective-permute-start(bf16[128,1024]{1,0:T(8,128)(2,1)S(1)} %get-tuple-element.344), channel_id=1, source_target_pairs={{0,24},{8,16},{16,8},{24,0},{1,25},{9,17},{17,9},{25,1},{2,26},{10... | collective-permute-start | bytes 786440 | tf_op jit(solution)/shard_map/ppermute | solution.py:907
  374.0 37.4 %collective-permute-start.38 = (bf16[256,1024]{1,0:T(8,128)(2,1)S(1)}, bf16[256,1024]{1,0:T(8,128)(2,1)S(1)}, u32[]{:S(2)}, u32[]{:S(2)}) collective-permute-start(bf16[256,1024]{1,0:T(8,128)(2,1)S(1)} %pad_maximum_fusion.14), channel_id=1, source_target_pairs={{0,24},{8,16},{16,8},{24,0},{1,25},{9,17},{17,9},{25,1},{2,26},{10... | collective-permute-start | bytes 1572872 | tf_op jit(solution)/shard_map/ppermute | solution.py:907
  384.9 26.4 %collective-permute-start.36 = (bf16[256,1024]{1,0:T(8,128)(2,1)S(1)}, bf16[256,1024]{1,0:T(8,128)(2,1)S(1)}, u32[]{:S(2)}, u32[]{:S(2)}) collective-permute-start(bf16[256,1024]{1,0:T(8,128)(2,1)S(1)} %pad_maximum_fusion.13), channel_id=1, source_target_pairs={{0,8},{8,0},{16,24},{24,16},{1,9},{9,1},{17,25},{25,17},{2,10},{10... | collective-permute-start | bytes 1572872 | tf_op jit(solution)/shard_map/ppermute | solution.py:907
  411.4 20.3 %collective-permute-start.43 = (bf16[256,1024]{1,0:T(8,128)(2,1)}, bf16[256,1024]{1,0:T(8,128)(2,1)}, u32[]{:S(2)}, u32[]{:S(2)}) collective-permute-start(bf16[256,1024]{1,0:T(8,128)(2,1)} %get-tuple-element.228), channel_id=1, source_target_pairs={{0,24},{8,16},{16,8},{24,0},{1,25},{9,17},{17,9},{25,1},{2,26},{10... | collective-permute-start | bytes 1572872 | tf_op jit(solution)/shard_map/ppermute | solution.py:907
  420.4 21.0 %collective-permute-start.39 = (f32[8,1,64]{2,1,0:T(1,128)S(1)}, f32[8,1,64]{2,1,0:T(1,128)S(1)}, u32[]{:S(2)}, u32[]{:S(2)}) collective-permute-start(f32[8,1,64]{2,1,0:T(1,128)S(1)} %get-tuple-element.229.d0), channel_id=1, source_target_pairs={{0,8},{8,0},{16,24},{24,16},{1,9},{9,1},{17,25},{25,17},{2,10},{10... | collective-permute-start | bytes 6152 | tf_op jit(solution)/shard_map/ppermute | solution.py:907
  420.4 21.0 %collective-permute-start.40 = (f32[8,1,64]{2,1,0:T(1,128)S(1)}, f32[8,1,64]{2,1,0:T(1,128)S(1)}, u32[]{:S(2)}, u32[]{:S(2)}) collective-permute-start(f32[8,1,64]{2,1,0:T(1,128)S(1)} %get-tuple-element.229.d0), channel_id=1, source_target_pairs={{0,16},{8,24},{16,0},{24,8},{1,17},{9,25},{17,1},{25,9},{2,18},{10... | collective-permute-start | bytes 6152 | tf_op jit(solution)/shard_map/ppermute | solution.py:907
  422.3 19.1 %collective-permute-start.41 = (f32[8,1,64]{2,1,0:T(1,128)S(1)}, f32[8,1,64]{2,1,0:T(1,128)S(1)}, u32[]{:S(2)}, u32[]{:S(2)}) collective-permute-start(f32[8,1,64]{2,1,0:T(1,128)S(1)} %get-tuple-element.229.d0), channel_id=1, source_target_pairs={{0,24},{8,16},{16,8},{24,0},{1,25},{9,17},{17,9},{25,1},{2,26},{10... | collective-permute-start | bytes 6152 | tf_op jit(solution)/shard_map/ppermute | solution.py:907
  423.9 15.3 %collective-permute-start.42 = (bf16[256,1024]{1,0:T(8,128)(2,1)}, bf16[256,1024]{1,0:T(8,128)(2,1)}, u32[]{:S(2)}, u32[]{:S(2)}) collective-permute-start(bf16[256,1024]{1,0:T(8,128)(2,1)} %get-tuple-element.226), channel_id=1, source_target_pairs={{0,8},{8,0},{16,24},{24,16},{1,9},{9,1},{17,25},{25,17},{2,10},{10... | collective-permute-start | bytes 1572872 | tf_op jit(solution)/shard_map/ppermute | solution.py:907
  443.2 29.7 %collective-permute-start.44 = (bf16[64,3072]{1,0:T(8,128)(2,1)S(1)}, bf16[64,3072]{1,0:T(8,128)(2,1)S(1)}, u32[]{:S(2)}, u32[]{:S(2)}) collective-permute-start(bf16[64,3072]{1,0:T(8,128)(2,1)S(1)} %get-tuple-element.317), channel_id=1, source_target_pairs={{0,8},{8,0},{16,24},{24,16},{1,9},{9,1},{17,25},{25,17},{2,10},{10... | collective-permute-start | bytes 1179656 | tf_op jit(solution)/shard_map/ppermute | solution.py:907
  445.7 27.2 %collective-permute-start.45 = (bf16[64,3072]{1,0:T(8,128)(2,1)S(1)}, bf16[64,3072]{1,0:T(8,128)(2,1)S(1)}, u32[]{:S(2)}, u32[]{:S(2)}) collective-permute-start(bf16[64,3072]{1,0:T(8,128)(2,1)S(1)} %get-tuple-element.316), channel_id=1, source_target_pairs={{0,16},{8,24},{16,0},{24,8},{1,17},{9,25},{17,1},{25,9},{2,18},{10... | collective-permute-start | bytes 1179656 | tf_op jit(solution)/shard_map/ppermute | solution.py:907
  445.9 27.8 %collective-permute-start.46 = (bf16[64,3072]{1,0:T(8,128)(2,1)S(1)}, bf16[64,3072]{1,0:T(8,128)(2,1)S(1)}, u32[]{:S(2)}, u32[]{:S(2)}) collective-permute-start(bf16[64,3072]{1,0:T(8,128)(2,1)S(1)} %get-tuple-element.315), channel_id=1, source_target_pairs={{0,24},{8,16},{16,8},{24,0},{1,25},{9,17},{17,9},{25,1},{2,26},{10... | collective-permute-start | bytes 1179656 | tf_op jit(solution)/shard_map/ppermute | solution.py:907
  505.3 17.8 %collective-permute-start.50 = (bf16[128,2688]{1,0:T(8,128)(2,1)S(1)}, bf16[128,2688]{1,0:T(8,128)(2,1)S(1)}, u32[]{:S(2)}, u32[]{:S(2)}) collective-permute-start(bf16[128,2688]{1,0:T(8,128)(2,1)S(1)} %get-tuple-element.252), channel_id=1, source_target_pairs={{0,4},{4,0},{1,5},{5,1},{2,6},{6,2},{3,7},{7,3},{8,12},{12,8},{9,1... | collective-permute-start | bytes 2064392 | tf_op jit(solution)/shard_map/ppermute | solution.py:907
  506.8 17.5 %collective-permute-start.51 = (bf16[128,2688]{1,0:T(8,128)(2,1)S(1)}, bf16[128,2688]{1,0:T(8,128)(2,1)S(1)}, u32[]{:S(2)}, u32[]{:S(2)}) collective-permute-start(bf16[128,2688]{1,0:T(8,128)(2,1)S(1)} %get-tuple-element.259), channel_id=1, source_target_pairs={{0,2},{2,0},{1,3},{3,1},{4,6},{6,4},{5,7},{7,5},{8,10},{10,8},{9,1... | collective-permute-start | bytes 2064392 | tf_op jit(solution)/shard_map/ppermute | solution.py:907
  512.9 19.6 %collective-permute-start.48 = (bf16[256,1024]{1,0:T(8,128)(2,1)}, bf16[256,1024]{1,0:T(8,128)(2,1)}, u32[]{:S(2)}, u32[]{:S(2)}) collective-permute-start(bf16[256,1024]{1,0:T(8,128)(2,1)} %get-tuple-element.253), channel_id=1, source_target_pairs={{0,8},{8,0},{16,24},{24,16},{1,9},{9,1},{17,25},{25,17},{2,10},{10... | collective-permute-start | bytes 1572872 | tf_op jit(solution)/shard_map/ppermute | solution.py:907
  516.0 24.1 %collective-permute-start.49 = (bf16[256,1024]{1,0:T(8,128)(2,1)}, bf16[256,1024]{1,0:T(8,128)(2,1)}, u32[]{:S(2)}, u32[]{:S(2)}) collective-permute-start(bf16[256,1024]{1,0:T(8,128)(2,1)} %get-tuple-element.254), channel_id=1, source_target_pairs={{0,24},{8,16},{16,8},{24,0},{1,25},{9,17},{17,9},{25,1},{2,26},{10... | collective-permute-start | bytes 1572872 | tf_op jit(solution)/shard_map/ppermute | solution.py:907
  528.7 51.0 %collective-permute-start.62 = (bf16[256,2688]{1,0:T(8,128)(2,1)}, bf16[256,2688]{1,0:T(8,128)(2,1)}, u32[]{:S(2)}, u32[]{:S(2)}) collective-permute-start(bf16[256,2688]{1,0:T(8,128)(2,1)} %get-tuple-element.263), channel_id=1, source_target_pairs={{0,4},{4,0},{1,5},{5,1},{2,6},{6,2},{3,7},{7,3},{8,12},{12,8},{9,1... | collective-permute-start | bytes 4128776 | tf_op jit(solution)/shard_map/ppermute | solution.py:907
  529.4 50.3 %collective-permute-start.63 = (bf16[256,2688]{1,0:T(8,128)(2,1)}, bf16[256,2688]{1,0:T(8,128)(2,1)}, u32[]{:S(2)}, u32[]{:S(2)}) collective-permute-start(bf16[256,2688]{1,0:T(8,128)(2,1)} %get-tuple-element.272), channel_id=1, source_target_pairs={{0,2},{2,0},{1,3},{3,1},{4,6},{6,4},{5,7},{7,5},{8,10},{10,8},{9,1... | collective-permute-start | bytes 4128776 | tf_op jit(solution)/shard_map/ppermute | solution.py:907
  543.1 22.9 %collective-permute-start.58 = (bf16[128,1024]{1,0:T(8,128)(2,1)S(1)}, bf16[128,1024]{1,0:T(8,128)(2,1)}, u32[]{:S(2)}, u32[]{:S(2)}) collective-permute-start(bf16[128,1024]{1,0:T(8,128)(2,1)S(1)} %slice.302), channel_id=1, source_target_pairs={{0,8},{8,0},{16,24},{24,16},{1,9},{9,1},{17,25},{25,17},{2,10},{10... | collective-permute-start | bytes 786440 | tf_op jit(solution)/shard_map/ppermute | solution.py:907
  547.7 17.7 %collective-permute-start.61 = (bf16[64,1024]{1,0:T(8,128)(2,1)S(1)}, bf16[64,1024]{1,0:T(8,128)(2,1)S(1)}, u32[]{:S(2)}, u32[]{:S(2)}) collective-permute-start(bf16[64,1024]{1,0:T(8,128)(2,1)S(1)} %get-tuple-element.339), channel_id=1, source_target_pairs={{0,24},{8,16},{16,8},{24,0},{1,25},{9,17},{17,9},{25,1},{2,26},{10... | collective-permute-start | bytes 393224 | tf_op jit(solution)/shard_map/ppermute | solution.py:907
  556.5 17.7 %collective-permute-start.57 = (bf16[128,1024]{1,0:T(8,128)(2,1)}, bf16[128,1024]{1,0:T(8,128)(2,1)S(1)}, u32[]{:S(2)}, u32[]{:S(2)}) collective-permute-start(bf16[128,1024]{1,0:T(8,128)(2,1)} %slice.303), channel_id=1, source_target_pairs={{0,24},{8,16},{16,8},{24,0},{1,25},{9,17},{17,9},{25,1},{2,26},{10... | collective-permute-start | bytes 786440 | tf_op jit(solution)/shard_map/ppermute | solution.py:907
  583.6 34.7 %collective-permute-start.64 = (bf16[64,2688]{1,0:T(8,128)(2,1)}, bf16[64,2688]{1,0:T(8,128)(2,1)S(1)}, u32[]{:S(2)}, u32[]{:S(2)}) collective-permute-start(bf16[64,2688]{1,0:T(8,128)(2,1)} %get-tuple-element.276), channel_id=1, source_target_pairs={{0,8},{8,0},{16,24},{24,16},{1,9},{9,1},{17,25},{25,17},{2,10},{10... | collective-permute-start | bytes 1032200 | tf_op jit(solution)/shard_map/ppermute | solution.py:907
  583.7 34.7 %collective-permute-start.65 = (bf16[64,2688]{1,0:T(8,128)(2,1)}, bf16[64,2688]{1,0:T(8,128)(2,1)S(1)}, u32[]{:S(2)}, u32[]{:S(2)}) collective-permute-start(bf16[64,2688]{1,0:T(8,128)(2,1)} %get-tuple-element.277), channel_id=1, source_target_pairs={{0,16},{8,24},{16,0},{24,8},{1,17},{9,25},{17,1},{25,9},{2,18},{10... | collective-permute-start | bytes 1032200 | tf_op jit(solution)/shard_map/ppermute | solution.py:907
  586.3 32.1 %collective-permute-start.66 = (bf16[64,2688]{1,0:T(8,128)(2,1)S(1)}, bf16[64,2688]{1,0:T(8,128)(2,1)S(1)}, u32[]{:S(2)}, u32[]{:S(2)}) collective-permute-start(bf16[64,2688]{1,0:T(8,128)(2,1)S(1)} %get-tuple-element.278), channel_id=1, source_target_pairs={{0,24},{8,16},{16,8},{24,0},{1,25},{9,17},{17,9},{25,1},{2,26},{10... | collective-permute-start | bytes 1032200 | tf_op jit(solution)/shard_map/ppermute | solution.py:907
  596.2 20.3 %collective-permute-start.68 = (f32[4,7204]{1,0:T(4,128)}, f32[4,7204]{1,0:T(4,128)}, u32[]{:S(2)}, u32[]{:S(2)}) collective-permute-start(f32[4,7204]{1,0:T(4,128)} %fusion.11), channel_id=1, source_target_pairs={{0,4},{4,0},{1,5},{5,1},{2,6},{6,2},{3,7},{7,3},{8,12},{12,8},{9,1... | collective-permute-start | bytes 345800 | tf_op jit(solution)/shard_map/ppermute | solution.py:907
  (131 other events, 939.4 us)
Sparse Core Ops, SparseCore 0:
  48.5 65.6 all-gather.3
  116.6 36.7 all-gather.5
  155.4 72.0 all-gather.7
  325.6 91.5 reduce-scatter.2
  431.8 50.9 reduce-scatter.4

commit v3 on v2

--- a/solution.py
+++ b/solution.py
@@ -429,10 +429,12 @@
 
 
 def feed_kernel(
-    slots_ref, s0, s1, s2, s3, s4, c0, c1, c2, c3, c4, gate_ref, up_ref, down_ref,
-    second_ref, down_grad_ref, product_ref, gate_grad_ref, up_grad_ref, h0, h1, h2, h3, total,
+    steps, blocks, slots_ref, table_ref, s0, s1, s2, s3, s4, c0, c1, c2, c3, c4, gate_ref, up_ref, down_ref,
+    product_ref, h0, h1, h2, h3, grads_ref,
+    second_ref, down_grad_ref, gate_grad_ref, up_grad_ref, total, second_turned, down_turned,
 ):
     step = pl.program_id(0)
+    tile = gate_ref.shape[1]
 
     @pl.when(step == 0)
     def _():
@@ -442,52 +444,107 @@
         down_grad_ref[...] = (inside * joined_rows((c0, c1, c2, c3, c4)).astype(f32)).astype(bf16)
         total[...] = jnp.zeros_like(total)
 
-    second = second_ref[...]
-    gate = jnp.dot(second, gate_ref[...], preferred_element_type=f32)
-    up = jnp.dot(second, up_ref[...], preferred_element_type=f32)
-    d_product = jnp.dot(down_grad_ref[...], down_ref[...], preferred_element_type=f32)
-    sig = jax.nn.sigmoid(gate)
-    swish = gate * sig
-    product_ref[...] = (swish * up).astype(bf16)
-    gate_grad = (d_product * up * sig * (1.0 + gate * (1.0 - sig))).astype(bf16)
-    up_grad = (d_product * swish).astype(bf16)
-    gate_grad_ref[...] = gate_grad
-    up_grad_ref[...] = up_grad
-    total[...] += dot_nt(gate_grad, gate_ref[...]) + dot_nt(up_grad, up_ref[...])
-
-    @pl.when(step == pl.num_programs(0) - 1)
+    @pl.when(step < steps)
+    def _():
+        second = second_ref[...]
+        gate = jnp.dot(second, gate_ref[...], preferred_element_type=f32)
+        up = jnp.dot(second, up_ref[...], preferred_element_type=f32)
+        d_product = jnp.dot(down_grad_ref[...], down_ref[...], preferred_element_type=f32)
+        sig = jax.nn.sigmoid(gate)
+        swish = gate * sig
+        gate_grad = (d_product * up * sig * (1.0 + gate * (1.0 - sig))).astype(bf16)
+        up_grad = (d_product * swish).astype(bf16)
+        at = pl.ds(pl.multiple_of(step * tile, tile), tile)
+        product_ref[:, at] = (swish * up).astype(bf16)
+        gate_grad_ref[:, at] = gate_grad
+        up_grad_ref[:, at] = up_grad
+        total[...] += dot_nt(gate_grad, gate_ref[...]) + dot_nt(up_grad, up_ref[...])
+
+    @pl.when(step == steps - 1)
     def _():
         middle = total.shape[1] // 2
         put_left(total[:, :middle], (h0, h1))
         put_right(total[:, middle:], (h0, h1, h2, h3))
-
-
-def feed_forward(slots, second, cotangent, weight, units, tile=512):
+        size = second_ref.shape[1] // blocks
+        for source, turned in ((second_ref, second_turned), (down_grad_ref, down_turned)):
+            plain = jnp.transpose(source[...])
+            total_rows = plain.shape[0]
+            grads_ref[:total_rows, : plain.shape[1]] = plain
+            for block in range(blocks):
+                start = pl.multiple_of(table_ref[block] * size, size)
+                turned[block * size : (block + 1) * size, :] = grads_ref[pl.ds(start, size), : plain.shape[1]]
+
+    for part, (turned, right) in enumerate(
+        ((second_turned, gate_grad_ref), (second_turned, up_grad_ref), (down_turned, product_ref))
+    ):
+
+        @pl.when((step >= (part + 1) * steps) & (step < (part + 2) * steps))
+        def _(part=part, turned=turned, right=right):
+            at = pl.multiple_of((step - (part + 1) * steps) * tile, tile)
+            grads_ref[...] = jnp.dot(
+                turned[...], right[:, pl.ds(at, tile)], preferred_element_type=f32
+            ).astype(bf16)
+
+
+def feed_forward(slots, table, second, cotangent, weight, units, tile=512):
     count, model = second[0].shape
     rows = TP * count
     steps = units // tile
     half_shapes = halves_out(rows, model, tile)[1]
     shapes = [p.shape for p in second]
-    unit = pl.BlockSpec((rows, tile), lambda j: (0, j))
     return pl.pallas_call(
-        feed_kernel,
-        grid=(steps,),
-        in_specs=[pl.BlockSpec(memory_space=pltpu.SMEM)]
+        functools.partial(feed_kernel, steps, table.shape[0]),
+        grid=(4 * steps,),
+        in_specs=[pl.BlockSpec(memory_space=pltpu.SMEM)] * 2
         + specs(*shapes, *shapes)
         + [
-            pl.BlockSpec((model, tile), lambda j, at=at: (0, at * steps + j))
+            pl.BlockSpec((model, tile), lambda j, at=at: (0, at * steps + jnp.minimum(j, steps - 1)))
             for at in range(3)
         ],
-        out_specs=specs((rows, model), (rows, model))
-        + [unit] * 3
-        + specs(*[h.shape for h in half_shapes]),
-        out_shape=[jax.ShapeDtypeStruct((rows, model), bf16)] * 2
-        + [jax.ShapeDtypeStruct((rows, units), bf16)] * 3
-        + half_shapes,
-        scratch_shapes=[pltpu.VMEM((rows, model), f32)],
+        out_specs=specs((rows, units), *[h.shape for h in half_shapes])
+        + [pl.BlockSpec((model, tile), lambda j: (0, jnp.maximum(j - steps, 0)))],
+        out_shape=[jax.ShapeDtypeStruct((rows, units), bf16)]
+        + half_shapes
+        + [jax.ShapeDtypeStruct((model, 3 * units), bf16)],
+        scratch_shapes=[pltpu.VMEM((rows, model), bf16)] * 2
+        + [pltpu.VMEM((rows, units), bf16)] * 2
+        + [pltpu.VMEM((rows, model), f32)]
+        + [pltpu.VMEM((model, rows), bf16)] * 2,
         compiler_params=big,
-        cost_estimate=costs(9),
-    )(slots, *second, *cotangent, weight, weight, weight)
+        cost_estimate=costs(30),
+    )(slots, table, *second, *cotangent, weight, weight, weight)
+
+
+def in_places(values, places):
+    size = values.shape[1] // len(places)
+    return jnp.concatenate([values[:, p * size : (p + 1) * size] for p in places], axis=1)
+
+
+def output_kernel(places, slots_ref, k0, k1, k2, k3, hidden_ref, output_ref):
+    seqs = slots_ref.shape[0]
+    inside = inside_all(slots_ref, seqs // TP, hidden_ref.shape[0] * TP // seqs)
+    output = (hidden_ref[...] + inside * both_halves((k0, k1, k2, k3))).astype(bf16)
+    output_ref[...] = in_places(output, places)
+
+
+def token_grad_kernel(places, k0, k1, k2, k3, hidden_ref, source_ref, gains_ref, grad_ref):
+    grad = both_halves((k0, k1, k2, k3)) * gains_ref[0:1, :]
+    source = source_ref[...].astype(f32)
+    total = hidden_ref[...] + norm_back(source, inverse_root(source), grad)
+    grad_ref[...] = in_places(total, places)
+
+
+def whole_call(kernel, dtype, scalars, *arrays):
+    shape = arrays[4].shape
+    return pl.pallas_call(
+        kernel,
+        grid=(1,),
+        in_specs=[pl.BlockSpec(memory_space=pltpu.SMEM)] * len(scalars) + specs(*[a.shape for a in arrays]),
+        out_specs=pl.BlockSpec(shape, lambda i: (0, 0)),
+        out_shape=jax.ShapeDtypeStruct(shape, dtype),
+        compiler_params=big,
+        cost_estimate=costs(3),
+    )(*scalars, *arrays)
 
 
 def back_hidden_kernel(slots_ref, k0, k1, k2, k3, hidden_ref, cotangent_ref, gains_ref, d_hidden_ref, branch_ref):
@@ -559,7 +616,7 @@
 
 def backward_kernel(
     inner, state, heads, slots_ref, proj_ref, taps_ref, bias_ref, steps_ref, skip_ref, turn_ref,
-    gain_ref, y_ref, grad_ref, root_ref, d0, d1, d2, d3, proj_grad_ref, conv_grad_ref, inner_grad_ref, step_grad_ref,
+    gain_ref, y_ref, grad_ref, root_ref, d0, d1, d2, d3, proj_grad_ref, small_ref,
 ):
     step_id = pl.program_id(0)
     start = slots_ref[step_id, 1]
@@ -635,15 +692,13 @@
         axis=0,
     )
 
+    rows = jnp.concatenate([conv_rows, inner_rows, step_rows], axis=1)
+
     @pl.when(step_id == 0)
     def _():
-        conv_grad_ref[...] = jnp.zeros_like(conv_grad_ref)
-        inner_grad_ref[...] = jnp.zeros_like(inner_grad_ref)
-        step_grad_ref[...] = jnp.zeros_like(step_grad_ref)
-
-    conv_grad_ref[...] += conv_rows
-    inner_grad_ref[...] += inner_rows
-    step_grad_ref[...] += step_rows
+        small_ref[...] = jnp.zeros_like(small_ref)
+
+    small_ref[...] += rows
 
     at = inner + conv_cols + pad
     cosine, sine = turn_ref[:, :HD], turn_ref[:, HD:]
@@ -680,12 +735,10 @@
         + [rows_spec(length, inner), rows_spec(length, grads.shape[1])]
         + [pl.BlockSpec((1, 1, length), lambda i: (i, 0, 0))]
         + [their_spec(length, seqs // TP, k) for k in range(TP)],
-        out_specs=[rows_spec(length, cols)] + specs((8, conv_cols), (8, inner), (8, pad)),
+        out_specs=[rows_spec(length, cols)] + specs((8, conv_cols + inner + pad)),
         out_shape=[
             jax.ShapeDtypeStruct((rows, cols), bf16),
-            jax.ShapeDtypeStruct((8, conv_cols), f32),
-            jax.ShapeDtypeStruct((8, inner), f32),
-            jax.ShapeDtypeStruct((8, pad), f32),
+            jax.ShapeDtypeStruct((8, conv_cols + inner + pad), f32),
         ],
         compiler_params=big,
         cost_estimate=costs(17),
@@ -934,6 +987,25 @@
         got_right = swap(last[half:].astype(bf16), 1)
         return pair[:half], got, last[:half], got_right
 
+    def pair_send(one, two):
+        return [swap(jnp.concatenate([one[i], two[i]], axis=0), k) for i, k in ((1, 1), (3, 3))]
+
+    def pair_finish(one, two, got, got_right):
+        rows = one[1].shape[0]
+        half = rows // 2
+        pairs = [
+            reduce_add(h, got[i * rows : (i + 1) * rows], got_right[i * rows : (i + 1) * rows])
+            for i, h in enumerate((one, two))
+        ]
+        sends = [
+            swap(jnp.concatenate([p[i][half:].astype(bf16) for p in pairs], axis=0), k)
+            for i, k in ((0, 3), (1, 1))
+        ]
+        return [
+            (p[0][:half], sends[0][i * half : (i + 1) * half], p[1][:half], sends[1][i * half : (i + 1) * half])
+            for i, p in enumerate(pairs)
+        ]
+
     def reduce(*halves):
         return reduce_second(*reduce_first(*halves))
 
@@ -957,14 +1029,14 @@
             split = jnp.swapaxes(values.reshape(lead + (TP, peers, shard)), -3, -2)
         return split.reshape(values.shape)
 
-    def unorder(values):
-        lead = values.shape[:-1]
+    def place(n):
+        group, at = divmod(n, peers)
         if cube:
-            split = values.reshape(lead + (2, 2, 2, TP, shard))
-            split = jnp.moveaxis(split, (-5, -4, -3, -2), (-2, -4, -3, -5))
-        else:
-            split = jnp.swapaxes(values.reshape(lead + (peers, TP, shard)), -3, -2)
-        return split.reshape(values.shape)
+            x, y, core = at // 4, at // 2 % 2, at % 2
+            at = core * 4 + x * 2 + y
+        return at * TP + group
+
+    places = [place(n) for n in range(peers * TP)]
 
     blocks = jnp.arange(peers * TP, dtype=jnp.int32)
     in_group = blocks ^ me
@@ -975,6 +1047,8 @@
 
     def kv(weight, t):
         return cut(weight, 0, HD, t * kv_heads // TP)
+
+    slot_column = jnp.concatenate([lengths[:, 0], offsets[:, 0]]).astype(bf16)[:, None]
 
     def in_slice(t):
         return jnp.concatenate(
@@ -985,7 +1059,7 @@
                 cut(mamba_in, 2 * inner + 2 * state, heads_t, t),
                 norm_gain[:, None],
                 second_gain[:, None],
-                jnp.zeros((shard, pad - heads_t - 2), bf16),
+                jnp.pad(slot_column, ((0, shard - 2 * batches), (0, pad - heads_t - 3))),
                 cut(query_weight, 0, q_t, t),
                 kv(key_weight, t),
                 kv(value_weight, t),
@@ -1041,131 +1115,109 @@
     gain_t = own(mamba_gain, inner_t)[None]
     sizes = (inner_t, state, heads_t)
 
-    in_parts = exchange(slices(in_slice))
-    w_in = gather(in_parts)
-    slots = jnp.stack([lengths[:, 0], offsets[:, 0]], axis=1)
-    slots = jnp.concatenate([slots] + [swap(slots, k) for k in (3, 1, 2)], axis=0)
-    turns = turn_table(slots[:, 1], width)
+    in_slices = slices(in_slice)
+    in_parts = exchange(in_slices)
+    tokens, cotangent = after((tokens, cotangent), in_slices)
     source = order(tokens.reshape(rows, model))
     upstream = order(cotangent.reshape(rows, model))
-    prepared = (slots, turns, taps_t, bias_t, steps_t, skip_t, gain_t, in_plane, in_group, upstream)
-    source, prepared = lax.optimization_barrier((source, (prepared, in_parts[1:])))
-    slots, turns, taps_t, bias_t, steps_t, skip_t, gain_t, in_plane, in_group, upstream = prepared[0]
-    source_all = spread(source)
-    out_parts = exchange(after(slices(out_slice), source_all))
+    prepared = (
+        source, upstream, slices(out_slice), slices(mlp_slice),
+        taps_t, bias_t, steps_t, skip_t, gain_t, in_plane, in_group,
+    )
+    in_parts, prepared = lax.optimization_barrier((in_parts, prepared))
+    source, upstream, out_slices, mlp_slices = prepared[:4]
+    taps_t, bias_t, steps_t, skip_t, gain_t, in_plane, in_group = prepared[4:]
+    w_in = gather(in_parts)
+    source_some, upstream_some = spread_first(source), spread_first(upstream)
+    column = inner_t + 2 * state + inner_t + heads_t + 2
+    slots = jnp.stack([in_parts[k][: 2 * batches, column] for k in (0, 3, 1, 2)])
+    slots = after(slots, source_some).astype(jnp.int32).reshape(TP, 2, batches)
+    slots = jnp.swapaxes(slots, 1, 2).reshape(TP * batches, 2)
+    turns = turn_table(slots[:, 1], width)
+    source_all = spread_second(source, *source_some)
+    out_parts = exchange(after(out_slices, (source_all, upstream_some)))
     w_out = gather(out_parts)
-    mlp_parts = exchange(after(slices(mlp_slice), out_parts[1:]))
+    mlp_slices, upstream_some = after((mlp_slices, upstream_some), out_parts[1:])
+    mlp_parts = exchange(mlp_slices)
+    upstream_all = spread_second(upstream, *upstream_some)
 
     normed, projected, y, squares, mixed, gains = mixer_inner(
-        slots, source_all, w_in, taps_t, bias_t, steps_t, skip_t, turns, *sizes
-    )
-    w_mlp = gather(after(mlp_parts, squares))
-    squares = everywhere(squares)
-    upstream_all = spread(after(upstream, squares))
+        slots, after(source_all, out_parts[1:]), w_in, taps_t, bias_t, steps_t, skip_t, turns, *sizes
+    )
+    squares = everywhere(after(squares, upstream_all))
+    w_mlp = gather(after(mlp_parts, squares[1:]))
     branches, root, *halves = mixer_outer(projected, y, mixed, gain_t, squares, w_out)
     hidden, second = row_call(hidden_kernel, slots, reduce(*halves), source, gains)
 
-    second_all, down_grad, product, gate_grad, up_grad, *halves = feed_forward(
-        slots, spread(second), upstream_all, w_mlp, ff_t
-    )
-    mlp_sums = weight_grads(
-        in_group,
-        1,
-        [
-            ([second_all], [gate_grad], 0, ff_t),
-            ([second_all], [up_grad], 0, ff_t),
-            ([down_grad], [product], 0, ff_t),
-        ],
-    )
-    sums = reduce_second(*reduce_add(halves, *after(reduce_send(halves), mlp_sums)))
-    mlp_sums = scatter(mlp_sums[0])
+    product, *halves, mlp_sums = feed_forward(
+        slots, in_group, spread(second), upstream_all, w_mlp, ff_t
+    )
+    mlp_sums = scatter(mlp_sums)
     d_hidden, branch_grad = row_call(
-        back_hidden_kernel, slots, sums, hidden, upstream, gains
-    )
+        back_hidden_kernel, slots, reduce(*halves), hidden, upstream, gains
+    )
+
     branch_all = spread(branch_grad)
     last_halves = back_out(product, w_mlp, 2)
     branch_grad = after(branch_all, last_halves)
     branch_all, d_branches, dots = back_outer(
         branch_grad, w_out, projected, y, gain_t, slots.shape[0]
     )
-    last_halves = after(last_halves, branch_grad)
-    last_pair = reduce_add(last_halves, *reduce_send(last_halves))
     out_sums = weight_grads(in_group, 1, [([branch_all], [branches], 0, inner_t + q_t)])
-    dots = after(everywhere(dots), (out_sums, last_pair))
+    dots = after(everywhere(dots), out_sums)
     out_sums = scatter(out_sums[0])
     mlp_grads = pass_on(after(mlp_sums, dots))
-    proj_grad, conv_rows, inner_rows, step_rows = mixer_backward(
+    proj_grad, small = mixer_backward(
         slots, projected, taps_t, bias_t, steps_t, skip_t, turns, gain_t, y, d_branches, root,
         dots, *sizes,
     )
-
-    normed, last_pair = after((normed, last_pair), mlp_grads)
+    small = everywhere(small)
     in_sums = weight_grads(
-        in_plane if cube else in_group, 2 if cube else 1, [([normed], [proj_grad], 0, in_cols)]
-    )
-    kernel = conv_taps.shape[0]
-    small = jnp.concatenate(
-        [
-            conv_rows[: kernel + 1].reshape(-1),
-            inner_rows[0],
-            step_rows[0, :heads_t],
-            step_rows[1, :heads_t],
-            inner_rows[1].reshape(heads_t, -1).sum(1),
-        ]
-    )
-    small, proj_grad = after((small, proj_grad), in_sums)
-    norm_halves = back_out(proj_grad, w_in, 0)
+        in_plane if cube else in_group,
+        2 if cube else 1,
+        [([after(normed, mlp_grads)], [proj_grad], 0, in_cols)],
+    )
+    norm_halves = back_out(after(proj_grad, in_sums), w_in, 0)
+    pairs = pair_send(norm_halves, last_halves)
     if cube:
         block, half = TP * shard, TP * shard // 2
         counts = (block, block, block, half, half)
         keep, send = in_sums
         mine, along_y, along_x, across_x, across_y = by_columns(
-            chip_kernel, counts, keep, after(swap(send, 1, "core"), (norm_halves, out_sums))
+            chip_kernel, counts, keep, after(swap(send, 1, "core"), (out_sums, norm_halves, small))
         )
-        in_parts = swap(across_x, 1, "x"), swap(across_y, 1, "y")
-        norm_halves, last_pair, small = after((norm_halves, last_pair, small), across_x)
-    norm_pair = reduce_send(norm_halves)
-    small = everywhere(small)
-    if cube:
         to_y, to_x = by_columns(
-            along_kernel, (block, block), along_y, along_x, *after(in_parts, small)
+            along_kernel, (block, block), along_y, along_x, swap(across_x, 1, "x"), swap(across_y, 1, "y")
         )
         in_parts = swap(to_x, 1, "x"), swap(to_y, 1, "y")
-        norm_pair, last_pair, out_sums = after((norm_pair, last_pair, out_sums), to_x)
-    norm_parts = reduce_second(*reduce_add(norm_halves, *norm_pair))
-    last_parts = reduce_second(*last_pair)
+        pairs, out_sums = after((pairs, out_sums), to_x)
+    norm_parts, last_parts = pair_finish(norm_halves, last_halves, *pairs)
     out_grads = pass_on(out_sums)
+    small = absolute(small)
     if cube:
-        in_parts = after(in_parts, (norm_parts, last_parts, out_grads))
+        small = small + swap(small, 1, "core")
+        in_parts = after(in_parts, (norm_parts, last_parts, out_grads, small))
         in_sums = by_columns(plane_kernel, (shard,) * TP, mine, *in_parts)
         in_grads = exchange(in_sums)
     else:
         in_sums = scatter(in_sums[0])
         in_grads = pass_on(in_sums)
-    last_parts, norm_parts, small, mlp_grads, out_grads = after(
-        (last_parts, norm_parts, small, mlp_grads, out_grads), in_sums
-    )
-    small = absolute(small)
+    small, mlp_grads, out_grads, norm_parts, last_parts = after(
+        (small, mlp_grads, out_grads, norm_parts, last_parts), in_sums
+    )
     if cube:
-        for axis in plane:
-            small = small + swap(small, 1, axis)
+        small = small + swap(small, 1, "x")
+        mlp_grads = after(mlp_grads, small)
+        small = small + swap(small, 1, "y")
+        out_grads = after(out_grads, small)
     else:
         small = lax.psum(small, plane)
-
-    inside_own = jnp.concatenate(
-        [inside_rows(slots[m, 0], slots[m, 1], width) for m in range(batches)], axis=0
-    )
-
-    def summed(parts):
-        keep, got, keep_right, got_right = parts
-        return jnp.concatenate([keep + got.astype(f32), keep_right + got_right.astype(f32)], axis=1)
-
-    output = hidden + inside_own * summed(last_parts)
-    output = unorder(output.astype(bf16)).reshape(tokens.shape)
-    d_normed = summed(norm_parts) * gains[0:1]
-    wide = source.astype(f32)
-    token_grads = d_hidden + norm_back(wide, inverse_root(wide), d_normed)
-    token_grads = unorder(token_grads).reshape(tokens.shape)
+    token_grads = whole_call(
+        functools.partial(token_grad_kernel, places), f32, (), *norm_parts, d_hidden, source, gains
+    )
+    output = whole_call(
+        functools.partial(output_kernel, places), bf16, (slots,), *last_parts, hidden
+    )
 
     at_group = me[None].astype(jnp.int32)
     grad_gate, grad_up, grad_down, grad_second_gain = unpack(
@@ -1188,23 +1240,25 @@
     grad_mamba_out, grad_output, grad_down = grad_mamba_out.T, grad_output.T, grad_down.T
     grad_norm_gain, grad_second_gain = grad_norm_gain[:, 0], grad_second_gain[:, 0]
 
-    conv = small[:, : (kernel + 1) * conv_cols].reshape(TP, kernel + 1, conv_cols)
+    kernel = conv_taps.shape[0]
+    conv = small[:, : kernel + 1, :conv_cols]
     conv = jnp.concatenate(
         [conv[:, :, :inner_t].transpose(1, 0, 2).reshape(kernel + 1, inner), conv[:, :, inner_t:].sum(0)],
         axis=1,
     )
-    at = (kernel + 1) * conv_cols
+    by_inner = small[:, :2, conv_cols : conv_cols + inner_t]
+    by_step = small[:, :2, conv_cols + inner_t : conv_cols + inner_t + heads_t]
     return (
-        output,
-        token_grads,
+        output.reshape(tokens.shape),
+        token_grads.reshape(tokens.shape),
         grad_norm_gain,
         grad_mamba_in,
         conv[:kernel],
         conv[kernel],
-        small[:, at + inner_t : at + inner_t + heads_t].reshape(-1),
-        small[:, at + inner_t + heads_t : at + inner_t + 2 * heads_t].reshape(-1),
-        small[:, at + inner_t + 2 * heads_t :].reshape(-1),
-        small[:, at : at + inner_t].reshape(-1),
+        by_step[:, 0].reshape(-1),
+        by_step[:, 1].reshape(-1),
+        by_inner[:, 1].reshape(heads, -1).sum(1),
+        by_inner[:, 0].reshape(-1),
         grad_mamba_out,
         grad_query,
         grad_key,

time: 640 us -> 609 us (0.952)
  waiting for transfers between devices: 283 us -> 266 us
  local copies, waits for them, and re-layouts: 62.5 us -> 49.6 us
    ppermute x70 -> x63, waiting for transfers between devices: 282 us -> 265 us  [swap(): return lax.ppermute(values, axis, [(i, i ^ k) for i in range(size)])]
    ppermute x70 -> x63, starting transfers between devices: 71.3 us -> 86.8 us  [swap(): return lax.ppermute(values, axis, [(i, i ^ k) for i in range(size)])]
    pallas_call x3 -> x2, Pallas kernels: 31 us -> 16.3 us  [weight_grads(): pl.pallas_call(functools.partial(weight_grad_kernel, tuple(bounds), mine,...]
    pallas_call x1 -> x3, Pallas kernels: 19.9 us -> 32.8 us  [the longest x1 29.4 us: feed_forward(): pl.pallas_call(functools.partial(feed_kernel, steps, table.shape[0]), gri...]
    reduce_scatter x2, starting transfers between devices: 11.5 us -> 0.08 us  [scatter(): return lax.psum_scatter(grads, plane, scatter_dimension=0, tiled=True)]
    transpose x2 -> x0, local copies, waits for them, and re-layouts: 7.71 us -> none  [unorder(): split = jnp.moveaxis(split, (-5, -4, -3, -2), (-2, -4, -3, -5))]
    another operation x8 -> x5, local copies, waits for them, and re-layouts: 8.17 us -> 1.48 us  [the longest x1 0.59 us: local(): by_step[:, 1].reshape(-1)]
  transfers between devices with their start and end apart: 75 -> 68, of which waited for: 41 -> 42; matrix products, arithmetic and copies ran while one was open for 10% -> 7% of each run, Pallas kernels for 18% -> 20%
where the time goes in v3:
time: 609 us; the launch traced here: 601 us
  waiting for transfers between devices  266 us (44%)
  Pallas kernels  152 us (25%)
  starting transfers between devices  87.3 us (14%)
  local copies, waits for them, and re-layouts  49.6 us (8%)
  other arithmetic  30.8 us (5%)
  between operations  15.5 us (3%)
    ppermute x63, waiting for transfers between devices, swap(): return lax.ppermute(values, axis, [(i, i ^ k) for i in range(size)])  265 us
    ppermute x63, starting transfers between devices, swap(): return lax.ppermute(values, axis, [(i, i ^ k) for i in range(size)])  86.8 us
    pallas_call x1, Pallas kernels, feed_forward(): pl.pallas_call(functools.partial(feed_kernel, steps, table.shape[0]), gri...  29.4 us
    pallas_call x1, Pallas kernels, mixer_inner(): pl.pallas_call(functools.partial(inner_kernel, inner, state, heads, tiles...  26.5 us
    pallas_call x1, Pallas kernels, mixer_backward(): pl.pallas_call(functools.partial(backward_kernel, inner, state, heads), g...  25.8 us
    unnamed x192, local copies, waits for them, and re-layouts  20 us
    pallas_call x2, Pallas kernels, weight_grads(): pl.pallas_call(functools.partial(weight_grad_kernel, tuple(bounds), mine,...  16.3 us
    pallas_call x2, Pallas kernels, back_out(): pl.pallas_call(back_out_kernel, grid=(model // tile,), in_specs=specs(lef...  15.8 us
  transfers between devices with their start and end apart: 68, of which 42 were waited for; matrix products, arithmetic and copies ran while one was open for 7% of the time, Pallas kernels for 20%

profile of v3, /device:TPU:8, one launch (start us, length us, event | category | flops | bytes accessed | tf_op | source)
XLA Modules:
  0.0 601.2 jit_solution(11853543967647248269)
XLA Ops:
  16.4 3.0 collective-permute-start.1
  25.8 2.9 reshape_reshape.7
  37.2 5.8 collective-permute-done.1
  43.0 9.7 %collective-permute-done.2 = bf16[64,2688]{1,0:T(8,128)(2,1)} collective-permute-done((bf16[64,2688]{1,0:T(8,128)(2,1)}, bf16[64,2688]{1,0:T(8,128)(2,1)}, u32[]{:S(2)}, u32[]{:S(2)}) %collective-permute-start.2) | collective-permute-done | bytes 344096 | tf_op jit(solution)/shard_map/ppermute | solution.py:960
  57.5 5.3 collective-permute-done.3.p1
  69.8 25.4 %collective-permute-done.8.c3 = bf16[128,1024]{1,0:T(8,128)(2,1)S(1)} collective-permute-done((bf16[128,1024]{1,0:T(8,128)(2,1)S(1)}, bf16[128,1024]{1,0:T(8,128)(2,1)S(1)}, u32[]{:S(2)}, u32[]{:S(2)}) %collective-permute-start.8) | collective-permute-done | bytes 262176 | tf_op jit(solution)/shard_map/ppermute | solution.py:960
  95.1 4.0 collective-permute-done.7.c1
  104.4 3.6 collective-permute-done.10
  128.7 26.5 %shard_map.348 = (bf16[512,2048]{1,0:T(8,128)(2,1)}, f32[512,2688]{1,0:T(8,128)}, f32[512,768]{1,0:T(8,128)}, f32[8,1,64]{2,1,0:T(1,128)S(1)}, bf16[512,256]{1,0:T(8,128)(2,1)S(1)}, /*index=5*/f32[8,2048]{1,0:T(8,128)S(1)}) custom-call(s32[8,2]{1,0:T(8,128)S(1)} %copy.121.slots_ref, bf16[128,2048]{1,0:T(8,128)(2,1)S(1)} %copy.113.p0, ...), custom_call_target="tpu_custom_call" | custom-call | flops 17999998976 | bytes 1800000 | tf_op jit(solution)/shard_map/pallas_call | solution.py:320
  155.2 17.8 %collective-permute-done.13.c4 = bf16[256,1024]{1,0:T(8,128)(2,1)} collective-permute-done((bf16[256,1024]{1,0:T(8,128)(2,1)}, bf16[256,1024]{1,0:T(8,128)(2,1)}, u32[]{:S(2)}, u32[]{:S(2)}) %collective-permute-start.13) | collective-permute-done | bytes 524320 | tf_op jit(solution)/shard_map/ppermute | solution.py:960
  176.6 2.9 collective-permute-done.15.s2
  182.5 7.4 %shard_map.349 = (bf16[512,1024]{1,0:T(8,128)(2,1)S(1)}, f32[8,1,64]{2,1,0:T(1,128)S(1)}, f32[256,1024]{1,0:T(8,128)S(1)}, bf16[256,1024]{1,0:T(8,128)(2,1)S(1)}...) custom-call(f32[512,2688]{1,0:T(8,128)} %get-tuple-element.190.gate_ref.proj_ref, ...), custom_call_target="tpu_custom_call" | custom-call | flops 4000000000 | bytes 400000 | tf_op jit(solution)/shard_map/pallas_call | solution.py:367
  192.5 12.3 %collective-permute-done.17 = bf16[256,1024]{1,0:T(8,128)(2,1)S(1)} collective-permute-done((bf16[256,1024]{1,0:T(8,128)(2,1)S(1)}, bf16[256,1024]{1,0:T(8,128)(2,1)S(1)}, u32[]{:S(2)}, u32[]{:S(2)}) %collective-permute-start.17) | collective-permute-done | bytes 524320 | tf_op jit(solution)/shard_map/ppermute | solution.py:960
  205.6 13.2 %collective-permute-done.19 = bf16[256,1024]{1,0:T(8,128)(2,1)S(1)} collective-permute-done((bf16[256,1024]{1,0:T(8,128)(2,1)S(1)}, bf16[256,1024]{1,0:T(8,128)(2,1)S(1)}, u32[]{:S(2)}, u32[]{:S(2)}) %collective-permute-start.19) | collective-permute-done | bytes 524320 | tf_op jit(solution)/shard_map/ppermute | solution.py:960
  219.3 5.4 collective-permute-done.18.k1
  224.7 3.7 collective-permute-done.20.k3
  232.2 3.2 collective-permute-start.23
  235.4 11.8 %collective-permute-done.21.s1 = bf16[128,1024]{1,0:T(8,128)(2,1)S(1)} collective-permute-done((bf16[128,1024]{1,0:T(8,128)(2,1)S(1)}, bf16[128,1024]{1,0:T(8,128)(2,1)S(1)}, u32[]{:S(2)}, u32[]{:S(2)}) %collective-permute-start.21) | collective-permute-done | bytes 262176 | tf_op jit(solution)/shard_map/ppermute | solution.py:960
  250.0 6.4 %collective-permute-done.22.s2 = bf16[256,1024]{1,0:T(8,128)(2,1)S(1)} collective-permute-done((bf16[256,1024]{1,0:T(8,128)(2,1)S(1)}, bf16[256,1024]{1,0:T(8,128)(2,1)S(1)}, u32[]{:S(2)}, u32[]{:S(2)}) %collective-permute-start.22) | collective-permute-done | bytes 524320 | tf_op jit(solution)/shard_map/ppermute | solution.py:960
  257.3 5.1 collective-permute-done.24.s4
  265.2 29.4 %shard_map.351 = (bf16[512,1024]{1,0:T(8,128)(2,1)}, f32[256,1024]{1,0:T(8,128)}, bf16[256,1024]{1,0:T(8,128)(2,1)S(1)}, f32[256,1024]{1,0:T(8,128)}, bf16[256,1...) custom-call(s32[8,2]{1,0:T(8,128)S(1)} %copy.121.slots_ref, s32[32]{0:T(128)S(1)} %get-tuple-element.193.table_ref, ...), custom_call_target="tpu_custom_call" | custom-call | flops 30000001024 | bytes 3000000 | tf_op jit(solution)/shard_map/pallas_call | solution.py:495
  296.4 3.2 collective-permute-start.28
  299.7 15.2 %collective-permute-done.28 = bf16[256,1024]{1,0:T(8,128)(2,1)S(1)} collective-permute-done((bf16[256,1024]{1,0:T(8,128)(2,1)S(1)}, bf16[256,1024]{1,0:T(8,128)(2,1)S(1)}, u32[]{:S(2)}, u32[]{:S(2)}) %collective-permute-start.28) | collective-permute-done | bytes 524320 | tf_op jit(solution)/shard_map/ppermute | solution.py:960
  316.8 3.3 collective-permute-done.30
  322.3 9.3 %collective-permute-done.29.k1 = bf16[128,1024]{1,0:T(8,128)(2,1)S(1)} collective-permute-done((bf16[128,1024]{1,0:T(8,128)(2,1)S(1)}, bf16[128,1024]{1,0:T(8,128)(2,1)S(1)}, u32[]{:S(2)}, u32[]{:S(2)}) %collective-permute-start.29) | collective-permute-done | bytes 262176 | tf_op jit(solution)/shard_map/ppermute | solution.py:960
  339.2 13.7 %collective-permute-done.32.b1 = bf16[128,1024]{1,0:T(8,128)(2,1)S(1)} collective-permute-done((bf16[128,1024]{1,0:T(8,128)(2,1)S(1)}, bf16[128,1024]{1,0:T(8,128)(2,1)S(1)}, u32[]{:S(2)}, u32[]{:S(2)}) %collective-permute-start.32) | collective-permute-done | bytes 262176 | tf_op jit(solution)/shard_map/ppermute | solution.py:960
  354.5 5.8 shard_map.353
  362.3 7.5 %shard_map.354 = (bf16[512,2048]{1,0:T(8,128)(2,1)}, f32[512,1024]{1,0:T(8,128)}, f32[8,1,64]{2,1,0:T(1,128)S(1)}) custom-call(bf16[128,2048]{1,0:T(8,128)(2,1)S(1)} %get-tuple-element.229.b0, bf16[128,1024]{1,0:T(8,128)(2,1)S(1)} %collective-permute-done.32.b1, bf16[256,1024]{1,0:T(8,128)(2,1)S(1)} %collective-permute-done.33.b2, ...), custom_call_target="tpu_custom_call" | custom-call | flops 5000000000 | bytes 500000 | tf_op jit(solution)/shard_map/pallas_call | solution.py:591
  371.2 8.9 %collective-permute-start.37 = (f32[8,1,64]{2,1,0:T(1,128)S(1)}, f32[8,1,64]{2,1,0:T(1,128)S(1)}, u32[]{:S(2)}, u32[]{:S(2)}) collective-permute-start(f32[8,1,64]{2,1,0:T(1,128)S(1)} %get-tuple-element.239.d0), channel_id=1, source_target_pairs={{0,16},{8,24},{16,0},{24,8},{1,17},{9,25},{17,1},{25,9},{2,18},{10... | collective-permute-start | bytes 6152 | tf_op jit(solution)/shard_map/ppermute | solution.py:960
  381.7 5.3 shard_map.355
  392.0 2.8 collective-permute-start.44
  398.4 25.8 %shard_map.356 = (bf16[512,2688]{1,0:T(8,128)(2,1)}, f32[8,2176]{1,0:T(8,128)S(1)}) custom-call(s32[8,2]{1,0:T(8,128)S(1)} %copy.121.slots_ref, f32[512,2688]{1,0:T(8,128)} %get-tuple-element.190.gate_ref.proj_ref, f32[4,1280]{1,0:T(4,128)S(1)} %copy-done.24, f32[1,1280]{1,0:T(1,128)S(1)} %broadcast_in_dim.14.bias_ref, f32[2,128]{1,0:T(2,128)S(1)} %copy-done.28, ...), custom_call_target="tpu_custom_call" | custom-call | flops 16999999488 | bytes 1700000 | tf_op jit(solution)/shard_map/pallas_call | solution.py:728
  425.7 11.0 %shard_map.357 = (bf16[1024,2688]{1,0:T(8,128)(2,1)}, bf16[1024,2688]{1,0:T(8,128)(2,1)}) custom-call(s32[32]{0:T(128)S(1)} %copy-done.29, bf16[512,2048]{1,0:T(8,128)(2,1)S(1)} %copy-done.72, bf16[512,2688]{1,0:T(8,128)(2,1)} %get-tuple-element.252.refs_1_.left_ref), custom_call_target="tpu_custom_call" | custom-call | flops 11000000512 | bytes 1100000 | tf_op jit(solution)/shard_map/pallas_call | solution.py:908
  437.4 4.3 collective-permute-start.40
  441.8 4.5 collective-permute-done.40
  447.3 10.0 %shard_map.358 = (f32[256,1024]{1,0:T(8,128)S(1)}, bf16[256,1024]{1,0:T(8,128)(2,1)S(1)}, f32[256,1024]{1,0:T(8,128)S(1)}, bf16[256,1024]{1,0:T(8,128)(2,1)S(1)}) custom-call(bf16[512,2688]{1,0:T(8,128)(2,1)} %get-tuple-element.252.refs_1_.left_ref, bf16[2048,2688]{1,0:T(8,128)(2,1)} %all-gather.4.cloned.1.call-done.weight_ref.gains_in_ref), custom_call_target="tpu_custom_call" | custom-call | flops 4000000000 | bytes 400000 | tf_op jit(solution)/shard_map/pallas_call | solution.py:394
  460.0 3.2 collective-permute-start.46
  463.2 6.3 %shard_map.359 = (bf16[256,2688]{1,0:T(8,128)(2,1)S(1)}, bf16[256,2688]{1,0:T(8,128)(2,1)S(1)}, bf16[256,2688]{1,0:T(8,128)(2,1)}, bf16[128,2688]{1,0:T(8,128)(2,1)S(1)}, bf16[128,2688]{1,0:T(8,128)(2,1)S(1)}) custom-call(bf16[1024,2688]{1,0:T(8,128)(2,1)} %get-tuple-element.250.keep_ref, bf16[1024,2688]{1,0:T(8,128)(2,1)} %collective-permute-done.48.got_ref), custom_call_target="tpu_custom_call" | custom-call | flops 3000000000 | bytes 300000 | tf_op jit(solution)/shard_map/pallas_call | solution.py:780
  472.8 14.7 %collective-permute-done.49.by_x_ref = bf16[128,2688]{1,0:T(8,128)(2,1)S(1)} collective-permute-done((bf16[128,2688]{1,0:T(8,128)(2,1)S(1)}, bf16[128,2688]{1,0:T(8,128)(2,1)S(1)}, u32[]{:S(2)}, u32[]{:S(2)}) %collective-permute-start.49) | collective-permute-done | bytes 688160 | tf_op jit(solution)/shard_map/ppermute | solution.py:960
  488.5 3.1 shard_map.360
  492.4 13.5 %collective-permute-done.47 = bf16[512,1024]{1,0:T(8,128)(2,1)} collective-permute-done((bf16[512,1024]{1,0:T(8,128)(2,1)}, bf16[512,1024]{1,0:T(8,128)(2,1)}, u32[]{:S(2)}, u32[]{:S(2)}) %collective-permute-start.47) | collective-permute-done | bytes 1048608 | tf_op jit(solution)/shard_map/ppermute | solution.py:960
  512.0 3.3 collective-permute-start.55
  518.4 18.8 %collective-permute-done.54 = bf16[256,1024]{1,0:T(8,128)(2,1)S(1)} collective-permute-done((bf16[256,1024]{1,0:T(8,128)(2,1)S(1)}, bf16[256,1024]{1,0:T(8,128)(2,1)S(1)}, u32[]{:S(2)}, u32[]{:S(2)}) %collective-permute-start.54) | collective-permute-done | bytes 524320 | tf_op jit(solution)/shard_map/ppermute | solution.py:960
  537.3 3.4 collective-permute-done.55
  549.0 3.4 shard_map.361
  561.2 2.6 collective-permute-done.61
  568.3 10.1 %collective-permute-done.59.g2 = bf16[64,2688]{1,0:T(8,128)(2,1)S(1)} collective-permute-done((bf16[64,2688]{1,0:T(8,128)(2,1)}, bf16[64,2688]{1,0:T(8,128)(2,1)S(1)}, u32[]{:S(2)}, u32[]{:S(2)}) %collective-permute-start.59) | collective-permute-done | bytes 344096 | tf_op jit(solution)/shard_map/ppermute | solution.py:960
  578.5 7.6 %collective-permute-done.60.g3 = bf16[64,2688]{1,0:T(8,128)(2,1)S(1)} collective-permute-done((bf16[64,2688]{1,0:T(8,128)(2,1)S(1)}, bf16[64,2688]{1,0:T(8,128)(2,1)S(1)}, u32[]{:S(2)}, u32[]{:S(2)}) %collective-permute-start.60) | collective-permute-done | bytes 344096 | tf_op jit(solution)/shard_map/ppermute | solution.py:960
  (443 shorter events, 160.2 us)
Async XLA Ops:
  7.2 120.4 %all-gather.4.cloned.1.call-start = ((), (), s32[]{:S(2)}) async-start(), calls=%async_computation.2 | async-start | bytes 12386304 | tf_op jit(solution)/shard_map/all_gather | solution.py:1093
  15.6 21.7 %collective-permute-start = (bf16[64,2688]{1,0:T(8,128)(2,1)}, bf16[64,2688]{1,0:T(8,128)(2,1)}, u32[]{:S(2)}, u32[]{:S(2)}) collective-permute-start(bf16[64,2688]{1,0:T(8,128)(2,1)} %concatenate.109), channel_id=1, source_target_pairs={{0,8},{8,0},{16,24},{24,16},{1,9},{9,1},{17,25},{25,17},{2,10},{10... | collective-permute-start | bytes 1032200 | tf_op jit(solution)/shard_map/ppermute | solution.py:960
  16.4 26.6 %collective-permute-start.1 = (bf16[64,2688]{1,0:T(8,128)(2,1)}, bf16[64,2688]{1,0:T(8,128)(2,1)}, u32[]{:S(2)}, u32[]{:S(2)}) collective-permute-start(bf16[64,2688]{1,0:T(8,128)(2,1)} %concatenate.110), channel_id=1, source_target_pairs={{0,16},{8,24},{16,0},{24,8},{1,17},{9,25},{17,1},{25,9},{2,18},{10... | collective-permute-start | bytes 1032200 | tf_op jit(solution)/shard_map/ppermute | solution.py:960
  20.3 32.4 %collective-permute-start.2 = (bf16[64,2688]{1,0:T(8,128)(2,1)}, bf16[64,2688]{1,0:T(8,128)(2,1)}, u32[]{:S(2)}, u32[]{:S(2)}) collective-permute-start(bf16[64,2688]{1,0:T(8,128)(2,1)} %concatenate.111), channel_id=1, source_target_pairs={{0,24},{8,16},{16,8},{24,0},{1,25},{9,17},{17,9},{25,1},{2,26},{10... | collective-permute-start | bytes 1032200 | tf_op jit(solution)/shard_map/ppermute | solution.py:960
  55.5 127.0 %all-gather.6.cloned.1.call-start = ((), (), s32[]{:S(2)}) async-start(), calls=%async_computation.3 | async-start | bytes 4718592 | tf_op jit(solution)/shard_map/all_gather | solution.py:1093
  63.6 35.5 %collective-permute-start.5 = (bf16[256,1024]{1,0:T(8,128)(2,1)}, bf16[256,1024]{1,0:T(8,128)(2,1)S(1)}, u32[]{:S(2)}, u32[]{:S(2)}) collective-permute-start(bf16[256,1024]{1,0:T(8,128)(2,1)} %pad_maximum_fusion.6), channel_id=1, source_target_pairs={{0,8},{8,0},{16,24},{24,16},{1,9},{9,1},{17,25},{25,17},{2,10},{10... | collective-permute-start | bytes 1572872 | tf_op jit(solution)/shard_map/ppermute | solution.py:960
  64.7 34.5 %collective-permute-start.6 = (bf16[256,1024]{1,0:T(8,128)(2,1)}, bf16[256,1024]{1,0:T(8,128)(2,1)}, u32[]{:S(2)}, u32[]{:S(2)}) collective-permute-start(bf16[256,1024]{1,0:T(8,128)(2,1)} %pad_maximum_fusion.7), channel_id=1, source_target_pairs={{0,24},{8,16},{16,8},{24,0},{1,25},{9,17},{17,9},{25,1},{2,26},{10... | collective-permute-start | bytes 1572872 | tf_op jit(solution)/shard_map/ppermute | solution.py:960
  66.4 28.7 %collective-permute-start.8 = (bf16[128,1024]{1,0:T(8,128)(2,1)S(1)}, bf16[128,1024]{1,0:T(8,128)(2,1)S(1)}, u32[]{:S(2)}, u32[]{:S(2)}) collective-permute-start(bf16[128,1024]{1,0:T(8,128)(2,1)S(1)} %get-tuple-element.357), channel_id=1, source_target_pairs={{0,8},{8,0},{16,24},{24,16},{1,9},{9,1},{17,25},{25,17},{2,10},{10... | collective-permute-start | bytes 786440 | tf_op jit(solution)/shard_map/ppermute | solution.py:960
  68.8 30.3 %collective-permute-start.7 = (bf16[128,1024]{1,0:T(8,128)(2,1)S(1)}, bf16[128,1024]{1,0:T(8,128)(2,1)S(1)}, u32[]{:S(2)}, u32[]{:S(2)}) collective-permute-start(bf16[128,1024]{1,0:T(8,128)(2,1)S(1)} %get-tuple-element.358), channel_id=1, source_target_pairs={{0,24},{8,16},{16,8},{24,0},{1,25},{9,17},{17,9},{25,1},{2,26},{10... | collective-permute-start | bytes 786440 | tf_op jit(solution)/shard_map/ppermute | solution.py:960
  111.1 152.1 %all-gather.8.cloned.1.call-start = ((), (), s32[]{:S(2)}) async-start(), calls=%async_computation.4 | async-start | bytes 14155776 | tf_op jit(solution)/shard_map/all_gather | solution.py:1093
  117.9 57.1 %collective-permute-start.25 = (bf16[64,3072]{1,0:T(8,128)(2,1)}, bf16[64,3072]{1,0:T(8,128)(2,1)}, u32[]{:S(2)}, u32[]{:S(2)}) collective-permute-start(bf16[64,3072]{1,0:T(8,128)(2,1)} %pad_maximum_fusion.20), channel_id=1, source_target_pairs={{0,8},{8,0},{16,24},{24,16},{1,9},{9,1},{17,25},{25,17},{2,10},{10... | collective-permute-start | bytes 1179656 | tf_op jit(solution)/shard_map/ppermute | solution.py:960
  119.0 57.5 %collective-permute-start.26 = (bf16[64,3072]{1,0:T(8,128)(2,1)}, bf16[64,3072]{1,0:T(8,128)(2,1)}, u32[]{:S(2)}, u32[]{:S(2)}) collective-permute-start(bf16[64,3072]{1,0:T(8,128)(2,1)} %pad_maximum_fusion.21), channel_id=1, source_target_pairs={{0,16},{8,24},{16,0},{24,8},{1,17},{9,25},{17,1},{25,9},{2,18},{10... | collective-permute-start | bytes 1179656 | tf_op jit(solution)/shard_map/ppermute | solution.py:960
  121.1 55.4 %collective-permute-start.27 = (bf16[64,3072]{1,0:T(8,128)(2,1)}, bf16[64,3072]{1,0:T(8,128)(2,1)}, u32[]{:S(2)}, u32[]{:S(2)}) collective-permute-start(bf16[64,3072]{1,0:T(8,128)(2,1)} %pad_maximum_fusion.22), channel_id=1, source_target_pairs={{0,24},{8,16},{16,8},{24,0},{1,25},{9,17},{17,9},{25,1},{2,26},{10... | collective-permute-start | bytes 1179656 | tf_op jit(solution)/shard_map/ppermute | solution.py:960
  123.2 49.7 %collective-permute-start.13 = (bf16[256,1024]{1,0:T(8,128)(2,1)}, bf16[256,1024]{1,0:T(8,128)(2,1)}, u32[]{:S(2)}, u32[]{:S(2)}) collective-permute-start(bf16[256,1024]{1,0:T(8,128)(2,1)} %pad_maximum_fusion.10), channel_id=1, source_target_pairs={{0,24},{8,16},{16,8},{24,0},{1,25},{9,17},{17,9},{25,1},{2,26},{10... | collective-permute-start | bytes 1572872 | tf_op jit(solution)/shard_map/ppermute | solution.py:960
  125.8 47.2 %collective-permute-start.12 = (bf16[256,1024]{1,0:T(8,128)(2,1)}, bf16[256,1024]{1,0:T(8,128)(2,1)}, u32[]{:S(2)}, u32[]{:S(2)}) collective-permute-start(bf16[256,1024]{1,0:T(8,128)(2,1)} %pad_maximum_fusion.9), channel_id=1, source_target_pairs={{0,8},{8,0},{16,24},{24,16},{1,9},{9,1},{17,25},{25,17},{2,10},{10... | collective-permute-start | bytes 1572872 | tf_op jit(solution)/shard_map/ppermute | solution.py:960
  182.4 206.5 %reduce-scatter.3.cloned.1.call-start = ((), (), s32[]{:S(2)}) async-start(), calls=%async_computation.5 | async-start | bytes 14155776 | tf_op jit(solution)/shard_map/reduce_scatter | solution.py:1096
  189.9 14.9 %collective-permute-start.17 = (bf16[256,1024]{1,0:T(8,128)(2,1)S(1)}, bf16[256,1024]{1,0:T(8,128)(2,1)S(1)}, u32[]{:S(2)}, u32[]{:S(2)}) collective-permute-start(bf16[256,1024]{1,0:T(8,128)(2,1)S(1)} %get-tuple-element.205), channel_id=1, source_target_pairs={{0,8},{8,0},{16,24},{24,16},{1,9},{9,1},{17,25},{25,17},{2,10},{10... | collective-permute-start | bytes 1572872 | tf_op jit(solution)/shard_map/ppermute | solution.py:960
  190.5 28.4 %collective-permute-start.19 = (bf16[256,1024]{1,0:T(8,128)(2,1)S(1)}, bf16[256,1024]{1,0:T(8,128)(2,1)S(1)}, u32[]{:S(2)}, u32[]{:S(2)}) collective-permute-start(bf16[256,1024]{1,0:T(8,128)(2,1)S(1)} %get-tuple-element.207), channel_id=1, source_target_pairs={{0,24},{8,16},{16,8},{24,0},{1,25},{9,17},{17,9},{25,1},{2,26},{10... | collective-permute-start | bytes 1572872 | tf_op jit(solution)/shard_map/ppermute | solution.py:960
  205.0 19.7 %collective-permute-start.18 = (bf16[128,1024]{1,0:T(8,128)(2,1)S(1)}, bf16[128,1024]{1,0:T(8,128)(2,1)S(1)}, u32[]{:S(2)}, u32[]{:S(2)}) collective-permute-start(bf16[128,1024]{1,0:T(8,128)(2,1)S(1)} %slice.334), channel_id=1, source_target_pairs={{0,24},{8,16},{16,8},{24,0},{1,25},{9,17},{17,9},{25,1},{2,26},{10... | collective-permute-start | bytes 786440 | tf_op jit(solution)/shard_map/ppermute | solution.py:960
  230.4 16.8 %collective-permute-start.21 = (bf16[128,1024]{1,0:T(8,128)(2,1)S(1)}, bf16[128,1024]{1,0:T(8,128)(2,1)S(1)}, u32[]{:S(2)}, u32[]{:S(2)}) collective-permute-start(bf16[128,1024]{1,0:T(8,128)(2,1)S(1)} %get-tuple-element.352), channel_id=1, source_target_pairs={{0,24},{8,16},{16,8},{24,0},{1,25},{9,17},{17,9},{25,1},{2,26},{10... | collective-permute-start | bytes 786440 | tf_op jit(solution)/shard_map/ppermute | solution.py:960
  232.2 15.8 %collective-permute-start.23 = (bf16[128,1024]{1,0:T(8,128)(2,1)S(1)}, bf16[128,1024]{1,0:T(8,128)(2,1)S(1)}, u32[]{:S(2)}, u32[]{:S(2)}) collective-permute-start(bf16[128,1024]{1,0:T(8,128)(2,1)S(1)} %get-tuple-element.351), channel_id=1, source_target_pairs={{0,8},{8,0},{16,24},{24,16},{1,9},{9,1},{17,25},{25,17},{2,10},{10... | collective-permute-start | bytes 786440 | tf_op jit(solution)/shard_map/ppermute | solution.py:960
  248.0 14.4 %collective-permute-start.24 = (bf16[256,1024]{1,0:T(8,128)(2,1)S(1)}, bf16[256,1024]{1,0:T(8,128)(2,1)S(1)}, u32[]{:S(2)}, u32[]{:S(2)}) collective-permute-start(bf16[256,1024]{1,0:T(8,128)(2,1)S(1)} %pad_maximum_fusion.14), channel_id=1, source_target_pairs={{0,24},{8,16},{16,8},{24,0},{1,25},{9,17},{17,9},{25,1},{2,26},{10... | collective-permute-start | bytes 1572872 | tf_op jit(solution)/shard_map/ppermute | solution.py:960
  295.4 167.8 %reduce-scatter.5.cloned.1.call-start = ((), (), s32[]{:S(2)}) async-start(), calls=%async_computation.6 | async-start | bytes 4718592 | tf_op jit(solution)/shard_map/reduce_scatter | solution.py:1096
  296.4 18.4 %collective-permute-start.28 = (bf16[256,1024]{1,0:T(8,128)(2,1)S(1)}, bf16[256,1024]{1,0:T(8,128)(2,1)S(1)}, u32[]{:S(2)}, u32[]{:S(2)}) collective-permute-start(bf16[256,1024]{1,0:T(8,128)(2,1)S(1)} %copy-done.35), channel_id=1, source_target_pairs={{0,8},{8,0},{16,24},{24,16},{1,9},{9,1},{17,25},{25,17},{2,10},{10... | collective-permute-start | bytes 1572872 | tf_op jit(solution)/shard_map/ppermute | solution.py:960
  299.7 20.4 %collective-permute-start.30 = (bf16[256,1024]{1,0:T(8,128)(2,1)S(1)}, bf16[256,1024]{1,0:T(8,128)(2,1)S(1)}, u32[]{:S(2)}, u32[]{:S(2)}) collective-permute-start(bf16[256,1024]{1,0:T(8,128)(2,1)S(1)} %get-tuple-element.221), channel_id=1, source_target_pairs={{0,24},{8,16},{16,8},{24,0},{1,25},{9,17},{17,9},{25,1},{2,26},{10... | collective-permute-start | bytes 1572872 | tf_op jit(solution)/shard_map/ppermute | solution.py:960
  316.4 15.2 %collective-permute-start.29 = (bf16[128,1024]{1,0:T(8,128)(2,1)S(1)}, bf16[128,1024]{1,0:T(8,128)(2,1)S(1)}, u32[]{:S(2)}, u32[]{:S(2)}) collective-permute-start(bf16[128,1024]{1,0:T(8,128)(2,1)S(1)} %slice.332), channel_id=1, source_target_pairs={{0,24},{8,16},{16,8},{24,0},{1,25},{9,17},{17,9},{25,1},{2,26},{10... | collective-permute-start | bytes 786440 | tf_op jit(solution)/shard_map/ppermute | solution.py:960
  335.3 17.6 %collective-permute-start.32 = (bf16[128,1024]{1,0:T(8,128)(2,1)S(1)}, bf16[128,1024]{1,0:T(8,128)(2,1)S(1)}, u32[]{:S(2)}, u32[]{:S(2)}) collective-permute-start(bf16[128,1024]{1,0:T(8,128)(2,1)S(1)} %get-tuple-element.350), channel_id=1, source_target_pairs={{0,24},{8,16},{16,8},{24,0},{1,25},{9,17},{17,9},{25,1},{2,26},{10... | collective-permute-start | bytes 786440 | tf_op jit(solution)/shard_map/ppermute | solution.py:960
  336.9 16.1 %collective-permute-start.34 = (bf16[128,1024]{1,0:T(8,128)(2,1)S(1)}, bf16[128,1024]{1,0:T(8,128)(2,1)S(1)}, u32[]{:S(2)}, u32[]{:S(2)}) collective-permute-start(bf16[128,1024]{1,0:T(8,128)(2,1)S(1)} %get-tuple-element.349), channel_id=1, source_target_pairs={{0,8},{8,0},{16,24},{24,16},{1,9},{9,1},{17,25},{25,17},{2,10},{10... | collective-permute-start | bytes 786440 | tf_op jit(solution)/shard_map/ppermute | solution.py:960
  369.8 17.2 %collective-permute-start.38 = (f32[8,1,64]{2,1,0:T(1,128)S(1)}, f32[8,1,64]{2,1,0:T(1,128)S(1)}, u32[]{:S(2)}, u32[]{:S(2)}) collective-permute-start(f32[8,1,64]{2,1,0:T(1,128)S(1)} %get-tuple-element.239.d0), channel_id=1, source_target_pairs={{0,24},{8,16},{16,8},{24,0},{1,25},{9,17},{17,9},{25,1},{2,26},{10... | collective-permute-start | bytes 6152 | tf_op jit(solution)/shard_map/ppermute | solution.py:960
  371.2 16.4 %collective-permute-start.37 = (f32[8,1,64]{2,1,0:T(1,128)S(1)}, f32[8,1,64]{2,1,0:T(1,128)S(1)}, u32[]{:S(2)}, u32[]{:S(2)}) collective-permute-start(f32[8,1,64]{2,1,0:T(1,128)S(1)} %get-tuple-element.239.d0), channel_id=1, source_target_pairs={{0,16},{8,24},{16,0},{24,8},{1,17},{9,25},{17,1},{25,9},{2,18},{10... | collective-permute-start | bytes 6152 | tf_op jit(solution)/shard_map/ppermute | solution.py:960
  390.5 33.6 %collective-permute-start.45 = (bf16[64,3072]{1,0:T(8,128)(2,1)S(1)}, bf16[64,3072]{1,0:T(8,128)(2,1)S(1)}, u32[]{:S(2)}, u32[]{:S(2)}) collective-permute-start(bf16[64,3072]{1,0:T(8,128)(2,1)S(1)} %get-tuple-element.313), channel_id=1, source_target_pairs={{0,24},{8,16},{16,8},{24,0},{1,25},{9,17},{17,9},{25,1},{2,26},{10... | collective-permute-start | bytes 1179656 | tf_op jit(solution)/shard_map/ppermute | solution.py:960
  392.0 33.7 %collective-permute-start.44 = (bf16[64,3072]{1,0:T(8,128)(2,1)S(1)}, bf16[64,3072]{1,0:T(8,128)(2,1)S(1)}, u32[]{:S(2)}, u32[]{:S(2)}) collective-permute-start(bf16[64,3072]{1,0:T(8,128)(2,1)S(1)} %get-tuple-element.314), channel_id=1, source_target_pairs={{0,16},{8,24},{16,0},{24,8},{1,17},{9,25},{17,1},{25,9},{2,18},{10... | collective-permute-start | bytes 1179656 | tf_op jit(solution)/shard_map/ppermute | solution.py:960
  394.9 30.8 %collective-permute-start.43 = (bf16[64,3072]{1,0:T(8,128)(2,1)S(1)}, bf16[64,3072]{1,0:T(8,128)(2,1)S(1)}, u32[]{:S(2)}, u32[]{:S(2)}) collective-permute-start(bf16[64,3072]{1,0:T(8,128)(2,1)S(1)} %get-tuple-element.315), channel_id=1, source_target_pairs={{0,8},{8,0},{16,24},{24,16},{1,9},{9,1},{17,25},{25,17},{2,10},{10... | collective-permute-start | bytes 1179656 | tf_op jit(solution)/shard_map/ppermute | solution.py:960
  436.8 26.5 %collective-permute-start.48 = (bf16[1024,2688]{1,0:T(8,128)(2,1)}, bf16[1024,2688]{1,0:T(8,128)(2,1)}, u32[]{:S(2)}, u32[]{:S(2)}) collective-permute-start(bf16[1024,2688]{1,0:T(8,128)(2,1)} %get-tuple-element.251), channel_id=1, source_target_pairs={{0,1},{1,0},{2,3},{3,2},{4,5},{5,4},{6,7},{7,6},{8,9},{9,8},{10,11... | collective-permute-start | bytes 16515080 | tf_op jit(solution)/shard_map/ppermute | solution.py:960
  458.4 47.5 %collective-permute-start.47 = (bf16[512,1024]{1,0:T(8,128)(2,1)}, bf16[512,1024]{1,0:T(8,128)(2,1)}, u32[]{:S(2)}, u32[]{:S(2)}) collective-permute-start(bf16[512,1024]{1,0:T(8,128)(2,1)} %pad_maximum_fusion.5), channel_id=1, source_target_pairs={{0,24},{8,16},{16,8},{24,0},{1,25},{9,17},{17,9},{25,1},{2,26},{10... | collective-permute-start | bytes 3145736 | tf_op jit(solution)/shard_map/ppermute | solution.py:960
  460.0 48.1 %collective-permute-start.46 = (bf16[512,1024]{1,0:T(8,128)(2,1)}, bf16[512,1024]{1,0:T(8,128)(2,1)}, u32[]{:S(2)}, u32[]{:S(2)}) collective-permute-start(bf16[512,1024]{1,0:T(8,128)(2,1)} %pad_maximum_fusion.4), channel_id=1, source_target_pairs={{0,8},{8,0},{16,24},{24,16},{1,9},{9,1},{17,25},{25,17},{2,10},{10... | collective-permute-start | bytes 3145736 | tf_op jit(solution)/shard_map/ppermute | solution.py:960
  470.7 16.8 %collective-permute-start.49 = (bf16[128,2688]{1,0:T(8,128)(2,1)S(1)}, bf16[128,2688]{1,0:T(8,128)(2,1)S(1)}, u32[]{:S(2)}, u32[]{:S(2)}) collective-permute-start(bf16[128,2688]{1,0:T(8,128)(2,1)S(1)} %get-tuple-element.260), channel_id=1, source_target_pairs={{0,4},{4,0},{1,5},{5,1},{2,6},{6,2},{3,7},{7,3},{8,12},{12,8},{9,1... | collective-permute-start | bytes 2064392 | tf_op jit(solution)/shard_map/ppermute | solution.py:960
  472.0 16.5 %collective-permute-start.50 = (bf16[128,2688]{1,0:T(8,128)(2,1)S(1)}, bf16[128,2688]{1,0:T(8,128)(2,1)S(1)}, u32[]{:S(2)}, u32[]{:S(2)}) collective-permute-start(bf16[128,2688]{1,0:T(8,128)(2,1)S(1)} %get-tuple-element.261), channel_id=1, source_target_pairs={{0,2},{2,0},{1,3},{3,1},{4,6},{6,4},{5,7},{7,5},{8,10},{10,8},{9,1... | collective-permute-start | bytes 2064392 | tf_op jit(solution)/shard_map/ppermute | solution.py:960
  472.8 43.9 %collective-permute-start.42 = (f32[4,8,2176]{2,1,0:T(8,128)S(1)}, f32[4,8,2176]{2,1,0:T(8,128)S(1)}, u32[]{:S(2)}, u32[]{:S(2)}) collective-permute-start(f32[4,8,2176]{2,1,0:T(8,128)S(1)} %pad_maximum_fusion.24), channel_id=1, source_target_pairs={{0,1},{1,0},{2,3},{3,2},{4,5},{5,4},{6,7},{7,6},{8,9},{9,8},{10,11... | collective-permute-start | bytes 835592 | tf_op jit(solution)/shard_map/ppermute | solution.py:960
  491.6 56.3 %collective-permute-start.56 = (bf16[256,2688]{1,0:T(8,128)(2,1)S(1)}, bf16[256,2688]{1,0:T(8,128)(2,1)S(1)}, u32[]{:S(2)}, u32[]{:S(2)}) collective-permute-start(bf16[256,2688]{1,0:T(8,128)(2,1)S(1)} %get-tuple-element.262), channel_id=1, source_target_pairs={{0,4},{4,0},{1,5},{5,1},{2,6},{6,2},{3,7},{7,3},{8,12},{12,8},{9,1... | collective-permute-start | bytes 4128776 | tf_op jit(solution)/shard_map/ppermute | solution.py:960
  511.3 25.9 %collective-permute-start.54 = (bf16[256,1024]{1,0:T(8,128)(2,1)S(1)}, bf16[256,1024]{1,0:T(8,128)(2,1)S(1)}, u32[]{:S(2)}, u32[]{:S(2)}) collective-permute-start(bf16[256,1024]{1,0:T(8,128)(2,1)S(1)} %pad_maximum_fusion.17), channel_id=1, source_target_pairs={{0,24},{8,16},{16,8},{24,0},{1,25},{9,17},{17,9},{25,1},{2,26},{10... | collective-permute-start | bytes 1572872 | tf_op jit(solution)/shard_map/ppermute | solution.py:960
  512.0 28.6 %collective-permute-start.55 = (bf16[256,1024]{1,0:T(8,128)(2,1)S(1)}, bf16[256,1024]{1,0:T(8,128)(2,1)S(1)}, u32[]{:S(2)}, u32[]{:S(2)}) collective-permute-start(bf16[256,1024]{1,0:T(8,128)(2,1)S(1)} %pad_maximum_fusion.18), channel_id=1, source_target_pairs={{0,8},{8,0},{16,24},{24,16},{1,9},{9,1},{17,25},{25,17},{2,10},{10... | collective-permute-start | bytes 1572872 | tf_op jit(solution)/shard_map/ppermute | solution.py:960
  515.4 32.5 %collective-permute-start.57 = (bf16[256,2688]{1,0:T(8,128)(2,1)S(1)}, bf16[256,2688]{1,0:T(8,128)(2,1)S(1)}, u32[]{:S(2)}, u32[]{:S(2)}) collective-permute-start(bf16[256,2688]{1,0:T(8,128)(2,1)S(1)} %get-tuple-element.267), channel_id=1, source_target_pairs={{0,2},{2,0},{1,3},{3,1},{4,6},{6,4},{5,7},{7,5},{8,10},{10,8},{9,1... | collective-permute-start | bytes 4128776 | tf_op jit(solution)/shard_map/ppermute | solution.py:960
  517.8 27.7 %collective-permute-start.53 = (bf16[64,1024]{1,0:T(8,128)(2,1)S(1)}, bf16[64,1024]{1,0:T(8,128)(2,1)S(1)}, u32[]{:S(2)}, u32[]{:S(2)}) collective-permute-start(bf16[64,1024]{1,0:T(8,128)(2,1)S(1)} %get-tuple-element.345), channel_id=1, source_target_pairs={{0,24},{8,16},{16,8},{24,0},{1,25},{9,17},{17,9},{25,1},{2,26},{10... | collective-permute-start | bytes 393224 | tf_op jit(solution)/shard_map/ppermute | solution.py:960
  552.3 16.0 %collective-permute-start.58 = (bf16[64,2688]{1,0:T(8,128)(2,1)}, bf16[64,2688]{1,0:T(8,128)(2,1)S(1)}, u32[]{:S(2)}, u32[]{:S(2)}) collective-permute-start(bf16[64,2688]{1,0:T(8,128)(2,1)} %get-tuple-element.271), channel_id=1, source_target_pairs={{0,8},{8,0},{16,24},{24,16},{1,9},{9,1},{17,25},{25,17},{2,10},{10... | collective-permute-start | bytes 1032200 | tf_op jit(solution)/shard_map/ppermute | solution.py:960
  554.9 23.6 %collective-permute-start.59 = (bf16[64,2688]{1,0:T(8,128)(2,1)}, bf16[64,2688]{1,0:T(8,128)(2,1)S(1)}, u32[]{:S(2)}, u32[]{:S(2)}) collective-permute-start(bf16[64,2688]{1,0:T(8,128)(2,1)} %get-tuple-element.272), channel_id=1, source_target_pairs={{0,16},{8,24},{16,0},{24,8},{1,17},{9,25},{17,1},{25,9},{2,18},{10... | collective-permute-start | bytes 1032200 | tf_op jit(solution)/shard_map/ppermute | solution.py:960
  554.9 31.2 %collective-permute-start.60 = (bf16[64,2688]{1,0:T(8,128)(2,1)S(1)}, bf16[64,2688]{1,0:T(8,128)(2,1)S(1)}, u32[]{:S(2)}, u32[]{:S(2)}) collective-permute-start(bf16[64,2688]{1,0:T(8,128)(2,1)S(1)} %get-tuple-element.273), channel_id=1, source_target_pairs={{0,24},{8,16},{16,8},{24,0},{1,25},{9,17},{17,9},{25,1},{2,26},{10... | collective-permute-start | bytes 1032200 | tf_op jit(solution)/shard_map/ppermute | solution.py:960
  564.5 23.9 %collective-permute-start.62 = (f32[4,8,2176]{2,1,0:T(8,128)}, f32[4,8,2176]{2,1,0:T(8,128)}, u32[]{:S(2)}, u32[]{:S(2)}) collective-permute-start(f32[4,8,2176]{2,1,0:T(8,128)} %add.271), channel_id=1, source_target_pairs={{0,2},{2,0},{1,3},{3,1},{4,6},{6,4},{5,7},{7,5},{8,10},{10,8},{9,1... | collective-permute-start | bytes 835592 | tf_op jit(solution)/shard_map/ppermute | solution.py:960
  (120 other events, 1563.0 us)
Sparse Core Ops, SparseCore 0:
  55.6 65.6 all-gather.3
  123.7 36.7 all-gather.5
  182.6 72.6 all-gather.7
  295.5 93.3 reduce-scatter.2
  392.1 51.3 reduce-scatter.4

commit v4 on v3

--- a/solution.py
+++ b/solution.py
@@ -693,6 +693,11 @@
     )
 
     rows = jnp.concatenate([conv_rows, inner_rows, step_rows], axis=1)
+    wide = small_ref.shape[1]
+    rows = jnp.concatenate(
+        [rows, jnp.zeros((8, small_ref.shape[0] // 8 * wide - rows.shape[1]), f32)], axis=1
+    )
+    rows = jnp.concatenate([rows[:, c : c + wide] for c in range(0, rows.shape[1], wide)], axis=0)
 
     @pl.when(step_id == 0)
     def _():
@@ -725,6 +730,7 @@
     length = rows // seqs
     conv_cols = inner + 2 * state
     pad = steps.shape[1]
+    small_shape = (8 * pl.cdiv(conv_cols + inner + pad, grads.shape[1]), grads.shape[1])
     return pl.pallas_call(
         functools.partial(backward_kernel, inner, state, heads),
         grid=(seqs,),
@@ -735,10 +741,10 @@
         + [rows_spec(length, inner), rows_spec(length, grads.shape[1])]
         + [pl.BlockSpec((1, 1, length), lambda i: (i, 0, 0))]
         + [their_spec(length, seqs // TP, k) for k in range(TP)],
-        out_specs=[rows_spec(length, cols)] + specs((8, conv_cols + inner + pad)),
+        out_specs=[rows_spec(length, cols)] + specs(small_shape),
         out_shape=[
             jax.ShapeDtypeStruct((rows, cols), bf16),
-            jax.ShapeDtypeStruct((8, conv_cols + inner + pad), f32),
+            jax.ShapeDtypeStruct(small_shape, f32),
         ],
         compiler_params=big,
         cost_estimate=costs(17),
@@ -987,16 +993,9 @@
         got_right = swap(last[half:].astype(bf16), 1)
         return pair[:half], got, last[:half], got_right
 
-    def pair_send(one, two):
-        return [swap(jnp.concatenate([one[i], two[i]], axis=0), k) for i, k in ((1, 1), (3, 3))]
-
-    def pair_finish(one, two, got, got_right):
-        rows = one[1].shape[0]
-        half = rows // 2
-        pairs = [
-            reduce_add(h, got[i * rows : (i + 1) * rows], got_right[i * rows : (i + 1) * rows])
-            for i, h in enumerate((one, two))
-        ]
+    def pair_finish(one, two, got_one, got_two):
+        pairs = [reduce_add(one, *got_one), reduce_add(two, *got_two)]
+        half = one[1].shape[0] // 2
         sends = [
             swap(jnp.concatenate([p[i][half:].astype(bf16) for p in pairs], axis=0), k)
             for i, k in ((0, 3), (1, 1))
@@ -1163,40 +1162,48 @@
     branch_all, d_branches, dots = back_outer(
         branch_grad, w_out, projected, y, gain_t, slots.shape[0]
     )
+    last_halves = after(last_halves, branch_grad)
+    last_pair = reduce_send(last_halves)
     out_sums = weight_grads(in_group, 1, [([branch_all], [branches], 0, inner_t + q_t)])
-    dots = after(everywhere(dots), out_sums)
+    dots = after(everywhere(dots), (out_sums, last_pair))
     out_sums = scatter(out_sums[0])
     mlp_grads = pass_on(after(mlp_sums, dots))
     proj_grad, small = mixer_backward(
         slots, projected, taps_t, bias_t, steps_t, skip_t, turns, gain_t, y, d_branches, root,
         dots, *sizes,
     )
-    small = everywhere(small)
     in_sums = weight_grads(
         in_plane if cube else in_group,
         2 if cube else 1,
         [([after(normed, mlp_grads)], [proj_grad], 0, in_cols)],
     )
+    riders = small.astype(bf16)
+    out_sums, riders = after((out_sums, riders), in_sums)
+    out_sums = out_sums.reshape(TP, shard, -1)
+    received = [
+        swap(jnp.concatenate([out_sums[k], riders], axis=0), k) for k in range(1, TP)
+    ]
     norm_halves = back_out(after(proj_grad, in_sums), w_in, 0)
-    pairs = pair_send(norm_halves, last_halves)
+    norm_pair = reduce_send(norm_halves)
     if cube:
         block, half = TP * shard, TP * shard // 2
         counts = (block, block, block, half, half)
         keep, send = in_sums
         mine, along_y, along_x, across_x, across_y = by_columns(
-            chip_kernel, counts, keep, after(swap(send, 1, "core"), (out_sums, norm_halves, small))
+            chip_kernel, counts, keep, after(swap(send, 1, "core"), (norm_halves, received))
         )
+        across = swap(across_x, 1, "x"), swap(across_y, 1, "y")
+        norm_pair, across = after((norm_pair, across), norm_pair)
         to_y, to_x = by_columns(
-            along_kernel, (block, block), along_y, along_x, swap(across_x, 1, "x"), swap(across_y, 1, "y")
+            along_kernel, (block, block), along_y, along_x, *across
         )
         in_parts = swap(to_x, 1, "x"), swap(to_y, 1, "y")
-        pairs, out_sums = after((pairs, out_sums), to_x)
-    norm_parts, last_parts = pair_finish(norm_halves, last_halves, *pairs)
-    out_grads = pass_on(out_sums)
-    small = absolute(small)
+    norm_parts, last_parts = pair_finish(norm_halves, last_halves, norm_pair, last_pair)
+    out_grads = [out_sums[0]] + [r[:shard] for r in received]
+    small = absolute([small] + [r[shard:].astype(f32) for r in received])
     if cube:
         small = small + swap(small, 1, "core")
-        in_parts = after(in_parts, (norm_parts, last_parts, out_grads, small))
+        in_parts = after(in_parts, (norm_parts, last_parts, small))
         in_sums = by_columns(plane_kernel, (shard,) * TP, mine, *in_parts)
         in_grads = exchange(in_sums)
     else:
@@ -1207,9 +1214,7 @@
     )
     if cube:
         small = small + swap(small, 1, "x")
-        mlp_grads = after(mlp_grads, small)
         small = small + swap(small, 1, "y")
-        out_grads = after(out_grads, small)
     else:
         small = lax.psum(small, plane)
     token_grads = whole_call(
@@ -1230,6 +1235,7 @@
     grad_mamba_out, grad_output = unpack(
         functools.partial(unpack_out_kernel, inner_t, q_t), at_group, out_grads, (), (inner, q_cols)
     )
+    in_grads = after(in_grads, (small, token_grads, output, grad_down, grad_output))
     grad_mamba_in, grad_query, grad_key, grad_value, grad_norm_gain = unpack(
         functools.partial(unpack_in_kernel, *sizes, pad),
         at_group,
@@ -1241,6 +1247,8 @@
     grad_norm_gain, grad_second_gain = grad_norm_gain[:, 0], grad_second_gain[:, 0]
 
     kernel = conv_taps.shape[0]
+    small = small.reshape(TP, -1, 8, small.shape[-1])
+    small = jnp.concatenate([small[:, i] for i in range(small.shape[1])], axis=-1)
     conv = small[:, : kernel + 1, :conv_cols]
     conv = jnp.concatenate(
         [conv[:, :, :inner_t].transpose(1, 0, 2).reshape(kernel + 1, inner), conv[:, :, inner_t:].sum(0)],

time: 609 us -> 593 us (0.974)
  starting transfers between devices: 87.3 us -> 74.5 us
  waiting for transfers between devices: 266 us -> 258 us
    ppermute x63 -> x62, starting transfers between devices: 86.8 us -> 74.1 us  [swap(): return lax.ppermute(values, axis, [(i, i ^ k) for i in range(size)])]
    ppermute x63 -> x62, waiting for transfers between devices: 265 us -> 258 us  [swap(): return lax.ppermute(values, axis, [(i, i ^ k) for i in range(size)])]
    unnamed x192 -> x229, local copies, waits for them, and re-layouts: 20 us -> 19.9 us
  transfers between devices with their start and end apart: 68 -> 67, of which waited for: 42 -> 40; matrix products, arithmetic and copies ran while one was open for 7% -> 9% of each run, Pallas kernels for 20% -> 20%
where the time goes in v4:
time: 593 us; the launch traced here: 585 us
  waiting for transfers between devices  258 us (44%)
  Pallas kernels  154 us (26%)
  starting transfers between devices  74.5 us (13%)
  local copies, waits for them, and re-layouts  54.1 us (9%)
  other arithmetic  28 us (5%)
  between operations  15.7 us (3%)
    ppermute x62, waiting for transfers between devices, swap(): return lax.ppermute(values, axis, [(i, i ^ k) for i in range(size)])  258 us
    ppermute x62, starting transfers between devices, swap(): return lax.ppermute(values, axis, [(i, i ^ k) for i in range(size)])  74.1 us
    pallas_call x1, Pallas kernels, feed_forward(): pl.pallas_call(functools.partial(feed_kernel, steps, table.shape[0]), gri...  29.1 us
    pallas_call x1, Pallas kernels, mixer_inner(): pl.pallas_call(functools.partial(inner_kernel, inner, state, heads, tiles...  26.6 us
    pallas_call x1, Pallas kernels, mixer_backward(): pl.pallas_call(functools.partial(backward_kernel, inner, state, heads), g...  25.6 us
    unnamed x229, local copies, waits for them, and re-layouts  19.9 us
    pallas_call x2, Pallas kernels, back_out(): pl.pallas_call(back_out_kernel, grid=(model // tile,), in_specs=specs(lef...  16.7 us
    pallas_call x2, Pallas kernels, weight_grads(): pl.pallas_call(functools.partial(weight_grad_kernel, tuple(bounds), mine,...  16.5 us
  transfers between devices with their start and end apart: 67, of which 40 were waited for; matrix products, arithmetic and copies ran while one was open for 9% of the time, Pallas kernels for 20%

profile of v4, /device:TPU:8, one launch (start us, length us, event | category | flops | bytes accessed | tf_op | source)
XLA Modules:
  0.0 584.9 jit_solution(10137156369231395640)
XLA Ops:
  16.4 3.0 collective-permute-start.1
  34.6 8.4 %collective-permute-done.1 = bf16[64,2688]{1,0:T(8,128)(2,1)} collective-permute-done((bf16[64,2688]{1,0:T(8,128)(2,1)}, bf16[64,2688]{1,0:T(8,128)(2,1)}, u32[]{:S(2)}, u32[]{:S(2)}) %collective-permute-start.1) | collective-permute-done | bytes 344096 | tf_op jit(solution)/shard_map/ppermute | solution.py:966
  43.0 9.7 %collective-permute-done.2 = bf16[64,2688]{1,0:T(8,128)(2,1)} collective-permute-done((bf16[64,2688]{1,0:T(8,128)(2,1)}, bf16[64,2688]{1,0:T(8,128)(2,1)}, u32[]{:S(2)}, u32[]{:S(2)}) %collective-permute-start.2) | collective-permute-done | bytes 344096 | tf_op jit(solution)/shard_map/ppermute | solution.py:966
  57.5 5.3 collective-permute-done.3.p1
  69.8 25.3 %collective-permute-done.8.c3 = bf16[128,1024]{1,0:T(8,128)(2,1)S(1)} collective-permute-done((bf16[128,1024]{1,0:T(8,128)(2,1)S(1)}, bf16[128,1024]{1,0:T(8,128)(2,1)S(1)}, u32[]{:S(2)}, u32[]{:S(2)}) %collective-permute-start.8) | collective-permute-done | bytes 262176 | tf_op jit(solution)/shard_map/ppermute | solution.py:966
  95.1 4.0 collective-permute-done.7.c1
  104.4 3.6 collective-permute-done.10
  128.8 26.6 %shard_map.348 = (bf16[512,2048]{1,0:T(8,128)(2,1)}, f32[512,2688]{1,0:T(8,128)}, f32[512,768]{1,0:T(8,128)}, f32[8,1,64]{2,1,0:T(1,128)S(1)}, bf16[512,256]{1,0:T(8,128)(2,1)S(1)}, /*index=5*/f32[8,2048]{1,0:T(8,128)S(1)}) custom-call(s32[8,2]{1,0:T(8,128)S(1)} %copy.127.slots_ref, bf16[128,2048]{1,0:T(8,128)(2,1)S(1)} %copy.119.p0, ...), custom_call_target="tpu_custom_call" | custom-call | flops 17999998976 | bytes 1800000 | tf_op jit(solution)/shard_map/pallas_call | solution.py:320
  155.4 17.6 %collective-permute-done.13.c4 = bf16[256,1024]{1,0:T(8,128)(2,1)} collective-permute-done((bf16[256,1024]{1,0:T(8,128)(2,1)}, bf16[256,1024]{1,0:T(8,128)(2,1)}, u32[]{:S(2)}, u32[]{:S(2)}) %collective-permute-start.13) | collective-permute-done | bytes 524320 | tf_op jit(solution)/shard_map/ppermute | solution.py:966
  176.6 2.9 collective-permute-done.15.s2
  182.6 7.3 %shard_map.349 = (bf16[512,1024]{1,0:T(8,128)(2,1)S(1)}, f32[8,1,64]{2,1,0:T(1,128)S(1)}, f32[256,1024]{1,0:T(8,128)S(1)}, bf16[256,1024]{1,0:T(8,128)(2,1)S(1)}...) custom-call(f32[512,2688]{1,0:T(8,128)} %get-tuple-element.193.gate_ref.proj_ref, ...), custom_call_target="tpu_custom_call" | custom-call | flops 4000000000 | bytes 400000 | tf_op jit(solution)/shard_map/pallas_call | solution.py:367
  192.6 12.3 %collective-permute-done.17 = bf16[256,1024]{1,0:T(8,128)(2,1)S(1)} collective-permute-done((bf16[256,1024]{1,0:T(8,128)(2,1)S(1)}, bf16[256,1024]{1,0:T(8,128)(2,1)S(1)}, u32[]{:S(2)}, u32[]{:S(2)}) %collective-permute-start.17) | collective-permute-done | bytes 524320 | tf_op jit(solution)/shard_map/ppermute | solution.py:966
  205.7 13.2 %collective-permute-done.19 = bf16[256,1024]{1,0:T(8,128)(2,1)S(1)} collective-permute-done((bf16[256,1024]{1,0:T(8,128)(2,1)S(1)}, bf16[256,1024]{1,0:T(8,128)(2,1)S(1)}, u32[]{:S(2)}, u32[]{:S(2)}) %collective-permute-start.19) | collective-permute-done | bytes 524320 | tf_op jit(solution)/shard_map/ppermute | solution.py:966
  219.3 7.4 %collective-permute-done.18.k1 = bf16[128,1024]{1,0:T(8,128)(2,1)S(1)} collective-permute-done((bf16[128,1024]{1,0:T(8,128)(2,1)S(1)}, bf16[128,1024]{1,0:T(8,128)(2,1)S(1)}, u32[]{:S(2)}, u32[]{:S(2)}) %collective-permute-start.18) | collective-permute-done | bytes 262176 | tf_op jit(solution)/shard_map/ppermute | solution.py:966
  231.9 3.4 collective-permute-start.23
  235.3 11.8 %collective-permute-done.21.s1 = bf16[128,1024]{1,0:T(8,128)(2,1)S(1)} collective-permute-done((bf16[128,1024]{1,0:T(8,128)(2,1)S(1)}, bf16[128,1024]{1,0:T(8,128)(2,1)S(1)}, u32[]{:S(2)}, u32[]{:S(2)}) %collective-permute-start.21) | collective-permute-done | bytes 262176 | tf_op jit(solution)/shard_map/ppermute | solution.py:966
  249.8 6.6 %collective-permute-done.22.s2 = bf16[256,1024]{1,0:T(8,128)(2,1)S(1)} collective-permute-done((bf16[256,1024]{1,0:T(8,128)(2,1)S(1)}, bf16[256,1024]{1,0:T(8,128)(2,1)S(1)}, u32[]{:S(2)}, u32[]{:S(2)}) %collective-permute-start.22) | collective-permute-done | bytes 524320 | tf_op jit(solution)/shard_map/ppermute | solution.py:966
  257.1 5.0 collective-permute-done.24.s4
  265.0 29.1 %shard_map.351 = (bf16[512,1024]{1,0:T(8,128)(2,1)}, f32[256,1024]{1,0:T(8,128)}, bf16[256,1024]{1,0:T(8,128)(2,1)S(1)}, f32[256,1024]{1,0:T(8,128)}, bf16[256,1...) custom-call(s32[8,2]{1,0:T(8,128)S(1)} %copy.127.slots_ref, s32[32]{0:T(128)S(1)} %get-tuple-element.196.table_ref, ...), custom_call_target="tpu_custom_call" | custom-call | flops 30000001024 | bytes 3000000 | tf_op jit(solution)/shard_map/pallas_call | solution.py:495
  295.9 3.2 collective-permute-start.28
  299.2 15.1 %collective-permute-done.28 = bf16[256,1024]{1,0:T(8,128)(2,1)S(1)} collective-permute-done((bf16[256,1024]{1,0:T(8,128)(2,1)S(1)}, bf16[256,1024]{1,0:T(8,128)(2,1)S(1)}, u32[]{:S(2)}, u32[]{:S(2)}) %collective-permute-start.28) | collective-permute-done | bytes 524320 | tf_op jit(solution)/shard_map/ppermute | solution.py:966
  315.2 4.3 collective-permute-done.30
  322.2 9.2 %collective-permute-done.29.k1 = bf16[128,1024]{1,0:T(8,128)(2,1)S(1)} collective-permute-done((bf16[128,1024]{1,0:T(8,128)(2,1)S(1)}, bf16[128,1024]{1,0:T(8,128)(2,1)S(1)}, u32[]{:S(2)}, u32[]{:S(2)}) %collective-permute-start.29) | collective-permute-done | bytes 262176 | tf_op jit(solution)/shard_map/ppermute | solution.py:966
  335.3 2.7 collective-permute-start.34
  337.9 11.6 %collective-permute-done.32.b1 = bf16[128,1024]{1,0:T(8,128)(2,1)S(1)} collective-permute-done((bf16[128,1024]{1,0:T(8,128)(2,1)S(1)}, bf16[128,1024]{1,0:T(8,128)(2,1)S(1)}, u32[]{:S(2)}, u32[]{:S(2)}) %collective-permute-start.32) | collective-permute-done | bytes 262176 | tf_op jit(solution)/shard_map/ppermute | solution.py:966
  353.2 6.8 %shard_map.353 = (f32[256,1024]{1,0:T(8,128)S(1)}, bf16[256,1024]{1,0:T(8,128)(2,1)}, f32[256,1024]{1,0:T(8,128)S(1)}, bf16[256,1024]{1,0:T(8,128)(2,1)}) custom-call(bf16[512,1024]{1,0:T(8,128)(2,1)} %get-tuple-element.227.left_ref, bf16[2048,3072]{1,0:T(8,128)(2,1)} %all-gather.8.cloned.1.call-done.gate_ref.up_ref.down_ref.weight_ref), custom_call_target="tpu_custom_call" | custom-call | flops 4000000000 | bytes 400000 | tf_op jit(solution)/shard_map/pallas_call | solution.py:394
  362.6 14.2 %collective-permute-done.35.b4 = bf16[256,1024]{1,0:T(8,128)(2,1)S(1)} collective-permute-done((bf16[256,1024]{1,0:T(8,128)(2,1)S(1)}, bf16[256,1024]{1,0:T(8,128)(2,1)S(1)}, u32[]{:S(2)}, u32[]{:S(2)}) %collective-permute-start.35) | collective-permute-done | bytes 524320 | tf_op jit(solution)/shard_map/ppermute | solution.py:966
  376.8 2.9 collective-permute-start.39
  379.7 7.5 %shard_map.354 = (bf16[512,2048]{1,0:T(8,128)(2,1)}, f32[512,1024]{1,0:T(8,128)}, f32[8,1,64]{2,1,0:T(1,128)S(1)}) custom-call(bf16[128,2048]{1,0:T(8,128)(2,1)S(1)} %get-tuple-element.232.b0, bf16[128,1024]{1,0:T(8,128)(2,1)S(1)} %collective-permute-done.32.b1, bf16[256,1024]{1,0:T(8,128)(2,1)S(1)} %collective-permute-done.33.b2, ...), custom_call_target="tpu_custom_call" | custom-call | flops 5000000000 | bytes 500000 | tf_op jit(solution)/shard_map/pallas_call | solution.py:591
  389.1 2.9 collective-permute-start.37
  393.6 5.3 shard_map.355
  398.9 5.2 collective-permute-done.38.d3
  407.9 3.3 collective-permute-start.42
  416.9 25.6 %shard_map.356 = (bf16[512,2688]{1,0:T(8,128)(2,1)}, f32[24,1024]{1,0:T(8,128)S(1)}) custom-call(s32[8,2]{1,0:T(8,128)S(1)} %copy-done.29, f32[512,2688]{1,0:T(8,128)} %get-tuple-element.193.gate_ref.proj_ref, f32[4,1280]{1,0:T(4,128)S(1)} %copy-done.25, f32[1,1280]{1,0:T(1,128)S(1)} %copy-done.27, f32[2,128]{1,0:T(2,128)S(1)} %copy-done.36, ...), custom_call_target="tpu_custom_call" | custom-call | flops 16999999488 | bytes 1700000 | tf_op jit(solution)/shard_map/pallas_call | solution.py:734
  442.6 11.2 %shard_map.357 = (bf16[1024,2688]{1,0:T(8,128)(2,1)}, bf16[1024,2688]{1,0:T(8,128)(2,1)}) custom-call(s32[32]{0:T(128)S(1)} %copy-done.37, bf16[512,2048]{1,0:T(8,128)(2,1)S(1)} %copy-done.74, bf16[512,2688]{1,0:T(8,128)(2,1)} %get-tuple-element.259.refs_1_.left_ref), custom_call_target="tpu_custom_call" | custom-call | flops 11000000512 | bytes 1100000 | tf_op jit(solution)/shard_map/pallas_call | solution.py:914
  462.6 9.9 %shard_map.358 = (f32[256,1024]{1,0:T(8,128)S(1)}, bf16[256,1024]{1,0:T(8,128)(2,1)S(1)}, f32[256,1024]{1,0:T(8,128)S(1)}, bf16[256,1024]{1,0:T(8,128)(2,1)S(1)}) custom-call(bf16[512,2688]{1,0:T(8,128)(2,1)} %get-tuple-element.259.refs_1_.left_ref, bf16[2048,2688]{1,0:T(8,128)(2,1)} %all-gather.4.cloned.1.call-done.weight_ref.gains_in_ref), custom_call_target="tpu_custom_call" | custom-call | flops 4000000000 | bytes 400000 | tf_op jit(solution)/shard_map/pallas_call | solution.py:394
  472.5 2.8 collective-permute-start.48
  475.4 4.2 collective-permute-done.46
  479.6 6.4 %shard_map.359 = (bf16[256,2688]{1,0:T(8,128)(2,1)S(1)}, bf16[256,2688]{1,0:T(8,128)(2,1)S(1)}, bf16[256,2688]{1,0:T(8,128)(2,1)}, bf16[128,2688]{1,0:T(8,128)(2,1)S(1)}, bf16[128,2688]{1,0:T(8,128)(2,1)S(1)}) custom-call(bf16[1024,2688]{1,0:T(8,128)(2,1)} %get-tuple-element.255.keep_ref, bf16[1024,2688]{1,0:T(8,128)(2,1)} %collective-permute-done.50.got_ref), custom_call_target="tpu_custom_call" | custom-call | flops 3000000000 | bytes 300000 | tf_op jit(solution)/shard_map/pallas_call | solution.py:786
  488.5 9.1 %collective-permute-done.48 = bf16[256,1024]{1,0:T(8,128)(2,1)S(1)} collective-permute-done((bf16[256,1024]{1,0:T(8,128)(2,1)S(1)}, bf16[256,1024]{1,0:T(8,128)(2,1)S(1)}, u32[]{:S(2)}, u32[]{:S(2)}) %collective-permute-start.48) | collective-permute-done | bytes 524320 | tf_op jit(solution)/shard_map/ppermute | solution.py:966
  497.5 4.0 collective-permute-done.49
  503.6 3.0 shard_map.360
  514.1 15.3 %collective-permute-done.53 = bf16[256,1024]{1,0:T(8,128)(2,1)S(1)} collective-permute-done((bf16[256,1024]{1,0:T(8,128)(2,1)S(1)}, bf16[256,1024]{1,0:T(8,128)(2,1)S(1)}, u32[]{:S(2)}, u32[]{:S(2)}) %collective-permute-start.53) | collective-permute-done | bytes 524320 | tf_op jit(solution)/shard_map/ppermute | solution.py:966
  531.1 5.8 collective-permute-done.55.by_x_ref
  539.2 3.5 shard_map.361
  556.8 6.4 %collective-permute-done.61 = f32[4,24,1024]{2,1,0:T(8,128)S(1)} collective-permute-done((f32[4,24,1024]{2,1,0:T(8,128)S(1)}, f32[4,24,1024]{2,1,0:T(8,128)S(1)}, u32[]{:S(2)}, u32[]{:S(2)}) %collective-permute-start.61) | collective-permute-done | bytes 393248 | tf_op jit(solution)/shard_map/ppermute | solution.py:966
  568.3 5.8 collective-permute-done.59.g3
  574.2 2.7 shard_map.366
  (487 shorter events, 156.9 us)
Async XLA Ops:
  7.2 120.5 %all-gather.4.cloned.1.call-start = ((), (), s32[]{:S(2)}) async-start(), calls=%async_computation.2 | async-start | bytes 12386304 | tf_op jit(solution)/shard_map/all_gather | solution.py:1092
  15.6 19.1 %collective-permute-start = (bf16[64,2688]{1,0:T(8,128)(2,1)}, bf16[64,2688]{1,0:T(8,128)(2,1)}, u32[]{:S(2)}, u32[]{:S(2)}) collective-permute-start(bf16[64,2688]{1,0:T(8,128)(2,1)} %concatenate.115), channel_id=1, source_target_pairs={{0,8},{8,0},{16,24},{24,16},{1,9},{9,1},{17,25},{25,17},{2,10},{10... | collective-permute-start | bytes 1032200 | tf_op jit(solution)/shard_map/ppermute | solution.py:966
  16.4 26.6 %collective-permute-start.1 = (bf16[64,2688]{1,0:T(8,128)(2,1)}, bf16[64,2688]{1,0:T(8,128)(2,1)}, u32[]{:S(2)}, u32[]{:S(2)}) collective-permute-start(bf16[64,2688]{1,0:T(8,128)(2,1)} %concatenate.116), channel_id=1, source_target_pairs={{0,16},{8,24},{16,0},{24,8},{1,17},{9,25},{17,1},{25,9},{2,18},{10... | collective-permute-start | bytes 1032200 | tf_op jit(solution)/shard_map/ppermute | solution.py:966
  20.3 32.4 %collective-permute-start.2 = (bf16[64,2688]{1,0:T(8,128)(2,1)}, bf16[64,2688]{1,0:T(8,128)(2,1)}, u32[]{:S(2)}, u32[]{:S(2)}) collective-permute-start(bf16[64,2688]{1,0:T(8,128)(2,1)} %concatenate.117), channel_id=1, source_target_pairs={{0,24},{8,16},{16,8},{24,0},{1,25},{9,17},{17,9},{25,1},{2,26},{10... | collective-permute-start | bytes 1032200 | tf_op jit(solution)/shard_map/ppermute | solution.py:966
  55.5 127.1 %all-gather.6.cloned.1.call-start = ((), (), s32[]{:S(2)}) async-start(), calls=%async_computation.3 | async-start | bytes 4718592 | tf_op jit(solution)/shard_map/all_gather | solution.py:1092
  63.6 35.5 %collective-permute-start.5 = (bf16[256,1024]{1,0:T(8,128)(2,1)}, bf16[256,1024]{1,0:T(8,128)(2,1)S(1)}, u32[]{:S(2)}, u32[]{:S(2)}) collective-permute-start(bf16[256,1024]{1,0:T(8,128)(2,1)} %pad_maximum_fusion.4), channel_id=1, source_target_pairs={{0,8},{8,0},{16,24},{24,16},{1,9},{9,1},{17,25},{25,17},{2,10},{10... | collective-permute-start | bytes 1572872 | tf_op jit(solution)/shard_map/ppermute | solution.py:966
  64.7 34.4 %collective-permute-start.6 = (bf16[256,1024]{1,0:T(8,128)(2,1)}, bf16[256,1024]{1,0:T(8,128)(2,1)}, u32[]{:S(2)}, u32[]{:S(2)}) collective-permute-start(bf16[256,1024]{1,0:T(8,128)(2,1)} %pad_maximum_fusion.5), channel_id=1, source_target_pairs={{0,24},{8,16},{16,8},{24,0},{1,25},{9,17},{17,9},{25,1},{2,26},{10... | collective-permute-start | bytes 1572872 | tf_op jit(solution)/shard_map/ppermute | solution.py:966
  66.4 28.7 %collective-permute-start.8 = (bf16[128,1024]{1,0:T(8,128)(2,1)S(1)}, bf16[128,1024]{1,0:T(8,128)(2,1)S(1)}, u32[]{:S(2)}, u32[]{:S(2)}) collective-permute-start(bf16[128,1024]{1,0:T(8,128)(2,1)S(1)} %get-tuple-element.357), channel_id=1, source_target_pairs={{0,8},{8,0},{16,24},{24,16},{1,9},{9,1},{17,25},{25,17},{2,10},{10... | collective-permute-start | bytes 786440 | tf_op jit(solution)/shard_map/ppermute | solution.py:966
  68.8 30.3 %collective-permute-start.7 = (bf16[128,1024]{1,0:T(8,128)(2,1)S(1)}, bf16[128,1024]{1,0:T(8,128)(2,1)S(1)}, u32[]{:S(2)}, u32[]{:S(2)}) collective-permute-start(bf16[128,1024]{1,0:T(8,128)(2,1)S(1)} %get-tuple-element.358), channel_id=1, source_target_pairs={{0,24},{8,16},{16,8},{24,0},{1,25},{9,17},{17,9},{25,1},{2,26},{10... | collective-permute-start | bytes 786440 | tf_op jit(solution)/shard_map/ppermute | solution.py:966
  111.1 151.8 %all-gather.8.cloned.1.call-start = ((), (), s32[]{:S(2)}) async-start(), calls=%async_computation.4 | async-start | bytes 14155776 | tf_op jit(solution)/shard_map/all_gather | solution.py:1092
  118.0 57.1 %collective-permute-start.25 = (bf16[64,3072]{1,0:T(8,128)(2,1)}, bf16[64,3072]{1,0:T(8,128)(2,1)}, u32[]{:S(2)}, u32[]{:S(2)}) collective-permute-start(bf16[64,3072]{1,0:T(8,128)(2,1)} %pad_maximum_fusion.18), channel_id=1, source_target_pairs={{0,8},{8,0},{16,24},{24,16},{1,9},{9,1},{17,25},{25,17},{2,10},{10... | collective-permute-start | bytes 1179656 | tf_op jit(solution)/shard_map/ppermute | solution.py:966
  118.9 57.7 %collective-permute-start.26 = (bf16[64,3072]{1,0:T(8,128)(2,1)}, bf16[64,3072]{1,0:T(8,128)(2,1)}, u32[]{:S(2)}, u32[]{:S(2)}) collective-permute-start(bf16[64,3072]{1,0:T(8,128)(2,1)} %pad_maximum_fusion.19), channel_id=1, source_target_pairs={{0,16},{8,24},{16,0},{24,8},{1,17},{9,25},{17,1},{25,9},{2,18},{10... | collective-permute-start | bytes 1179656 | tf_op jit(solution)/shard_map/ppermute | solution.py:966
  121.2 55.4 %collective-permute-start.27 = (bf16[64,3072]{1,0:T(8,128)(2,1)}, bf16[64,3072]{1,0:T(8,128)(2,1)}, u32[]{:S(2)}, u32[]{:S(2)}) collective-permute-start(bf16[64,3072]{1,0:T(8,128)(2,1)} %pad_maximum_fusion.20), channel_id=1, source_target_pairs={{0,24},{8,16},{16,8},{24,0},{1,25},{9,17},{17,9},{25,1},{2,26},{10... | collective-permute-start | bytes 1179656 | tf_op jit(solution)/shard_map/ppermute | solution.py:966
  123.3 49.7 %collective-permute-start.13 = (bf16[256,1024]{1,0:T(8,128)(2,1)}, bf16[256,1024]{1,0:T(8,128)(2,1)}, u32[]{:S(2)}, u32[]{:S(2)}) collective-permute-start(bf16[256,1024]{1,0:T(8,128)(2,1)} %pad_maximum_fusion.8), channel_id=1, source_target_pairs={{0,24},{8,16},{16,8},{24,0},{1,25},{9,17},{17,9},{25,1},{2,26},{10... | collective-permute-start | bytes 1572872 | tf_op jit(solution)/shard_map/ppermute | solution.py:966
  125.8 47.2 %collective-permute-start.12 = (bf16[256,1024]{1,0:T(8,128)(2,1)}, bf16[256,1024]{1,0:T(8,128)(2,1)}, u32[]{:S(2)}, u32[]{:S(2)}) collective-permute-start(bf16[256,1024]{1,0:T(8,128)(2,1)} %pad_maximum_fusion.7), channel_id=1, source_target_pairs={{0,8},{8,0},{16,24},{24,16},{1,9},{9,1},{17,25},{25,17},{2,10},{10... | collective-permute-start | bytes 1572872 | tf_op jit(solution)/shard_map/ppermute | solution.py:966
  182.5 223.4 %reduce-scatter.5.cloned.1.call-start = ((), (), s32[]{:S(2)}) async-start(), calls=%async_computation.6 | async-start | bytes 14155776 | tf_op jit(solution)/shard_map/reduce_scatter | solution.py:1095
  190.5 28.4 %collective-permute-start.19 = (bf16[256,1024]{1,0:T(8,128)(2,1)S(1)}, bf16[256,1024]{1,0:T(8,128)(2,1)S(1)}, u32[]{:S(2)}, u32[]{:S(2)}) collective-permute-start(bf16[256,1024]{1,0:T(8,128)(2,1)S(1)} %get-tuple-element.210), channel_id=1, source_target_pairs={{0,24},{8,16},{16,8},{24,0},{1,25},{9,17},{17,9},{25,1},{2,26},{10... | collective-permute-start | bytes 1572872 | tf_op jit(solution)/shard_map/ppermute | solution.py:966
  205.1 21.6 %collective-permute-start.18 = (bf16[128,1024]{1,0:T(8,128)(2,1)S(1)}, bf16[128,1024]{1,0:T(8,128)(2,1)S(1)}, u32[]{:S(2)}, u32[]{:S(2)}) collective-permute-start(bf16[128,1024]{1,0:T(8,128)(2,1)S(1)} %slice.367), channel_id=1, source_target_pairs={{0,24},{8,16},{16,8},{24,0},{1,25},{9,17},{17,9},{25,1},{2,26},{10... | collective-permute-start | bytes 786440 | tf_op jit(solution)/shard_map/ppermute | solution.py:966
  229.6 17.5 %collective-permute-start.21 = (bf16[128,1024]{1,0:T(8,128)(2,1)S(1)}, bf16[128,1024]{1,0:T(8,128)(2,1)S(1)}, u32[]{:S(2)}, u32[]{:S(2)}) collective-permute-start(bf16[128,1024]{1,0:T(8,128)(2,1)S(1)} %get-tuple-element.352), channel_id=1, source_target_pairs={{0,24},{8,16},{16,8},{24,0},{1,25},{9,17},{17,9},{25,1},{2,26},{10... | collective-permute-start | bytes 786440 | tf_op jit(solution)/shard_map/ppermute | solution.py:966
  294.9 162.3 %reduce-scatter.3.cloned.1.call-start = ((), (), s32[]{:S(2)}) async-start(), calls=%async_computation.5 | async-start | bytes 4718592 | tf_op jit(solution)/shard_map/reduce_scatter | solution.py:1095
  295.9 18.3 %collective-permute-start.28 = (bf16[256,1024]{1,0:T(8,128)(2,1)S(1)}, bf16[256,1024]{1,0:T(8,128)(2,1)S(1)}, u32[]{:S(2)}, u32[]{:S(2)}) collective-permute-start(bf16[256,1024]{1,0:T(8,128)(2,1)S(1)} %copy-done.43), channel_id=1, source_target_pairs={{0,8},{8,0},{16,24},{24,16},{1,9},{9,1},{17,25},{25,17},{2,10},{10... | collective-permute-start | bytes 1572872 | tf_op jit(solution)/shard_map/ppermute | solution.py:966
  299.2 20.4 %collective-permute-start.30 = (bf16[256,1024]{1,0:T(8,128)(2,1)S(1)}, bf16[256,1024]{1,0:T(8,128)(2,1)S(1)}, u32[]{:S(2)}, u32[]{:S(2)}) collective-permute-start(bf16[256,1024]{1,0:T(8,128)(2,1)S(1)} %get-tuple-element.224), channel_id=1, source_target_pairs={{0,24},{8,16},{16,8},{24,0},{1,25},{9,17},{17,9},{25,1},{2,26},{10... | collective-permute-start | bytes 1572872 | tf_op jit(solution)/shard_map/ppermute | solution.py:966
  314.4 17.0 %collective-permute-start.29 = (bf16[128,1024]{1,0:T(8,128)(2,1)S(1)}, bf16[128,1024]{1,0:T(8,128)(2,1)S(1)}, u32[]{:S(2)}, u32[]{:S(2)}) collective-permute-start(bf16[128,1024]{1,0:T(8,128)(2,1)S(1)} %slice.365), channel_id=1, source_target_pairs={{0,24},{8,16},{16,8},{24,0},{1,25},{9,17},{17,9},{25,1},{2,26},{10... | collective-permute-start | bytes 786440 | tf_op jit(solution)/shard_map/ppermute | solution.py:966
  333.6 15.9 %collective-permute-start.32 = (bf16[128,1024]{1,0:T(8,128)(2,1)S(1)}, bf16[128,1024]{1,0:T(8,128)(2,1)S(1)}, u32[]{:S(2)}, u32[]{:S(2)}) collective-permute-start(bf16[128,1024]{1,0:T(8,128)(2,1)S(1)} %get-tuple-element.350), channel_id=1, source_target_pairs={{0,24},{8,16},{16,8},{24,0},{1,25},{9,17},{17,9},{25,1},{2,26},{10... | collective-permute-start | bytes 786440 | tf_op jit(solution)/shard_map/ppermute | solution.py:966
  335.3 15.5 %collective-permute-start.34 = (bf16[128,1024]{1,0:T(8,128)(2,1)S(1)}, bf16[128,1024]{1,0:T(8,128)(2,1)S(1)}, u32[]{:S(2)}, u32[]{:S(2)}) collective-permute-start(bf16[128,1024]{1,0:T(8,128)(2,1)S(1)} %get-tuple-element.349), channel_id=1, source_target_pairs={{0,8},{8,0},{16,24},{24,16},{1,9},{9,1},{17,25},{25,17},{2,10},{10... | collective-permute-start | bytes 786440 | tf_op jit(solution)/shard_map/ppermute | solution.py:966
  350.9 26.0 %collective-permute-start.35 = (bf16[256,1024]{1,0:T(8,128)(2,1)S(1)}, bf16[256,1024]{1,0:T(8,128)(2,1)S(1)}, u32[]{:S(2)}, u32[]{:S(2)}) collective-permute-start(bf16[256,1024]{1,0:T(8,128)(2,1)S(1)} %pad_maximum_fusion.14), channel_id=1, source_target_pairs={{0,24},{8,16},{16,8},{24,0},{1,25},{9,17},{17,9},{25,1},{2,26},{10... | collective-permute-start | bytes 1572872 | tf_op jit(solution)/shard_map/ppermute | solution.py:966
  376.8 29.1 %collective-permute-start.39 = (bf16[256,1024]{1,0:T(8,128)(2,1)}, bf16[256,1024]{1,0:T(8,128)(2,1)}, u32[]{:S(2)}, u32[]{:S(2)}) collective-permute-start(bf16[256,1024]{1,0:T(8,128)(2,1)} %get-tuple-element.242), channel_id=1, source_target_pairs={{0,8},{8,0},{16,24},{24,16},{1,9},{9,1},{17,25},{25,17},{2,10},{10... | collective-permute-start | bytes 1572872 | tf_op jit(solution)/shard_map/ppermute | solution.py:966
  379.7 26.2 %collective-permute-start.40 = (bf16[256,1024]{1,0:T(8,128)(2,1)}, bf16[256,1024]{1,0:T(8,128)(2,1)}, u32[]{:S(2)}, u32[]{:S(2)}) collective-permute-start(bf16[256,1024]{1,0:T(8,128)(2,1)} %get-tuple-element.243), channel_id=1, source_target_pairs={{0,24},{8,16},{16,8},{24,0},{1,25},{9,17},{17,9},{25,1},{2,26},{10... | collective-permute-start | bytes 1572872 | tf_op jit(solution)/shard_map/ppermute | solution.py:966
  387.2 16.9 %collective-permute-start.38 = (f32[8,1,64]{2,1,0:T(1,128)S(1)}, f32[8,1,64]{2,1,0:T(1,128)S(1)}, u32[]{:S(2)}, u32[]{:S(2)}) collective-permute-start(f32[8,1,64]{2,1,0:T(1,128)S(1)} %get-tuple-element.244.d0), channel_id=1, source_target_pairs={{0,24},{8,16},{16,8},{24,0},{1,25},{9,17},{17,9},{25,1},{2,26},{10... | collective-permute-start | bytes 6152 | tf_op jit(solution)/shard_map/ppermute | solution.py:966
  389.1 15.6 %collective-permute-start.37 = (f32[8,1,64]{2,1,0:T(1,128)S(1)}, f32[8,1,64]{2,1,0:T(1,128)S(1)}, u32[]{:S(2)}, u32[]{:S(2)}) collective-permute-start(f32[8,1,64]{2,1,0:T(1,128)S(1)} %get-tuple-element.244.d0), channel_id=1, source_target_pairs={{0,16},{8,24},{16,0},{24,8},{1,17},{9,25},{17,1},{25,9},{2,18},{10... | collective-permute-start | bytes 6152 | tf_op jit(solution)/shard_map/ppermute | solution.py:966
  407.8 34.8 %collective-permute-start.43 = (bf16[64,3072]{1,0:T(8,128)(2,1)S(1)}, bf16[64,3072]{1,0:T(8,128)(2,1)S(1)}, u32[]{:S(2)}, u32[]{:S(2)}) collective-permute-start(bf16[64,3072]{1,0:T(8,128)(2,1)S(1)} %get-tuple-element.317), channel_id=1, source_target_pairs={{0,24},{8,16},{16,8},{24,0},{1,25},{9,17},{17,9},{25,1},{2,26},{10... | collective-permute-start | bytes 1179656 | tf_op jit(solution)/shard_map/ppermute | solution.py:966
  407.9 34.7 %collective-permute-start.42 = (bf16[64,3072]{1,0:T(8,128)(2,1)S(1)}, bf16[64,3072]{1,0:T(8,128)(2,1)S(1)}, u32[]{:S(2)}, u32[]{:S(2)}) collective-permute-start(bf16[64,3072]{1,0:T(8,128)(2,1)S(1)} %get-tuple-element.318), channel_id=1, source_target_pairs={{0,16},{8,24},{16,0},{24,8},{1,17},{9,25},{17,1},{25,9},{2,18},{10... | collective-permute-start | bytes 1179656 | tf_op jit(solution)/shard_map/ppermute | solution.py:966
  411.1 31.4 %collective-permute-start.41 = (bf16[64,3072]{1,0:T(8,128)(2,1)S(1)}, bf16[64,3072]{1,0:T(8,128)(2,1)S(1)}, u32[]{:S(2)}, u32[]{:S(2)}) collective-permute-start(bf16[64,3072]{1,0:T(8,128)(2,1)S(1)} %get-tuple-element.319), channel_id=1, source_target_pairs={{0,8},{8,0},{16,24},{24,16},{1,9},{9,1},{17,25},{25,17},{2,10},{10... | collective-permute-start | bytes 1179656 | tf_op jit(solution)/shard_map/ppermute | solution.py:966
  453.8 25.8 %collective-permute-start.50 = (bf16[1024,2688]{1,0:T(8,128)(2,1)}, bf16[1024,2688]{1,0:T(8,128)(2,1)}, u32[]{:S(2)}, u32[]{:S(2)}) collective-permute-start(bf16[1024,2688]{1,0:T(8,128)(2,1)} %get-tuple-element.256), channel_id=1, source_target_pairs={{0,1},{1,0},{2,3},{3,2},{4,5},{5,4},{6,7},{7,6},{8,9},{9,8},{10,11... | collective-permute-start | bytes 16515080 | tf_op jit(solution)/shard_map/ppermute | solution.py:966
  459.0 16.3 %collective-permute-start.44 = (bf16[88,1024]{1,0:T(8,128)(2,1)S(1)}, bf16[88,1024]{1,0:T(8,128)(2,1)S(1)}, u32[]{:S(2)}, u32[]{:S(2)}) collective-permute-start(bf16[88,1024]{1,0:T(8,128)(2,1)S(1)} %get-tuple-element.396), channel_id=1, source_target_pairs={{0,8},{8,0},{16,24},{24,16},{1,9},{9,1},{17,25},{25,17},{2,10},{10... | collective-permute-start | bytes 540680 | tf_op jit(solution)/shard_map/ppermute | solution.py:966
  460.9 18.6 %collective-permute-start.46 = (bf16[88,1024]{1,0:T(8,128)(2,1)S(1)}, bf16[88,1024]{1,0:T(8,128)(2,1)S(1)}, u32[]{:S(2)}, u32[]{:S(2)}) collective-permute-start(bf16[88,1024]{1,0:T(8,128)(2,1)S(1)} %get-tuple-element.398), channel_id=1, source_target_pairs={{0,24},{8,16},{16,8},{24,0},{1,25},{9,17},{17,9},{25,1},{2,26},{10... | collective-permute-start | bytes 540680 | tf_op jit(solution)/shard_map/ppermute | solution.py:966
  472.5 25.0 %collective-permute-start.48 = (bf16[256,1024]{1,0:T(8,128)(2,1)S(1)}, bf16[256,1024]{1,0:T(8,128)(2,1)S(1)}, u32[]{:S(2)}, u32[]{:S(2)}) collective-permute-start(bf16[256,1024]{1,0:T(8,128)(2,1)S(1)} %get-tuple-element.261), channel_id=1, source_target_pairs={{0,8},{8,0},{16,24},{24,16},{1,9},{9,1},{17,25},{25,17},{2,10},{10... | collective-permute-start | bytes 1572872 | tf_op jit(solution)/shard_map/ppermute | solution.py:966
  475.3 26.2 %collective-permute-start.49 = (bf16[256,1024]{1,0:T(8,128)(2,1)S(1)}, bf16[256,1024]{1,0:T(8,128)(2,1)S(1)}, u32[]{:S(2)}, u32[]{:S(2)}) collective-permute-start(bf16[256,1024]{1,0:T(8,128)(2,1)S(1)} %get-tuple-element.262), channel_id=1, source_target_pairs={{0,24},{8,16},{16,8},{24,0},{1,25},{9,17},{17,9},{25,1},{2,26},{10... | collective-permute-start | bytes 1572872 | tf_op jit(solution)/shard_map/ppermute | solution.py:966
  486.1 16.3 %collective-permute-start.51 = (bf16[128,2688]{1,0:T(8,128)(2,1)S(1)}, bf16[128,2688]{1,0:T(8,128)(2,1)S(1)}, u32[]{:S(2)}, u32[]{:S(2)}) collective-permute-start(bf16[128,2688]{1,0:T(8,128)(2,1)S(1)} %get-tuple-element.265), channel_id=1, source_target_pairs={{0,4},{4,0},{1,5},{5,1},{2,6},{6,2},{3,7},{7,3},{8,12},{12,8},{9,1... | collective-permute-start | bytes 2064392 | tf_op jit(solution)/shard_map/ppermute | solution.py:966
  487.5 16.0 %collective-permute-start.52 = (bf16[128,2688]{1,0:T(8,128)(2,1)S(1)}, bf16[128,2688]{1,0:T(8,128)(2,1)S(1)}, u32[]{:S(2)}, u32[]{:S(2)}) collective-permute-start(bf16[128,2688]{1,0:T(8,128)(2,1)S(1)} %get-tuple-element.266), channel_id=1, source_target_pairs={{0,2},{2,0},{1,3},{3,1},{4,6},{6,4},{5,7},{7,5},{8,10},{10,8},{9,1... | collective-permute-start | bytes 2064392 | tf_op jit(solution)/shard_map/ppermute | solution.py:966
  488.5 23.7 %collective-permute-start.47 = (f32[4,24,1024]{2,1,0:T(8,128)}, f32[4,24,1024]{2,1,0:T(8,128)}, u32[]{:S(2)}, u32[]{:S(2)}) collective-permute-start(f32[4,24,1024]{2,1,0:T(8,128)} %pad_maximum_fusion.22), channel_id=1, source_target_pairs={{0,1},{1,0},{2,3},{3,2},{4,5},{5,4},{6,7},{7,6},{8,9},{9,8},{10,11... | collective-permute-start | bytes 1179656 | tf_op jit(solution)/shard_map/ppermute | solution.py:966
  506.5 30.4 %collective-permute-start.55 = (bf16[256,2688]{1,0:T(8,128)(2,1)S(1)}, bf16[256,2688]{1,0:T(8,128)(2,1)S(1)}, u32[]{:S(2)}, u32[]{:S(2)}) collective-permute-start(bf16[256,2688]{1,0:T(8,128)(2,1)S(1)} %get-tuple-element.276), channel_id=1, source_target_pairs={{0,4},{4,0},{1,5},{5,1},{2,6},{6,2},{3,7},{7,3},{8,12},{12,8},{9,1... | collective-permute-start | bytes 4128776 | tf_op jit(solution)/shard_map/ppermute | solution.py:966
  507.2 30.9 %collective-permute-start.56 = (bf16[256,2688]{1,0:T(8,128)(2,1)S(1)}, bf16[256,2688]{1,0:T(8,128)(2,1)S(1)}, u32[]{:S(2)}, u32[]{:S(2)}) collective-permute-start(bf16[256,2688]{1,0:T(8,128)(2,1)S(1)} %get-tuple-element.277), channel_id=1, source_target_pairs={{0,2},{2,0},{1,3},{3,1},{4,6},{6,4},{5,7},{7,5},{8,10},{10,8},{9,1... | collective-permute-start | bytes 4128776 | tf_op jit(solution)/shard_map/ppermute | solution.py:966
  508.2 21.1 %collective-permute-start.53 = (bf16[256,1024]{1,0:T(8,128)(2,1)S(1)}, bf16[256,1024]{1,0:T(8,128)(2,1)S(1)}, u32[]{:S(2)}, u32[]{:S(2)}) collective-permute-start(bf16[256,1024]{1,0:T(8,128)(2,1)S(1)} %pad_maximum_fusion.15), channel_id=1, source_target_pairs={{0,24},{8,16},{16,8},{24,0},{1,25},{9,17},{17,9},{25,1},{2,26},{10... | collective-permute-start | bytes 1572872 | tf_op jit(solution)/shard_map/ppermute | solution.py:966
  509.2 21.1 %collective-permute-start.54 = (bf16[256,1024]{1,0:T(8,128)(2,1)S(1)}, bf16[256,1024]{1,0:T(8,128)(2,1)S(1)}, u32[]{:S(2)}, u32[]{:S(2)}) collective-permute-start(bf16[256,1024]{1,0:T(8,128)(2,1)S(1)} %pad_maximum_fusion.16), channel_id=1, source_target_pairs={{0,8},{8,0},{16,24},{24,16},{1,9},{9,1},{17,25},{25,17},{2,10},{10... | collective-permute-start | bytes 1572872 | tf_op jit(solution)/shard_map/ppermute | solution.py:966
  542.6 23.9 %collective-permute-start.57 = (bf16[64,2688]{1,0:T(8,128)(2,1)}, bf16[64,2688]{1,0:T(8,128)(2,1)}, u32[]{:S(2)}, u32[]{:S(2)}) collective-permute-start(bf16[64,2688]{1,0:T(8,128)(2,1)} %get-tuple-element.281), channel_id=1, source_target_pairs={{0,8},{8,0},{16,24},{24,16},{1,9},{9,1},{17,25},{25,17},{2,10},{10... | collective-permute-start | bytes 1032200 | tf_op jit(solution)/shard_map/ppermute | solution.py:966
  542.6 25.6 %collective-permute-start.58 = (bf16[64,2688]{1,0:T(8,128)(2,1)}, bf16[64,2688]{1,0:T(8,128)(2,1)}, u32[]{:S(2)}, u32[]{:S(2)}) collective-permute-start(bf16[64,2688]{1,0:T(8,128)(2,1)} %get-tuple-element.282), channel_id=1, source_target_pairs={{0,16},{8,24},{16,0},{24,8},{1,17},{9,25},{17,1},{25,9},{2,18},{10... | collective-permute-start | bytes 1032200 | tf_op jit(solution)/shard_map/ppermute | solution.py:966
  544.7 29.4 %collective-permute-start.59 = (bf16[64,2688]{1,0:T(8,128)(2,1)}, bf16[64,2688]{1,0:T(8,128)(2,1)}, u32[]{:S(2)}, u32[]{:S(2)}) collective-permute-start(bf16[64,2688]{1,0:T(8,128)(2,1)} %get-tuple-element.283), channel_id=1, source_target_pairs={{0,24},{8,16},{16,8},{24,0},{1,25},{9,17},{17,9},{25,1},{2,26},{10... | collective-permute-start | bytes 1032200 | tf_op jit(solution)/shard_map/ppermute | solution.py:966
  (137 other events, 2309.4 us)
Sparse Core Ops, SparseCore 0:
  55.6 65.6 all-gather.3
  123.7 36.9 all-gather.5
  182.7 72.6 all-gather.7
  295.0 93.3 reduce-scatter.4
  399.0 50.8 reduce-scatter.2

commit v5 on v4

--- a/solution.py
+++ b/solution.py
@@ -11,6 +11,7 @@
 
 HD = 128
 TP = 4
+PAD = 128
 
 epsilon = 1e-05
 rope_base = 100000000000.0
@@ -80,6 +81,16 @@
 
 def head_sums(values, spread):
     return mm(values, spread, NT)
+
+
+def parameters(ref, inner):
+    values = ref[...]
+    last = values.shape[0] - 1
+    steps = jnp.concatenate([values[last:, :PAD], values[last:, PAD : 2 * PAD]], axis=0)
+    return (
+        values[: last - 3], values[last - 3 : last - 2], steps,
+        values[last - 2 : last - 1, :inner], values[last - 1 : last, :inner],
+    )
 
 
 def mamba_shared(proj, start, count, taps_ref, bias_ref, steps_ref, inner, state, heads):
@@ -252,8 +263,8 @@
 
 
 def inner_kernel(
-    inner, state, heads, tiles, slots_ref, p0, p1, p2, p3, p4, weight_ref, gains_in_ref, taps_ref, bias_ref,
-    steps_ref, skip_ref, turn_ref, normed_ref, proj_ref, y_ref, square_ref, mixed_ref, gains_ref,
+    inner, state, heads, tiles, slots_ref, p0, p1, p2, p3, p4, weight_ref, gains_in_ref, params_ref,
+    turn_ref, normed_ref, proj_ref, y_ref, square_ref, mixed_ref, gains_ref,
 ):
     step = pl.program_id(0)
     tile = weight_ref.shape[1]
@@ -280,19 +291,20 @@
         proj = proj_ref[pl.ds(pl.multiple_of(seq * length, length), length), :]
         start = slots_ref[seq, 1]
         count = slots_ref[seq, 0]
-        m = mamba_shared(proj, start, count, taps_ref, bias_ref, steps_ref, inner, state, heads)
+        taps, bias, steps, skip, _ = parameters(params_ref, inner)
+        m = mamba_shared(proj, start, count, taps, bias, steps, inner, state, heads)
         scaled = m["xs"] * m["step_x"]
         wide = 2 * length
         parts = [
             mm(m["mixing"][:, c : c + wide], two_blocks(scaled[:, c : c + wide]), NN)
             for c in range(0, inner, wide)
         ]
-        y = jnp.concatenate(parts, axis=1) + skip_ref[...] * m["xs"]
+        y = jnp.concatenate(parts, axis=1) + skip * m["xs"]
         y_ref[...] = y
         gate = proj[:, :inner]
         gated = y * gate * jax.nn.sigmoid(gate)
         square_ref[0] = as_row(jnp.sum(gated * gated, axis=1, keepdims=True))
-        at = 2 * inner + 2 * state + steps_ref.shape[1]
+        at = 2 * inner + 2 * state + PAD
         _, _, values, probs = attention_shared(
             proj, at, start, count, turn_ref[:, :HD], turn_ref[:, HD:]
         )
@@ -302,14 +314,14 @@
         ).astype(mixed_ref.dtype)
 
 
-def mixer_inner(slots, rows, weight, taps, bias, steps, skip, turns, inner, state, heads, tile=384):
+def mixer_inner(slots, rows, weight, params, turns, inner, state, heads, tile=384):
     model, cols = weight.shape
     seqs = slots.shape[0]
     pieces = rows
     rows = TP * pieces[0].shape[0]
     length = rows // seqs
     tiles = cols // tile
-    pad = steps.shape[1]
+    pad = PAD
     at_steps = (2 * inner + 2 * state) // pad
     q_cols = cols - 2 * inner - 2 * state - pad - 2 * HD
 
@@ -326,7 +338,7 @@
             pl.BlockSpec((model, tile), lambda j: (0, jnp.minimum(j, tiles - 1))),
             pl.BlockSpec((model, pad), lambda j: (0, at_steps)),
         ]
-        + specs(taps.shape, bias.shape, steps.shape, skip.shape)
+        + specs(params.shape)
         + [seq_spec(length, turns.shape[1])],
         out_specs=specs((rows, model), (rows, cols))
         + [seq_spec(length, inner), seq_spec(1, 1, length), seq_spec(length, q_cols)]
@@ -341,7 +353,7 @@
         ],
         compiler_params=big,
         cost_estimate=costs(18),
-    )(slots, *pieces, weight, weight, taps, bias, steps, skip, turns)
+    )(slots, *pieces, weight, weight, params, turns)
 
 
 def outer_kernel(inner, gate_ref, y_ref, mixed_ref, gain_ref, s0, s1, s2, s3, weight_ref, branches_ref, root_ref, *halves):
@@ -615,8 +627,7 @@
 
 
 def backward_kernel(
-    inner, state, heads, slots_ref, proj_ref, taps_ref, bias_ref, steps_ref, skip_ref, turn_ref,
-    gain_ref, y_ref, grad_ref, root_ref, d0, d1, d2, d3, proj_grad_ref, small_ref,
+    inner, state, heads, slots_ref, proj_ref, params_ref, turn_ref, y_ref, grad_ref, root_ref, d0, d1, d2, d3, proj_grad_ref, small_ref,
 ):
     step_id = pl.program_id(0)
     start = slots_ref[step_id, 1]
@@ -624,8 +635,9 @@
     proj = proj_ref[...]
     length = proj.shape[0]
     conv_cols = inner + 2 * state
-    pad = steps_ref.shape[1]
-    m = mamba_shared(proj, start, count, taps_ref, bias_ref, steps_ref, inner, state, heads)
+    pad = PAD
+    taps, bias, steps, skip, gain = parameters(params_ref, inner)
+    m = mamba_shared(proj, start, count, taps, bias, steps, inner, state, heads)
     xs, decay, mixing = m["xs"], m["decay"], m["mixing"]
     scaled = xs * m["step_x"]
     gate = proj[:, :inner]
@@ -635,7 +647,7 @@
     mean = as_column(sum(ref[0] for ref in (d0, d1, d2, d3))) / (TP * inner)
     gated = y * gate * gate_sig
     d_norm = grad_ref[:, :inner]
-    d_gated = root * (d_norm * gain_ref[...]) - gated * (root * root * root * mean)
+    d_gated = root * (d_norm * gain) - gated * (root * root * root * mean)
     dy = d_gated * gate * gate_sig
     d_gate = d_gated * y * gate_sig * (1.0 + gate * (1.0 - gate_sig))
     wide = 2 * length
@@ -648,7 +660,7 @@
         d_mix.append(mm(dy_pair, two_blocks(scaled[:, c : c + wide]), NT))
     back = jnp.concatenate(back, axis=1)
     d_mix = jnp.concatenate(d_mix, axis=1)
-    d_xs = skip_ref[...] * dy + m["step_x"] * back
+    d_xs = skip * dy + m["step_x"] * back
     flow = d_mix * mixing
     flow = flow - jnp.where(m["diagonal"], jnp.sum(flow, axis=0, keepdims=True), 0.0)
     d_cum = head_sums(flow, m["spread"])
@@ -665,12 +677,12 @@
     d_active = jnp.concatenate([d_xs, d_b, d_c], axis=1)
     sig, conv = m["sig"], m["conv"]
     d_conv = d_active * sig * (1.0 + conv * (1.0 - sig))
-    kernel = taps_ref.shape[0]
+    kernel = taps.shape[0]
     d_in = jnp.zeros_like(d_conv)
     conv_rows = []
     for tap in range(kernel):
         back_by = kernel - 1 - tap
-        d_in = d_in + taps_ref[tap : tap + 1, :] * up_rows(d_conv, back_by)
+        d_in = d_in + taps[tap : tap + 1, :] * up_rows(d_conv, back_by)
         conv_rows.append(jnp.sum(d_conv * down_rows(m["conv_in"], back_by), axis=0, keepdims=True))
     conv_rows.append(jnp.sum(d_conv, axis=0, keepdims=True))
     conv_rows.append(jnp.zeros((8 - kernel - 1, conv_cols), f32))
@@ -723,21 +735,20 @@
 
 
 def mixer_backward(
-    slots, proj, taps, bias, steps, skip, turns, gain, y, grads, root, dots, inner, state, heads
+    slots, proj, params, turns, y, grads, root, dots, inner, state, heads
 ):
     seqs = slots.shape[0]
     rows, cols = proj.shape
     length = rows // seqs
     conv_cols = inner + 2 * state
-    pad = steps.shape[1]
+    pad = PAD
     small_shape = (8 * pl.cdiv(conv_cols + inner + pad, grads.shape[1]), grads.shape[1])
     return pl.pallas_call(
         functools.partial(backward_kernel, inner, state, heads),
         grid=(seqs,),
         in_specs=[pl.BlockSpec(memory_space=pltpu.SMEM), rows_spec(length, cols)]
-        + specs(taps.shape, bias.shape, steps.shape, skip.shape)
+        + specs(params.shape)
         + [rows_spec(length, turns.shape[1])]
-        + specs(gain.shape)
         + [rows_spec(length, inner), rows_spec(length, grads.shape[1])]
         + [pl.BlockSpec((1, 1, length), lambda i: (i, 0, 0))]
         + [their_spec(length, seqs // TP, k) for k in range(TP)],
@@ -748,7 +759,7 @@
         ],
         compiler_params=big,
         cost_estimate=costs(17),
-    )(slots, proj, taps, bias, steps, skip, turns, gain, y, grads, root, *dots)
+    )(slots, proj, params, turns, y, grads, root, *dots)
 
 
 def chip_kernel(keep_ref, got_ref, mine_ref, along_y_ref, along_x_ref, across_x_ref, across_y_ref):
@@ -1114,6 +1125,13 @@
     gain_t = own(mamba_gain, inner_t)[None]
     sizes = (inner_t, state, heads_t)
 
+    def widened(values):
+        return jnp.pad(values, ((0, 0), (0, conv_cols - values.shape[1])))
+
+    params = jnp.concatenate(
+        [taps_t, bias_t, widened(skip_t), widened(gain_t), widened(steps_t.reshape(1, -1))], axis=0
+    )
+
     in_slices = slices(in_slice)
     in_parts = exchange(in_slices)
     tokens, cotangent = after((tokens, cotangent), in_slices)
@@ -1121,11 +1139,11 @@
     upstream = order(cotangent.reshape(rows, model))
     prepared = (
         source, upstream, slices(out_slice), slices(mlp_slice),
-        taps_t, bias_t, steps_t, skip_t, gain_t, in_plane, in_group,
+        params, gain_t, in_plane, in_group,
     )
     in_parts, prepared = lax.optimization_barrier((in_parts, prepared))
     source, upstream, out_slices, mlp_slices = prepared[:4]
-    taps_t, bias_t, steps_t, skip_t, gain_t, in_plane, in_group = prepared[4:]
+    params, gain_t, in_plane, in_group = prepared[4:]
     w_in = gather(in_parts)
     source_some, upstream_some = spread_first(source), spread_first(upstream)
     column = inner_t + 2 * state + inner_t + heads_t + 2
@@ -1141,7 +1159,7 @@
     upstream_all = spread_second(upstream, *upstream_some)
 
     normed, projected, y, squares, mixed, gains = mixer_inner(
-        slots, after(source_all, out_parts[1:]), w_in, taps_t, bias_t, steps_t, skip_t, turns, *sizes
+        slots, after(source_all, (out_parts[1:], mlp_parts[1])), w_in, params, turns, *sizes
     )
     squares = everywhere(after(squares, upstream_all))
     w_mlp = gather(after(mlp_parts, squares[1:]))
@@ -1169,8 +1187,7 @@
     out_sums = scatter(out_sums[0])
     mlp_grads = pass_on(after(mlp_sums, dots))
     proj_grad, small = mixer_backward(
-        slots, projected, taps_t, bias_t, steps_t, skip_t, turns, gain_t, y, d_branches, root,
-        dots, *sizes,
+        slots, projected, params, turns, y, d_branches, root, dots, *sizes,
     )
     in_sums = weight_grads(
         in_plane if cube else in_group,
@@ -1198,6 +1215,7 @@
             along_kernel, (block, block), along_y, along_x, *across
         )
         in_parts = swap(to_x, 1, "x"), swap(to_y, 1, "y")
+    last_pair = after(last_pair, norm_pair)
     norm_parts, last_parts = pair_finish(norm_halves, last_halves, norm_pair, last_pair)
     out_grads = [out_sums[0]] + [r[:shard] for r in received]
     small = absolute([small] + [r[shard:].astype(f32) for r in received])

time: 593 us -> 587 us (0.990)
    unnamed x229 -> x201, local copies, waits for them, and re-layouts: 19.9 us -> 17.2 us
  transfers between devices with their start and end apart: 67 -> 67, of which waited for: 40 -> 42; matrix products, arithmetic and copies ran while one was open for 9% -> 9% of each run, Pallas kernels for 20% -> 21%
where the time goes in v5:
time: 587 us; the launch traced here: 580 us
  waiting for transfers between devices  253 us (43%)
  Pallas kernels  154 us (26%)
  starting transfers between devices  74.7 us (13%)
  local copies, waits for them, and re-layouts  50.2 us (9%)
  other arithmetic  31.6 us (5%)
  between operations  15.6 us (3%)
    ppermute x62, waiting for transfers between devices, swap(): return lax.ppermute(values, axis, [(i, i ^ k) for i in range(size)])  253 us
    ppermute x62, starting transfers between devices, swap(): return lax.ppermute(values, axis, [(i, i ^ k) for i in range(size)])  74.3 us
    pallas_call x1, Pallas kernels, feed_forward(): pl.pallas_call(functools.partial(feed_kernel, steps, table.shape[0]), gri...  29 us
    pallas_call x1, Pallas kernels, mixer_inner(): pl.pallas_call(functools.partial(inner_kernel, inner, state, heads, tiles...  26.9 us
    pallas_call x1, Pallas kernels, mixer_backward(): pl.pallas_call(functools.partial(backward_kernel, inner, state, heads), g...  25.5 us
    unnamed x201, local copies, waits for them, and re-layouts  17.2 us
    pallas_call x2, Pallas kernels, back_out(): pl.pallas_call(back_out_kernel, grid=(model // tile,), in_specs=specs(lef...  16.7 us
    pallas_call x2, Pallas kernels, weight_grads(): pl.pallas_call(functools.partial(weight_grad_kernel, tuple(bounds), mine,...  16.5 us
  transfers between devices with their start and end apart: 67, of which 42 were waited for; matrix products, arithmetic and copies ran while one was open for 9% of the time, Pallas kernels for 21%

profile of v5, /device:TPU:8, one launch (start us, length us, event | category | flops | bytes accessed | tf_op | source)
XLA Modules:
  0.0 579.5 jit_solution(1707269826897247231)
XLA Ops:
  16.4 3.0 collective-permute-start.1
  35.2 7.8 %collective-permute-done.1 = bf16[64,2688]{1,0:T(8,128)(2,1)} collective-permute-done((bf16[64,2688]{1,0:T(8,128)(2,1)}, bf16[64,2688]{1,0:T(8,128)(2,1)}, u32[]{:S(2)}, u32[]{:S(2)}) %collective-permute-start.1) | collective-permute-done | bytes 344096 | tf_op jit(solution)/shard_map/ppermute | solution.py:977
  43.0 9.7 %collective-permute-done.2 = bf16[64,2688]{1,0:T(8,128)(2,1)} collective-permute-done((bf16[64,2688]{1,0:T(8,128)(2,1)}, bf16[64,2688]{1,0:T(8,128)(2,1)}, u32[]{:S(2)}, u32[]{:S(2)}) %collective-permute-start.2) | collective-permute-done | bytes 344096 | tf_op jit(solution)/shard_map/ppermute | solution.py:977
  57.5 5.3 collective-permute-done.3.p1
  69.8 25.3 %collective-permute-done.8.c3 = bf16[128,1024]{1,0:T(8,128)(2,1)S(1)} collective-permute-done((bf16[128,1024]{1,0:T(8,128)(2,1)S(1)}, bf16[128,1024]{1,0:T(8,128)(2,1)S(1)}, u32[]{:S(2)}, u32[]{:S(2)}) %collective-permute-start.8) | collective-permute-done | bytes 262176 | tf_op jit(solution)/shard_map/ppermute | solution.py:977
  95.2 4.0 collective-permute-done.7.c1
  104.4 3.6 collective-permute-done.10
  130.3 26.9 %shard_map.348 = (bf16[512,2048]{1,0:T(8,128)(2,1)}, f32[512,2688]{1,0:T(8,128)}, f32[512,768]{1,0:T(8,128)}, f32[8,1,64]{2,1,0:T(1,128)S(1)}, bf16[512,256]{1,0:T(8,128)(2,1)S(1)}, /*index=5*/f32[8,2048]{1,0:T(8,128)S(1)}) custom-call(s32[8,2]{1,0:T(8,128)S(1)} %copy.127.slots_ref, bf16[128,2048]{1,0:T(8,128)(2,1)S(1)} %copy.119.p0, ...), custom_call_target="tpu_custom_call" | custom-call | flops 17999998976 | bytes 1800000 | tf_op jit(solution)/shard_map/pallas_call | solution.py:332
  157.2 14.3 %collective-permute-done.14.c4 = bf16[256,1024]{1,0:T(8,128)(2,1)} collective-permute-done((bf16[256,1024]{1,0:T(8,128)(2,1)}, bf16[256,1024]{1,0:T(8,128)(2,1)}, u32[]{:S(2)}, u32[]{:S(2)}) %collective-permute-start.14) | collective-permute-done | bytes 524320 | tf_op jit(solution)/shard_map/ppermute | solution.py:977
  175.2 2.9 collective-permute-done.16.s2
  181.1 7.4 %shard_map.349 = (bf16[512,1024]{1,0:T(8,128)(2,1)S(1)}, f32[8,1,64]{2,1,0:T(1,128)S(1)}, f32[256,1024]{1,0:T(8,128)S(1)}, bf16[256,1024]{1,0:T(8,128)(2,1)S(1)}...) custom-call(f32[512,2688]{1,0:T(8,128)} %get-tuple-element.194.gate_ref.proj_ref, ...), custom_call_target="tpu_custom_call" | custom-call | flops 4000000000 | bytes 400000 | tf_op jit(solution)/shard_map/pallas_call | solution.py:379
  191.0 12.3 %collective-permute-done.18 = bf16[256,1024]{1,0:T(8,128)(2,1)S(1)} collective-permute-done((bf16[256,1024]{1,0:T(8,128)(2,1)S(1)}, bf16[256,1024]{1,0:T(8,128)(2,1)S(1)}, u32[]{:S(2)}, u32[]{:S(2)}) %collective-permute-start.18) | collective-permute-done | bytes 524320 | tf_op jit(solution)/shard_map/ppermute | solution.py:977
  204.2 14.0 %collective-permute-done.20 = bf16[256,1024]{1,0:T(8,128)(2,1)S(1)} collective-permute-done((bf16[256,1024]{1,0:T(8,128)(2,1)S(1)}, bf16[256,1024]{1,0:T(8,128)(2,1)S(1)}, u32[]{:S(2)}, u32[]{:S(2)}) %collective-permute-start.20) | collective-permute-done | bytes 524320 | tf_op jit(solution)/shard_map/ppermute | solution.py:977
  218.6 5.8 collective-permute-done.19.k1
  224.4 3.3 collective-permute-done.21.k3
  230.7 3.4 collective-permute-start.24
  234.1 10.7 %collective-permute-done.22.s1 = bf16[128,1024]{1,0:T(8,128)(2,1)S(1)} collective-permute-done((bf16[128,1024]{1,0:T(8,128)(2,1)S(1)}, bf16[128,1024]{1,0:T(8,128)(2,1)S(1)}, u32[]{:S(2)}, u32[]{:S(2)}) %collective-permute-start.22) | collective-permute-done | bytes 262176 | tf_op jit(solution)/shard_map/ppermute | solution.py:977
  248.0 6.1 %collective-permute-done.23.s2 = bf16[256,1024]{1,0:T(8,128)(2,1)S(1)} collective-permute-done((bf16[256,1024]{1,0:T(8,128)(2,1)S(1)}, bf16[256,1024]{1,0:T(8,128)(2,1)S(1)}, u32[]{:S(2)}, u32[]{:S(2)}) %collective-permute-start.23) | collective-permute-done | bytes 524320 | tf_op jit(solution)/shard_map/ppermute | solution.py:977
  254.9 5.5 collective-permute-done.25.s4
  263.2 29.0 %shard_map.351 = (bf16[512,1024]{1,0:T(8,128)(2,1)}, f32[256,1024]{1,0:T(8,128)}, bf16[256,1024]{1,0:T(8,128)(2,1)S(1)}, f32[256,1024]{1,0:T(8,128)}, bf16[256,1...) custom-call(s32[8,2]{1,0:T(8,128)S(1)} %copy.127.slots_ref, s32[32]{0:T(128)S(1)} %get-tuple-element.196.table_ref, ...), custom_call_target="tpu_custom_call" | custom-call | flops 30000001024 | bytes 3000000 | tf_op jit(solution)/shard_map/pallas_call | solution.py:507
  294.1 3.2 collective-permute-start.28
  297.3 15.1 %collective-permute-done.28 = bf16[256,1024]{1,0:T(8,128)(2,1)S(1)} collective-permute-done((bf16[256,1024]{1,0:T(8,128)(2,1)S(1)}, bf16[256,1024]{1,0:T(8,128)(2,1)S(1)}, u32[]{:S(2)}, u32[]{:S(2)}) %collective-permute-start.28) | collective-permute-done | bytes 524320 | tf_op jit(solution)/shard_map/ppermute | solution.py:977
  313.4 4.6 collective-permute-done.30
  320.6 9.0 %collective-permute-done.29.k1 = bf16[128,1024]{1,0:T(8,128)(2,1)S(1)} collective-permute-done((bf16[128,1024]{1,0:T(8,128)(2,1)S(1)}, bf16[128,1024]{1,0:T(8,128)(2,1)S(1)}, u32[]{:S(2)}, u32[]{:S(2)}) %collective-permute-start.29) | collective-permute-done | bytes 262176 | tf_op jit(solution)/shard_map/ppermute | solution.py:977
  336.1 11.9 %collective-permute-done.32.b1 = bf16[128,1024]{1,0:T(8,128)(2,1)S(1)} collective-permute-done((bf16[128,1024]{1,0:T(8,128)(2,1)S(1)}, bf16[128,1024]{1,0:T(8,128)(2,1)S(1)}, u32[]{:S(2)}, u32[]{:S(2)}) %collective-permute-start.32) | collective-permute-done | bytes 262176 | tf_op jit(solution)/shard_map/ppermute | solution.py:977
  351.8 6.8 %shard_map.353 = (f32[256,1024]{1,0:T(8,128)S(1)}, bf16[256,1024]{1,0:T(8,128)(2,1)}, f32[256,1024]{1,0:T(8,128)S(1)}, bf16[256,1024]{1,0:T(8,128)(2,1)}) custom-call(bf16[512,1024]{1,0:T(8,128)(2,1)} %get-tuple-element.223.left_ref, bf16[2048,3072]{1,0:T(8,128)(2,1)} %all-gather.8.cloned.1.call-done.gate_ref.up_ref.down_ref.weight_ref), custom_call_target="tpu_custom_call" | custom-call | flops 4000000000 | bytes 400000 | tf_op jit(solution)/shard_map/pallas_call | solution.py:406
  358.5 2.8 collective-permute-done.33.b2
  361.3 14.0 %collective-permute-done.35.b4 = bf16[256,1024]{1,0:T(8,128)(2,1)S(1)} collective-permute-done((bf16[256,1024]{1,0:T(8,128)(2,1)S(1)}, bf16[256,1024]{1,0:T(8,128)(2,1)S(1)}, u32[]{:S(2)}, u32[]{:S(2)}) %collective-permute-start.35) | collective-permute-done | bytes 524320 | tf_op jit(solution)/shard_map/ppermute | solution.py:977
  375.3 2.8 collective-permute-start.39
  378.1 7.5 %shard_map.354 = (bf16[512,2048]{1,0:T(8,128)(2,1)}, f32[512,1024]{1,0:T(8,128)}, f32[8,1,64]{2,1,0:T(1,128)S(1)}) custom-call(bf16[128,2048]{1,0:T(8,128)(2,1)S(1)} %get-tuple-element.228.b0, bf16[128,1024]{1,0:T(8,128)(2,1)S(1)} %collective-permute-done.32.b1, bf16[256,1024]{1,0:T(8,128)(2,1)S(1)} %collective-permute-done.33.b2, ...), custom_call_target="tpu_custom_call" | custom-call | flops 5000000000 | bytes 500000 | tf_op jit(solution)/shard_map/pallas_call | solution.py:603
  387.6 2.9 collective-permute-start.37
  392.0 5.3 shard_map.355
  397.3 5.2 collective-permute-done.38.d3
  406.2 3.3 collective-permute-start.42
  412.6 25.5 %shard_map.356 = (bf16[512,2688]{1,0:T(8,128)(2,1)}, f32[24,1024]{1,0:T(8,128)S(1)}) custom-call(s32[8,2]{1,0:T(8,128)S(1)} %copy-done.26, f32[512,2688]{1,0:T(8,128)} %get-tuple-element.194.gate_ref.proj_ref, f32[8,1280]{1,0:T(8,128)S(1)} %copy-done.23, f32[512,256]{1,0:T(8,128)S(1)} %copy-done.8, f32[512,768]{1,0:T(8,128)S(1)} %copy-done.53, ...), custom_call_target="tpu_custom_call" | custom-call | flops 16999999488 | bytes 1700000 | tf_op jit(solution)/shard_map/pallas_call | solution.py:746
  438.2 11.2 %shard_map.357 = (bf16[1024,2688]{1,0:T(8,128)(2,1)}, bf16[1024,2688]{1,0:T(8,128)(2,1)}) custom-call(s32[32]{0:T(128)S(1)} %copy-done.28, bf16[512,2048]{1,0:T(8,128)(2,1)S(1)} %copy-done.65, bf16[512,2688]{1,0:T(8,128)(2,1)} %get-tuple-element.255.refs_1_.left_ref), custom_call_target="tpu_custom_call" | custom-call | flops 11000000512 | bytes 1100000 | tf_op jit(solution)/shard_map/pallas_call | solution.py:925
  456.3 9.9 %shard_map.358 = (f32[256,1024]{1,0:T(8,128)S(1)}, bf16[256,1024]{1,0:T(8,128)(2,1)S(1)}, f32[256,1024]{1,0:T(8,128)S(1)}, bf16[256,1024]{1,0:T(8,128)(2,1)S(1)}) custom-call(bf16[512,2688]{1,0:T(8,128)(2,1)} %get-tuple-element.255.refs_1_.left_ref, bf16[2048,2688]{1,0:T(8,128)(2,1)} %all-gather.4.cloned.1.call-done.weight_ref.gains_in_ref), custom_call_target="tpu_custom_call" | custom-call | flops 4000000000 | bytes 400000 | tf_op jit(solution)/shard_map/pallas_call | solution.py:406
  469.0 4.2 collective-permute-done.46
  473.3 6.4 %shard_map.359 = (bf16[256,2688]{1,0:T(8,128)(2,1)S(1)}, bf16[256,2688]{1,0:T(8,128)(2,1)S(1)}, bf16[256,2688]{1,0:T(8,128)(2,1)}, bf16[128,2688]{1,0:T(8,128)(2,1)S(1)}, bf16[128,2688]{1,0:T(8,128)(2,1)S(1)}) custom-call(bf16[1024,2688]{1,0:T(8,128)(2,1)} %get-tuple-element.251.keep_ref, bf16[1024,2688]{1,0:T(8,128)(2,1)} %collective-permute-done.50.got_ref), custom_call_target="tpu_custom_call" | custom-call | flops 3000000000 | bytes 300000 | tf_op jit(solution)/shard_map/pallas_call | solution.py:797
  482.2 9.0 %collective-permute-done.48 = bf16[256,1024]{1,0:T(8,128)(2,1)S(1)} collective-permute-done((bf16[256,1024]{1,0:T(8,128)(2,1)S(1)}, bf16[256,1024]{1,0:T(8,128)(2,1)S(1)}, u32[]{:S(2)}, u32[]{:S(2)}) %collective-permute-start.48) | collective-permute-done | bytes 524320 | tf_op jit(solution)/shard_map/ppermute | solution.py:977
  491.2 3.9 collective-permute-done.49
  500.2 2.9 shard_map.360
  511.6 3.6 collective-permute-done.54
  516.0 12.9 %collective-permute-done.53 = bf16[256,1024]{1,0:T(8,128)(2,1)S(1)} collective-permute-done((bf16[256,1024]{1,0:T(8,128)(2,1)S(1)}, bf16[256,1024]{1,0:T(8,128)(2,1)S(1)}, u32[]{:S(2)}, u32[]{:S(2)}) %collective-permute-start.53) | collective-permute-done | bytes 524320 | tf_op jit(solution)/shard_map/ppermute | solution.py:977
  529.7 3.4 collective-permute-done.55.by_x_ref
  535.0 3.5 shard_map.361
  553.6 5.8 collective-permute-done.61
  563.8 5.6 collective-permute-done.59.g3
  (463 shorter events, 161.4 us)
Async XLA Ops:
  7.2 122.1 %all-gather.4.cloned.1.call-start = ((), (), s32[]{:S(2)}) async-start(), calls=%async_computation.2 | async-start | bytes 12386304 | tf_op jit(solution)/shard_map/all_gather | solution.py:1103
  15.6 19.6 %collective-permute-start = (bf16[64,2688]{1,0:T(8,128)(2,1)}, bf16[64,2688]{1,0:T(8,128)(2,1)}, u32[]{:S(2)}, u32[]{:S(2)}) collective-permute-start(bf16[64,2688]{1,0:T(8,128)(2,1)} %concatenate.118), channel_id=1, source_target_pairs={{0,8},{8,0},{16,24},{24,16},{1,9},{9,1},{17,25},{25,17},{2,10},{10... | collective-permute-start | bytes 1032200 | tf_op jit(solution)/shard_map/ppermute | solution.py:977
  16.4 26.6 %collective-permute-start.1 = (bf16[64,2688]{1,0:T(8,128)(2,1)}, bf16[64,2688]{1,0:T(8,128)(2,1)}, u32[]{:S(2)}, u32[]{:S(2)}) collective-permute-start(bf16[64,2688]{1,0:T(8,128)(2,1)} %concatenate.119), channel_id=1, source_target_pairs={{0,16},{8,24},{16,0},{24,8},{1,17},{9,25},{17,1},{25,9},{2,18},{10... | collective-permute-start | bytes 1032200 | tf_op jit(solution)/shard_map/ppermute | solution.py:977
  20.3 32.4 %collective-permute-start.2 = (bf16[64,2688]{1,0:T(8,128)(2,1)}, bf16[64,2688]{1,0:T(8,128)(2,1)}, u32[]{:S(2)}, u32[]{:S(2)}) collective-permute-start(bf16[64,2688]{1,0:T(8,128)(2,1)} %concatenate.120), channel_id=1, source_target_pairs={{0,24},{8,16},{16,8},{24,0},{1,25},{9,17},{17,9},{25,1},{2,26},{10... | collective-permute-start | bytes 1032200 | tf_op jit(solution)/shard_map/ppermute | solution.py:977
  55.5 125.6 %all-gather.6.cloned.1.call-start = ((), (), s32[]{:S(2)}) async-start(), calls=%async_computation.3 | async-start | bytes 4718592 | tf_op jit(solution)/shard_map/all_gather | solution.py:1103
  63.7 35.5 %collective-permute-start.5 = (bf16[256,1024]{1,0:T(8,128)(2,1)}, bf16[256,1024]{1,0:T(8,128)(2,1)S(1)}, u32[]{:S(2)}, u32[]{:S(2)}) collective-permute-start(bf16[256,1024]{1,0:T(8,128)(2,1)} %pad_maximum_fusion.4), channel_id=1, source_target_pairs={{0,8},{8,0},{16,24},{24,16},{1,9},{9,1},{17,25},{25,17},{2,10},{10... | collective-permute-start | bytes 1572872 | tf_op jit(solution)/shard_map/ppermute | solution.py:977
  64.7 34.4 %collective-permute-start.6 = (bf16[256,1024]{1,0:T(8,128)(2,1)}, bf16[256,1024]{1,0:T(8,128)(2,1)}, u32[]{:S(2)}, u32[]{:S(2)}) collective-permute-start(bf16[256,1024]{1,0:T(8,128)(2,1)} %pad_maximum_fusion.5), channel_id=1, source_target_pairs={{0,24},{8,16},{16,8},{24,0},{1,25},{9,17},{17,9},{25,1},{2,26},{10... | collective-permute-start | bytes 1572872 | tf_op jit(solution)/shard_map/ppermute | solution.py:977
  66.5 28.7 %collective-permute-start.8 = (bf16[128,1024]{1,0:T(8,128)(2,1)S(1)}, bf16[128,1024]{1,0:T(8,128)(2,1)S(1)}, u32[]{:S(2)}, u32[]{:S(2)}) collective-permute-start(bf16[128,1024]{1,0:T(8,128)(2,1)S(1)} %get-tuple-element.355), channel_id=1, source_target_pairs={{0,8},{8,0},{16,24},{24,16},{1,9},{9,1},{17,25},{25,17},{2,10},{10... | collective-permute-start | bytes 786440 | tf_op jit(solution)/shard_map/ppermute | solution.py:977
  68.8 30.3 %collective-permute-start.7 = (bf16[128,1024]{1,0:T(8,128)(2,1)S(1)}, bf16[128,1024]{1,0:T(8,128)(2,1)S(1)}, u32[]{:S(2)}, u32[]{:S(2)}) collective-permute-start(bf16[128,1024]{1,0:T(8,128)(2,1)S(1)} %get-tuple-element.356), channel_id=1, source_target_pairs={{0,24},{8,16},{16,8},{24,0},{1,25},{9,17},{17,9},{25,1},{2,26},{10... | collective-permute-start | bytes 786440 | tf_op jit(solution)/shard_map/ppermute | solution.py:977
  111.1 150.0 %all-gather.8.cloned.1.call-start = ((), (), s32[]{:S(2)}) async-start(), calls=%async_computation.4 | async-start | bytes 14155776 | tf_op jit(solution)/shard_map/all_gather | solution.py:1103
  117.4 57.6 %collective-permute-start.26 = (bf16[64,3072]{1,0:T(8,128)(2,1)}, bf16[64,3072]{1,0:T(8,128)(2,1)}, u32[]{:S(2)}, u32[]{:S(2)}) collective-permute-start(bf16[64,3072]{1,0:T(8,128)(2,1)} %pad_maximum_fusion.19), channel_id=1, source_target_pairs={{0,16},{8,24},{16,0},{24,8},{1,17},{9,25},{17,1},{25,9},{2,18},{10... | collective-permute-start | bytes 1179656 | tf_op jit(solution)/shard_map/ppermute | solution.py:977
  119.8 55.3 %collective-permute-start.27 = (bf16[64,3072]{1,0:T(8,128)(2,1)}, bf16[64,3072]{1,0:T(8,128)(2,1)}, u32[]{:S(2)}, u32[]{:S(2)}) collective-permute-start(bf16[64,3072]{1,0:T(8,128)(2,1)} %pad_maximum_fusion.20), channel_id=1, source_target_pairs={{0,24},{8,16},{16,8},{24,0},{1,25},{9,17},{17,9},{25,1},{2,26},{10... | collective-permute-start | bytes 1179656 | tf_op jit(solution)/shard_map/ppermute | solution.py:977
  121.9 49.6 %collective-permute-start.14 = (bf16[256,1024]{1,0:T(8,128)(2,1)}, bf16[256,1024]{1,0:T(8,128)(2,1)}, u32[]{:S(2)}, u32[]{:S(2)}) collective-permute-start(bf16[256,1024]{1,0:T(8,128)(2,1)} %pad_maximum_fusion.8), channel_id=1, source_target_pairs={{0,24},{8,16},{16,8},{24,0},{1,25},{9,17},{17,9},{25,1},{2,26},{10... | collective-permute-start | bytes 1572872 | tf_op jit(solution)/shard_map/ppermute | solution.py:977
  125.4 46.2 %collective-permute-start.13 = (bf16[256,1024]{1,0:T(8,128)(2,1)}, bf16[256,1024]{1,0:T(8,128)(2,1)}, u32[]{:S(2)}, u32[]{:S(2)}) collective-permute-start(bf16[256,1024]{1,0:T(8,128)(2,1)} %pad_maximum_fusion.7), channel_id=1, source_target_pairs={{0,8},{8,0},{16,24},{24,16},{1,9},{9,1},{17,25},{25,17},{2,10},{10... | collective-permute-start | bytes 1572872 | tf_op jit(solution)/shard_map/ppermute | solution.py:977
  181.0 223.3 %reduce-scatter.5.cloned.1.call-start = ((), (), s32[]{:S(2)}) async-start(), calls=%async_computation.6 | async-start | bytes 14155776 | tf_op jit(solution)/shard_map/reduce_scatter | solution.py:1106
  189.0 29.2 %collective-permute-start.20 = (bf16[256,1024]{1,0:T(8,128)(2,1)S(1)}, bf16[256,1024]{1,0:T(8,128)(2,1)S(1)}, u32[]{:S(2)}, u32[]{:S(2)}) collective-permute-start(bf16[256,1024]{1,0:T(8,128)(2,1)S(1)} %get-tuple-element.207), channel_id=1, source_target_pairs={{0,24},{8,16},{16,8},{24,0},{1,25},{9,17},{17,9},{25,1},{2,26},{10... | collective-permute-start | bytes 1572872 | tf_op jit(solution)/shard_map/ppermute | solution.py:977
  203.6 20.9 %collective-permute-start.19 = (bf16[128,1024]{1,0:T(8,128)(2,1)S(1)}, bf16[128,1024]{1,0:T(8,128)(2,1)S(1)}, u32[]{:S(2)}, u32[]{:S(2)}) collective-permute-start(bf16[128,1024]{1,0:T(8,128)(2,1)S(1)} %slice.367), channel_id=1, source_target_pairs={{0,24},{8,16},{16,8},{24,0},{1,25},{9,17},{17,9},{25,1},{2,26},{10... | collective-permute-start | bytes 786440 | tf_op jit(solution)/shard_map/ppermute | solution.py:977
  228.8 16.0 %collective-permute-start.22 = (bf16[128,1024]{1,0:T(8,128)(2,1)S(1)}, bf16[128,1024]{1,0:T(8,128)(2,1)S(1)}, u32[]{:S(2)}, u32[]{:S(2)}) collective-permute-start(bf16[128,1024]{1,0:T(8,128)(2,1)S(1)} %get-tuple-element.350), channel_id=1, source_target_pairs={{0,24},{8,16},{16,8},{24,0},{1,25},{9,17},{17,9},{25,1},{2,26},{10... | collective-permute-start | bytes 786440 | tf_op jit(solution)/shard_map/ppermute | solution.py:977
  230.7 16.2 %collective-permute-start.24 = (bf16[128,1024]{1,0:T(8,128)(2,1)S(1)}, bf16[128,1024]{1,0:T(8,128)(2,1)S(1)}, u32[]{:S(2)}, u32[]{:S(2)}) collective-permute-start(bf16[128,1024]{1,0:T(8,128)(2,1)S(1)} %get-tuple-element.349), channel_id=1, source_target_pairs={{0,8},{8,0},{16,24},{24,16},{1,9},{9,1},{17,25},{25,17},{2,10},{10... | collective-permute-start | bytes 786440 | tf_op jit(solution)/shard_map/ppermute | solution.py:977
  293.1 157.0 %reduce-scatter.3.cloned.1.call-start = ((), (), s32[]{:S(2)}) async-start(), calls=%async_computation.5 | async-start | bytes 4718592 | tf_op jit(solution)/shard_map/reduce_scatter | solution.py:1106
  294.1 18.3 %collective-permute-start.28 = (bf16[256,1024]{1,0:T(8,128)(2,1)S(1)}, bf16[256,1024]{1,0:T(8,128)(2,1)S(1)}, u32[]{:S(2)}, u32[]{:S(2)}) collective-permute-start(bf16[256,1024]{1,0:T(8,128)(2,1)S(1)} %copy-done.34), channel_id=1, source_target_pairs={{0,8},{8,0},{16,24},{24,16},{1,9},{9,1},{17,25},{25,17},{2,10},{10... | collective-permute-start | bytes 1572872 | tf_op jit(solution)/shard_map/ppermute | solution.py:977
  297.3 20.7 %collective-permute-start.30 = (bf16[256,1024]{1,0:T(8,128)(2,1)S(1)}, bf16[256,1024]{1,0:T(8,128)(2,1)S(1)}, u32[]{:S(2)}, u32[]{:S(2)}) collective-permute-start(bf16[256,1024]{1,0:T(8,128)(2,1)S(1)} %get-tuple-element.220), channel_id=1, source_target_pairs={{0,24},{8,16},{16,8},{24,0},{1,25},{9,17},{17,9},{25,1},{2,26},{10... | collective-permute-start | bytes 1572872 | tf_op jit(solution)/shard_map/ppermute | solution.py:977
  312.6 17.0 %collective-permute-start.29 = (bf16[128,1024]{1,0:T(8,128)(2,1)S(1)}, bf16[128,1024]{1,0:T(8,128)(2,1)S(1)}, u32[]{:S(2)}, u32[]{:S(2)}) collective-permute-start(bf16[128,1024]{1,0:T(8,128)(2,1)S(1)} %slice.365), channel_id=1, source_target_pairs={{0,24},{8,16},{16,8},{24,0},{1,25},{9,17},{17,9},{25,1},{2,26},{10... | collective-permute-start | bytes 786440 | tf_op jit(solution)/shard_map/ppermute | solution.py:977
  331.8 16.3 %collective-permute-start.32 = (bf16[128,1024]{1,0:T(8,128)(2,1)S(1)}, bf16[128,1024]{1,0:T(8,128)(2,1)S(1)}, u32[]{:S(2)}, u32[]{:S(2)}) collective-permute-start(bf16[128,1024]{1,0:T(8,128)(2,1)S(1)} %get-tuple-element.348), channel_id=1, source_target_pairs={{0,24},{8,16},{16,8},{24,0},{1,25},{9,17},{17,9},{25,1},{2,26},{10... | collective-permute-start | bytes 786440 | tf_op jit(solution)/shard_map/ppermute | solution.py:977
  333.9 15.2 %collective-permute-start.34 = (bf16[128,1024]{1,0:T(8,128)(2,1)S(1)}, bf16[128,1024]{1,0:T(8,128)(2,1)S(1)}, u32[]{:S(2)}, u32[]{:S(2)}) collective-permute-start(bf16[128,1024]{1,0:T(8,128)(2,1)S(1)} %get-tuple-element.347), channel_id=1, source_target_pairs={{0,8},{8,0},{16,24},{24,16},{1,9},{9,1},{17,25},{25,17},{2,10},{10... | collective-permute-start | bytes 786440 | tf_op jit(solution)/shard_map/ppermute | solution.py:977
  349.1 26.2 %collective-permute-start.35 = (bf16[256,1024]{1,0:T(8,128)(2,1)S(1)}, bf16[256,1024]{1,0:T(8,128)(2,1)S(1)}, u32[]{:S(2)}, u32[]{:S(2)}) collective-permute-start(bf16[256,1024]{1,0:T(8,128)(2,1)S(1)} %pad_maximum_fusion.14), channel_id=1, source_target_pairs={{0,24},{8,16},{16,8},{24,0},{1,25},{9,17},{17,9},{25,1},{2,26},{10... | collective-permute-start | bytes 1572872 | tf_op jit(solution)/shard_map/ppermute | solution.py:977
  375.3 29.0 %collective-permute-start.39 = (bf16[256,1024]{1,0:T(8,128)(2,1)}, bf16[256,1024]{1,0:T(8,128)(2,1)}, u32[]{:S(2)}, u32[]{:S(2)}) collective-permute-start(bf16[256,1024]{1,0:T(8,128)(2,1)} %get-tuple-element.238), channel_id=1, source_target_pairs={{0,8},{8,0},{16,24},{24,16},{1,9},{9,1},{17,25},{25,17},{2,10},{10... | collective-permute-start | bytes 1572872 | tf_op jit(solution)/shard_map/ppermute | solution.py:977
  378.1 26.2 %collective-permute-start.40 = (bf16[256,1024]{1,0:T(8,128)(2,1)}, bf16[256,1024]{1,0:T(8,128)(2,1)}, u32[]{:S(2)}, u32[]{:S(2)}) collective-permute-start(bf16[256,1024]{1,0:T(8,128)(2,1)} %get-tuple-element.239), channel_id=1, source_target_pairs={{0,24},{8,16},{16,8},{24,0},{1,25},{9,17},{17,9},{25,1},{2,26},{10... | collective-permute-start | bytes 1572872 | tf_op jit(solution)/shard_map/ppermute | solution.py:977
  385.6 16.9 %collective-permute-start.38 = (f32[8,1,64]{2,1,0:T(1,128)S(1)}, f32[8,1,64]{2,1,0:T(1,128)S(1)}, u32[]{:S(2)}, u32[]{:S(2)}) collective-permute-start(f32[8,1,64]{2,1,0:T(1,128)S(1)} %get-tuple-element.240.d0), channel_id=1, source_target_pairs={{0,24},{8,16},{16,8},{24,0},{1,25},{9,17},{17,9},{25,1},{2,26},{10... | collective-permute-start | bytes 6152 | tf_op jit(solution)/shard_map/ppermute | solution.py:977
  387.6 15.5 %collective-permute-start.37 = (f32[8,1,64]{2,1,0:T(1,128)S(1)}, f32[8,1,64]{2,1,0:T(1,128)S(1)}, u32[]{:S(2)}, u32[]{:S(2)}) collective-permute-start(f32[8,1,64]{2,1,0:T(1,128)S(1)} %get-tuple-element.240.d0), channel_id=1, source_target_pairs={{0,16},{8,24},{16,0},{24,8},{1,17},{9,25},{17,1},{25,9},{2,18},{10... | collective-permute-start | bytes 6152 | tf_op jit(solution)/shard_map/ppermute | solution.py:977
  406.1 32.0 %collective-permute-start.43 = (bf16[64,3072]{1,0:T(8,128)(2,1)S(1)}, bf16[64,3072]{1,0:T(8,128)(2,1)S(1)}, u32[]{:S(2)}, u32[]{:S(2)}) collective-permute-start(bf16[64,3072]{1,0:T(8,128)(2,1)S(1)} %get-tuple-element.315), channel_id=1, source_target_pairs={{0,24},{8,16},{16,8},{24,0},{1,25},{9,17},{17,9},{25,1},{2,26},{10... | collective-permute-start | bytes 1179656 | tf_op jit(solution)/shard_map/ppermute | solution.py:977
  406.2 31.9 %collective-permute-start.42 = (bf16[64,3072]{1,0:T(8,128)(2,1)S(1)}, bf16[64,3072]{1,0:T(8,128)(2,1)S(1)}, u32[]{:S(2)}, u32[]{:S(2)}) collective-permute-start(bf16[64,3072]{1,0:T(8,128)(2,1)S(1)} %get-tuple-element.316), channel_id=1, source_target_pairs={{0,16},{8,24},{16,0},{24,8},{1,17},{9,25},{17,1},{25,9},{2,18},{10... | collective-permute-start | bytes 1179656 | tf_op jit(solution)/shard_map/ppermute | solution.py:977
  409.5 28.6 %collective-permute-start.41 = (bf16[64,3072]{1,0:T(8,128)(2,1)S(1)}, bf16[64,3072]{1,0:T(8,128)(2,1)S(1)}, u32[]{:S(2)}, u32[]{:S(2)}) collective-permute-start(bf16[64,3072]{1,0:T(8,128)(2,1)S(1)} %get-tuple-element.317), channel_id=1, source_target_pairs={{0,8},{8,0},{16,24},{24,16},{1,9},{9,1},{17,25},{25,17},{2,10},{10... | collective-permute-start | bytes 1179656 | tf_op jit(solution)/shard_map/ppermute | solution.py:977
  449.4 23.9 %collective-permute-start.50 = (bf16[1024,2688]{1,0:T(8,128)(2,1)}, bf16[1024,2688]{1,0:T(8,128)(2,1)}, u32[]{:S(2)}, u32[]{:S(2)}) collective-permute-start(bf16[1024,2688]{1,0:T(8,128)(2,1)} %get-tuple-element.252), channel_id=1, source_target_pairs={{0,1},{1,0},{2,3},{3,2},{4,5},{5,4},{6,7},{7,6},{8,9},{9,8},{10,11... | collective-permute-start | bytes 16515080 | tf_op jit(solution)/shard_map/ppermute | solution.py:977
  452.7 16.3 %collective-permute-start.44 = (bf16[88,1024]{1,0:T(8,128)(2,1)S(1)}, bf16[88,1024]{1,0:T(8,128)(2,1)S(1)}, u32[]{:S(2)}, u32[]{:S(2)}) collective-permute-start(bf16[88,1024]{1,0:T(8,128)(2,1)S(1)} %get-tuple-element.394), channel_id=1, source_target_pairs={{0,8},{8,0},{16,24},{24,16},{1,9},{9,1},{17,25},{25,17},{2,10},{10... | collective-permute-start | bytes 540680 | tf_op jit(solution)/shard_map/ppermute | solution.py:977
  454.6 18.6 %collective-permute-start.46 = (bf16[88,1024]{1,0:T(8,128)(2,1)S(1)}, bf16[88,1024]{1,0:T(8,128)(2,1)S(1)}, u32[]{:S(2)}, u32[]{:S(2)}) collective-permute-start(bf16[88,1024]{1,0:T(8,128)(2,1)S(1)} %get-tuple-element.396), channel_id=1, source_target_pairs={{0,24},{8,16},{16,8},{24,0},{1,25},{9,17},{17,9},{25,1},{2,26},{10... | collective-permute-start | bytes 540680 | tf_op jit(solution)/shard_map/ppermute | solution.py:977
  466.2 25.0 %collective-permute-start.48 = (bf16[256,1024]{1,0:T(8,128)(2,1)S(1)}, bf16[256,1024]{1,0:T(8,128)(2,1)S(1)}, u32[]{:S(2)}, u32[]{:S(2)}) collective-permute-start(bf16[256,1024]{1,0:T(8,128)(2,1)S(1)} %get-tuple-element.257), channel_id=1, source_target_pairs={{0,8},{8,0},{16,24},{24,16},{1,9},{9,1},{17,25},{25,17},{2,10},{10... | collective-permute-start | bytes 1572872 | tf_op jit(solution)/shard_map/ppermute | solution.py:977
  469.0 26.2 %collective-permute-start.49 = (bf16[256,1024]{1,0:T(8,128)(2,1)S(1)}, bf16[256,1024]{1,0:T(8,128)(2,1)S(1)}, u32[]{:S(2)}, u32[]{:S(2)}) collective-permute-start(bf16[256,1024]{1,0:T(8,128)(2,1)S(1)} %get-tuple-element.258), channel_id=1, source_target_pairs={{0,24},{8,16},{16,8},{24,0},{1,25},{9,17},{17,9},{25,1},{2,26},{10... | collective-permute-start | bytes 1572872 | tf_op jit(solution)/shard_map/ppermute | solution.py:977
  479.7 16.3 %collective-permute-start.51 = (bf16[128,2688]{1,0:T(8,128)(2,1)S(1)}, bf16[128,2688]{1,0:T(8,128)(2,1)S(1)}, u32[]{:S(2)}, u32[]{:S(2)}) collective-permute-start(bf16[128,2688]{1,0:T(8,128)(2,1)S(1)} %get-tuple-element.261), channel_id=1, source_target_pairs={{0,4},{4,0},{1,5},{5,1},{2,6},{6,2},{3,7},{7,3},{8,12},{12,8},{9,1... | collective-permute-start | bytes 2064392 | tf_op jit(solution)/shard_map/ppermute | solution.py:977
  481.2 16.1 %collective-permute-start.52 = (bf16[128,2688]{1,0:T(8,128)(2,1)S(1)}, bf16[128,2688]{1,0:T(8,128)(2,1)S(1)}, u32[]{:S(2)}, u32[]{:S(2)}) collective-permute-start(bf16[128,2688]{1,0:T(8,128)(2,1)S(1)} %get-tuple-element.262), channel_id=1, source_target_pairs={{0,2},{2,0},{1,3},{3,1},{4,6},{6,4},{5,7},{7,5},{8,10},{10,8},{9,1... | collective-permute-start | bytes 2064392 | tf_op jit(solution)/shard_map/ppermute | solution.py:977
  482.2 27.1 %collective-permute-start.47 = (f32[4,24,1024]{2,1,0:T(8,128)}, f32[4,24,1024]{2,1,0:T(8,128)}, u32[]{:S(2)}, u32[]{:S(2)}) collective-permute-start(f32[4,24,1024]{2,1,0:T(8,128)} %pad_maximum_fusion.22), channel_id=1, source_target_pairs={{0,1},{1,0},{2,3},{3,2},{4,5},{5,4},{6,7},{7,6},{8,9},{9,8},{10,11... | collective-permute-start | bytes 1179656 | tf_op jit(solution)/shard_map/ppermute | solution.py:977
  500.2 15.1 %collective-permute-start.54 = (bf16[256,1024]{1,0:T(8,128)(2,1)}, bf16[256,1024]{1,0:T(8,128)(2,1)S(1)}, u32[]{:S(2)}, u32[]{:S(2)}) collective-permute-start(bf16[256,1024]{1,0:T(8,128)(2,1)} %pad_maximum_fusion.16), channel_id=1, source_target_pairs={{0,8},{8,0},{16,24},{24,16},{1,9},{9,1},{17,25},{25,17},{2,10},{10... | collective-permute-start | bytes 1572872 | tf_op jit(solution)/shard_map/ppermute | solution.py:977
  503.1 30.0 %collective-permute-start.55 = (bf16[256,2688]{1,0:T(8,128)(2,1)S(1)}, bf16[256,2688]{1,0:T(8,128)(2,1)S(1)}, u32[]{:S(2)}, u32[]{:S(2)}) collective-permute-start(bf16[256,2688]{1,0:T(8,128)(2,1)S(1)} %get-tuple-element.274), channel_id=1, source_target_pairs={{0,4},{4,0},{1,5},{5,1},{2,6},{6,2},{3,7},{7,3},{8,12},{12,8},{9,1... | collective-permute-start | bytes 4128776 | tf_op jit(solution)/shard_map/ppermute | solution.py:977
  503.7 30.3 %collective-permute-start.56 = (bf16[256,2688]{1,0:T(8,128)(2,1)S(1)}, bf16[256,2688]{1,0:T(8,128)(2,1)S(1)}, u32[]{:S(2)}, u32[]{:S(2)}) collective-permute-start(bf16[256,2688]{1,0:T(8,128)(2,1)S(1)} %get-tuple-element.275), channel_id=1, source_target_pairs={{0,2},{2,0},{1,3},{3,1},{4,6},{6,4},{5,7},{7,5},{8,10},{10,8},{9,1... | collective-permute-start | bytes 4128776 | tf_op jit(solution)/shard_map/ppermute | solution.py:977
  506.5 22.4 %collective-permute-start.53 = (bf16[256,1024]{1,0:T(8,128)(2,1)S(1)}, bf16[256,1024]{1,0:T(8,128)(2,1)S(1)}, u32[]{:S(2)}, u32[]{:S(2)}) collective-permute-start(bf16[256,1024]{1,0:T(8,128)(2,1)S(1)} %pad_maximum_fusion.15), channel_id=1, source_target_pairs={{0,24},{8,16},{16,8},{24,0},{1,25},{9,17},{17,9},{25,1},{2,26},{10... | collective-permute-start | bytes 1572872 | tf_op jit(solution)/shard_map/ppermute | solution.py:977
  538.5 24.8 %collective-permute-start.57 = (bf16[64,2688]{1,0:T(8,128)(2,1)}, bf16[64,2688]{1,0:T(8,128)(2,1)}, u32[]{:S(2)}, u32[]{:S(2)}) collective-permute-start(bf16[64,2688]{1,0:T(8,128)(2,1)} %get-tuple-element.279), channel_id=1, source_target_pairs={{0,8},{8,0},{16,24},{24,16},{1,9},{9,1},{17,25},{25,17},{2,10},{10... | collective-permute-start | bytes 1032200 | tf_op jit(solution)/shard_map/ppermute | solution.py:977
  540.3 23.5 %collective-permute-start.58 = (bf16[64,2688]{1,0:T(8,128)(2,1)}, bf16[64,2688]{1,0:T(8,128)(2,1)}, u32[]{:S(2)}, u32[]{:S(2)}) collective-permute-start(bf16[64,2688]{1,0:T(8,128)(2,1)} %get-tuple-element.280), channel_id=1, source_target_pairs={{0,16},{8,24},{16,0},{24,8},{1,17},{9,25},{17,1},{25,9},{2,18},{10... | collective-permute-start | bytes 1032200 | tf_op jit(solution)/shard_map/ppermute | solution.py:977
  540.6 28.8 %collective-permute-start.59 = (bf16[64,2688]{1,0:T(8,128)(2,1)}, bf16[64,2688]{1,0:T(8,128)(2,1)}, u32[]{:S(2)}, u32[]{:S(2)}) collective-permute-start(bf16[64,2688]{1,0:T(8,128)(2,1)} %get-tuple-element.281), channel_id=1, source_target_pairs={{0,24},{8,16},{16,8},{24,0},{1,25},{9,17},{17,9},{25,1},{2,26},{10... | collective-permute-start | bytes 1032200 | tf_op jit(solution)/shard_map/ppermute | solution.py:977
  (123 other events, 1581.2 us)
Sparse Core Ops, SparseCore 0:
  55.6 65.6 all-gather.3
  123.8 36.7 all-gather.5
  181.1 72.6 all-gather.7
  293.2 93.3 reduce-scatter.4
  397.5 50.8 reduce-scatter.2

commit v6 on v5

--- a/solution.py
+++ b/solution.py
@@ -314,7 +314,7 @@
         ).astype(mixed_ref.dtype)
 
 
-def mixer_inner(slots, rows, weight, params, turns, inner, state, heads, tile=384):
+def mixer_inner(slots, rows, weight, params, turns, inner, state, heads, tile=896):
     model, cols = weight.shape
     seqs = slots.shape[0]
     pieces = rows
@@ -1193,6 +1193,7 @@
         in_plane if cube else in_group,
         2 if cube else 1,
         [([after(normed, mlp_grads)], [proj_grad], 0, in_cols)],
+        tile=896,
     )
     riders = small.astype(bf16)
     out_sums, riders = after((out_sums, riders), in_sums)

time: 587 us -> 587 us (level)
  transfers between devices with their start and end apart: 67 -> 67, of which waited for: 42 -> 41; matrix products, arithmetic and copies ran while one was open for 9% -> 9% of each run, Pallas kernels for 21% -> 20%
where the time goes in v6:
time: 587 us; the launch traced here: 580 us
  waiting for transfers between devices  255 us (43%)
  Pallas kernels  153 us (26%)
  starting transfers between devices  74.7 us (13%)
  local copies, waits for them, and re-layouts  50.2 us (9%)
  other arithmetic  31.6 us (5%)
  between operations  15.7 us (3%)
    ppermute x62, waiting for transfers between devices, swap(): return lax.ppermute(values, axis, [(i, i ^ k) for i in range(size)])  254 us
    ppermute x62, starting transfers between devices, swap(): return lax.ppermute(values, axis, [(i, i ^ k) for i in range(size)])  74.3 us
    pallas_call x1, Pallas kernels, feed_forward(): pl.pallas_call(functools.partial(feed_kernel, steps, table.shape[0]), gri...  29.2 us
    pallas_call x1, Pallas kernels, mixer_backward(): pl.pallas_call(functools.partial(backward_kernel, inner, state, heads), g...  25.5 us
    pallas_call x1, Pallas kernels, mixer_inner(): pl.pallas_call(functools.partial(inner_kernel, inner, state, heads, tiles...  25.3 us
    unnamed x201, local copies, waits for them, and re-layouts  17.2 us
    pallas_call x2, Pallas kernels, weight_grads(): pl.pallas_call(functools.partial(weight_grad_kernel, tuple(bounds), mine,...  16.7 us
    pallas_call x2, Pallas kernels, back_out(): pl.pallas_call(back_out_kernel, grid=(model // tile,), in_specs=specs(lef...  16.5 us
  transfers between devices with their start and end apart: 67, of which 41 were waited for; matrix products, arithmetic and copies ran while one was open for 9% of the time, Pallas kernels for 20%

profile of v6, /device:TPU:8, one launch (start us, length us, event | category | flops | bytes accessed | tf_op | source)
XLA Modules:
  0.0 579.7 jit_solution(2733941733698465415)
XLA Ops:
  16.4 3.0 collective-permute-start.1
  35.2 7.8 %collective-permute-done.1 = bf16[64,2688]{1,0:T(8,128)(2,1)} collective-permute-done((bf16[64,2688]{1,0:T(8,128)(2,1)}, bf16[64,2688]{1,0:T(8,128)(2,1)}, u32[]{:S(2)}, u32[]{:S(2)}) %collective-permute-start.1) | collective-permute-done | bytes 344096 | tf_op jit(solution)/shard_map/ppermute | solution.py:977
  43.0 9.7 %collective-permute-done.2 = bf16[64,2688]{1,0:T(8,128)(2,1)} collective-permute-done((bf16[64,2688]{1,0:T(8,128)(2,1)}, bf16[64,2688]{1,0:T(8,128)(2,1)}, u32[]{:S(2)}, u32[]{:S(2)}) %collective-permute-start.2) | collective-permute-done | bytes 344096 | tf_op jit(solution)/shard_map/ppermute | solution.py:977
  57.5 5.3 collective-permute-done.3.p1
  69.8 25.3 %collective-permute-done.8.c3 = bf16[128,1024]{1,0:T(8,128)(2,1)S(1)} collective-permute-done((bf16[128,1024]{1,0:T(8,128)(2,1)S(1)}, bf16[128,1024]{1,0:T(8,128)(2,1)S(1)}, u32[]{:S(2)}, u32[]{:S(2)}) %collective-permute-start.8) | collective-permute-done | bytes 262176 | tf_op jit(solution)/shard_map/ppermute | solution.py:977
  95.2 4.0 collective-permute-done.7.c1
  104.4 3.6 collective-permute-done.10
  130.4 25.3 %shard_map.348 = (bf16[512,2048]{1,0:T(8,128)(2,1)}, f32[512,2688]{1,0:T(8,128)}, f32[512,768]{1,0:T(8,128)}, f32[8,1,64]{2,1,0:T(1,128)S(1)}, bf16[512,256]{1,0:T(8,128)(2,1)S(1)}, /*index=5*/f32[8,2048]{1,0:T(8,128)S(1)}) custom-call(s32[8,2]{1,0:T(8,128)S(1)} %copy.127.slots_ref, bf16[128,2048]{1,0:T(8,128)(2,1)S(1)} %copy.119.p0, ...), custom_call_target="tpu_custom_call" | custom-call | flops 17999998976 | bytes 1800000 | tf_op jit(solution)/shard_map/pallas_call | solution.py:332
  155.7 15.9 %collective-permute-done.14.c4 = bf16[256,1024]{1,0:T(8,128)(2,1)} collective-permute-done((bf16[256,1024]{1,0:T(8,128)(2,1)}, bf16[256,1024]{1,0:T(8,128)(2,1)}, u32[]{:S(2)}, u32[]{:S(2)}) %collective-permute-start.14) | collective-permute-done | bytes 524320 | tf_op jit(solution)/shard_map/ppermute | solution.py:977
  175.2 2.9 collective-permute-done.16.s2
  181.1 7.4 %shard_map.349 = (bf16[512,1024]{1,0:T(8,128)(2,1)S(1)}, f32[8,1,64]{2,1,0:T(1,128)S(1)}, f32[256,1024]{1,0:T(8,128)S(1)}, bf16[256,1024]{1,0:T(8,128)(2,1)S(1)}...) custom-call(f32[512,2688]{1,0:T(8,128)} %get-tuple-element.194.gate_ref.proj_ref, ...), custom_call_target="tpu_custom_call" | custom-call | flops 4000000000 | bytes 400000 | tf_op jit(solution)/shard_map/pallas_call | solution.py:379
  191.1 12.3 %collective-permute-done.18 = bf16[256,1024]{1,0:T(8,128)(2,1)S(1)} collective-permute-done((bf16[256,1024]{1,0:T(8,128)(2,1)S(1)}, bf16[256,1024]{1,0:T(8,128)(2,1)S(1)}, u32[]{:S(2)}, u32[]{:S(2)}) %collective-permute-start.18) | collective-permute-done | bytes 524320 | tf_op jit(solution)/shard_map/ppermute | solution.py:977
  204.3 14.0 %collective-permute-done.20 = bf16[256,1024]{1,0:T(8,128)(2,1)S(1)} collective-permute-done((bf16[256,1024]{1,0:T(8,128)(2,1)S(1)}, bf16[256,1024]{1,0:T(8,128)(2,1)S(1)}, u32[]{:S(2)}, u32[]{:S(2)}) %collective-permute-start.20) | collective-permute-done | bytes 524320 | tf_op jit(solution)/shard_map/ppermute | solution.py:977
  218.7 5.8 collective-permute-done.19.k1
  224.5 3.3 collective-permute-done.21.k3
  230.8 3.4 collective-permute-start.24
  234.1 10.7 %collective-permute-done.22.s1 = bf16[128,1024]{1,0:T(8,128)(2,1)S(1)} collective-permute-done((bf16[128,1024]{1,0:T(8,128)(2,1)S(1)}, bf16[128,1024]{1,0:T(8,128)(2,1)S(1)}, u32[]{:S(2)}, u32[]{:S(2)}) %collective-permute-start.22) | collective-permute-done | bytes 262176 | tf_op jit(solution)/shard_map/ppermute | solution.py:977
  248.1 6.1 %collective-permute-done.23.s2 = bf16[256,1024]{1,0:T(8,128)(2,1)S(1)} collective-permute-done((bf16[256,1024]{1,0:T(8,128)(2,1)S(1)}, bf16[256,1024]{1,0:T(8,128)(2,1)S(1)}, u32[]{:S(2)}, u32[]{:S(2)}) %collective-permute-start.23) | collective-permute-done | bytes 524320 | tf_op jit(solution)/shard_map/ppermute | solution.py:977
  254.9 5.5 collective-permute-done.25.s4
  263.3 29.2 %shard_map.351 = (bf16[512,1024]{1,0:T(8,128)(2,1)}, f32[256,1024]{1,0:T(8,128)}, bf16[256,1024]{1,0:T(8,128)(2,1)S(1)}, f32[256,1024]{1,0:T(8,128)}, bf16[256,1...) custom-call(s32[8,2]{1,0:T(8,128)S(1)} %copy.127.slots_ref, s32[32]{0:T(128)S(1)} %get-tuple-element.196.table_ref, ...), custom_call_target="tpu_custom_call" | custom-call | flops 30000001024 | bytes 3000000 | tf_op jit(solution)/shard_map/pallas_call | solution.py:507
  294.3 3.2 collective-permute-start.28
  297.6 15.1 %collective-permute-done.28 = bf16[256,1024]{1,0:T(8,128)(2,1)S(1)} collective-permute-done((bf16[256,1024]{1,0:T(8,128)(2,1)S(1)}, bf16[256,1024]{1,0:T(8,128)(2,1)S(1)}, u32[]{:S(2)}, u32[]{:S(2)}) %collective-permute-start.28) | collective-permute-done | bytes 524320 | tf_op jit(solution)/shard_map/ppermute | solution.py:977
  313.7 4.6 collective-permute-done.30
  320.9 9.0 %collective-permute-done.29.k1 = bf16[128,1024]{1,0:T(8,128)(2,1)S(1)} collective-permute-done((bf16[128,1024]{1,0:T(8,128)(2,1)S(1)}, bf16[128,1024]{1,0:T(8,128)(2,1)S(1)}, u32[]{:S(2)}, u32[]{:S(2)}) %collective-permute-start.29) | collective-permute-done | bytes 262176 | tf_op jit(solution)/shard_map/ppermute | solution.py:977
  336.3 11.9 %collective-permute-done.32.b1 = bf16[128,1024]{1,0:T(8,128)(2,1)S(1)} collective-permute-done((bf16[128,1024]{1,0:T(8,128)(2,1)S(1)}, bf16[128,1024]{1,0:T(8,128)(2,1)S(1)}, u32[]{:S(2)}, u32[]{:S(2)}) %collective-permute-start.32) | collective-permute-done | bytes 262176 | tf_op jit(solution)/shard_map/ppermute | solution.py:977
  352.0 6.5 %shard_map.353 = (f32[256,1024]{1,0:T(8,128)S(1)}, bf16[256,1024]{1,0:T(8,128)(2,1)}, f32[256,1024]{1,0:T(8,128)S(1)}, bf16[256,1024]{1,0:T(8,128)(2,1)}) custom-call(bf16[512,1024]{1,0:T(8,128)(2,1)} %get-tuple-element.223.left_ref, bf16[2048,3072]{1,0:T(8,128)(2,1)} %all-gather.8.cloned.1.call-done.gate_ref.up_ref.down_ref.weight_ref), custom_call_target="tpu_custom_call" | custom-call | flops 4000000000 | bytes 400000 | tf_op jit(solution)/shard_map/pallas_call | solution.py:406
  358.5 2.9 collective-permute-done.33.b2
  361.4 14.1 %collective-permute-done.35.b4 = bf16[256,1024]{1,0:T(8,128)(2,1)S(1)} collective-permute-done((bf16[256,1024]{1,0:T(8,128)(2,1)S(1)}, bf16[256,1024]{1,0:T(8,128)(2,1)S(1)}, u32[]{:S(2)}, u32[]{:S(2)}) %collective-permute-start.35) | collective-permute-done | bytes 524320 | tf_op jit(solution)/shard_map/ppermute | solution.py:977
  375.5 2.8 collective-permute-start.39
  378.4 7.5 %shard_map.354 = (bf16[512,2048]{1,0:T(8,128)(2,1)}, f32[512,1024]{1,0:T(8,128)}, f32[8,1,64]{2,1,0:T(1,128)S(1)}) custom-call(bf16[128,2048]{1,0:T(8,128)(2,1)S(1)} %get-tuple-element.228.b0, bf16[128,1024]{1,0:T(8,128)(2,1)S(1)} %collective-permute-done.32.b1, bf16[256,1024]{1,0:T(8,128)(2,1)S(1)} %collective-permute-done.33.b2, ...), custom_call_target="tpu_custom_call" | custom-call | flops 5000000000 | bytes 500000 | tf_op jit(solution)/shard_map/pallas_call | solution.py:603
  387.8 2.9 collective-permute-start.37
  392.3 5.3 shard_map.355
  397.6 5.2 collective-permute-done.38.d3
  406.5 3.3 collective-permute-start.42
  412.8 25.5 %shard_map.356 = (bf16[512,2688]{1,0:T(8,128)(2,1)}, f32[24,1024]{1,0:T(8,128)S(1)}) custom-call(s32[8,2]{1,0:T(8,128)S(1)} %copy-done.26, f32[512,2688]{1,0:T(8,128)} %get-tuple-element.194.gate_ref.proj_ref, f32[8,1280]{1,0:T(8,128)S(1)} %copy-done.23, f32[512,256]{1,0:T(8,128)S(1)} %copy-done.8, f32[512,768]{1,0:T(8,128)S(1)} %copy-done.53, ...), custom_call_target="tpu_custom_call" | custom-call | flops 16999999488 | bytes 1700000 | tf_op jit(solution)/shard_map/pallas_call | solution.py:746
  438.4 11.4 %shard_map.357 = (bf16[1024,2688]{1,0:T(8,128)(2,1)}, bf16[1024,2688]{1,0:T(8,128)(2,1)}) custom-call(s32[32]{0:T(128)S(1)} %copy-done.28, bf16[512,2048]{1,0:T(8,128)(2,1)S(1)} %copy-done.65, bf16[512,2688]{1,0:T(8,128)(2,1)} %get-tuple-element.255.refs_1_.left_ref), custom_call_target="tpu_custom_call" | custom-call | flops 11000000512 | bytes 1100000 | tf_op jit(solution)/shard_map/pallas_call | solution.py:925
  456.7 9.9 %shard_map.358 = (f32[256,1024]{1,0:T(8,128)S(1)}, bf16[256,1024]{1,0:T(8,128)(2,1)S(1)}, f32[256,1024]{1,0:T(8,128)S(1)}, bf16[256,1024]{1,0:T(8,128)(2,1)S(1)}) custom-call(bf16[512,2688]{1,0:T(8,128)(2,1)} %get-tuple-element.255.refs_1_.left_ref, bf16[2048,2688]{1,0:T(8,128)(2,1)} %all-gather.4.cloned.1.call-done.weight_ref.gains_in_ref), custom_call_target="tpu_custom_call" | custom-call | flops 4000000000 | bytes 400000 | tf_op jit(solution)/shard_map/pallas_call | solution.py:406
  469.5 4.2 collective-permute-done.46
  473.7 6.6 %shard_map.359 = (bf16[256,2688]{1,0:T(8,128)(2,1)S(1)}, bf16[256,2688]{1,0:T(8,128)(2,1)S(1)}, bf16[256,2688]{1,0:T(8,128)(2,1)}, bf16[128,2688]{1,0:T(8,128)(2,1)S(1)}, bf16[128,2688]{1,0:T(8,128)(2,1)S(1)}) custom-call(bf16[1024,2688]{1,0:T(8,128)(2,1)} %get-tuple-element.251.keep_ref, bf16[1024,2688]{1,0:T(8,128)(2,1)} %collective-permute-done.50.got_ref), custom_call_target="tpu_custom_call" | custom-call | flops 3000000000 | bytes 300000 | tf_op jit(solution)/shard_map/pallas_call | solution.py:797
  483.0 8.7 %collective-permute-done.48 = bf16[256,1024]{1,0:T(8,128)(2,1)S(1)} collective-permute-done((bf16[256,1024]{1,0:T(8,128)(2,1)S(1)}, bf16[256,1024]{1,0:T(8,128)(2,1)S(1)}, u32[]{:S(2)}, u32[]{:S(2)}) %collective-permute-start.48) | collective-permute-done | bytes 524320 | tf_op jit(solution)/shard_map/ppermute | solution.py:977
  491.7 3.9 collective-permute-done.49
  500.9 2.8 shard_map.360
  512.2 3.8 collective-permute-done.54
  516.7 12.8 %collective-permute-done.53 = bf16[256,1024]{1,0:T(8,128)(2,1)S(1)} collective-permute-done((bf16[256,1024]{1,0:T(8,128)(2,1)S(1)}, bf16[256,1024]{1,0:T(8,128)(2,1)S(1)}, u32[]{:S(2)}, u32[]{:S(2)}) %collective-permute-start.53) | collective-permute-done | bytes 524320 | tf_op jit(solution)/shard_map/ppermute | solution.py:977
  530.2 3.5 collective-permute-done.55.by_x_ref
  535.4 3.5 shard_map.361
  553.9 6.1 %collective-permute-done.61 = f32[4,24,1024]{2,1,0:T(8,128)S(1)} collective-permute-done((f32[4,24,1024]{2,1,0:T(8,128)S(1)}, f32[4,24,1024]{2,1,0:T(8,128)S(1)}, u32[]{:S(2)}, u32[]{:S(2)}) %collective-permute-start.61) | collective-permute-done | bytes 393248 | tf_op jit(solution)/shard_map/ppermute | solution.py:977
  564.0 5.5 collective-permute-done.59.g3
  (463 shorter events, 161.0 us)
Async XLA Ops:
  7.2 122.1 %all-gather.4.cloned.1.call-start = ((), (), s32[]{:S(2)}) async-start(), calls=%async_computation.2 | async-start | bytes 12386304 | tf_op jit(solution)/shard_map/all_gather | solution.py:1103
  15.6 19.6 %collective-permute-start = (bf16[64,2688]{1,0:T(8,128)(2,1)}, bf16[64,2688]{1,0:T(8,128)(2,1)}, u32[]{:S(2)}, u32[]{:S(2)}) collective-permute-start(bf16[64,2688]{1,0:T(8,128)(2,1)} %concatenate.118), channel_id=1, source_target_pairs={{0,8},{8,0},{16,24},{24,16},{1,9},{9,1},{17,25},{25,17},{2,10},{10... | collective-permute-start | bytes 1032200 | tf_op jit(solution)/shard_map/ppermute | solution.py:977
  16.4 26.6 %collective-permute-start.1 = (bf16[64,2688]{1,0:T(8,128)(2,1)}, bf16[64,2688]{1,0:T(8,128)(2,1)}, u32[]{:S(2)}, u32[]{:S(2)}) collective-permute-start(bf16[64,2688]{1,0:T(8,128)(2,1)} %concatenate.119), channel_id=1, source_target_pairs={{0,16},{8,24},{16,0},{24,8},{1,17},{9,25},{17,1},{25,9},{2,18},{10... | collective-permute-start | bytes 1032200 | tf_op jit(solution)/shard_map/ppermute | solution.py:977
  20.3 32.4 %collective-permute-start.2 = (bf16[64,2688]{1,0:T(8,128)(2,1)}, bf16[64,2688]{1,0:T(8,128)(2,1)}, u32[]{:S(2)}, u32[]{:S(2)}) collective-permute-start(bf16[64,2688]{1,0:T(8,128)(2,1)} %concatenate.120), channel_id=1, source_target_pairs={{0,24},{8,16},{16,8},{24,0},{1,25},{9,17},{17,9},{25,1},{2,26},{10... | collective-permute-start | bytes 1032200 | tf_op jit(solution)/shard_map/ppermute | solution.py:977
  55.5 125.6 %all-gather.6.cloned.1.call-start = ((), (), s32[]{:S(2)}) async-start(), calls=%async_computation.3 | async-start | bytes 4718592 | tf_op jit(solution)/shard_map/all_gather | solution.py:1103
  63.7 35.5 %collective-permute-start.5 = (bf16[256,1024]{1,0:T(8,128)(2,1)}, bf16[256,1024]{1,0:T(8,128)(2,1)S(1)}, u32[]{:S(2)}, u32[]{:S(2)}) collective-permute-start(bf16[256,1024]{1,0:T(8,128)(2,1)} %pad_maximum_fusion.4), channel_id=1, source_target_pairs={{0,8},{8,0},{16,24},{24,16},{1,9},{9,1},{17,25},{25,17},{2,10},{10... | collective-permute-start | bytes 1572872 | tf_op jit(solution)/shard_map/ppermute | solution.py:977
  64.7 34.4 %collective-permute-start.6 = (bf16[256,1024]{1,0:T(8,128)(2,1)}, bf16[256,1024]{1,0:T(8,128)(2,1)}, u32[]{:S(2)}, u32[]{:S(2)}) collective-permute-start(bf16[256,1024]{1,0:T(8,128)(2,1)} %pad_maximum_fusion.5), channel_id=1, source_target_pairs={{0,24},{8,16},{16,8},{24,0},{1,25},{9,17},{17,9},{25,1},{2,26},{10... | collective-permute-start | bytes 1572872 | tf_op jit(solution)/shard_map/ppermute | solution.py:977
  66.5 28.7 %collective-permute-start.8 = (bf16[128,1024]{1,0:T(8,128)(2,1)S(1)}, bf16[128,1024]{1,0:T(8,128)(2,1)S(1)}, u32[]{:S(2)}, u32[]{:S(2)}) collective-permute-start(bf16[128,1024]{1,0:T(8,128)(2,1)S(1)} %get-tuple-element.355), channel_id=1, source_target_pairs={{0,8},{8,0},{16,24},{24,16},{1,9},{9,1},{17,25},{25,17},{2,10},{10... | collective-permute-start | bytes 786440 | tf_op jit(solution)/shard_map/ppermute | solution.py:977
  68.8 30.3 %collective-permute-start.7 = (bf16[128,1024]{1,0:T(8,128)(2,1)S(1)}, bf16[128,1024]{1,0:T(8,128)(2,1)S(1)}, u32[]{:S(2)}, u32[]{:S(2)}) collective-permute-start(bf16[128,1024]{1,0:T(8,128)(2,1)S(1)} %get-tuple-element.356), channel_id=1, source_target_pairs={{0,24},{8,16},{16,8},{24,0},{1,25},{9,17},{17,9},{25,1},{2,26},{10... | collective-permute-start | bytes 786440 | tf_op jit(solution)/shard_map/ppermute | solution.py:977
  111.1 150.1 %all-gather.8.cloned.1.call-start = ((), (), s32[]{:S(2)}) async-start(), calls=%async_computation.4 | async-start | bytes 14155776 | tf_op jit(solution)/shard_map/all_gather | solution.py:1103
  117.5 57.6 %collective-permute-start.26 = (bf16[64,3072]{1,0:T(8,128)(2,1)}, bf16[64,3072]{1,0:T(8,128)(2,1)}, u32[]{:S(2)}, u32[]{:S(2)}) collective-permute-start(bf16[64,3072]{1,0:T(8,128)(2,1)} %pad_maximum_fusion.19), channel_id=1, source_target_pairs={{0,16},{8,24},{16,0},{24,8},{1,17},{9,25},{17,1},{25,9},{2,18},{10... | collective-permute-start | bytes 1179656 | tf_op jit(solution)/shard_map/ppermute | solution.py:977
  119.8 55.3 %collective-permute-start.27 = (bf16[64,3072]{1,0:T(8,128)(2,1)}, bf16[64,3072]{1,0:T(8,128)(2,1)}, u32[]{:S(2)}, u32[]{:S(2)}) collective-permute-start(bf16[64,3072]{1,0:T(8,128)(2,1)} %pad_maximum_fusion.20), channel_id=1, source_target_pairs={{0,24},{8,16},{16,8},{24,0},{1,25},{9,17},{17,9},{25,1},{2,26},{10... | collective-permute-start | bytes 1179656 | tf_op jit(solution)/shard_map/ppermute | solution.py:977
  121.9 49.6 %collective-permute-start.14 = (bf16[256,1024]{1,0:T(8,128)(2,1)}, bf16[256,1024]{1,0:T(8,128)(2,1)}, u32[]{:S(2)}, u32[]{:S(2)}) collective-permute-start(bf16[256,1024]{1,0:T(8,128)(2,1)} %pad_maximum_fusion.8), channel_id=1, source_target_pairs={{0,24},{8,16},{16,8},{24,0},{1,25},{9,17},{17,9},{25,1},{2,26},{10... | collective-permute-start | bytes 1572872 | tf_op jit(solution)/shard_map/ppermute | solution.py:977
  125.4 46.2 %collective-permute-start.13 = (bf16[256,1024]{1,0:T(8,128)(2,1)}, bf16[256,1024]{1,0:T(8,128)(2,1)}, u32[]{:S(2)}, u32[]{:S(2)}) collective-permute-start(bf16[256,1024]{1,0:T(8,128)(2,1)} %pad_maximum_fusion.7), channel_id=1, source_target_pairs={{0,8},{8,0},{16,24},{24,16},{1,9},{9,1},{17,25},{25,17},{2,10},{10... | collective-permute-start | bytes 1572872 | tf_op jit(solution)/shard_map/ppermute | solution.py:977
  181.1 223.5 %reduce-scatter.5.cloned.1.call-start = ((), (), s32[]{:S(2)}) async-start(), calls=%async_computation.6 | async-start | bytes 14155776 | tf_op jit(solution)/shard_map/reduce_scatter | solution.py:1106
  189.1 29.2 %collective-permute-start.20 = (bf16[256,1024]{1,0:T(8,128)(2,1)S(1)}, bf16[256,1024]{1,0:T(8,128)(2,1)S(1)}, u32[]{:S(2)}, u32[]{:S(2)}) collective-permute-start(bf16[256,1024]{1,0:T(8,128)(2,1)S(1)} %get-tuple-element.207), channel_id=1, source_target_pairs={{0,24},{8,16},{16,8},{24,0},{1,25},{9,17},{17,9},{25,1},{2,26},{10... | collective-permute-start | bytes 1572872 | tf_op jit(solution)/shard_map/ppermute | solution.py:977
  203.6 20.9 %collective-permute-start.19 = (bf16[128,1024]{1,0:T(8,128)(2,1)S(1)}, bf16[128,1024]{1,0:T(8,128)(2,1)S(1)}, u32[]{:S(2)}, u32[]{:S(2)}) collective-permute-start(bf16[128,1024]{1,0:T(8,128)(2,1)S(1)} %slice.367), channel_id=1, source_target_pairs={{0,24},{8,16},{16,8},{24,0},{1,25},{9,17},{17,9},{25,1},{2,26},{10... | collective-permute-start | bytes 786440 | tf_op jit(solution)/shard_map/ppermute | solution.py:977
  228.9 16.0 %collective-permute-start.22 = (bf16[128,1024]{1,0:T(8,128)(2,1)S(1)}, bf16[128,1024]{1,0:T(8,128)(2,1)S(1)}, u32[]{:S(2)}, u32[]{:S(2)}) collective-permute-start(bf16[128,1024]{1,0:T(8,128)(2,1)S(1)} %get-tuple-element.350), channel_id=1, source_target_pairs={{0,24},{8,16},{16,8},{24,0},{1,25},{9,17},{17,9},{25,1},{2,26},{10... | collective-permute-start | bytes 786440 | tf_op jit(solution)/shard_map/ppermute | solution.py:977
  230.8 16.2 %collective-permute-start.24 = (bf16[128,1024]{1,0:T(8,128)(2,1)S(1)}, bf16[128,1024]{1,0:T(8,128)(2,1)S(1)}, u32[]{:S(2)}, u32[]{:S(2)}) collective-permute-start(bf16[128,1024]{1,0:T(8,128)(2,1)S(1)} %get-tuple-element.349), channel_id=1, source_target_pairs={{0,8},{8,0},{16,24},{24,16},{1,9},{9,1},{17,25},{25,17},{2,10},{10... | collective-permute-start | bytes 786440 | tf_op jit(solution)/shard_map/ppermute | solution.py:977
  293.3 157.2 %reduce-scatter.3.cloned.1.call-start = ((), (), s32[]{:S(2)}) async-start(), calls=%async_computation.5 | async-start | bytes 4718592 | tf_op jit(solution)/shard_map/reduce_scatter | solution.py:1106
  294.3 18.3 %collective-permute-start.28 = (bf16[256,1024]{1,0:T(8,128)(2,1)S(1)}, bf16[256,1024]{1,0:T(8,128)(2,1)S(1)}, u32[]{:S(2)}, u32[]{:S(2)}) collective-permute-start(bf16[256,1024]{1,0:T(8,128)(2,1)S(1)} %copy-done.34), channel_id=1, source_target_pairs={{0,8},{8,0},{16,24},{24,16},{1,9},{9,1},{17,25},{25,17},{2,10},{10... | collective-permute-start | bytes 1572872 | tf_op jit(solution)/shard_map/ppermute | solution.py:977
  297.6 20.7 %collective-permute-start.30 = (bf16[256,1024]{1,0:T(8,128)(2,1)S(1)}, bf16[256,1024]{1,0:T(8,128)(2,1)S(1)}, u32[]{:S(2)}, u32[]{:S(2)}) collective-permute-start(bf16[256,1024]{1,0:T(8,128)(2,1)S(1)} %get-tuple-element.220), channel_id=1, source_target_pairs={{0,24},{8,16},{16,8},{24,0},{1,25},{9,17},{17,9},{25,1},{2,26},{10... | collective-permute-start | bytes 1572872 | tf_op jit(solution)/shard_map/ppermute | solution.py:977
  312.8 17.0 %collective-permute-start.29 = (bf16[128,1024]{1,0:T(8,128)(2,1)S(1)}, bf16[128,1024]{1,0:T(8,128)(2,1)S(1)}, u32[]{:S(2)}, u32[]{:S(2)}) collective-permute-start(bf16[128,1024]{1,0:T(8,128)(2,1)S(1)} %slice.365), channel_id=1, source_target_pairs={{0,24},{8,16},{16,8},{24,0},{1,25},{9,17},{17,9},{25,1},{2,26},{10... | collective-permute-start | bytes 786440 | tf_op jit(solution)/shard_map/ppermute | solution.py:977
  332.0 16.2 %collective-permute-start.32 = (bf16[128,1024]{1,0:T(8,128)(2,1)S(1)}, bf16[128,1024]{1,0:T(8,128)(2,1)S(1)}, u32[]{:S(2)}, u32[]{:S(2)}) collective-permute-start(bf16[128,1024]{1,0:T(8,128)(2,1)S(1)} %get-tuple-element.348), channel_id=1, source_target_pairs={{0,24},{8,16},{16,8},{24,0},{1,25},{9,17},{17,9},{25,1},{2,26},{10... | collective-permute-start | bytes 786440 | tf_op jit(solution)/shard_map/ppermute | solution.py:977
  334.1 15.2 %collective-permute-start.34 = (bf16[128,1024]{1,0:T(8,128)(2,1)S(1)}, bf16[128,1024]{1,0:T(8,128)(2,1)S(1)}, u32[]{:S(2)}, u32[]{:S(2)}) collective-permute-start(bf16[128,1024]{1,0:T(8,128)(2,1)S(1)} %get-tuple-element.347), channel_id=1, source_target_pairs={{0,8},{8,0},{16,24},{24,16},{1,9},{9,1},{17,25},{25,17},{2,10},{10... | collective-permute-start | bytes 786440 | tf_op jit(solution)/shard_map/ppermute | solution.py:977
  349.3 26.3 %collective-permute-start.35 = (bf16[256,1024]{1,0:T(8,128)(2,1)S(1)}, bf16[256,1024]{1,0:T(8,128)(2,1)S(1)}, u32[]{:S(2)}, u32[]{:S(2)}) collective-permute-start(bf16[256,1024]{1,0:T(8,128)(2,1)S(1)} %pad_maximum_fusion.14), channel_id=1, source_target_pairs={{0,24},{8,16},{16,8},{24,0},{1,25},{9,17},{17,9},{25,1},{2,26},{10... | collective-permute-start | bytes 1572872 | tf_op jit(solution)/shard_map/ppermute | solution.py:977
  375.5 29.0 %collective-permute-start.39 = (bf16[256,1024]{1,0:T(8,128)(2,1)}, bf16[256,1024]{1,0:T(8,128)(2,1)}, u32[]{:S(2)}, u32[]{:S(2)}) collective-permute-start(bf16[256,1024]{1,0:T(8,128)(2,1)} %get-tuple-element.238), channel_id=1, source_target_pairs={{0,8},{8,0},{16,24},{24,16},{1,9},{9,1},{17,25},{25,17},{2,10},{10... | collective-permute-start | bytes 1572872 | tf_op jit(solution)/shard_map/ppermute | solution.py:977
  378.4 26.2 %collective-permute-start.40 = (bf16[256,1024]{1,0:T(8,128)(2,1)}, bf16[256,1024]{1,0:T(8,128)(2,1)}, u32[]{:S(2)}, u32[]{:S(2)}) collective-permute-start(bf16[256,1024]{1,0:T(8,128)(2,1)} %get-tuple-element.239), channel_id=1, source_target_pairs={{0,24},{8,16},{16,8},{24,0},{1,25},{9,17},{17,9},{25,1},{2,26},{10... | collective-permute-start | bytes 1572872 | tf_op jit(solution)/shard_map/ppermute | solution.py:977
  385.8 16.9 %collective-permute-start.38 = (f32[8,1,64]{2,1,0:T(1,128)S(1)}, f32[8,1,64]{2,1,0:T(1,128)S(1)}, u32[]{:S(2)}, u32[]{:S(2)}) collective-permute-start(f32[8,1,64]{2,1,0:T(1,128)S(1)} %get-tuple-element.240.d0), channel_id=1, source_target_pairs={{0,24},{8,16},{16,8},{24,0},{1,25},{9,17},{17,9},{25,1},{2,26},{10... | collective-permute-start | bytes 6152 | tf_op jit(solution)/shard_map/ppermute | solution.py:977
  387.8 15.5 %collective-permute-start.37 = (f32[8,1,64]{2,1,0:T(1,128)S(1)}, f32[8,1,64]{2,1,0:T(1,128)S(1)}, u32[]{:S(2)}, u32[]{:S(2)}) collective-permute-start(f32[8,1,64]{2,1,0:T(1,128)S(1)} %get-tuple-element.240.d0), channel_id=1, source_target_pairs={{0,16},{8,24},{16,0},{24,8},{1,17},{9,25},{17,1},{25,9},{2,18},{10... | collective-permute-start | bytes 6152 | tf_op jit(solution)/shard_map/ppermute | solution.py:977
  406.4 32.0 %collective-permute-start.43 = (bf16[64,3072]{1,0:T(8,128)(2,1)S(1)}, bf16[64,3072]{1,0:T(8,128)(2,1)S(1)}, u32[]{:S(2)}, u32[]{:S(2)}) collective-permute-start(bf16[64,3072]{1,0:T(8,128)(2,1)S(1)} %get-tuple-element.315), channel_id=1, source_target_pairs={{0,24},{8,16},{16,8},{24,0},{1,25},{9,17},{17,9},{25,1},{2,26},{10... | collective-permute-start | bytes 1179656 | tf_op jit(solution)/shard_map/ppermute | solution.py:977
  406.5 31.9 %collective-permute-start.42 = (bf16[64,3072]{1,0:T(8,128)(2,1)S(1)}, bf16[64,3072]{1,0:T(8,128)(2,1)S(1)}, u32[]{:S(2)}, u32[]{:S(2)}) collective-permute-start(bf16[64,3072]{1,0:T(8,128)(2,1)S(1)} %get-tuple-element.316), channel_id=1, source_target_pairs={{0,16},{8,24},{16,0},{24,8},{1,17},{9,25},{17,1},{25,9},{2,18},{10... | collective-permute-start | bytes 1179656 | tf_op jit(solution)/shard_map/ppermute | solution.py:977
  409.7 28.7 %collective-permute-start.41 = (bf16[64,3072]{1,0:T(8,128)(2,1)S(1)}, bf16[64,3072]{1,0:T(8,128)(2,1)S(1)}, u32[]{:S(2)}, u32[]{:S(2)}) collective-permute-start(bf16[64,3072]{1,0:T(8,128)(2,1)S(1)} %get-tuple-element.317), channel_id=1, source_target_pairs={{0,8},{8,0},{16,24},{24,16},{1,9},{9,1},{17,25},{25,17},{2,10},{10... | collective-permute-start | bytes 1179656 | tf_op jit(solution)/shard_map/ppermute | solution.py:977
  449.8 23.9 %collective-permute-start.50 = (bf16[1024,2688]{1,0:T(8,128)(2,1)}, bf16[1024,2688]{1,0:T(8,128)(2,1)}, u32[]{:S(2)}, u32[]{:S(2)}) collective-permute-start(bf16[1024,2688]{1,0:T(8,128)(2,1)} %get-tuple-element.252), channel_id=1, source_target_pairs={{0,1},{1,0},{2,3},{3,2},{4,5},{5,4},{6,7},{7,6},{8,9},{9,8},{10,11... | collective-permute-start | bytes 16515080 | tf_op jit(solution)/shard_map/ppermute | solution.py:977
  453.2 16.2 %collective-permute-start.44 = (bf16[88,1024]{1,0:T(8,128)(2,1)S(1)}, bf16[88,1024]{1,0:T(8,128)(2,1)S(1)}, u32[]{:S(2)}, u32[]{:S(2)}) collective-permute-start(bf16[88,1024]{1,0:T(8,128)(2,1)S(1)} %get-tuple-element.394), channel_id=1, source_target_pairs={{0,8},{8,0},{16,24},{24,16},{1,9},{9,1},{17,25},{25,17},{2,10},{10... | collective-permute-start | bytes 540680 | tf_op jit(solution)/shard_map/ppermute | solution.py:977
  455.1 18.6 %collective-permute-start.46 = (bf16[88,1024]{1,0:T(8,128)(2,1)S(1)}, bf16[88,1024]{1,0:T(8,128)(2,1)S(1)}, u32[]{:S(2)}, u32[]{:S(2)}) collective-permute-start(bf16[88,1024]{1,0:T(8,128)(2,1)S(1)} %get-tuple-element.396), channel_id=1, source_target_pairs={{0,24},{8,16},{16,8},{24,0},{1,25},{9,17},{17,9},{25,1},{2,26},{10... | collective-permute-start | bytes 540680 | tf_op jit(solution)/shard_map/ppermute | solution.py:977
  466.7 25.0 %collective-permute-start.48 = (bf16[256,1024]{1,0:T(8,128)(2,1)S(1)}, bf16[256,1024]{1,0:T(8,128)(2,1)S(1)}, u32[]{:S(2)}, u32[]{:S(2)}) collective-permute-start(bf16[256,1024]{1,0:T(8,128)(2,1)S(1)} %get-tuple-element.257), channel_id=1, source_target_pairs={{0,8},{8,0},{16,24},{24,16},{1,9},{9,1},{17,25},{25,17},{2,10},{10... | collective-permute-start | bytes 1572872 | tf_op jit(solution)/shard_map/ppermute | solution.py:977
  469.4 26.2 %collective-permute-start.49 = (bf16[256,1024]{1,0:T(8,128)(2,1)S(1)}, bf16[256,1024]{1,0:T(8,128)(2,1)S(1)}, u32[]{:S(2)}, u32[]{:S(2)}) collective-permute-start(bf16[256,1024]{1,0:T(8,128)(2,1)S(1)} %get-tuple-element.258), channel_id=1, source_target_pairs={{0,24},{8,16},{16,8},{24,0},{1,25},{9,17},{17,9},{25,1},{2,26},{10... | collective-permute-start | bytes 1572872 | tf_op jit(solution)/shard_map/ppermute | solution.py:977
  480.4 16.4 %collective-permute-start.51 = (bf16[128,2688]{1,0:T(8,128)(2,1)S(1)}, bf16[128,2688]{1,0:T(8,128)(2,1)S(1)}, u32[]{:S(2)}, u32[]{:S(2)}) collective-permute-start(bf16[128,2688]{1,0:T(8,128)(2,1)S(1)} %get-tuple-element.261), channel_id=1, source_target_pairs={{0,4},{4,0},{1,5},{5,1},{2,6},{6,2},{3,7},{7,3},{8,12},{12,8},{9,1... | collective-permute-start | bytes 2064392 | tf_op jit(solution)/shard_map/ppermute | solution.py:977
  481.9 16.1 %collective-permute-start.52 = (bf16[128,2688]{1,0:T(8,128)(2,1)S(1)}, bf16[128,2688]{1,0:T(8,128)(2,1)S(1)}, u32[]{:S(2)}, u32[]{:S(2)}) collective-permute-start(bf16[128,2688]{1,0:T(8,128)(2,1)S(1)} %get-tuple-element.262), channel_id=1, source_target_pairs={{0,2},{2,0},{1,3},{3,1},{4,6},{6,4},{5,7},{7,5},{8,10},{10,8},{9,1... | collective-permute-start | bytes 2064392 | tf_op jit(solution)/shard_map/ppermute | solution.py:977
  483.0 26.9 %collective-permute-start.47 = (f32[4,24,1024]{2,1,0:T(8,128)}, f32[4,24,1024]{2,1,0:T(8,128)}, u32[]{:S(2)}, u32[]{:S(2)}) collective-permute-start(f32[4,24,1024]{2,1,0:T(8,128)} %pad_maximum_fusion.22), channel_id=1, source_target_pairs={{0,1},{1,0},{2,3},{3,2},{4,5},{5,4},{6,7},{7,6},{8,9},{9,8},{10,11... | collective-permute-start | bytes 1179656 | tf_op jit(solution)/shard_map/ppermute | solution.py:977
  500.9 15.1 %collective-permute-start.54 = (bf16[256,1024]{1,0:T(8,128)(2,1)}, bf16[256,1024]{1,0:T(8,128)(2,1)S(1)}, u32[]{:S(2)}, u32[]{:S(2)}) collective-permute-start(bf16[256,1024]{1,0:T(8,128)(2,1)} %pad_maximum_fusion.16), channel_id=1, source_target_pairs={{0,8},{8,0},{16,24},{24,16},{1,9},{9,1},{17,25},{25,17},{2,10},{10... | collective-permute-start | bytes 1572872 | tf_op jit(solution)/shard_map/ppermute | solution.py:977
  503.8 30.0 %collective-permute-start.55 = (bf16[256,2688]{1,0:T(8,128)(2,1)S(1)}, bf16[256,2688]{1,0:T(8,128)(2,1)S(1)}, u32[]{:S(2)}, u32[]{:S(2)}) collective-permute-start(bf16[256,2688]{1,0:T(8,128)(2,1)S(1)} %get-tuple-element.274), channel_id=1, source_target_pairs={{0,4},{4,0},{1,5},{5,1},{2,6},{6,2},{3,7},{7,3},{8,12},{12,8},{9,1... | collective-permute-start | bytes 4128776 | tf_op jit(solution)/shard_map/ppermute | solution.py:977
  504.3 30.0 %collective-permute-start.56 = (bf16[256,2688]{1,0:T(8,128)(2,1)S(1)}, bf16[256,2688]{1,0:T(8,128)(2,1)S(1)}, u32[]{:S(2)}, u32[]{:S(2)}) collective-permute-start(bf16[256,2688]{1,0:T(8,128)(2,1)S(1)} %get-tuple-element.275), channel_id=1, source_target_pairs={{0,2},{2,0},{1,3},{3,1},{4,6},{6,4},{5,7},{7,5},{8,10},{10,8},{9,1... | collective-permute-start | bytes 4128776 | tf_op jit(solution)/shard_map/ppermute | solution.py:977
  507.1 22.4 %collective-permute-start.53 = (bf16[256,1024]{1,0:T(8,128)(2,1)S(1)}, bf16[256,1024]{1,0:T(8,128)(2,1)S(1)}, u32[]{:S(2)}, u32[]{:S(2)}) collective-permute-start(bf16[256,1024]{1,0:T(8,128)(2,1)S(1)} %pad_maximum_fusion.15), channel_id=1, source_target_pairs={{0,24},{8,16},{16,8},{24,0},{1,25},{9,17},{17,9},{25,1},{2,26},{10... | collective-permute-start | bytes 1572872 | tf_op jit(solution)/shard_map/ppermute | solution.py:977
  538.9 25.1 %collective-permute-start.57 = (bf16[64,2688]{1,0:T(8,128)(2,1)}, bf16[64,2688]{1,0:T(8,128)(2,1)}, u32[]{:S(2)}, u32[]{:S(2)}) collective-permute-start(bf16[64,2688]{1,0:T(8,128)(2,1)} %get-tuple-element.279), channel_id=1, source_target_pairs={{0,8},{8,0},{16,24},{24,16},{1,9},{9,1},{17,25},{25,17},{2,10},{10... | collective-permute-start | bytes 1032200 | tf_op jit(solution)/shard_map/ppermute | solution.py:977
  540.6 23.4 %collective-permute-start.58 = (bf16[64,2688]{1,0:T(8,128)(2,1)}, bf16[64,2688]{1,0:T(8,128)(2,1)}, u32[]{:S(2)}, u32[]{:S(2)}) collective-permute-start(bf16[64,2688]{1,0:T(8,128)(2,1)} %get-tuple-element.280), channel_id=1, source_target_pairs={{0,16},{8,24},{16,0},{24,8},{1,17},{9,25},{17,1},{25,9},{2,18},{10... | collective-permute-start | bytes 1032200 | tf_op jit(solution)/shard_map/ppermute | solution.py:977
  541.0 28.5 %collective-permute-start.59 = (bf16[64,2688]{1,0:T(8,128)(2,1)}, bf16[64,2688]{1,0:T(8,128)(2,1)}, u32[]{:S(2)}, u32[]{:S(2)}) collective-permute-start(bf16[64,2688]{1,0:T(8,128)(2,1)} %get-tuple-element.281), channel_id=1, source_target_pairs={{0,24},{8,16},{16,8},{24,0},{1,25},{9,17},{17,9},{25,1},{2,26},{10... | collective-permute-start | bytes 1032200 | tf_op jit(solution)/shard_map/ppermute | solution.py:977
  (123 other events, 1584.3 us)
Sparse Core Ops, SparseCore 0:
  55.6 65.6 all-gather.3
  123.8 36.7 all-gather.5
  181.2 72.6 all-gather.7
  293.4 93.3 reduce-scatter.4
  397.7 50.8 reduce-scatter.2
